TPU v7x, 32 devices: a whole 2x2x4 slice. The times are simulated.
32 devices in a mesh: parts: 2 (over y), row: 4 (over z), col: 4 (over x, core).
Axes of the slice: x: 2, y: 2, z: 4, core: 2. Of those that a mesh axis runs over, the one named last changes fastest.
Arguments:
- pair_act: bfloat16 [64, 32, 128], P(('parts', 'row'), 'col'), parts along dimension 0, may hold values from -6 to 6
- pair_mask: int32 [64, 32], P(('parts', 'row'), 'col'), parts along dimension 0, may hold values 0 or 1
- crop_length: int32 [2], P('parts'), parts along dimension 0, may hold values from 16 to 32
- weights: bfloat16 [6, 128, 128], replicated, may hold values from -0.5 to 0.5
- in_gain: float32 [128], replicated, may hold values from 0.25 to 1.75
- out_gain: float32 [128], replicated, may hold values from 0.25 to 1.75
- cotangent: bfloat16 [64, 32, 128], P(('parts', 'row'), 'col'), parts along dimension 0, may hold values from -6 to 6
Outputs:
- update: bfloat16 [64, 32, 128], P(('parts', 'row'), 'col'), parts along dimension 0
- pair_grad: bfloat16 [64, 32, 128], P(('parts', 'row'), 'col'), parts along dimension 0
- weight_grad: float32 [12, 128, 128], P('parts'), parts along dimension 0
There are 2 independent parts, one for each index of `parts`. A program takes and returns all parts, laid end to end along the dimension named above; an argument that names none is the same for every part. Nothing has to cross between parts.
All inputs are finite; a program needn't handle non-finite values. No bound on the sum of `pair_mask` on one device may be relied on, other than what follows from the above.
Results may differ from a plain program's by a relative error of at most 0.014.
Values may be sent and summed in bfloat16 or wider, within the bound.
No kernel may reach another device: no remote copies, remote signals or barrier semaphores. Data moves between devices by JAX's collectives and lax.ppermute only.
A program may use at most 64 MiB of HBM per device.

v0:
```python
import jax
import jax.numpy as jnp
from jax import lax
from jax.sharding import PartitionSpec as P


def normalize(values):
    average = jnp.mean(values, axis=-1, keepdims=True)
    centered = values - average
    inverse = lax.rsqrt(jnp.mean(centered * centered, axis=-1, keepdims=True) + 1e-05)
    return (centered * inverse, inverse)


def norm_back(grad_hat, values_hat, inverse):
    first = jnp.mean(grad_hat, axis=-1, keepdims=True)
    second = jnp.mean(grad_hat * values_hat, axis=-1, keepdims=True)
    return (grad_hat - first - values_hat * second) * inverse


def gate_back(grad_act, proj_value, proj_gate, keep_mask):
    gate_sig = jax.nn.sigmoid(proj_gate)
    masked = grad_act * keep_mask
    grad_value = (masked * gate_sig).astype(jnp.bfloat16)
    grad_gate = (masked * proj_value * gate_sig * (1.0 - gate_sig)).astype(jnp.bfloat16)
    return (grad_value, grad_gate)


def body(pair_act, pair_mask, crop_length, weights, in_gain, out_gain, cotangent):
    tile_rows, tile_cols, channels = pair_act.shape
    residues = tile_rows * lax.axis_size("row")
    row_pos = lax.axis_index("row") * tile_rows + jnp.arange(tile_rows, dtype=jnp.int32)
    col_pos = lax.axis_index("col") * tile_cols + jnp.arange(tile_cols, dtype=jnp.int32)
    row_in = (row_pos < crop_length[0]).astype(jnp.float32)
    col_in = (col_pos < crop_length[0]).astype(jnp.float32)
    keep_mask = (pair_mask.astype(jnp.float32) * row_in[:, None] * col_in[None, :])[:, :, None]
    z_hat, z_inverse = normalize(pair_act.astype(jnp.float32))
    normed = (z_hat * in_gain).astype(jnp.bfloat16)
    flat_norm = normed.reshape(tile_rows * tile_cols, channels)
    projections = jnp.einsum(
        "pc,scd->spd", flat_norm, weights[:5], preferred_element_type=jnp.float32
    )
    projections = projections.reshape(5, tile_rows, tile_cols, channels)
    left_act = (jax.nn.sigmoid(projections[1]) * projections[0] * keep_mask).astype(jnp.bfloat16)
    right_act = (jax.nn.sigmoid(projections[3]) * projections[2] * keep_mask).astype(jnp.bfloat16)
    partial_value = jnp.einsum(
        "ikh,jkh->ijh",
        left_act,
        lax.all_gather(right_act, "row", axis=0, tiled=True),
        preferred_element_type=jnp.float32,
    )
    tri_sum = lax.psum_scatter(
        partial_value.astype(jnp.bfloat16), "col", scatter_dimension=1, tiled=True
    ).astype(jnp.float32)
    x_hat, x_inverse = normalize(tri_sum)
    normed_out = (x_hat * out_gain).astype(jnp.bfloat16)
    flat_out = normed_out.reshape(tile_rows * tile_cols, channels)
    update_lin = jnp.dot(flat_out, weights[5], preferred_element_type=jnp.float32)
    update_lin = update_lin.reshape(tile_rows, tile_cols, channels)
    out_gate = jax.nn.sigmoid(projections[4])
    update = (out_gate * update_lin).astype(jnp.bfloat16)
    cot_value = cotangent.astype(jnp.float32)
    grad_lin = (cot_value * out_gate).astype(jnp.bfloat16)
    grad_gate_out = (cot_value * update_lin * out_gate * (1.0 - out_gate)).astype(jnp.bfloat16)
    flat_lin = grad_lin.reshape(tile_rows * tile_cols, channels)
    grad_norm_out = jnp.einsum(
        "pd,cd->pc", flat_lin, weights[5], preferred_element_type=jnp.float32
    )
    grad_norm_out = grad_norm_out.reshape(tile_rows, tile_cols, channels)
    grad_tri = norm_back(grad_norm_out * out_gain, x_hat, x_inverse).astype(jnp.bfloat16)
    grad_full = lax.all_gather(grad_tri, "col", axis=1, tiled=True)
    grad_slab = grad_full
    grad_left = jnp.einsum(
        "ijh,jkh->ikh",
        grad_slab,
        lax.all_gather(right_act, "row", axis=0, tiled=True),
        preferred_element_type=jnp.float32,
    )
    grad_slab = grad_full
    grad_right = lax.psum_scatter(
        jnp.einsum("ijh,ikh->jkh", grad_slab, left_act, preferred_element_type=jnp.float32).astype(
            jnp.bfloat16
        ),
        "row",
        scatter_dimension=0,
        tiled=True,
    ).astype(jnp.float32)
    grad_pa, grad_ga = gate_back(grad_left, projections[0], projections[1], keep_mask)
    grad_pb, grad_gb = gate_back(grad_right, projections[2], projections[3], keep_mask)
    grads = jnp.stack([grad_pa, grad_ga, grad_pb, grad_gb, grad_gate_out]).reshape(
        5, tile_rows * tile_cols, channels
    )
    grad_normed = jnp.einsum("spd,scd->pc", grads, weights[:5], preferred_element_type=jnp.float32)
    grad_normed = grad_normed.reshape(tile_rows, tile_cols, channels)
    pair_grad = norm_back(grad_normed * in_gain, z_hat, z_inverse).astype(jnp.bfloat16)
    local_in = jnp.einsum("pc,spd->scd", flat_norm, grads, preferred_element_type=jnp.float32)
    local_out = jnp.dot(flat_out.T, flat_lin, preferred_element_type=jnp.float32)
    local_grads = jnp.concatenate([local_in, local_out[None]], axis=0) / residues
    weight_grad = lax.psum(local_grads, ("row", "col"))
    return (update, pair_grad, weight_grad)


def solution(mesh):
    return jax.shard_map(
        body,
        mesh=mesh,
        in_specs=(
            P(("parts", "row"), "col", None),
            P(("parts", "row"), "col"),
            P("parts"),
            P(),
            P(),
            P(),
            P(("parts", "row"), "col", None),
        ),
        out_specs=(
            P(("parts", "row"), "col", None),
            P(("parts", "row"), "col", None),
            P("parts", None, None),
        ),
        check_vma=False,
    )
```

profile of v0, /device:TPU:0, one launch (start us, length us, event | category | flops | bytes accessed | tf_op | source)
XLA Modules:
  0.0 177.3 jit_solution(13153082537720262800)
XLA Ops:
  7.2 0.0 reduce-scatter.3.cloned.1.call-start
  7.9 0.0 copy-done
  7.9 0.1 convert_reduce_fusion.1
  8.0 0.2 fusion.28
  8.1 0.0 copy-start.5
  8.2 0.7 copy-done.5
  8.8 0.1 multiply_multiply_fusion
  8.9 0.6 copy-done.6
  9.5 1.1 convolution_bitcast_fusion.1
  10.6 0.1 multiply_convert_fusion.5
  10.7 14.9 %all_gather.7 = bf16[32,8,128]{2,1,0:T(8,128)(2,1)S(1)} all-gather(bf16[8,8,128]{2,1,0:T(8,128)(2,1)S(1)} %get-tuple-element.33), channel_id=1, replica_groups=mesh['parts'=2,'row'=4,'col'=4] {'row'}, dimensions={0}, use_global_device_ids=true | all-gather | bytes 81920 | tf_op jit(solution)/shard_map/all_gather | solution.py:48
  25.6 0.2 copy.136
  25.8 0.2 copy.139
  26.0 0.4 fusion
  26.4 0.0 copy-start.2
  26.4 0.8 copy.133
  27.2 0.0 reduce-scatter.3.cloned.1.call-update
  27.2 0.0 reduce-scatter.5.cloned.1.call-start
  27.3 20.6 %reduce-scatter.3.cloned.1.call-done = bf16[8,8,128]{2,0,1:T(8,128)(2,1)} async-done(((bf16[8,32,128]{2,0,1:T(8,128)(2,1)}), bf16[8,8,128]{2,0,1:T(8,128)(2,1)}) %reduce-scatter.3.cloned.1.call-update) | async-done | bytes 16400 | tf_op jit(solution)/shard_map/reduce_scatter | solution.py:51
  47.9 0.9 convert_reduce_fusion
  48.8 0.0 copy-start.4
  48.8 0.2 fusion.22
  49.0 0.5 copy-done.4
  49.5 0.1 copy-done.7
  49.6 0.2 fusion.61
  49.9 0.1 fusion.21
  50.0 5.2 %all_gather.8 = bf16[8,32,128]{2,0,1:T(8,128)(2,1)S(1)} all-gather(bf16[8,8,128]{2,0,1:T(8,128)(2,1)S(1)} %copy.135), channel_id=1, replica_groups=mesh['parts'=2,'row'=4,'col'=4] {'col'}, dimensions={1}, use_global_device_ids=true | all-gather | bytes 81920 | tf_op jit(solution)/shard_map/all_gather | solution.py:70
  55.2 0.2 copy.137
  55.4 0.3 fusion.1
  55.7 0.3 fusion.63
  56.0 0.8 copy.141
  56.8 0.2 copy.138
  57.0 0.0 reduce-scatter.5.cloned.1.call-update
  57.1 0.0 all-reduce.2.cloned.1.call-start
  57.1 0.1 constant_dynamic-update-slice_fusion.9
  57.2 0.1 constant_dynamic-update-slice_fusion.8
  57.3 0.8 multiply_convert_fusion.4
  58.1 0.2 convolution_bitcast_fusion.2
  58.4 17.9 %reduce-scatter.5.cloned.1.call-done = bf16[8,8,128]{2,1,0:T(8,128)(2,1)} async-done(((bf16[32,8,128]{2,1,0:T(8,128)(2,1)}), bf16[8,8,128]{2,1,0:T(8,128)(2,1)}) %reduce-scatter.5.cloned.1.call-update) | async-done | bytes 16400 | tf_op jit(solution)/shard_map/reduce_scatter | solution.py:79
  76.2 0.9 constant_dynamic-update-slice_fusion.7
  77.1 0.1 constant_dynamic-update-slice_fusion.6
  77.3 0.3 fusion.60
  77.6 0.3 convolution_bitcast_fusion
  77.9 0.8 maximum_multiply_fusion
  78.7 0.0 all-reduce.2.cloned.1.call-update
  78.7 0.7 fusion.27
  79.4 89.5 %all-reduce.2.cloned.1.call-done = f32[6,128,128]{1,2,0:T(8,128)} async-done(((f32[6,128,128]{1,2,0:T(8,128)}), f32[6,128,128]{1,2,0:T(8,128)}) %all-reduce.2.cloned.1.call-update) | async-done | bytes 393232 | tf_op jit(solution)/shard_map/psum | solution.py:98
  168.9 1.9 %copy.143 = f32[6,128,128]{2,1,0:T(8,128)} copy(f32[6,128,128]{1,2,0:T(8,128)} %all-reduce.2.cloned.1.call-done) | data formatting | bytes 786432
  (24 shorter events, 0.1 us)
Async XLA Ops:
  7.2 0.7 copy-start
  7.2 40.7 %reduce-scatter.3.cloned.1.call-start = ((), (), s32[]{:S(2)}) async-start(), calls=%async_computation.2 | async-start | bytes 81920 | tf_op jit(solution)/shard_map/reduce_scatter | solution.py:51
  8.1 0.7 copy-start.5
  8.8 0.7 copy-start.6
  26.4 22.6 %copy-start.2 = (bf16[6,128,128]{2,1,0:T(8,128)(2,1)S(1)}, bf16[6,128,128]{2,1,0:T(8,128)(2,1)}, u32[]{:S(2)}) copy-start(bf16[6,128,128]{2,1,0:T(8,128)(2,1)} %param.10) | copy-start | bytes 589828
  27.2 49.0 %reduce-scatter.5.cloned.1.call-start = ((), (), s32[]{:S(2)}) async-start(), calls=%async_computation.3 | async-start | bytes 81920 | tf_op jit(solution)/shard_map/reduce_scatter | solution.py:79
  47.9 0.9 copy-start.1
  48.8 0.7 copy-start.4
  48.9 0.7 copy-start.7
  57.1 111.8 %all-reduce.2.cloned.1.call-start = ((), (), s32[]{:S(2)}) async-start(), calls=%async_computation.4 | async-start | bytes 786432 | tf_op jit(solution)/shard_map/psum | solution.py:98
  76.2 0.9 copy-start.3
Sparse Core Ops, SparseCore 0:
  27.3 20.5 reduce-scatter.2
  57.2 18.9 reduce-scatter.4
  80.1 88.6 all-reduce.1
where the time goes:
time: 178 us; the launch traced here: 177 us
  waiting for transfers between devices  128 us (72%)
  blocking collectives  20.1 us (11%)
  between operations  14.6 us (8%)
  local copies, waits for them, and re-layouts  6.31 us (4%)
  other arithmetic  4.21 us (2%)
  matrix products  3.87 us (2%)
    psum x1, waiting for transfers between devices, body(): weight_grad = lax.psum(local_grads, ('row', 'col'))  89.5 us
    reduce_scatter x1, waiting for transfers between devices, body(): lax.psum_scatter(partial_value.astype(jnp.bfloat16), 'col', scatter_dimen...  20.6 us
    reduce_scatter x1, waiting for transfers between devices, body(): lax.psum_scatter(jnp.einsum('ijh,ikh->jkh', grad_slab, left_act, preferre...  17.9 us
    all_gather x1, blocking collectives, body(): lax.all_gather(right_act, 'row', axis=0, tiled=True)  14.9 us
    all_gather x1, blocking collectives, body(): grad_full = lax.all_gather(grad_tri, 'col', axis=1, tiled=True)  5.25 us
    unnamed x21, local copies, waits for them, and re-layouts  3.86 us
  transfers between devices with their start and end apart: 3, of which 3 were waited for; matrix products, arithmetic and copies ran while one was open for 1% of the time, Pallas kernels for 0%

commit v1 on v0

--- a/solution.py
+++ b/solution.py
@@ -1,7 +1,14 @@
+import functools
+
 import jax
 import jax.numpy as jnp
 from jax import lax
+from jax.experimental import pallas as pl
+from jax.experimental.pallas import tpu as pltpu
 from jax.sharding import PartitionSpec as P
+
+SUB = 8
+EPS = 1e-05
 
 
 def normalize(values):
@@ -25,7 +32,7 @@
     return (grad_value, grad_gate)
 
 
-def body(pair_act, pair_mask, crop_length, weights, in_gain, out_gain, cotangent):
+def spread_body(pair_act, pair_mask, crop_length, weights, in_gain, out_gain, cotangent):
     tile_rows, tile_cols, channels = pair_act.shape
     residues = tile_rows * lax.axis_size("row")
     row_pos = lax.axis_index("row") * tile_rows + jnp.arange(tile_rows, dtype=jnp.int32)
@@ -99,9 +106,211 @@
     return (update, pair_grad, weight_grad)
 
 
+def pack_kernel(crop_ref, act_ref, mask_ref, cot_ref, gain_ref, out_ref):
+    tile_rows, tile_cols, channels = act_ref.shape
+    pairs = tile_rows * tile_cols
+    z_hat, _ = normalize(act_ref[...].astype(jnp.float32).reshape(pairs, channels))
+    out_ref[0:pairs] = (z_hat * gain_ref[...]).astype(jnp.bfloat16)
+    out_ref[pairs : 2 * pairs] = cot_ref[...].reshape(pairs, channels)
+    row_at = lax.axis_index("row") * tile_rows
+    col_at = lax.axis_index("col") * tile_cols
+    rows = row_at + lax.broadcasted_iota(jnp.int32, (tile_rows, tile_cols), 0)
+    cols = col_at + lax.broadcasted_iota(jnp.int32, (tile_rows, tile_cols), 1)
+    inside = (rows < crop_ref[0]) & (cols < crop_ref[0])
+    keep = jnp.where(inside, mask_ref[...], 0).astype(jnp.float32)
+    wide = jnp.concatenate([keep, jnp.zeros((tile_rows, channels - tile_cols), jnp.float32)], axis=1)
+    tall = jnp.concatenate([wide, jnp.zeros((channels - tile_rows, channels), jnp.float32)], axis=0)
+    flipped = tall.T
+    extra = out_ref.shape[0] - 2 * pairs
+    out_ref[2 * pairs :] = flipped[0:extra].astype(jnp.bfloat16)
+
+
+def triangle(residues, vector_at, scalar_at, store_at):
+    groups = residues // SUB
+
+    def block(a, _):
+        def step(q, totals):
+            totals = list(totals)
+            for inner in range(SUB):
+                m = q * SUB + inner
+                vectors = [vector_at(m, g) for g in range(groups)]
+                for lane in range(SUB):
+                    factor = scalar_at(a * SUB + lane, m)
+                    for g in range(groups):
+                        at = lane * groups + g
+                        totals[at] = totals[at] + factor * vectors[g]
+            return tuple(totals)
+
+        zero = jnp.zeros((SUB, 128), jnp.float32)
+        totals = lax.fori_loop(0, groups, step, (zero,) * (SUB * groups))
+        for lane in range(SUB):
+            for g in range(groups):
+                store_at(a * SUB + lane, g, totals[lane * groups + g])
+        return 0
+
+    lax.fori_loop(0, groups, block, 0)
+
+
+def part_kernel(
+    n_row, n_col, all_ref, act_ref, weights_ref, in_gain_ref, out_gain_ref,
+    update_ref, pair_grad_ref, weight_grad_ref,
+    proj_ref, left_ref, right_ref, keep_ref, tri_ref, lin_ref, gate_ref, hat_ref, upd_ref, d_ref,
+):
+    tile_rows, tile_cols, channels = act_ref.shape
+    tile = tile_rows * tile_cols
+    residues = n_row * tile_rows
+    pairs = residues * residues
+    blocks = n_row * n_col
+    chunk = 4 * tile
+    bf16, f32 = jnp.bfloat16, jnp.float32
+
+    def row_of(i, k):
+        return ((i // tile_rows * n_col + k // tile_cols) * tile_rows + i % tile_rows) * tile_cols + k % tile_cols
+
+    def vector(ref, i, k):
+        return ref[pl.ds(pl.multiple_of(row_of(i, k), SUB), SUB), :]
+
+    def spread(ref, i, k):
+        return jnp.broadcast_to(ref[pl.ds(row_of(i, k), 1), :], (SUB, channels))
+
+    def chunks():
+        return [(at, slice(at, at + chunk)) for at in range(0, pairs, chunk)]
+
+    def normed_rows(at):
+        first = at // tile
+        return all_ref[first : first + chunk // tile, 0:tile, :].reshape(chunk, channels)
+
+    def cot_rows(at):
+        first = at // tile
+        return all_ref[first : first + chunk // tile, tile : 2 * tile, :].reshape(chunk, channels)
+
+    for at, rows in chunks():
+        normed = normed_rows(at)
+        for s in range(5):
+            proj_ref[s, rows, :] = jnp.dot(normed, weights_ref[s], preferred_element_type=f32)
+        for b in range(at // tile, (at + chunk) // tile):
+            keep = all_ref[b, 2 * tile : 2 * tile + 16, :].astype(f32)[0:tile_cols]
+            for ii in range(tile_rows):
+                spot = (b * tile_rows + ii) * tile_cols
+                keep_ref[spot : spot + tile_cols, :] = jnp.broadcast_to(keep[:, ii : ii + 1], (tile_cols, channels))
+        kept = keep_ref[rows, :]
+        left = jax.nn.sigmoid(proj_ref[1, rows, :]) * proj_ref[0, rows, :] * kept
+        right = jax.nn.sigmoid(proj_ref[3, rows, :]) * proj_ref[2, rows, :] * kept
+        left_ref[rows, :] = left.astype(bf16).astype(f32)
+        right_ref[rows, :] = right.astype(bf16).astype(f32)
+
+    def right_flipped(k, g):
+        return right_ref[pl.ds(row_of(g * SUB, k), SUB, stride=tile_cols), :]
+
+    def keep_tri(i, g, total):
+        tri_ref[pl.ds(pl.multiple_of(row_of(i, g * SUB), SUB), SUB), :] = total
+
+    triangle(residues, right_flipped, lambda i, k: spread(left_ref, i, k), keep_tri)
+
+    out_gain = out_gain_ref[...]
+    for at, rows in chunks():
+        x_hat, inverse = normalize(tri_ref[rows, :])
+        normed_out = (x_hat * out_gain).astype(bf16)
+        hat_ref[rows, :] = normed_out
+        lin = jnp.dot(normed_out, weights_ref[5], preferred_element_type=f32)
+        out_gate = jax.nn.sigmoid(proj_ref[4, rows, :])
+        cot = cot_rows(at).astype(f32)
+        upd_ref[rows, :] = out_gate * lin
+        grad_lin = (cot * out_gate).astype(bf16)
+        lin_ref[rows, :] = grad_lin
+        d_ref[4, rows, :] = (cot * lin * out_gate * (1.0 - out_gate)).astype(bf16)
+        back = lax.dot_general(grad_lin, weights_ref[5], (((1,), (1,)), ((), ())), preferred_element_type=f32)
+        tri_ref[rows, :] = norm_back(back * out_gain, x_hat, inverse).astype(bf16).astype(f32)
+
+    def keep_left(i, g, total):
+        gate_ref[0, pl.ds(pl.multiple_of(row_of(i, g * SUB), SUB), SUB), :] = total
+
+    def keep_right(j, g, total):
+        gate_ref[1, pl.ds(pl.multiple_of(row_of(j, g * SUB), SUB), SUB), :] = total
+
+    triangle(residues, lambda j, g: vector(right_ref, j, g * SUB), lambda i, j: spread(tri_ref, i, j), keep_left)
+    triangle(residues, lambda i, g: vector(left_ref, i, g * SUB), lambda j, i: spread(tri_ref, i, j), keep_right)
+
+    for at, rows in chunks():
+        kept = keep_ref[rows, :]
+        for side in range(2):
+            value, gate = gate_back(gate_ref[side, rows, :], proj_ref[2 * side, rows, :], proj_ref[2 * side + 1, rows, :], kept)
+            d_ref[2 * side, rows, :] = value
+            d_ref[2 * side + 1, rows, :] = gate
+
+    normed_all = all_ref[:, 0:tile, :].reshape(pairs, channels)
+    for s in range(5):
+        weight_grad_ref[s] = lax.dot_general(
+            normed_all, d_ref[s], (((0,), (0,)), ((), ())), preferred_element_type=f32
+        ) / residues
+    weight_grad_ref[5] = lax.dot_general(
+        hat_ref[...], lin_ref[...], (((0,), (0,)), ((), ())), preferred_element_type=f32
+    ) / residues
+
+    mine = pl.multiple_of((lax.axis_index("row") * n_col + lax.axis_index("col")) * tile, tile)
+    own = pl.ds(mine, tile)
+    update_ref[...] = upd_ref[own, :].astype(bf16).reshape(update_ref.shape)
+    total = jnp.zeros((tile, channels), f32)
+    for s in range(5):
+        total = total + lax.dot_general(d_ref[s, own, :], weights_ref[s], (((1,), (1,)), ((), ())), preferred_element_type=f32)
+    z_hat, z_inverse = normalize(act_ref[...].astype(f32).reshape(tile, channels))
+    grad = norm_back(total * in_gain_ref[...], z_hat, z_inverse)
+    pair_grad_ref[...] = grad.astype(bf16).reshape(pair_grad_ref.shape)
+
+
+def gathered_body(n_row, n_col, pair_act, pair_mask, crop_length, weights, in_gain, out_gain, cotangent):
+    tile_rows, tile_cols, channels = pair_act.shape
+    tile = tile_rows * tile_cols
+    pairs = tile * n_row * n_col
+    vmem = pl.BlockSpec(memory_space=pltpu.VMEM)
+    smem = pl.BlockSpec(memory_space=pltpu.SMEM)
+    packed = pl.pallas_call(
+        pack_kernel,
+        name="pack",
+        out_shape=jax.ShapeDtypeStruct((2 * tile + 16, channels), jnp.bfloat16),
+        in_specs=[smem, vmem, vmem, vmem, vmem],
+        out_specs=vmem,
+    )(crop_length, pair_act, pair_mask, cotangent, in_gain.reshape(1, channels))
+    everyone = lax.all_gather(packed, ("row", "col"), axis=0)
+    f32, bf16 = jnp.float32, jnp.bfloat16
+    return pl.pallas_call(
+        functools.partial(part_kernel, n_row, n_col),
+        name="part",
+        out_shape=(
+            jax.ShapeDtypeStruct(pair_act.shape, bf16),
+            jax.ShapeDtypeStruct(pair_act.shape, bf16),
+            jax.ShapeDtypeStruct(weights.shape, f32),
+        ),
+        in_specs=[vmem] * 5,
+        out_specs=(vmem, vmem, vmem),
+        scratch_shapes=[
+            pltpu.VMEM((5, pairs, channels), f32),
+            pltpu.VMEM((pairs, channels), f32),
+            pltpu.VMEM((pairs, channels), f32),
+            pltpu.VMEM((pairs, channels), f32),
+            pltpu.VMEM((pairs, channels), f32),
+            pltpu.VMEM((pairs, channels), bf16),
+            pltpu.VMEM((2, pairs, channels), f32),
+            pltpu.VMEM((pairs, channels), bf16),
+            pltpu.VMEM((pairs, channels), f32),
+            pltpu.VMEM((5, pairs, channels), bf16),
+        ],
+        compiler_params=pltpu.CompilerParams(vmem_limit_bytes=32 * 1024 * 1024),
+    )(everyone, pair_act, weights, in_gain.reshape(1, channels), out_gain.reshape(1, channels))
+
+
+def body(n_row, n_col, pair_act, *others):
+    tile_rows, tile_cols, channels = pair_act.shape
+    pairs = tile_rows * n_row * tile_cols * n_col
+    small = pairs * channels * 4 <= 1024 * 1024
+    if small and channels == 128 and tile_rows % SUB == 0 and tile_cols % SUB == 0 and tile_cols <= 16:
+        return gathered_body(n_row, n_col, pair_act, *others)
+    return spread_body(pair_act, *others)
+
+
 def solution(mesh):
     return jax.shard_map(
-        body,
+        functools.partial(body, mesh.shape["row"], mesh.shape["col"]),
         mesh=mesh,
         in_specs=(
             P(("parts", "row"), "col", None),

time: 178 us -> 42.9 us (0.24)
  waiting for transfers between devices: 128 us -> 0 us
  Pallas kernels: 0 us -> 15.5 us
  between operations: 14.6 us -> 1.29 us
  local copies, waits for them, and re-layouts: 6.31 us -> 0.67 us
  blocking collectives: 20.1 us -> 25.2 us
  other arithmetic: 4.21 us -> 0 us
  matrix products: 3.87 us -> 0 us
    psum x1 -> x0, waiting for transfers between devices: 89.5 us -> none  [body(): weight_grad = lax.psum(local_grads, ('row', 'col'))]
    reduce_scatter x2 -> x0, waiting for transfers between devices: 38.5 us -> none  [the longest x1 20.6 us: body(): lax.psum_scatter(partial_value.astype(jnp.bfloat16), 'col', scatter_dimen...]
    pallas_call x0 -> x2, Pallas kernels: none -> 15.5 us  [the longest x1 14 us: gathered_body(): pl.pallas_call(functools.partial(part_kernel, n_row, n_col), name='part',...]
    all_gather x2 -> x1, blocking collectives: 20.1 us -> 25.2 us  [gathered_body(): everyone = lax.all_gather(packed, ('row', 'col'), axis=0)]
    dot_general x9 -> x0, matrix products: 3.87 us -> none  [the longest x1 1.12 us: body(): jnp.einsum('pc,scd->spd', flat_norm, weights[:5], preferred_element_type=...]
    unnamed x21 -> x8, local copies, waits for them, and re-layouts: 3.86 us -> 0.67 us
    convert_element_type x4 -> x0, local copies, waits for them, and re-layouts: 1.85 us -> none  [the longest x1 0.83 us: body(): jnp.einsum('ijh,ikh->jkh', grad_slab, left_act, preferred_element_type=jn...]
  transfers between devices with their start and end apart: 3 -> 0, of which waited for: 3 -> 0; matrix products, arithmetic and copies ran while one was open for 1% -> 0% of each run, Pallas kernels for 0% -> 0%
where the time goes in v1:
time: 42.9 us; the launch traced here: 42.7 us
  blocking collectives  25.2 us (59%)
  Pallas kernels  15.5 us (36%)
  between operations  1.29 us (3%)
  local copies, waits for them, and re-layouts  0.67 us (2%)
    all_gather x1, blocking collectives, gathered_body(): everyone = lax.all_gather(packed, ('row', 'col'), axis=0)  25.2 us
    pallas_call x1, Pallas kernels, gathered_body(): pl.pallas_call(functools.partial(part_kernel, n_row, n_col), name='part',...  14 us
    pallas_call x1, Pallas kernels, gathered_body(): pl.pallas_call(pack_kernel, name='pack', out_shape=jax.ShapeDtypeStruct((...  1.55 us

profile of v1, /device:TPU:0, one launch (start us, length us, event | category | flops | bytes accessed | tf_op | source)
XLA Modules:
  0.0 42.7 jit_solution(4270749135977513446)
XLA Ops:
  1.3 1.6 %pack.1 = bf16[144,128]{1,0:T(8,128)(2,1)} custom-call(s32[1]{0:T(128)S(6)} %copy.10.crop_ref, bf16[8,8,128]{2,1,0:T(8,128)(2,1)} %act_ref.3, s32[8,8]{1,0:T(8,128)} %mask_ref.1, bf16[8,8,128]{2,1,0:T(8,128)(2,1)} %cot_ref.1, f32[1,128]{1,0:T(1,128)} %bitcast.4), custom_call_target="tpu_custom_call" | custom-call | tf_op jit(solution)/shard_map/pack/pallas_call | solution.py:267
  2.8 0.0 copy-start
  2.8 0.0 copy-start.1
  2.8 25.2 %all-gather = bf16[2304,128]{1,0:T(8,128)(2,1)S(1)} all-gather(bf16[144,128]{1,0:T(8,128)(2,1)} %pack.1), channel_id=2, replica_groups=mesh['parts'=2,'row'=4,'col'=4] {'row','col'}, dimensions={0}, use_global_device_ids=true | all-gather | bytes 626688 | tf_op jit(solution)/shard_map/all_gather | solution.py:274
  28.0 0.0 copy-start.2
  28.0 0.0 copy-start.3
  28.0 0.0 copy-done
  28.0 0.0 copy-done.1
  28.0 0.6 %copy-done.2 = f32[128]{0:T(128)S(1)} copy-done((f32[128]{0:T(128)S(1)}, f32[128]{0:T(128)}, u32[]{:S(2)}) %copy-start.2) | copy-done | bytes 536
  28.7 0.0 copy-done.3
  28.7 14.0 %part.1 = (bf16[8,8,128]{2,1,0:T(8,128)(2,1)}, bf16[8,8,128]{2,1,0:T(8,128)(2,1)}, f32[6,128,128]{2,1,0:T(8,128)}) custom-call(bf16[16,144,128]{2,1,0:T(8,128)(2,1)S(1)} %bitcast.3, bf16[8,8,128]{2,1,0:T(8,128)(2,1)S(1)} %copy-done.1, bf16[6,128,128]{2,1,0:T(8,128)(2,1)S(1)} %copy-done, f32[1,128]{1,0:T(1,128)S(1)} %bitcast.5, f32[1,128]{1,0:T(1,128)S(1)} %bitcast.6), custom_call_target="tpu_custom_call" | custom-call | tf_op jit(solution)/shard_map/part/pallas_call | solution.py:276
Async XLA Ops:
  2.8 25.2 %copy-start = (bf16[6,128,128]{2,1,0:T(8,128)(2,1)S(1)}, bf16[6,128,128]{2,1,0:T(8,128)(2,1)}, u32[]{:S(2)}) copy-start(bf16[6,128,128]{2,1,0:T(8,128)(2,1)} %weights_ref.1) | copy-start | bytes 589828
  2.8 25.2 %copy-start.1 = (bf16[8,8,128]{2,1,0:T(8,128)(2,1)S(1)}, bf16[8,8,128]{2,1,0:T(8,128)(2,1)}, u32[]{:S(2)}) copy-start(bf16[8,8,128]{2,1,0:T(8,128)(2,1)} %act_ref.3) | copy-start | bytes 49156
  28.0 0.7 %copy-start.2 = (f32[128]{0:T(128)S(1)}, f32[128]{0:T(128)}, u32[]{:S(2)}) copy-start(f32[128]{0:T(128)} %param.11) | copy-start | bytes 1540
  28.0 0.7 %copy-start.3 = (f32[128]{0:T(128)S(1)}, f32[128]{0:T(128)}, u32[]{:S(2)}) copy-start(f32[128]{0:T(128)} %param.12) | copy-start | bytes 1540

commit v2 on v1

--- a/solution.py
+++ b/solution.py
@@ -125,34 +125,39 @@
     out_ref[2 * pairs :] = flipped[0:extra].astype(jnp.bfloat16)
 
 
-def triangle(residues, vector_at, scalar_at, store_at):
-    groups = residues // SUB
-
+def triangle(groups, vectors_at, factors_at, store_at):
     def block(a, _):
         def step(q, totals):
             totals = list(totals)
+            vectors = vectors_at(q)
+            factors = factors_at(a, q)
             for inner in range(SUB):
-                m = q * SUB + inner
-                vectors = [vector_at(m, g) for g in range(groups)]
+                rows = [vectors(g, inner) for g in range(groups)]
                 for lane in range(SUB):
-                    factor = scalar_at(a * SUB + lane, m)
+                    factor = factors(lane, inner)
                     for g in range(groups):
                         at = lane * groups + g
-                        totals[at] = totals[at] + factor * vectors[g]
+                        totals[at] = totals[at] + factor * rows[g]
             return tuple(totals)
 
         zero = jnp.zeros((SUB, 128), jnp.float32)
         totals = lax.fori_loop(0, groups, step, (zero,) * (SUB * groups))
-        for lane in range(SUB):
-            for g in range(groups):
-                store_at(a * SUB + lane, g, totals[lane * groups + g])
+        for g in range(groups):
+            store_at(a, g, [totals[lane * groups + g] for lane in range(SUB)])
         return 0
 
     lax.fori_loop(0, groups, block, 0)
 
 
 def part_kernel(
-    n_row, n_col, all_ref, act_ref, weights_ref, in_gain_ref, out_gain_ref,
+    n_row, n_col, act_ref, weights_ref, in_gain_ref, out_gain_ref, *refs,
+):
+    blocks = n_row * n_col
+    part_refs(n_row, n_col, act_ref, weights_ref, in_gain_ref, out_gain_ref, refs[:blocks], *refs[blocks:])
+
+
+def part_refs(
+    n_row, n_col, act_ref, weights_ref, in_gain_ref, out_gain_ref, all_refs,
     update_ref, pair_grad_ref, weight_grad_ref,
     proj_ref, left_ref, right_ref, keep_ref, tri_ref, lin_ref, gate_ref, hat_ref, upd_ref, d_ref,
 ):
@@ -160,36 +165,49 @@
     tile = tile_rows * tile_cols
     residues = n_row * tile_rows
     pairs = residues * residues
-    blocks = n_row * n_col
     chunk = 4 * tile
     bf16, f32 = jnp.bfloat16, jnp.float32
 
-    def row_of(i, k):
-        return ((i // tile_rows * n_col + k // tile_cols) * tile_rows + i % tile_rows) * tile_cols + k % tile_cols
-
-    def vector(ref, i, k):
-        return ref[pl.ds(pl.multiple_of(row_of(i, k), SUB), SUB), :]
-
-    def spread(ref, i, k):
-        return jnp.broadcast_to(ref[pl.ds(row_of(i, k), 1), :], (SUB, channels))
+    row_me, col_me = lax.axis_index("row"), lax.axis_index("col")
+
+    def base(row, col):
+        slot = lax.rem(row_me + n_row - row, n_row) * n_col + (col ^ col_me)
+        return pl.multiple_of(slot * tile, tile)
+
+    def spread(ref, row):
+        return jnp.broadcast_to(ref[pl.ds(row, 1), :], (SUB, channels))
+
+    def line(ref, row):
+        return ref[pl.ds(pl.multiple_of(row, SUB), SUB), :]
+
+    def lines(ref):
+        def store(row, col, values):
+            first = base(row, col)
+            for lane in range(SUB):
+                ref[pl.ds(pl.multiple_of(first + lane * SUB, SUB), SUB), :] = values[lane]
+        return store
+
+    def across(ref):
+        def at(q):
+            firsts = [base(q, g) for g in range(n_col)]
+            return lambda g, inner: line(ref, firsts[g] + inner * SUB)
+        return at
 
     def chunks():
         return [(at, slice(at, at + chunk)) for at in range(0, pairs, chunk)]
 
     def normed_rows(at):
-        first = at // tile
-        return all_ref[first : first + chunk // tile, 0:tile, :].reshape(chunk, channels)
+        return jnp.concatenate([all_refs[b][0:tile] for b in range(at // tile, (at + chunk) // tile)], axis=0)
 
     def cot_rows(at):
-        first = at // tile
-        return all_ref[first : first + chunk // tile, tile : 2 * tile, :].reshape(chunk, channels)
+        return jnp.concatenate([all_refs[b][tile : 2 * tile] for b in range(at // tile, (at + chunk) // tile)], axis=0)
 
     for at, rows in chunks():
         normed = normed_rows(at)
         for s in range(5):
             proj_ref[s, rows, :] = jnp.dot(normed, weights_ref[s], preferred_element_type=f32)
         for b in range(at // tile, (at + chunk) // tile):
-            keep = all_ref[b, 2 * tile : 2 * tile + 16, :].astype(f32)[0:tile_cols]
+            keep = all_refs[b][2 * tile : 2 * tile + 16, :].astype(f32)[0:tile_cols]
             for ii in range(tile_rows):
                 spot = (b * tile_rows + ii) * tile_cols
                 keep_ref[spot : spot + tile_cols, :] = jnp.broadcast_to(keep[:, ii : ii + 1], (tile_cols, channels))
@@ -199,13 +217,23 @@
         left_ref[rows, :] = left.astype(bf16).astype(f32)
         right_ref[rows, :] = right.astype(bf16).astype(f32)
 
-    def right_flipped(k, g):
-        return right_ref[pl.ds(row_of(g * SUB, k), SUB, stride=tile_cols), :]
-
-    def keep_tri(i, g, total):
-        tri_ref[pl.ds(pl.multiple_of(row_of(i, g * SUB), SUB), SUB), :] = total
-
-    triangle(residues, right_flipped, lambda i, k: spread(left_ref, i, k), keep_tri)
+    def flipped(q):
+        firsts = [base(g, q) for g in range(n_row)]
+        return lambda g, inner: right_ref[pl.ds(firsts[g] + inner, SUB, stride=SUB), :]
+
+    def along(ref):
+        def at(a, q):
+            first = base(a, q)
+            return lambda lane, inner: spread(ref, first + lane * SUB + inner)
+        return at
+
+    def down(ref):
+        def at(a, q):
+            first = base(q, a)
+            return lambda lane, inner: spread(ref, first + inner * SUB + lane)
+        return at
+
+    triangle(n_row, flipped, along(left_ref), lines(tri_ref))
 
     out_gain = out_gain_ref[...]
     for at, rows in chunks():
@@ -222,14 +250,8 @@
         back = lax.dot_general(grad_lin, weights_ref[5], (((1,), (1,)), ((), ())), preferred_element_type=f32)
         tri_ref[rows, :] = norm_back(back * out_gain, x_hat, inverse).astype(bf16).astype(f32)
 
-    def keep_left(i, g, total):
-        gate_ref[0, pl.ds(pl.multiple_of(row_of(i, g * SUB), SUB), SUB), :] = total
-
-    def keep_right(j, g, total):
-        gate_ref[1, pl.ds(pl.multiple_of(row_of(j, g * SUB), SUB), SUB), :] = total
-
-    triangle(residues, lambda j, g: vector(right_ref, j, g * SUB), lambda i, j: spread(tri_ref, i, j), keep_left)
-    triangle(residues, lambda i, g: vector(left_ref, i, g * SUB), lambda j, i: spread(tri_ref, i, j), keep_right)
+    triangle(n_row, across(right_ref), along(tri_ref), lines(gate_ref.at[0]))
+    triangle(n_row, across(left_ref), down(tri_ref), lines(gate_ref.at[1]))
 
     for at, rows in chunks():
         kept = keep_ref[rows, :]
@@ -238,7 +260,7 @@
             d_ref[2 * side, rows, :] = value
             d_ref[2 * side + 1, rows, :] = gate
 
-    normed_all = all_ref[:, 0:tile, :].reshape(pairs, channels)
+    normed_all = jnp.concatenate([ref[0:tile] for ref in all_refs], axis=0)
     for s in range(5):
         weight_grad_ref[s] = lax.dot_general(
             normed_all, d_ref[s], (((0,), (0,)), ((), ())), preferred_element_type=f32
@@ -247,8 +269,7 @@
         hat_ref[...], lin_ref[...], (((0,), (0,)), ((), ())), preferred_element_type=f32
     ) / residues
 
-    mine = pl.multiple_of((lax.axis_index("row") * n_col + lax.axis_index("col")) * tile, tile)
-    own = pl.ds(mine, tile)
+    own = slice(0, tile)
     update_ref[...] = upd_ref[own, :].astype(bf16).reshape(update_ref.shape)
     total = jnp.zeros((tile, channels), f32)
     for s in range(5):
@@ -256,6 +277,18 @@
     z_hat, z_inverse = normalize(act_ref[...].astype(f32).reshape(tile, channels))
     grad = norm_back(total * in_gain_ref[...], z_hat, z_inverse)
     pair_grad_ref[...] = grad.astype(bf16).reshape(pair_grad_ref.shape)
+
+
+def gather_tree(own, n_row, n_col):
+    blocks = {(0, 0): own}
+    for shift in range(1, n_row):
+        blocks[shift, 0] = lax.ppermute(own, "row", [(r, (r + shift) % n_row) for r in range(n_row)])
+    bit = n_col // 2
+    while bit > 0:
+        for (shift, flip), piece in list(blocks.items()):
+            blocks[shift, flip ^ bit] = lax.ppermute(piece, "col", [(c, c ^ bit) for c in range(n_col)])
+        bit //= 2
+    return [blocks[shift, flip] for shift in range(n_row) for flip in range(n_col)]
 
 
 def gathered_body(n_row, n_col, pair_act, pair_mask, crop_length, weights, in_gain, out_gain, cotangent):
@@ -271,7 +304,7 @@
         in_specs=[smem, vmem, vmem, vmem, vmem],
         out_specs=vmem,
     )(crop_length, pair_act, pair_mask, cotangent, in_gain.reshape(1, channels))
-    everyone = lax.all_gather(packed, ("row", "col"), axis=0)
+    everyone = gather_tree(packed, n_row, n_col)
     f32, bf16 = jnp.float32, jnp.bfloat16
     return pl.pallas_call(
         functools.partial(part_kernel, n_row, n_col),
@@ -281,7 +314,7 @@
             jax.ShapeDtypeStruct(pair_act.shape, bf16),
             jax.ShapeDtypeStruct(weights.shape, f32),
         ),
-        in_specs=[vmem] * 5,
+        in_specs=[vmem] * (4 + n_row * n_col),
         out_specs=(vmem, vmem, vmem),
         scratch_shapes=[
             pltpu.VMEM((5, pairs, channels), f32),
@@ -296,14 +329,15 @@
             pltpu.VMEM((5, pairs, channels), bf16),
         ],
         compiler_params=pltpu.CompilerParams(vmem_limit_bytes=32 * 1024 * 1024),
-    )(everyone, pair_act, weights, in_gain.reshape(1, channels), out_gain.reshape(1, channels))
+    )(pair_act, weights, in_gain.reshape(1, channels), out_gain.reshape(1, channels), *everyone)
 
 
 def body(n_row, n_col, pair_act, *others):
     tile_rows, tile_cols, channels = pair_act.shape
     pairs = tile_rows * n_row * tile_cols * n_col
-    small = pairs * channels * 4 <= 1024 * 1024
-    if small and channels == 128 and tile_rows % SUB == 0 and tile_cols % SUB == 0 and tile_cols <= 16:
+    small = pairs * channels * 4 <= 1024 * 1024 and channels == 128
+    square = n_row == n_col and tile_rows == SUB and tile_cols == SUB and n_col & (n_col - 1) == 0
+    if small and square:
         return gathered_body(n_row, n_col, pair_act, *others)
     return spread_body(pair_act, *others)
 

time: 42.9 us -> 30.2 us (0.70)
  blocking collectives: 25.2 us -> 0 us
  starting transfers between devices: 0 us -> 11.6 us
  Pallas kernels: 15.5 us -> 9.16 us
  waiting for transfers between devices: 0 us -> 6.12 us
  local copies, waits for them, and re-layouts: 0.67 us -> 1.7 us
    all_gather x1 -> x0, blocking collectives: 25.2 us -> none  [gathered_body(): everyone = lax.all_gather(packed, ('row', 'col'), axis=0)]
    ppermute x0 -> x15, starting transfers between devices: none -> 11.6 us  [the longest x3 6.06 us: gather_tree(): lax.ppermute(own, 'row', [(r, (r + shift) % n_row) for r in range(n_row)])]
    pallas_call x1, Pallas kernels: 14 us -> 7.58 us  [gathered_body(): pl.pallas_call(functools.partial(part_kernel, n_row, n_col), name='part',...]
    ppermute x0 -> x15, waiting for transfers between devices: none -> 6.12 us  [the longest x12 3.59 us: gather_tree(): lax.ppermute(piece, 'col', [(c, c ^ bit) for c in range(n_col)])]
    unnamed x8 -> x10, local copies, waits for them, and re-layouts: 0.67 us -> 1.7 us
  transfers between devices with their start and end apart: 0 -> 15, of which waited for: 0 -> 5; matrix products, arithmetic and copies ran while one was open for 0% -> 0% of each run, Pallas kernels for 0% -> 0%
where the time goes in v2:
time: 30.2 us; the launch traced here: 29.9 us
  starting transfers between devices  11.6 us (38%)
  Pallas kernels  9.16 us (30%)
  waiting for transfers between devices  6.12 us (20%)
  local copies, waits for them, and re-layouts  1.7 us (6%)
  between operations  1.34 us (4%)
    pallas_call x1, Pallas kernels, gathered_body(): pl.pallas_call(functools.partial(part_kernel, n_row, n_col), name='part',...  7.58 us
    ppermute x3, starting transfers between devices, gather_tree(): lax.ppermute(own, 'row', [(r, (r + shift) % n_row) for r in range(n_row)])  6.06 us
    ppermute x12, starting transfers between devices, gather_tree(): lax.ppermute(piece, 'col', [(c, c ^ bit) for c in range(n_col)])  5.55 us
    ppermute x12, waiting for transfers between devices, gather_tree(): lax.ppermute(piece, 'col', [(c, c ^ bit) for c in range(n_col)])  3.59 us
    ppermute x3, waiting for transfers between devices, gather_tree(): lax.ppermute(own, 'row', [(r, (r + shift) % n_row) for r in range(n_row)])  2.52 us
    unnamed x10, local copies, waits for them, and re-layouts  1.7 us
    pallas_call x1, Pallas kernels, gathered_body(): pl.pallas_call(pack_kernel, name='pack', out_shape=jax.ShapeDtypeStruct((...  1.58 us
  transfers between devices with their start and end apart: 15, of which 5 were waited for; matrix products, arithmetic and copies ran while one was open for 0% of the time, Pallas kernels for 0%

profile of v2, /device:TPU:0, one launch (start us, length us, event | category | flops | bytes accessed | tf_op | source)
XLA Modules:
  0.0 29.9 jit_solution(10616489776425863477)
XLA Ops:
  1.3 0.0 copy-start.2
  1.3 1.6 %pack.1.refs_0_ = bf16[144,128]{1,0:T(8,128)(2,1)} custom-call(s32[1]{0:T(128)S(6)} %copy.10.crop_ref, bf16[8,8,128]{2,1,0:T(8,128)(2,1)} %act_ref.3, s32[8,8]{1,0:T(8,128)} %mask_ref.1, bf16[8,8,128]{2,1,0:T(8,128)(2,1)} %cot_ref.1, f32[1,128]{1,0:T(1,128)} %bitcast.2), custom_call_target="tpu_custom_call" | custom-call | tf_op jit(solution)/shard_map/pack/pallas_call | solution.py:300
  2.9 0.0 copy-start.3
  2.9 0.0 copy-start.4
  2.9 5.0 %collective-permute-start.11 = (bf16[144,128]{1,0:T(8,128)(2,1)}, bf16[144,128]{1,0:T(8,128)(2,1)S(1)}, u32[]{:S(2)}, u32[]{:S(2)}) collective-permute-start(bf16[144,128]{1,0:T(8,128)(2,1)} %pack.1.refs_0_), channel_id=1, source_target_pairs={{0,12},{4,0},{8,4},{12,8},{1,13},{5,1},{9,5},{13,9},{2,14},{6,2},{... | collective-permute-start | bytes 110600 | tf_op jit(solution)/shard_map/ppermute | solution.py:285
  7.9 0.0 collective-permute-start.7
  7.9 1.0 %collective-permute-start.3 = (bf16[144,128]{1,0:T(8,128)(2,1)}, bf16[144,128]{1,0:T(8,128)(2,1)S(1)}, u32[]{:S(2)}, u32[]{:S(2)}) collective-permute-start(bf16[144,128]{1,0:T(8,128)(2,1)} %pack.1.refs_0_), channel_id=1, source_target_pairs={{0,4},{4,8},{8,12},{12,0},{1,5},{5,9},{9,13},{13,1},{2,6},{6,10},{... | collective-permute-start | bytes 110600 | tf_op jit(solution)/shard_map/ppermute | solution.py:285
  8.9 1.5 %collective-permute-start.1 = (bf16[144,128]{1,0:T(8,128)(2,1)}, bf16[144,128]{1,0:T(8,128)(2,1)S(1)}, u32[]{:S(2)}, u32[]{:S(2)}) collective-permute-start(bf16[144,128]{1,0:T(8,128)(2,1)} %pack.1.refs_0_), channel_id=1, source_target_pairs={{0,2},{1,3},{2,0},{3,1},{4,6},{5,7},{6,4},{7,5},{8,10},{9,11},{10,... | collective-permute-start | bytes 110600 | tf_op jit(solution)/shard_map/ppermute | solution.py:289
  10.4 0.0 collective-permute-start
  10.4 0.0 collective-permute-done.11.refs_12_
  10.4 0.9 %collective-permute-start.13 = (bf16[144,128]{1,0:T(8,128)(2,1)S(1)}, bf16[144,128]{1,0:T(8,128)(2,1)S(1)}, u32[]{:S(2)}, u32[]{:S(2)}) collective-permute-start(bf16[144,128]{1,0:T(8,128)(2,1)S(1)} %collective-permute-done.11.refs_12_), channel_id=1, source_target_pairs={{0,2},{1,3},{2,0},{3,1},{4,6},{5,7},{6,4},{7,5},{8,10},{9,11},{10,... | collective-permute-start | bytes 110600 | tf_op jit(solution)/shard_map/ppermute | solution.py:289
  11.4 1.6 %collective-permute-done.7.refs_8_ = bf16[144,128]{1,0:T(8,128)(2,1)S(1)} collective-permute-done((bf16[144,128]{1,0:T(8,128)(2,1)}, bf16[144,128]{1,0:T(8,128)(2,1)S(1)}, u32[]{:S(2)}, u32[]{:S(2)}) %collective-permute-start.7) | collective-permute-done | bytes 36896 | tf_op jit(solution)/shard_map/ppermute | solution.py:285
  13.0 0.0 collective-permute-start.12
  13.0 0.9 %collective-permute-done.3.refs_4_ = bf16[144,128]{1,0:T(8,128)(2,1)S(1)} collective-permute-done((bf16[144,128]{1,0:T(8,128)(2,1)}, bf16[144,128]{1,0:T(8,128)(2,1)S(1)}, u32[]{:S(2)}, u32[]{:S(2)}) %collective-permute-start.3) | collective-permute-done | bytes 36896 | tf_op jit(solution)/shard_map/ppermute | solution.py:285
  13.9 1.5 %collective-permute-start.9 = (bf16[144,128]{1,0:T(8,128)(2,1)S(1)}, bf16[144,128]{1,0:T(8,128)(2,1)S(1)}, u32[]{:S(2)}, u32[]{:S(2)}) collective-permute-start(bf16[144,128]{1,0:T(8,128)(2,1)S(1)} %collective-permute-done.7.refs_8_), channel_id=1, source_target_pairs={{0,2},{1,3},{2,0},{3,1},{4,6},{5,7},{6,4},{7,5},{8,10},{9,11},{10,... | collective-permute-start | bytes 110600 | tf_op jit(solution)/shard_map/ppermute | solution.py:289
  15.4 0.0 collective-permute-done.1.refs_2_
  15.4 0.0 collective-permute-start.8
  15.4 0.0 collective-permute-done.refs_1_
  15.4 0.6 %collective-permute-start.5 = (bf16[144,128]{1,0:T(8,128)(2,1)S(1)}, bf16[144,128]{1,0:T(8,128)(2,1)S(1)}, u32[]{:S(2)}, u32[]{:S(2)}) collective-permute-start(bf16[144,128]{1,0:T(8,128)(2,1)S(1)} %collective-permute-done.3.refs_4_), channel_id=1, source_target_pairs={{0,2},{1,3},{2,0},{3,1},{4,6},{5,7},{6,4},{7,5},{8,10},{9,11},{10,... | collective-permute-start | bytes 110600 | tf_op jit(solution)/shard_map/ppermute | solution.py:289
  16.0 0.0 collective-permute-done.13.refs_14_
  16.0 0.2 collective-permute-start.4
  16.2 0.0 collective-permute-done.12.refs_13_
  16.2 0.3 %collective-permute-start.2 = (bf16[144,128]{1,0:T(8,128)(2,1)S(1)}, bf16[144,128]{1,0:T(8,128)(2,1)S(1)}, u32[]{:S(2)}, u32[]{:S(2)}) collective-permute-start(bf16[144,128]{1,0:T(8,128)(2,1)S(1)} %collective-permute-done.1.refs_2_), channel_id=1, source_target_pairs={{0,1},{1,0},{2,3},{3,2},{4,5},{5,4},{6,7},{7,6},{8,9},{9,8},{10,11... | collective-permute-start | bytes 110600 | tf_op jit(solution)/shard_map/ppermute | solution.py:289
  16.5 1.3 %collective-permute-done.9.refs_10_ = bf16[144,128]{1,0:T(8,128)(2,1)S(1)} collective-permute-done((bf16[144,128]{1,0:T(8,128)(2,1)S(1)}, bf16[144,128]{1,0:T(8,128)(2,1)S(1)}, u32[]{:S(2)}, u32[]{:S(2)}) %collective-permute-start.9) | collective-permute-done | bytes 36896 | tf_op jit(solution)/shard_map/ppermute | solution.py:289
  17.9 0.0 collective-permute-start.14
  17.9 0.0 collective-permute-done.8.refs_9_
  17.9 0.5 %collective-permute-start.10 = (bf16[144,128]{1,0:T(8,128)(2,1)S(1)}, bf16[144,128]{1,0:T(8,128)(2,1)S(1)}, u32[]{:S(2)}, u32[]{:S(2)}) collective-permute-start(bf16[144,128]{1,0:T(8,128)(2,1)S(1)} %collective-permute-done.9.refs_10_), channel_id=1, source_target_pairs={{0,1},{1,0},{2,3},{3,2},{4,5},{5,4},{6,7},{7,6},{8,9},{9,8},{10,11... | collective-permute-start | bytes 110600 | tf_op jit(solution)/shard_map/ppermute | solution.py:289
  18.4 1.1 %collective-permute-done.5.refs_6_ = bf16[144,128]{1,0:T(8,128)(2,1)S(1)} collective-permute-done((bf16[144,128]{1,0:T(8,128)(2,1)S(1)}, bf16[144,128]{1,0:T(8,128)(2,1)S(1)}, u32[]{:S(2)}, u32[]{:S(2)}) %collective-permute-start.5) | collective-permute-done | bytes 36896 | tf_op jit(solution)/shard_map/ppermute | solution.py:289
  19.4 0.0 collective-permute-start.6
  19.4 0.0 collective-permute-done.4.refs_5_
  19.4 0.0 collective-permute-done.2.refs_3_
  19.4 0.0 collective-permute-done.14.refs_15_
  19.4 0.0 collective-permute-done.10.refs_11_
  19.5 1.2 %collective-permute-done.6.refs_7_ = bf16[144,128]{1,0:T(8,128)(2,1)S(1)} collective-permute-done((bf16[144,128]{1,0:T(8,128)(2,1)S(1)}, bf16[144,128]{1,0:T(8,128)(2,1)S(1)}, u32[]{:S(2)}, u32[]{:S(2)}) %collective-permute-start.6) | collective-permute-done | bytes 36896 | tf_op jit(solution)/shard_map/ppermute | solution.py:289
  20.6 0.0 copy-done.2
  20.6 0.0 copy-done.3
  20.6 0.0 copy-done.4
  20.6 0.0 copy-start
  20.7 0.9 %copy-done = bf16[6,128,128]{2,1,0:T(8,128)(2,1)S(1)} copy-done((bf16[6,128,128]{2,1,0:T(8,128)(2,1)S(1)}, bf16[6,128,128]{2,1,0:T(8,128)(2,1)}, u32[]{:S(2)}) %copy-start) | copy-done | bytes 196632
  21.6 0.0 copy-start.1
  21.6 0.8 %copy-done.1 = bf16[144,128]{1,0:T(8,128)(2,1)S(1)} copy-done((bf16[144,128]{1,0:T(8,128)(2,1)S(1)}, bf16[144,128]{1,0:T(8,128)(2,1)}, u32[]{:S(2)}) %copy-start.1) | copy-done | bytes 36888
  22.3 7.6 %part.1 = (bf16[8,8,128]{2,1,0:T(8,128)(2,1)}, bf16[8,8,128]{2,1,0:T(8,128)(2,1)}, f32[6,128,128]{2,1,0:T(8,128)}) custom-call(bf16[8,8,128]{2,1,0:T(8,128)(2,1)S(1)} %copy-done.2, bf16[6,128,128]{2,1,0:T(8,128)(2,1)S(1)} %copy-done, f32[1,128]{1,0:T(1,128)S(1)} %bitcast.3, f32[1,128]{1,0:T(1,128)S(1)} %bitcast.4, bf16[144,128]{1,0:T(8,128)(2,1)S(1)} %copy-done.1, ...), custom_call_target="tpu_custom_call" | custom-call | tf_op jit(solution)/shard_map/part/pallas_call | solution.py:309
Async XLA Ops:
  1.3 19.4 %copy-start.2 = (bf16[8,8,128]{2,1,0:T(8,128)(2,1)S(1)}, bf16[8,8,128]{2,1,0:T(8,128)(2,1)}, u32[]{:S(2)}) copy-start(bf16[8,8,128]{2,1,0:T(8,128)(2,1)} %act_ref.3) | copy-start | bytes 49156
  2.9 17.8 %copy-start.3 = (f32[128]{0:T(128)S(1)}, f32[128]{0:T(128)}, u32[]{:S(2)}) copy-start(f32[128]{0:T(128)} %param.11) | copy-start | bytes 1540
  2.9 17.8 %copy-start.4 = (f32[128]{0:T(128)S(1)}, f32[128]{0:T(128)}, u32[]{:S(2)}) copy-start(f32[128]{0:T(128)} %param.12) | copy-start | bytes 1540
  2.9 7.6 %collective-permute-start.11 = (bf16[144,128]{1,0:T(8,128)(2,1)}, bf16[144,128]{1,0:T(8,128)(2,1)S(1)}, u32[]{:S(2)}, u32[]{:S(2)}) collective-permute-start(bf16[144,128]{1,0:T(8,128)(2,1)} %pack.1.refs_0_), channel_id=1, source_target_pairs={{0,12},{4,0},{8,4},{12,8},{1,13},{5,1},{9,5},{13,9},{2,14},{6,2},{... | collective-permute-start | bytes 110600 | tf_op jit(solution)/shard_map/ppermute | solution.py:285
  7.9 5.1 %collective-permute-start.7 = (bf16[144,128]{1,0:T(8,128)(2,1)}, bf16[144,128]{1,0:T(8,128)(2,1)S(1)}, u32[]{:S(2)}, u32[]{:S(2)}) collective-permute-start(bf16[144,128]{1,0:T(8,128)(2,1)} %pack.1.refs_0_), channel_id=1, source_target_pairs={{0,8},{4,12},{8,0},{12,4},{1,9},{5,13},{9,1},{13,5},{2,10},{6,14},... | collective-permute-start | bytes 110600 | tf_op jit(solution)/shard_map/ppermute | solution.py:285
  7.9 6.0 %collective-permute-start.3 = (bf16[144,128]{1,0:T(8,128)(2,1)}, bf16[144,128]{1,0:T(8,128)(2,1)S(1)}, u32[]{:S(2)}, u32[]{:S(2)}) collective-permute-start(bf16[144,128]{1,0:T(8,128)(2,1)} %pack.1.refs_0_), channel_id=1, source_target_pairs={{0,4},{4,8},{8,12},{12,0},{1,5},{5,9},{9,13},{13,1},{2,6},{6,10},{... | collective-permute-start | bytes 110600 | tf_op jit(solution)/shard_map/ppermute | solution.py:285
  8.9 6.5 %collective-permute-start.1 = (bf16[144,128]{1,0:T(8,128)(2,1)}, bf16[144,128]{1,0:T(8,128)(2,1)S(1)}, u32[]{:S(2)}, u32[]{:S(2)}) collective-permute-start(bf16[144,128]{1,0:T(8,128)(2,1)} %pack.1.refs_0_), channel_id=1, source_target_pairs={{0,2},{1,3},{2,0},{3,1},{4,6},{5,7},{6,4},{7,5},{8,10},{9,11},{10,... | collective-permute-start | bytes 110600 | tf_op jit(solution)/shard_map/ppermute | solution.py:289
  10.4 5.0 %collective-permute-start = (bf16[144,128]{1,0:T(8,128)(2,1)}, bf16[144,128]{1,0:T(8,128)(2,1)S(1)}, u32[]{:S(2)}, u32[]{:S(2)}) collective-permute-start(bf16[144,128]{1,0:T(8,128)(2,1)} %pack.1.refs_0_), channel_id=1, source_target_pairs={{0,1},{1,0},{2,3},{3,2},{4,5},{5,4},{6,7},{7,6},{8,9},{9,8},{10,11... | collective-permute-start | bytes 110600 | tf_op jit(solution)/shard_map/ppermute | solution.py:289
  10.4 5.6 %collective-permute-start.13 = (bf16[144,128]{1,0:T(8,128)(2,1)S(1)}, bf16[144,128]{1,0:T(8,128)(2,1)S(1)}, u32[]{:S(2)}, u32[]{:S(2)}) collective-permute-start(bf16[144,128]{1,0:T(8,128)(2,1)S(1)} %collective-permute-done.11.refs_12_), channel_id=1, source_target_pairs={{0,2},{1,3},{2,0},{3,1},{4,6},{5,7},{6,4},{7,5},{8,10},{9,11},{10,... | collective-permute-start | bytes 110600 | tf_op jit(solution)/shard_map/ppermute | solution.py:289
  13.0 3.2 %collective-permute-start.12 = (bf16[144,128]{1,0:T(8,128)(2,1)S(1)}, bf16[144,128]{1,0:T(8,128)(2,1)S(1)}, u32[]{:S(2)}, u32[]{:S(2)}) collective-permute-start(bf16[144,128]{1,0:T(8,128)(2,1)S(1)} %collective-permute-done.11.refs_12_), channel_id=1, source_target_pairs={{0,1},{1,0},{2,3},{3,2},{4,5},{5,4},{6,7},{7,6},{8,9},{9,8},{10,11... | collective-permute-start | bytes 110600 | tf_op jit(solution)/shard_map/ppermute | solution.py:289
  13.9 4.0 %collective-permute-start.9 = (bf16[144,128]{1,0:T(8,128)(2,1)S(1)}, bf16[144,128]{1,0:T(8,128)(2,1)S(1)}, u32[]{:S(2)}, u32[]{:S(2)}) collective-permute-start(bf16[144,128]{1,0:T(8,128)(2,1)S(1)} %collective-permute-done.7.refs_8_), channel_id=1, source_target_pairs={{0,2},{1,3},{2,0},{3,1},{4,6},{5,7},{6,4},{7,5},{8,10},{9,11},{10,... | collective-permute-start | bytes 110600 | tf_op jit(solution)/shard_map/ppermute | solution.py:289
  15.4 2.5 %collective-permute-start.8 = (bf16[144,128]{1,0:T(8,128)(2,1)S(1)}, bf16[144,128]{1,0:T(8,128)(2,1)S(1)}, u32[]{:S(2)}, u32[]{:S(2)}) collective-permute-start(bf16[144,128]{1,0:T(8,128)(2,1)S(1)} %collective-permute-done.7.refs_8_), channel_id=1, source_target_pairs={{0,1},{1,0},{2,3},{3,2},{4,5},{5,4},{6,7},{7,6},{8,9},{9,8},{10,11... | collective-permute-start | bytes 110600 | tf_op jit(solution)/shard_map/ppermute | solution.py:289
  15.4 4.0 %collective-permute-start.5 = (bf16[144,128]{1,0:T(8,128)(2,1)S(1)}, bf16[144,128]{1,0:T(8,128)(2,1)S(1)}, u32[]{:S(2)}, u32[]{:S(2)}) collective-permute-start(bf16[144,128]{1,0:T(8,128)(2,1)S(1)} %collective-permute-done.3.refs_4_), channel_id=1, source_target_pairs={{0,2},{1,3},{2,0},{3,1},{4,6},{5,7},{6,4},{7,5},{8,10},{9,11},{10,... | collective-permute-start | bytes 110600 | tf_op jit(solution)/shard_map/ppermute | solution.py:289
  16.0 3.4 %collective-permute-start.4 = (bf16[144,128]{1,0:T(8,128)(2,1)S(1)}, bf16[144,128]{1,0:T(8,128)(2,1)S(1)}, u32[]{:S(2)}, u32[]{:S(2)}) collective-permute-start(bf16[144,128]{1,0:T(8,128)(2,1)S(1)} %collective-permute-done.3.refs_4_), channel_id=1, source_target_pairs={{0,1},{1,0},{2,3},{3,2},{4,5},{5,4},{6,7},{7,6},{8,9},{9,8},{10,11... | collective-permute-start | bytes 110600 | tf_op jit(solution)/shard_map/ppermute | solution.py:289
  16.2 3.3 %collective-permute-start.2 = (bf16[144,128]{1,0:T(8,128)(2,1)S(1)}, bf16[144,128]{1,0:T(8,128)(2,1)S(1)}, u32[]{:S(2)}, u32[]{:S(2)}) collective-permute-start(bf16[144,128]{1,0:T(8,128)(2,1)S(1)} %collective-permute-done.1.refs_2_), channel_id=1, source_target_pairs={{0,1},{1,0},{2,3},{3,2},{4,5},{5,4},{6,7},{7,6},{8,9},{9,8},{10,11... | collective-permute-start | bytes 110600 | tf_op jit(solution)/shard_map/ppermute | solution.py:289
  17.9 1.6 %collective-permute-start.14 = (bf16[144,128]{1,0:T(8,128)(2,1)S(1)}, bf16[144,128]{1,0:T(8,128)(2,1)S(1)}, u32[]{:S(2)}, u32[]{:S(2)}) collective-permute-start(bf16[144,128]{1,0:T(8,128)(2,1)S(1)} %collective-permute-done.13.refs_14_), channel_id=1, source_target_pairs={{0,1},{1,0},{2,3},{3,2},{4,5},{5,4},{6,7},{7,6},{8,9},{9,8},{10,11... | collective-permute-start | bytes 110600 | tf_op jit(solution)/shard_map/ppermute | solution.py:289
  17.9 1.6 %collective-permute-start.10 = (bf16[144,128]{1,0:T(8,128)(2,1)S(1)}, bf16[144,128]{1,0:T(8,128)(2,1)S(1)}, u32[]{:S(2)}, u32[]{:S(2)}) collective-permute-start(bf16[144,128]{1,0:T(8,128)(2,1)S(1)} %collective-permute-done.9.refs_10_), channel_id=1, source_target_pairs={{0,1},{1,0},{2,3},{3,2},{4,5},{5,4},{6,7},{7,6},{8,9},{9,8},{10,11... | collective-permute-start | bytes 110600 | tf_op jit(solution)/shard_map/ppermute | solution.py:289
  19.4 1.2 %collective-permute-start.6 = (bf16[144,128]{1,0:T(8,128)(2,1)S(1)}, bf16[144,128]{1,0:T(8,128)(2,1)S(1)}, u32[]{:S(2)}, u32[]{:S(2)}) collective-permute-start(bf16[144,128]{1,0:T(8,128)(2,1)S(1)} %collective-permute-done.5.refs_6_), channel_id=1, source_target_pairs={{0,1},{1,0},{2,3},{3,2},{4,5},{5,4},{6,7},{7,6},{8,9},{9,8},{10,11... | collective-permute-start | bytes 110600 | tf_op jit(solution)/shard_map/ppermute | solution.py:289
  20.6 0.9 %copy-start = (bf16[6,128,128]{2,1,0:T(8,128)(2,1)S(1)}, bf16[6,128,128]{2,1,0:T(8,128)(2,1)}, u32[]{:S(2)}) copy-start(bf16[6,128,128]{2,1,0:T(8,128)(2,1)} %weights_ref.1) | copy-start | bytes 589828
  21.6 0.8 %copy-start.1 = (bf16[144,128]{1,0:T(8,128)(2,1)S(1)}, bf16[144,128]{1,0:T(8,128)(2,1)}, u32[]{:S(2)}) copy-start(bf16[144,128]{1,0:T(8,128)(2,1)} %pack.1.refs_0_) | copy-start | bytes 110596

commit v3 on v2

--- a/solution.py
+++ b/solution.py
@@ -150,14 +150,14 @@
 
 
 def part_kernel(
-    n_row, n_col, act_ref, weights_ref, in_gain_ref, out_gain_ref, *refs,
+    n_row, n_col, counts, slot_of, act_ref, weights_ref, in_gain_ref, out_gain_ref, *refs,
 ):
-    blocks = n_row * n_col
-    part_refs(n_row, n_col, act_ref, weights_ref, in_gain_ref, out_gain_ref, refs[:blocks], *refs[blocks:])
+    pieces = [ref.at[b] for ref, count in zip(refs, counts) for b in range(count)]
+    part_refs(n_row, n_col, slot_of, act_ref, weights_ref, in_gain_ref, out_gain_ref, pieces, *refs[len(counts) :])
 
 
 def part_refs(
-    n_row, n_col, act_ref, weights_ref, in_gain_ref, out_gain_ref, all_refs,
+    n_row, n_col, slot_of, act_ref, weights_ref, in_gain_ref, out_gain_ref, all_refs,
     update_ref, pair_grad_ref, weight_grad_ref,
     proj_ref, left_ref, right_ref, keep_ref, tri_ref, lin_ref, gate_ref, hat_ref, upd_ref, d_ref,
 ):
@@ -171,8 +171,7 @@
     row_me, col_me = lax.axis_index("row"), lax.axis_index("col")
 
     def base(row, col):
-        slot = lax.rem(row_me + n_row - row, n_row) * n_col + (col ^ col_me)
-        return pl.multiple_of(slot * tile, tile)
+        return pl.multiple_of(slot_of(row, col, row_me, col_me) * tile, tile)
 
     def spread(ref, row):
         return jnp.broadcast_to(ref[pl.ds(row, 1), :], (SUB, channels))
@@ -269,7 +268,7 @@
         hat_ref[...], lin_ref[...], (((0,), (0,)), ((), ())), preferred_element_type=f32
     ) / residues
 
-    own = slice(0, tile)
+    own = pl.ds(base(row_me, col_me), tile)
     update_ref[...] = upd_ref[own, :].astype(bf16).reshape(update_ref.shape)
     total = jnp.zeros((tile, channels), f32)
     for s in range(5):
@@ -279,16 +278,14 @@
     pair_grad_ref[...] = grad.astype(bf16).reshape(pair_grad_ref.shape)
 
 
-def gather_tree(own, n_row, n_col):
-    blocks = {(0, 0): own}
-    for shift in range(1, n_row):
-        blocks[shift, 0] = lax.ppermute(own, "row", [(r, (r + shift) % n_row) for r in range(n_row)])
-    bit = n_col // 2
-    while bit > 0:
-        for (shift, flip), piece in list(blocks.items()):
-            blocks[shift, flip ^ bit] = lax.ppermute(piece, "col", [(c, c ^ bit) for c in range(n_col)])
-        bit //= 2
-    return [blocks[shift, flip] for shift in range(n_row) for flip in range(n_col)]
+def gather(own, n_row, n_col):
+    along = lax.all_gather(own, "row", axis=0)
+    everyone = lax.all_gather(along, "col", axis=0, tiled=True)
+
+    def slot_of(row, col, row_me, col_me):
+        return col * n_row + row
+
+    return [everyone], slot_of
 
 
 def gathered_body(n_row, n_col, pair_act, pair_mask, crop_length, weights, in_gain, out_gain, cotangent):
@@ -304,17 +301,18 @@
         in_specs=[smem, vmem, vmem, vmem, vmem],
         out_specs=vmem,
     )(crop_length, pair_act, pair_mask, cotangent, in_gain.reshape(1, channels))
-    everyone = gather_tree(packed, n_row, n_col)
+    everyone, slot_of = gather(packed, n_row, n_col)
+    counts = tuple(piece.shape[0] for piece in everyone)
     f32, bf16 = jnp.float32, jnp.bfloat16
     return pl.pallas_call(
-        functools.partial(part_kernel, n_row, n_col),
+        functools.partial(part_kernel, n_row, n_col, counts, slot_of),
         name="part",
         out_shape=(
             jax.ShapeDtypeStruct(pair_act.shape, bf16),
             jax.ShapeDtypeStruct(pair_act.shape, bf16),
             jax.ShapeDtypeStruct(weights.shape, f32),
         ),
-        in_specs=[vmem] * (4 + n_row * n_col),
+        in_specs=[vmem] * (4 + len(counts)),
         out_specs=(vmem, vmem, vmem),
         scratch_shapes=[
             pltpu.VMEM((5, pairs, channels), f32),

time: 30.2 us -> 33.2 us (1.099)
  blocking collectives: 0 us -> 23 us
  starting transfers between devices: 11.6 us -> 0 us
  waiting for transfers between devices: 6.12 us -> 0 us
  local copies, waits for them, and re-layouts: 1.7 us -> 0.02 us
  Pallas kernels: 9.16 us -> 8.65 us
    all_gather x0 -> x2, blocking collectives: none -> 23 us  [the longest x1 15.4 us: gather(): along = lax.all_gather(own, 'row', axis=0)]
    ppermute x15 -> x0, starting transfers between devices: 11.6 us -> none  [the longest x3 6.06 us: gather_tree(): lax.ppermute(own, 'row', [(r, (r + shift) % n_row) for r in range(n_row)])]
    ppermute x15 -> x0, waiting for transfers between devices: 6.12 us -> none  [the longest x12 3.59 us: gather_tree(): lax.ppermute(piece, 'col', [(c, c ^ bit) for c in range(n_col)])]
    unnamed x10 -> x8, local copies, waits for them, and re-layouts: 1.7 us -> 0.02 us
    pallas_call x1, Pallas kernels: 7.58 us -> 7.09 us  [gathered_body(): pl.pallas_call(functools.partial(part_kernel, n_row, n_col, counts, slot_...]
  transfers between devices with their start and end apart: 15 -> 0, of which waited for: 5 -> 0; matrix products, arithmetic and copies ran while one was open for 0% -> 0% of each run, Pallas kernels for 0% -> 0%
where the time goes in v3:
time: 33.2 us; the launch traced here: 33 us
  blocking collectives  23 us (69%)
  Pallas kernels  8.65 us (26%)
  between operations  1.3 us (4%)
    all_gather x1, blocking collectives, gather(): along = lax.all_gather(own, 'row', axis=0)  15.4 us
    all_gather x1, blocking collectives, gather(): everyone = lax.all_gather(along, 'col', axis=0, tiled=True)  7.66 us
    pallas_call x1, Pallas kernels, gathered_body(): pl.pallas_call(functools.partial(part_kernel, n_row, n_col, counts, slot_...  7.09 us
    pallas_call x1, Pallas kernels, gathered_body(): pl.pallas_call(pack_kernel, name='pack', out_shape=jax.ShapeDtypeStruct((...  1.55 us

profile of v3, /device:TPU:0, one launch (start us, length us, event | category | flops | bytes accessed | tf_op | source)
XLA Modules:
  0.0 33.0 jit_solution(3158076841607574790)
XLA Ops:
  1.3 1.6 %pack.1 = bf16[144,128]{1,0:T(8,128)(2,1)} custom-call(s32[1]{0:T(128)S(6)} %copy.10.crop_ref, bf16[8,8,128]{2,1,0:T(8,128)(2,1)} %act_ref.3, s32[8,8]{1,0:T(8,128)} %mask_ref.1, bf16[8,8,128]{2,1,0:T(8,128)(2,1)} %cot_ref.1, f32[1,128]{1,0:T(1,128)} %bitcast.3), custom_call_target="tpu_custom_call" | custom-call | tf_op jit(solution)/shard_map/pack/pallas_call | solution.py:297
  2.8 15.4 %all-gather = bf16[576,128]{1,0:T(8,128)(2,1)S(1)} all-gather(bf16[144,128]{1,0:T(8,128)(2,1)} %pack.1), channel_id=2, replica_groups=mesh['parts'=2,'row'=4,'col'=4] {'row'}, dimensions={0}, use_global_device_ids=true | all-gather | bytes 184320 | tf_op jit(solution)/shard_map/all_gather | solution.py:282
  18.2 0.0 copy-start
  18.2 0.0 copy-start.1
  18.2 0.0 copy-start.2
  18.2 0.0 copy-start.3
  18.2 7.7 %all_gather.11.refs_0_ = bf16[16,144,128]{2,1,0:T(8,128)(2,1)S(1)} all-gather(bf16[4,144,128]{2,1,0:T(8,128)(2,1)S(1)} %bitcast.6), channel_id=1, replica_groups=mesh['parts'=2,'row'=4,'col'=4] {'col'}, dimensions={0}, use_global_device_ids=true | all-gather | bytes 737280 | tf_op jit(solution)/shard_map/all_gather | solution.py:283
  25.9 0.0 copy-done
  25.9 0.0 copy-done.1
  25.9 0.0 copy-done.2
  25.9 0.0 copy-done.3
  25.9 7.1 %part.1 = (bf16[8,8,128]{2,1,0:T(8,128)(2,1)}, bf16[8,8,128]{2,1,0:T(8,128)(2,1)}, f32[6,128,128]{2,1,0:T(8,128)}) custom-call(bf16[8,8,128]{2,1,0:T(8,128)(2,1)S(1)} %copy-done.1, bf16[6,128,128]{2,1,0:T(8,128)(2,1)S(1)} %copy-done, f32[1,128]{1,0:T(1,128)S(1)} %bitcast.4, f32[1,128]{1,0:T(1,128)S(1)} %bitcast.5, bf16[16,144,128]{2,1,0:T(8,128)(2,1)S(1)} %all_gather.11.refs_0_), custom_call_target="tpu_custom_call" | custom-call | tf_op jit(solution)/shard_map/part/pallas_call | solution.py:307
Async XLA Ops:
  18.2 7.7 %copy-start = (bf16[6,128,128]{2,1,0:T(8,128)(2,1)S(1)}, bf16[6,128,128]{2,1,0:T(8,128)(2,1)}, u32[]{:S(2)}) copy-start(bf16[6,128,128]{2,1,0:T(8,128)(2,1)} %weights_ref.1) | copy-start | bytes 589828
  18.2 7.7 %copy-start.1 = (bf16[8,8,128]{2,1,0:T(8,128)(2,1)S(1)}, bf16[8,8,128]{2,1,0:T(8,128)(2,1)}, u32[]{:S(2)}) copy-start(bf16[8,8,128]{2,1,0:T(8,128)(2,1)} %act_ref.3) | copy-start | bytes 49156
  18.2 7.7 %copy-start.2 = (f32[128]{0:T(128)S(1)}, f32[128]{0:T(128)}, u32[]{:S(2)}) copy-start(f32[128]{0:T(128)} %param.11) | copy-start | bytes 1540
  18.2 7.7 %copy-start.3 = (f32[128]{0:T(128)S(1)}, f32[128]{0:T(128)}, u32[]{:S(2)}) copy-start(f32[128]{0:T(128)} %param.12) | copy-start | bytes 1540

commit v4 on v3

--- a/solution.py
+++ b/solution.py
@@ -279,11 +279,11 @@
 
 
 def gather(own, n_row, n_col):
-    along = lax.all_gather(own, "row", axis=0)
-    everyone = lax.all_gather(along, "col", axis=0, tiled=True)
+    repeated = jnp.broadcast_to(own, (n_row * n_col,) + own.shape)
+    everyone = lax.all_to_all(repeated, ("row", "col"), split_axis=0, concat_axis=0, tiled=True)
 
     def slot_of(row, col, row_me, col_me):
-        return col * n_row + row
+        return row * n_col + col
 
     return [everyone], slot_of
 

time: 33.2 us -> 36.3 us (1.093)
  blocking collectives: 23 us -> 24.6 us
  local copies, waits for them, and re-layouts: 0.02 us -> 1.52 us
    all_to_all x0 -> x1, blocking collectives: none -> 24.6 us  [gather(): lax.all_to_all(repeated, ('row', 'col'), split_axis=0, concat_axis=0, til...]
    all_gather x2 -> x0, blocking collectives: 23 us -> none  [the longest x1 15.4 us: gather(): along = lax.all_gather(own, 'row', axis=0)]
    broadcast_in_dim x0 -> x1, local copies, waits for them, and re-layouts: none -> 0.84 us  [gather(): repeated = jnp.broadcast_to(own, (n_row * n_col,) + own.shape)]
    unnamed x8, local copies, waits for them, and re-layouts: 0.02 us -> 0.67 us
where the time goes in v4:
time: 36.3 us; the launch traced here: 36 us
  blocking collectives  24.6 us (68%)
  Pallas kernels  8.65 us (24%)
  local copies, waits for them, and re-layouts  1.52 us (4%)
  between operations  1.3 us (4%)
    all_to_all x1, blocking collectives, gather(): lax.all_to_all(repeated, ('row', 'col'), split_axis=0, concat_axis=0, til...  24.6 us
    pallas_call x1, Pallas kernels, gathered_body(): pl.pallas_call(functools.partial(part_kernel, n_row, n_col, counts, slot_...  7.1 us
    pallas_call x1, Pallas kernels, gathered_body(): pl.pallas_call(pack_kernel, name='pack', out_shape=jax.ShapeDtypeStruct((...  1.55 us
    broadcast_in_dim x1, local copies, waits for them, and re-layouts, gather(): repeated = jnp.broadcast_to(own, (n_row * n_col,) + own.shape)  0.84 us

profile of v4, /device:TPU:0, one launch (start us, length us, event | category | flops | bytes accessed | tf_op | source)
XLA Modules:
  0.0 36.0 jit_solution(17345897195519822934)
XLA Ops:
  1.3 1.6 %pack.1 = bf16[144,128]{1,0:T(8,128)(2,1)} custom-call(s32[1]{0:T(128)S(6)} %copy.10.crop_ref, bf16[8,8,128]{2,1,0:T(8,128)(2,1)} %act_ref.3, s32[8,8]{1,0:T(8,128)} %mask_ref.1, bf16[8,8,128]{2,1,0:T(8,128)(2,1)} %cot_ref.1, f32[1,128]{1,0:T(1,128)} %bitcast.2), custom_call_target="tpu_custom_call" | custom-call | tf_op jit(solution)/shard_map/pack/pallas_call | solution.py:297
  2.8 0.8 %broadcast_in_dim.3 = bf16[16,144,128]{2,1,0:T(8,128)(2,1)S(1)} broadcast(bf16[144,128]{1,0:T(8,128)(2,1)} %pack.1), dimensions={1,2} | broadcast | bytes 626688 | tf_op jit(solution)/shard_map/broadcast_in_dim | solution.py:282
  3.7 0.0 copy-start
  3.7 0.0 copy-start.1
  3.7 24.6 %all_to_all.5.refs_0_ = bf16[16,144,128]{2,1,0:T(8,128)(2,1)S(1)} all-to-all(bf16[16,144,128]{2,1,0:T(8,128)(2,1)S(1)} %broadcast_in_dim.3), channel_id=1, replica_groups=mesh['parts'=2,'row'=4,'col'=4] {'row','col'}, dimensions={0} | all-to-all | bytes 1179648 | tf_op jit(solution)/shard_map/all_to_all | solution.py:283
  28.3 0.0 copy-start.2
  28.3 0.0 copy-start.3
  28.3 0.0 copy-done
  28.3 0.0 copy-done.1
  28.3 0.6 %copy-done.2 = f32[128]{0:T(128)S(1)} copy-done((f32[128]{0:T(128)S(1)}, f32[128]{0:T(128)}, u32[]{:S(2)}) %copy-start.2) | copy-done | bytes 536
  28.9 0.0 copy-done.3
  28.9 7.1 %part.1 = (bf16[8,8,128]{2,1,0:T(8,128)(2,1)}, bf16[8,8,128]{2,1,0:T(8,128)(2,1)}, f32[6,128,128]{2,1,0:T(8,128)}) custom-call(bf16[8,8,128]{2,1,0:T(8,128)(2,1)S(1)} %copy-done.1, bf16[6,128,128]{2,1,0:T(8,128)(2,1)S(1)} %copy-done, f32[1,128]{1,0:T(1,128)S(1)} %bitcast.3, f32[1,128]{1,0:T(1,128)S(1)} %bitcast.4, bf16[16,144,128]{2,1,0:T(8,128)(2,1)S(1)} %all_to_all.5.refs_0_), custom_call_target="tpu_custom_call" | custom-call | tf_op jit(solution)/shard_map/part/pallas_call | solution.py:307
Async XLA Ops:
  3.7 24.6 %copy-start = (bf16[6,128,128]{2,1,0:T(8,128)(2,1)S(1)}, bf16[6,128,128]{2,1,0:T(8,128)(2,1)}, u32[]{:S(2)}) copy-start(bf16[6,128,128]{2,1,0:T(8,128)(2,1)} %weights_ref.1) | copy-start | bytes 589828
  3.7 24.6 %copy-start.1 = (bf16[8,8,128]{2,1,0:T(8,128)(2,1)S(1)}, bf16[8,8,128]{2,1,0:T(8,128)(2,1)}, u32[]{:S(2)}) copy-start(bf16[8,8,128]{2,1,0:T(8,128)(2,1)} %act_ref.3) | copy-start | bytes 49156
  28.3 0.7 %copy-start.2 = (f32[128]{0:T(128)S(1)}, f32[128]{0:T(128)}, u32[]{:S(2)}) copy-start(f32[128]{0:T(128)} %param.11) | copy-start | bytes 1540
  28.3 0.7 %copy-start.3 = (f32[128]{0:T(128)S(1)}, f32[128]{0:T(128)}, u32[]{:S(2)}) copy-start(f32[128]{0:T(128)} %param.12) | copy-start | bytes 1540

commit v5 on v4

--- a/solution.py
+++ b/solution.py
@@ -150,16 +150,16 @@
 
 
 def part_kernel(
-    n_row, n_col, counts, slot_of, act_ref, weights_ref, in_gain_ref, out_gain_ref, *refs,
+    n_row, n_col, counts, owners, act_ref, weights_ref, in_gain_ref, out_gain_ref, *refs,
 ):
     pieces = [ref.at[b] for ref, count in zip(refs, counts) for b in range(count)]
-    part_refs(n_row, n_col, slot_of, act_ref, weights_ref, in_gain_ref, out_gain_ref, pieces, *refs[len(counts) :])
+    part_refs(n_row, n_col, owners, act_ref, weights_ref, in_gain_ref, out_gain_ref, pieces, *refs[len(counts) :])
 
 
 def part_refs(
-    n_row, n_col, slot_of, act_ref, weights_ref, in_gain_ref, out_gain_ref, all_refs,
+    n_row, n_col, owners, act_ref, weights_ref, in_gain_ref, out_gain_ref, all_refs,
     update_ref, pair_grad_ref, weight_grad_ref,
-    proj_ref, left_ref, right_ref, keep_ref, tri_ref, lin_ref, gate_ref, hat_ref, upd_ref, d_ref,
+    proj_ref, left_ref, right_ref, keep_ref, tri_ref, lin_ref, gate_ref, hat_ref, upd_ref, d_ref, slot_ref,
 ):
     tile_rows, tile_cols, channels = act_ref.shape
     tile = tile_rows * tile_cols
@@ -170,8 +170,13 @@
 
     row_me, col_me = lax.axis_index("row"), lax.axis_index("col")
 
+    core_me = col_me % 2
+    for slot, (near, far) in enumerate(owners):
+        shift = [jnp.where(core_me == 0, a, b) for a, b in zip(near, far)]
+        slot_ref[(row_me ^ shift[0]) * n_col + (col_me ^ shift[1])] = slot * tile
+
     def base(row, col):
-        return pl.multiple_of(slot_of(row, col, row_me, col_me) * tile, tile)
+        return pl.multiple_of(slot_ref[row * n_col + col], tile)
 
     def spread(ref, row):
         return jnp.broadcast_to(ref[pl.ds(row, 1), :], (SUB, channels))
@@ -268,7 +273,7 @@
         hat_ref[...], lin_ref[...], (((0,), (0,)), ((), ())), preferred_element_type=f32
     ) / residues
 
-    own = pl.ds(base(row_me, col_me), tile)
+    own = slice(0, tile)
     update_ref[...] = upd_ref[own, :].astype(bf16).reshape(update_ref.shape)
     total = jnp.zeros((tile, channels), f32)
     for s in range(5):
@@ -278,14 +283,35 @@
     pair_grad_ref[...] = grad.astype(bf16).reshape(pair_grad_ref.shape)
 
 
+def flip_by(block, n_row, n_col, near, far):
+    pairs = []
+    for row in range(n_row):
+        for col in range(n_col):
+            shift = near if col % 2 == 0 else far
+            pairs.append((row * n_col + col, (row ^ shift[0]) * n_col + (col ^ shift[1])))
+    return lax.ppermute(block, ("row", "col"), pairs)
+
+
 def gather(own, n_row, n_col):
-    repeated = jnp.broadcast_to(own, (n_row * n_col,) + own.shape)
-    everyone = lax.all_to_all(repeated, ("row", "col"), split_axis=0, concat_axis=0, tiled=True)
-
-    def slot_of(row, col, row_me, col_me):
-        return row * n_col + col
-
-    return [everyone], slot_of
+    def other(block):
+        return flip_by(block, n_row, n_col, (0, 1), (0, 1))
+
+    both = jnp.stack([own, other(own)])
+    chips = [(row, col) for row in range(n_row) for col in range(0, n_col, 2) if row + col > 0]
+    chips.sort(key=lambda chip: (bin(chip[0]).count("1") + chip[1] // 2, chip))
+    pieces = [both]
+    owners = [((0, 0), (0, 0)), ((0, 1), (0, 1))]
+    while len(chips) > 1:
+        near, far = chips.pop(0), chips.pop(0)
+        piece = flip_by(both, n_row, n_col, near, far)
+        pieces += [piece, other(piece)]
+        for a, b, core in ((near, far, 0), (near, far, 1), (far, near, 1), (far, near, 0)):
+            owners.append(((a[0], a[1] ^ core), (b[0], b[1] ^ core)))
+    for last in chips:
+        piece = flip_by(own[None], n_row, n_col, last, last)
+        pieces += [piece, other(piece)]
+        owners += [(last, last), ((last[0], last[1] ^ 1),) * 2]
+    return pieces, tuple(owners)
 
 
 def gathered_body(n_row, n_col, pair_act, pair_mask, crop_length, weights, in_gain, out_gain, cotangent):
@@ -300,12 +326,13 @@
         out_shape=jax.ShapeDtypeStruct((2 * tile + 16, channels), jnp.bfloat16),
         in_specs=[smem, vmem, vmem, vmem, vmem],
         out_specs=vmem,
+        compiler_params=pltpu.CompilerParams(vmem_limit_bytes=2 * 1024 * 1024),
     )(crop_length, pair_act, pair_mask, cotangent, in_gain.reshape(1, channels))
-    everyone, slot_of = gather(packed, n_row, n_col)
+    everyone, owners = gather(packed, n_row, n_col)
     counts = tuple(piece.shape[0] for piece in everyone)
     f32, bf16 = jnp.float32, jnp.bfloat16
     return pl.pallas_call(
-        functools.partial(part_kernel, n_row, n_col, counts, slot_of),
+        functools.partial(part_kernel, n_row, n_col, counts, owners),
         name="part",
         out_shape=(
             jax.ShapeDtypeStruct(pair_act.shape, bf16),
@@ -325,8 +352,9 @@
             pltpu.VMEM((pairs, channels), bf16),
             pltpu.VMEM((pairs, channels), f32),
             pltpu.VMEM((5, pairs, channels), bf16),
+            pltpu.SMEM((n_row * n_col,), jnp.int32),
         ],
-        compiler_params=pltpu.CompilerParams(vmem_limit_bytes=32 * 1024 * 1024),
+        compiler_params=pltpu.CompilerParams(vmem_limit_bytes=24 * 1024 * 1024),
     )(pair_act, weights, in_gain.reshape(1, channels), out_gain.reshape(1, channels), *everyone)
 
 

time: 36.3 us -> 27.1 us (0.75)
  blocking collectives: 24.6 us -> 0 us
  starting transfers between devices: 0 us -> 11.8 us
  waiting for transfers between devices: 0 us -> 3.24 us
  local copies, waits for them, and re-layouts: 1.52 us -> 2.79 us
  Pallas kernels: 8.65 us -> 7.5 us
    all_to_all x1 -> x0, blocking collectives: 24.6 us -> none  [gather(): lax.all_to_all(repeated, ('row', 'col'), split_axis=0, concat_axis=0, til...]
    ppermute x0 -> x9, starting transfers between devices: none -> 11.8 us  [flip_by(): return lax.ppermute(block, ('row', 'col'), pairs)]
    ppermute x0 -> x9, waiting for transfers between devices: none -> 3.24 us  [flip_by(): return lax.ppermute(block, ('row', 'col'), pairs)]
    unnamed x8 -> x16, local copies, waits for them, and re-layouts: 0.67 us -> 2.79 us
    pallas_call x1, Pallas kernels: 1.55 us -> 0.17 us  [gathered_body(): pl.pallas_call(pack_kernel, name='pack', out_shape=jax.ShapeDtypeStruct((...]
    broadcast_in_dim x1 -> x0, local copies, waits for them, and re-layouts: 0.84 us -> none  [gather(): repeated = jnp.broadcast_to(own, (n_row * n_col,) + own.shape)]
  transfers between devices with their start and end apart: 0 -> 9, of which waited for: 0 -> 4; matrix products, arithmetic and copies ran while one was open for 0% -> 0% of each run, Pallas kernels for 0% -> 0%
where the time goes in v5:
time: 27.1 us; the launch traced here: 26.7 us
  starting transfers between devices  11.8 us (44%)
  Pallas kernels  7.5 us (28%)
  waiting for transfers between devices  3.24 us (12%)
  local copies, waits for them, and re-layouts  2.79 us (10%)
  between operations  1.4 us (5%)
    ppermute x9, starting transfers between devices, flip_by(): return lax.ppermute(block, ('row', 'col'), pairs)  11.8 us
    pallas_call x1, Pallas kernels, gathered_body(): pl.pallas_call(functools.partial(part_kernel, n_row, n_col, counts, owner...  7.32 us
    ppermute x9, waiting for transfers between devices, flip_by(): return lax.ppermute(block, ('row', 'col'), pairs)  3.24 us
    unnamed x16, local copies, waits for them, and re-layouts  2.79 us
  transfers between devices with their start and end apart: 9, of which 4 were waited for; matrix products, arithmetic and copies ran while one was open for 0% of the time, Pallas kernels for 0%

profile of v5, /device:TPU:0, one launch (start us, length us, event | category | flops | bytes accessed | tf_op | source)
XLA Modules:
  0.0 26.7 jit_solution(5867432082108493252)
XLA Ops:
  0.6 0.0 copy-start
  1.3 0.0 copy-start.1
  1.3 0.7 %copy-done.1 = bf16[8,8,128]{2,1,0:T(8,128)(2,1)S(1)} copy-done((bf16[8,8,128]{2,1,0:T(8,128)(2,1)S(1)}, bf16[8,8,128]{2,1,0:T(8,128)(2,1)}, u32[]{:S(2)}) %copy-start.1) | copy-done | bytes 16408
  2.0 0.0 copy-start.3
  2.0 0.7 %copy-done.3 = bf16[8,8,128]{2,1,0:T(8,128)(2,1)S(1)} copy-done((bf16[8,8,128]{2,1,0:T(8,128)(2,1)S(1)}, bf16[8,8,128]{2,1,0:T(8,128)(2,1)}, u32[]{:S(2)}) %copy-start.3) | copy-done | bytes 16408
  2.8 0.0 copy-start.4
  2.8 0.7 %copy-done.4 = s32[8,8]{1,0:T(8,128)S(1)} copy-done((s32[8,8]{1,0:T(8,128)S(1)}, s32[8,8]{1,0:T(8,128)}, u32[]{:S(2)}) %copy-start.4) | copy-done | bytes 280
  3.5 0.0 copy-start.5
  3.5 0.7 %copy-done.5 = f32[128]{0:T(128)S(1)} copy-done((f32[128]{0:T(128)S(1)}, f32[128]{0:T(128)}, u32[]{:S(2)}) %copy-start.5) | copy-done | bytes 536
  4.1 0.2 pack.1
  4.3 0.5 %collective-permute-start = (bf16[144,128]{1,0:T(8,128)(2,1)S(1)}, bf16[144,128]{1,0:T(8,128)(2,1)S(1)}, u32[]{:S(2)}, u32[]{:S(2)}) collective-permute-start(bf16[144,128]{1,0:T(8,128)(2,1)S(1)} %pack.1), channel_id=1, source_target_pairs={{0,1},{1,0},{2,3},{3,2},{4,5},{5,4},{6,7},{7,6},{8,9},{9,8},{10,11... | collective-permute-start | bytes 110600 | tf_op jit(solution)/shard_map/ppermute | solution.py:292
  4.8 0.9 %collective-permute-done = bf16[144,128]{1,0:T(8,128)(2,1)S(1)} collective-permute-done((bf16[144,128]{1,0:T(8,128)(2,1)S(1)}, bf16[144,128]{1,0:T(8,128)(2,1)S(1)}, u32[]{:S(2)}, u32[]{:S(2)}) %collective-permute-start) | collective-permute-done | bytes 36896 | tf_op jit(solution)/shard_map/ppermute | solution.py:292
  5.7 0.0 copy-start.2
  5.7 0.0 copy-start.6
  5.7 0.0 copy-start.7
  5.7 4.9 %collective-permute-start.5 = (bf16[2,144,128]{2,1,0:T(8,128)(2,1)S(1)}, bf16[2,144,128]{2,1,0:T(8,128)(2,1)S(1)}, u32[]{:S(2)}, u32[]{:S(2)}) collective-permute-start(bf16[2,144,128]{2,1,0:T(8,128)(2,1)S(1)} %pad_maximum_fusion.refs_0_), channel_id=1, source_target_pairs={{0,10},{1,13},{2,8},{3,15},{4,14},{5,9},{6,12},{7,11},{8,2},{9,5},... | collective-permute-start | bytes 221192 | tf_op jit(solution)/shard_map/ppermute | solution.py:292
  10.6 0.3 %collective-permute-start.3 = (bf16[2,144,128]{2,1,0:T(8,128)(2,1)S(1)}, bf16[2,144,128]{2,1,0:T(8,128)(2,1)S(1)}, u32[]{:S(2)}, u32[]{:S(2)}) collective-permute-start(bf16[2,144,128]{2,1,0:T(8,128)(2,1)S(1)} %pad_maximum_fusion.refs_0_), channel_id=1, source_target_pairs={{0,8},{1,7},{2,10},{3,5},{4,12},{5,3},{6,14},{7,1},{8,0},{9,15},{1... | collective-permute-start | bytes 221192 | tf_op jit(solution)/shard_map/ppermute | solution.py:292
  11.0 0.3 %collective-permute-start.1 = (bf16[2,144,128]{2,1,0:T(8,128)(2,1)S(1)}, bf16[2,144,128]{2,1,0:T(8,128)(2,1)S(1)}, u32[]{:S(2)}, u32[]{:S(2)}) collective-permute-start(bf16[2,144,128]{2,1,0:T(8,128)(2,1)S(1)} %pad_maximum_fusion.refs_0_), channel_id=1, source_target_pairs={{0,2},{1,5},{2,0},{3,7},{4,6},{5,1},{6,4},{7,3},{8,10},{9,13},{10,... | collective-permute-start | bytes 221192 | tf_op jit(solution)/shard_map/ppermute | solution.py:292
  11.3 4.8 %collective-permute-start.7 = (bf16[1,144,128]{2,1,0:T(8,128)(2,1)S(1)}, bf16[1,144,128]{2,1,0:T(8,128)(2,1)S(1)}, u32[]{:S(2)}, u32[]{:S(2)}) collective-permute-start(bf16[1,144,128]{2,1,0:T(8,128)(2,1)S(1)} %bitcast.5), channel_id=1, source_target_pairs={{0,14},{1,15},{2,12},{3,13},{4,10},{5,11},{6,8},{7,9},{8,6},{9,7},... | collective-permute-start | bytes 110600 | tf_op jit(solution)/shard_map/ppermute | solution.py:292
  16.0 0.0 collective-permute-done.5.refs_5_
  16.0 0.0 collective-permute-start.6
  16.0 1.0 %collective-permute-done.3.refs_3_ = bf16[2,144,128]{2,1,0:T(8,128)(2,1)S(1)} collective-permute-done((bf16[2,144,128]{2,1,0:T(8,128)(2,1)S(1)}, bf16[2,144,128]{2,1,0:T(8,128)(2,1)S(1)}, u32[]{:S(2)}, u32[]{:S(2)}) %collective-permute-start.3) | collective-permute-done | bytes 73760 | tf_op jit(solution)/shard_map/ppermute | solution.py:292
  17.1 0.0 collective-permute-start.4
  17.1 0.0 collective-permute-done.1.refs_1_
  17.1 0.5 %collective-permute-start.2 = (bf16[2,144,128]{2,1,0:T(8,128)(2,1)S(1)}, bf16[2,144,128]{2,1,0:T(8,128)(2,1)S(1)}, u32[]{:S(2)}, u32[]{:S(2)}) collective-permute-start(bf16[2,144,128]{2,1,0:T(8,128)(2,1)S(1)} %collective-permute-done.1.refs_1_), channel_id=1, source_target_pairs={{0,1},{1,0},{2,3},{3,2},{4,5},{5,4},{6,7},{7,6},{8,9},{9,8},{10,11... | collective-permute-start | bytes 221192 | tf_op jit(solution)/shard_map/ppermute | solution.py:292
  17.6 0.5 %collective-permute-done.7.refs_7_ = bf16[1,144,128]{2,1,0:T(8,128)(2,1)S(1)} collective-permute-done((bf16[1,144,128]{2,1,0:T(8,128)(2,1)S(1)}, bf16[1,144,128]{2,1,0:T(8,128)(2,1)S(1)}, u32[]{:S(2)}, u32[]{:S(2)}) %collective-permute-start.7) | collective-permute-done | bytes 36896 | tf_op jit(solution)/shard_map/ppermute | solution.py:292
  18.1 0.4 %collective-permute-start.8 = (bf16[1,144,128]{2,1,0:T(8,128)(2,1)S(1)}, bf16[1,144,128]{2,1,0:T(8,128)(2,1)S(1)}, u32[]{:S(2)}, u32[]{:S(2)}) collective-permute-start(bf16[1,144,128]{2,1,0:T(8,128)(2,1)S(1)} %collective-permute-done.7.refs_7_), channel_id=1, source_target_pairs={{0,1},{1,0},{2,3},{3,2},{4,5},{5,4},{6,7},{7,6},{8,9},{9,8},{10,11... | collective-permute-start | bytes 110600 | tf_op jit(solution)/shard_map/ppermute | solution.py:292
  18.5 0.9 %collective-permute-done.8.refs_8_ = bf16[1,144,128]{2,1,0:T(8,128)(2,1)S(1)} collective-permute-done((bf16[1,144,128]{2,1,0:T(8,128)(2,1)S(1)}, bf16[1,144,128]{2,1,0:T(8,128)(2,1)S(1)}, u32[]{:S(2)}, u32[]{:S(2)}) %collective-permute-start.8) | collective-permute-done | bytes 36896 | tf_op jit(solution)/shard_map/ppermute | solution.py:292
  19.4 0.0 collective-permute-done.6.refs_6_
  19.4 0.0 collective-permute-done.4.refs_4_
  19.4 0.0 collective-permute-done.2.refs_2_
  19.4 0.0 copy-done
  19.4 0.0 copy-done.2
  19.4 0.0 copy-done.6
  19.4 0.0 copy-done.7
  19.4 7.3 %part.1 = (bf16[8,8,128]{2,1,0:T(8,128)(2,1)}, bf16[8,8,128]{2,1,0:T(8,128)(2,1)}, f32[6,128,128]{2,1,0:T(8,128)}) custom-call(bf16[8,8,128]{2,1,0:T(8,128)(2,1)S(1)} %copy-done.2, bf16[6,128,128]{2,1,0:T(8,128)(2,1)S(1)} %copy-done, f32[1,128]{1,0:T(1,128)S(1)} %bitcast.7, f32[1,128]{1,0:T(1,128)S(1)} %bitcast.8, ...), custom_call_target="tpu_custom_call" | custom-call | tf_op jit(solution)/shard_map/part/pallas_call | solution.py:334
  (1 shorter events, 0.0 us)
Async XLA Ops:
  0.6 18.8 %copy-start = (bf16[6,128,128]{2,1,0:T(8,128)(2,1)S(1)}, bf16[6,128,128]{2,1,0:T(8,128)(2,1)}, u32[]{:S(2)}) copy-start(bf16[6,128,128]{2,1,0:T(8,128)(2,1)} %weights_ref.1) | copy-start | bytes 589828
  1.3 0.7 %copy-start.1 = (bf16[8,8,128]{2,1,0:T(8,128)(2,1)S(1)}, bf16[8,8,128]{2,1,0:T(8,128)(2,1)}, u32[]{:S(2)}) copy-start(bf16[8,8,128]{2,1,0:T(8,128)(2,1)} %act_ref.3) | copy-start | bytes 49156
  2.0 0.7 %copy-start.3 = (bf16[8,8,128]{2,1,0:T(8,128)(2,1)S(1)}, bf16[8,8,128]{2,1,0:T(8,128)(2,1)}, u32[]{:S(2)}) copy-start(bf16[8,8,128]{2,1,0:T(8,128)(2,1)} %cot_ref.1) | copy-start | bytes 49156
  2.8 0.7 %copy-start.4 = (s32[8,8]{1,0:T(8,128)S(1)}, s32[8,8]{1,0:T(8,128)}, u32[]{:S(2)}) copy-start(s32[8,8]{1,0:T(8,128)} %mask_ref.1) | copy-start | bytes 772
  3.5 0.7 %copy-start.5 = (f32[128]{0:T(128)S(1)}, f32[128]{0:T(128)}, u32[]{:S(2)}) copy-start(f32[128]{0:T(128)} %param.11) | copy-start | bytes 1540
  4.3 1.4 %collective-permute-start = (bf16[144,128]{1,0:T(8,128)(2,1)S(1)}, bf16[144,128]{1,0:T(8,128)(2,1)S(1)}, u32[]{:S(2)}, u32[]{:S(2)}) collective-permute-start(bf16[144,128]{1,0:T(8,128)(2,1)S(1)} %pack.1), channel_id=1, source_target_pairs={{0,1},{1,0},{2,3},{3,2},{4,5},{5,4},{6,7},{7,6},{8,9},{9,8},{10,11... | collective-permute-start | bytes 110600 | tf_op jit(solution)/shard_map/ppermute | solution.py:292
  5.7 13.7 %copy-start.2 = (bf16[8,8,128]{2,1,0:T(8,128)(2,1)S(1)}, bf16[8,8,128]{2,1,0:T(8,128)(2,1)}, u32[]{:S(2)}) copy-start(bf16[8,8,128]{2,1,0:T(8,128)(2,1)} %act_ref.3) | copy-start | bytes 49156
  5.7 13.7 %copy-start.6 = (f32[128]{0:T(128)S(1)}, f32[128]{0:T(128)}, u32[]{:S(2)}) copy-start(f32[128]{0:T(128)} %param.11) | copy-start | bytes 1540
  5.7 13.7 %copy-start.7 = (f32[128]{0:T(128)S(1)}, f32[128]{0:T(128)}, u32[]{:S(2)}) copy-start(f32[128]{0:T(128)} %param.12) | copy-start | bytes 1540
  5.7 10.3 %collective-permute-start.5 = (bf16[2,144,128]{2,1,0:T(8,128)(2,1)S(1)}, bf16[2,144,128]{2,1,0:T(8,128)(2,1)S(1)}, u32[]{:S(2)}, u32[]{:S(2)}) collective-permute-start(bf16[2,144,128]{2,1,0:T(8,128)(2,1)S(1)} %pad_maximum_fusion.refs_0_), channel_id=1, source_target_pairs={{0,10},{1,13},{2,8},{3,15},{4,14},{5,9},{6,12},{7,11},{8,2},{9,5},... | collective-permute-start | bytes 221192 | tf_op jit(solution)/shard_map/ppermute | solution.py:292
  10.6 6.4 %collective-permute-start.3 = (bf16[2,144,128]{2,1,0:T(8,128)(2,1)S(1)}, bf16[2,144,128]{2,1,0:T(8,128)(2,1)S(1)}, u32[]{:S(2)}, u32[]{:S(2)}) collective-permute-start(bf16[2,144,128]{2,1,0:T(8,128)(2,1)S(1)} %pad_maximum_fusion.refs_0_), channel_id=1, source_target_pairs={{0,8},{1,7},{2,10},{3,5},{4,12},{5,3},{6,14},{7,1},{8,0},{9,15},{1... | collective-permute-start | bytes 221192 | tf_op jit(solution)/shard_map/ppermute | solution.py:292
  11.0 6.1 %collective-permute-start.1 = (bf16[2,144,128]{2,1,0:T(8,128)(2,1)S(1)}, bf16[2,144,128]{2,1,0:T(8,128)(2,1)S(1)}, u32[]{:S(2)}, u32[]{:S(2)}) collective-permute-start(bf16[2,144,128]{2,1,0:T(8,128)(2,1)S(1)} %pad_maximum_fusion.refs_0_), channel_id=1, source_target_pairs={{0,2},{1,5},{2,0},{3,7},{4,6},{5,1},{6,4},{7,3},{8,10},{9,13},{10,... | collective-permute-start | bytes 221192 | tf_op jit(solution)/shard_map/ppermute | solution.py:292
  11.3 6.8 %collective-permute-start.7 = (bf16[1,144,128]{2,1,0:T(8,128)(2,1)S(1)}, bf16[1,144,128]{2,1,0:T(8,128)(2,1)S(1)}, u32[]{:S(2)}, u32[]{:S(2)}) collective-permute-start(bf16[1,144,128]{2,1,0:T(8,128)(2,1)S(1)} %bitcast.5), channel_id=1, source_target_pairs={{0,14},{1,15},{2,12},{3,13},{4,10},{5,11},{6,8},{7,9},{8,6},{9,7},... | collective-permute-start | bytes 110600 | tf_op jit(solution)/shard_map/ppermute | solution.py:292
  16.0 3.3 %collective-permute-start.6 = (bf16[2,144,128]{2,1,0:T(8,128)(2,1)S(1)}, bf16[2,144,128]{2,1,0:T(8,128)(2,1)S(1)}, u32[]{:S(2)}, u32[]{:S(2)}) collective-permute-start(bf16[2,144,128]{2,1,0:T(8,128)(2,1)S(1)} %collective-permute-done.5.refs_5_), channel_id=1, source_target_pairs={{0,1},{1,0},{2,3},{3,2},{4,5},{5,4},{6,7},{7,6},{8,9},{9,8},{10,11... | collective-permute-start | bytes 221192 | tf_op jit(solution)/shard_map/ppermute | solution.py:292
  17.1 2.3 %collective-permute-start.4 = (bf16[2,144,128]{2,1,0:T(8,128)(2,1)S(1)}, bf16[2,144,128]{2,1,0:T(8,128)(2,1)S(1)}, u32[]{:S(2)}, u32[]{:S(2)}) collective-permute-start(bf16[2,144,128]{2,1,0:T(8,128)(2,1)S(1)} %collective-permute-done.3.refs_3_), channel_id=1, source_target_pairs={{0,1},{1,0},{2,3},{3,2},{4,5},{5,4},{6,7},{7,6},{8,9},{9,8},{10,11... | collective-permute-start | bytes 221192 | tf_op jit(solution)/shard_map/ppermute | solution.py:292
  17.1 2.3 %collective-permute-start.2 = (bf16[2,144,128]{2,1,0:T(8,128)(2,1)S(1)}, bf16[2,144,128]{2,1,0:T(8,128)(2,1)S(1)}, u32[]{:S(2)}, u32[]{:S(2)}) collective-permute-start(bf16[2,144,128]{2,1,0:T(8,128)(2,1)S(1)} %collective-permute-done.1.refs_1_), channel_id=1, source_target_pairs={{0,1},{1,0},{2,3},{3,2},{4,5},{5,4},{6,7},{7,6},{8,9},{9,8},{10,11... | collective-permute-start | bytes 221192 | tf_op jit(solution)/shard_map/ppermute | solution.py:292
  18.1 1.3 %collective-permute-start.8 = (bf16[1,144,128]{2,1,0:T(8,128)(2,1)S(1)}, bf16[1,144,128]{2,1,0:T(8,128)(2,1)S(1)}, u32[]{:S(2)}, u32[]{:S(2)}) collective-permute-start(bf16[1,144,128]{2,1,0:T(8,128)(2,1)S(1)} %collective-permute-done.7.refs_7_), channel_id=1, source_target_pairs={{0,1},{1,0},{2,3},{3,2},{4,5},{5,4},{6,7},{7,6},{8,9},{9,8},{10,11... | collective-permute-start | bytes 110600 | tf_op jit(solution)/shard_map/ppermute | solution.py:292

commit v6 on v5

--- a/solution.py
+++ b/solution.py
@@ -106,18 +106,24 @@
     return (update, pair_grad, weight_grad)
 
 
-def pack_kernel(crop_ref, act_ref, mask_ref, cot_ref, gain_ref, out_ref):
+def pack_kernel(
+    act_hbm, mask_hbm, cot_hbm, gain_hbm, out_ref, act_ref, mask_ref, gain_ref, sems
+):
     tile_rows, tile_cols, channels = act_ref.shape
     pairs = tile_rows * tile_cols
+    pack_copies = [
+        pltpu.make_async_copy(act_hbm, act_ref, sems.at[0]),
+        pltpu.make_async_copy(gain_hbm, gain_ref, sems.at[1]),
+        pltpu.make_async_copy(mask_hbm, mask_ref, sems.at[2]),
+        pltpu.make_async_copy(cot_hbm, out_ref.at[pairs : 2 * pairs], sems.at[3]),
+    ]
+    for copy in pack_copies:
+        copy.start()
+    for copy in pack_copies:
+        copy.wait()
     z_hat, _ = normalize(act_ref[...].astype(jnp.float32).reshape(pairs, channels))
     out_ref[0:pairs] = (z_hat * gain_ref[...]).astype(jnp.bfloat16)
-    out_ref[pairs : 2 * pairs] = cot_ref[...].reshape(pairs, channels)
-    row_at = lax.axis_index("row") * tile_rows
-    col_at = lax.axis_index("col") * tile_cols
-    rows = row_at + lax.broadcasted_iota(jnp.int32, (tile_rows, tile_cols), 0)
-    cols = col_at + lax.broadcasted_iota(jnp.int32, (tile_rows, tile_cols), 1)
-    inside = (rows < crop_ref[0]) & (cols < crop_ref[0])
-    keep = jnp.where(inside, mask_ref[...], 0).astype(jnp.float32)
+    keep = mask_ref[...].astype(jnp.float32)
     wide = jnp.concatenate([keep, jnp.zeros((tile_rows, channels - tile_cols), jnp.float32)], axis=1)
     tall = jnp.concatenate([wide, jnp.zeros((channels - tile_rows, channels), jnp.float32)], axis=0)
     flipped = tall.T
@@ -150,14 +156,14 @@
 
 
 def part_kernel(
-    n_row, n_col, counts, owners, act_ref, weights_ref, in_gain_ref, out_gain_ref, *refs,
+    n_row, n_col, counts, owners, crop_ref, act_ref, weights_ref, in_gain_ref, out_gain_ref, *refs,
 ):
     pieces = [ref.at[b] for ref, count in zip(refs, counts) for b in range(count)]
-    part_refs(n_row, n_col, owners, act_ref, weights_ref, in_gain_ref, out_gain_ref, pieces, *refs[len(counts) :])
+    part_refs(n_row, n_col, owners, crop_ref, act_ref, weights_ref, in_gain_ref, out_gain_ref, pieces, *refs[len(counts) :])
 
 
 def part_refs(
-    n_row, n_col, owners, act_ref, weights_ref, in_gain_ref, out_gain_ref, all_refs,
+    n_row, n_col, owners, crop_ref, act_ref, weights_ref, in_gain_ref, out_gain_ref, all_refs,
     update_ref, pair_grad_ref, weight_grad_ref,
     proj_ref, left_ref, right_ref, keep_ref, tri_ref, lin_ref, gate_ref, hat_ref, upd_ref, d_ref, slot_ref,
 ):
@@ -171,9 +177,14 @@
     row_me, col_me = lax.axis_index("row"), lax.axis_index("col")
 
     core_me = col_me % 2
+    crop = crop_ref[0]
+    spots = []
     for slot, (near, far) in enumerate(owners):
         shift = [jnp.where(core_me == 0, a, b) for a, b in zip(near, far)]
-        slot_ref[(row_me ^ shift[0]) * n_col + (col_me ^ shift[1])] = slot * tile
+        spots.append((row_me ^ shift[0], col_me ^ shift[1]))
+        slot_ref[spots[slot][0] * n_col + spots[slot][1]] = slot * tile
+    col_offset = lax.broadcasted_iota(jnp.int32, (tile_cols, channels), 0)
+    row_offset = lax.broadcasted_iota(jnp.int32, (tile_cols, channels), 1)
 
     def base(row, col):
         return pl.multiple_of(slot_ref[row * n_col + col], tile)
@@ -212,6 +223,9 @@
             proj_ref[s, rows, :] = jnp.dot(normed, weights_ref[s], preferred_element_type=f32)
         for b in range(at // tile, (at + chunk) // tile):
             keep = all_refs[b][2 * tile : 2 * tile + 16, :].astype(f32)[0:tile_cols]
+            rows_in = row_offset < crop - spots[b][0] * tile_rows
+            cols_in = col_offset < crop - spots[b][1] * tile_cols
+            keep = jnp.where(rows_in & cols_in, keep, 0.0)
             for ii in range(tile_rows):
                 spot = (b * tile_rows + ii) * tile_cols
                 keep_ref[spot : spot + tile_cols, :] = jnp.broadcast_to(keep[:, ii : ii + 1], (tile_cols, channels))
@@ -320,14 +334,22 @@
     pairs = tile * n_row * n_col
     vmem = pl.BlockSpec(memory_space=pltpu.VMEM)
     smem = pl.BlockSpec(memory_space=pltpu.SMEM)
+    hbm = pl.BlockSpec(memory_space=pltpu.HBM)
     packed = pl.pallas_call(
         pack_kernel,
         name="pack",
         out_shape=jax.ShapeDtypeStruct((2 * tile + 16, channels), jnp.bfloat16),
-        in_specs=[smem, vmem, vmem, vmem, vmem],
+        in_specs=[hbm] * 4,
         out_specs=vmem,
-        compiler_params=pltpu.CompilerParams(vmem_limit_bytes=2 * 1024 * 1024),
-    )(crop_length, pair_act, pair_mask, cotangent, in_gain.reshape(1, channels))
+        scratch_shapes=[
+            pltpu.VMEM(pair_act.shape, pair_act.dtype),
+            pltpu.VMEM(pair_mask.shape, jnp.int32),
+            pltpu.VMEM((1, channels), jnp.float32),
+            pltpu.SemaphoreType.DMA((4,)),
+        ],
+        compiler_params=pltpu.CompilerParams(vmem_limit_bytes=60 * 1024 * 1024),
+    )(pair_act, pair_mask, cotangent.reshape(tile, channels), in_gain.reshape(1, channels))
+    crop_length, packed = lax.optimization_barrier((crop_length, packed))
     everyone, owners = gather(packed, n_row, n_col)
     counts = tuple(piece.shape[0] for piece in everyone)
     f32, bf16 = jnp.float32, jnp.bfloat16
@@ -339,7 +361,7 @@
             jax.ShapeDtypeStruct(pair_act.shape, bf16),
             jax.ShapeDtypeStruct(weights.shape, f32),
         ),
-        in_specs=[vmem] * (4 + len(counts)),
+        in_specs=[smem] + [vmem] * (4 + len(counts)),
         out_specs=(vmem, vmem, vmem),
         scratch_shapes=[
             pltpu.VMEM((5, pairs, channels), f32),
@@ -355,7 +377,7 @@
             pltpu.SMEM((n_row * n_col,), jnp.int32),
         ],
         compiler_params=pltpu.CompilerParams(vmem_limit_bytes=24 * 1024 * 1024),
-    )(pair_act, weights, in_gain.reshape(1, channels), out_gain.reshape(1, channels), *everyone)
+    )(crop_length, pair_act, weights, in_gain.reshape(1, channels), out_gain.reshape(1, channels), *everyone)
 
 
 def body(n_row, n_col, pair_act, *others):

time: 27.1 us -> 26.5 us (0.978)
  local copies, waits for them, and re-layouts: 2.79 us -> 0.44 us
  Pallas kernels: 7.5 us -> 8.95 us
  other arithmetic: 0.01 us -> 0.79 us
  waiting for transfers between devices: 3.24 us -> 2.9 us
    unnamed x16 -> x8, local copies, waits for them, and re-layouts: 2.79 us -> 0.44 us
    pallas_call x1, Pallas kernels: 0.17 us -> 1.64 us  [gathered_body(): pl.pallas_call(pack_kernel, name='pack', out_shape=jax.ShapeDtypeStruct((...]
    another operation x1, other arithmetic: 0.01 us -> 0.79 us  [gather(): both = jnp.stack([own, other(own)])]
    ppermute x9, waiting for transfers between devices: 3.24 us -> 2.9 us  [flip_by(): return lax.ppermute(block, ('row', 'col'), pairs)]
where the time goes in v6:
time: 26.5 us; the launch traced here: 26.2 us
  starting transfers between devices  11.8 us (45%)
  Pallas kernels  8.95 us (34%)
  waiting for transfers between devices  2.9 us (11%)
  between operations  1.34 us (5%)
  other arithmetic  0.79 us (3%)
  local copies, waits for them, and re-layouts  0.44 us (2%)
    ppermute x9, starting transfers between devices, flip_by(): return lax.ppermute(block, ('row', 'col'), pairs)  11.8 us
    pallas_call x1, Pallas kernels, gathered_body(): pl.pallas_call(functools.partial(part_kernel, n_row, n_col, counts, owner...  7.31 us
    ppermute x9, waiting for transfers between devices, flip_by(): return lax.ppermute(block, ('row', 'col'), pairs)  2.9 us
    pallas_call x1, Pallas kernels, gathered_body(): pl.pallas_call(pack_kernel, name='pack', out_shape=jax.ShapeDtypeStruct((...  1.64 us
    another operation x1, other arithmetic, gather(): both = jnp.stack([own, other(own)])  0.79 us
  transfers between devices with their start and end apart: 9, of which 4 were waited for; matrix products, arithmetic and copies ran while one was open for 0% of the time, Pallas kernels for 0%

profile of v6, /device:TPU:0, one launch (start us, length us, event | category | flops | bytes accessed | tf_op | source)
XLA Modules:
  0.0 26.2 jit_solution(11454422077728471675)
XLA Ops:
  0.6 0.0 copy-start
  0.6 1.6 %pack.1 = bf16[144,128]{1,0:T(8,128)(2,1)} custom-call(bf16[8,8,128]{2,1,0:T(8,128)(2,1)} %act_ref.1, s32[8,8]{1,0:T(8,128)} %mask_hbm.1, bf16[64,128]{1,0:T(8,128)(2,1)} %bitcast.11, f32[1,128]{1,0:T(1,128)} %bitcast.5), custom_call_target="tpu_custom_call" | custom-call | tf_op jit(solution)/shard_map/pack/pallas_call | solution.py:338
  2.3 0.5 %collective-permute-start = (bf16[144,128]{1,0:T(8,128)(2,1)}, bf16[144,128]{1,0:T(8,128)(2,1)S(1)}, u32[]{:S(2)}, u32[]{:S(2)}) collective-permute-start(bf16[144,128]{1,0:T(8,128)(2,1)} %pack.1), channel_id=1, source_target_pairs={{0,1},{1,0},{2,3},{3,2},{4,5},{5,4},{6,7},{7,6},{8,9},{9,8},{10,11... | collective-permute-start | bytes 110600 | tf_op jit(solution)/shard_map/ppermute | solution.py:306
  2.8 1.1 %collective-permute-done = bf16[144,128]{1,0:T(8,128)(2,1)S(1)} collective-permute-done((bf16[144,128]{1,0:T(8,128)(2,1)}, bf16[144,128]{1,0:T(8,128)(2,1)S(1)}, u32[]{:S(2)}, u32[]{:S(2)}) %collective-permute-start) | collective-permute-done | bytes 36896 | tf_op jit(solution)/shard_map/ppermute | solution.py:306
  3.9 0.0 copy-start.1
  3.9 0.8 %pad_maximum_fusion.refs_0_ = bf16[2,144,128]{2,1,0:T(8,128)(2,1)S(1)} fusion(bf16[1,144,128]{2,1,0:T(8,128)(2,1)S(1)} %bitcast.10, bf16[1,144,128]{2,1,0:T(8,128)(2,1)} %bitcast.8), kind=kLoop, calls=%fused_computation | loop fusion | flops 36864 | bytes 147456 | tf_op jit(solution)/shard_map/stack | solution.py:313
  4.7 4.9 %collective-permute-start.5 = (bf16[2,144,128]{2,1,0:T(8,128)(2,1)S(1)}, bf16[2,144,128]{2,1,0:T(8,128)(2,1)S(1)}, u32[]{:S(2)}, u32[]{:S(2)}) collective-permute-start(bf16[2,144,128]{2,1,0:T(8,128)(2,1)S(1)} %pad_maximum_fusion.refs_0_), channel_id=1, source_target_pairs={{0,10},{1,13},{2,8},{3,15},{4,14},{5,9},{6,12},{7,11},{8,2},{9,5},... | collective-permute-start | bytes 221192 | tf_op jit(solution)/shard_map/ppermute | solution.py:306
  9.5 0.3 %collective-permute-start.3 = (bf16[2,144,128]{2,1,0:T(8,128)(2,1)S(1)}, bf16[2,144,128]{2,1,0:T(8,128)(2,1)S(1)}, u32[]{:S(2)}, u32[]{:S(2)}) collective-permute-start(bf16[2,144,128]{2,1,0:T(8,128)(2,1)S(1)} %pad_maximum_fusion.refs_0_), channel_id=1, source_target_pairs={{0,8},{1,7},{2,10},{3,5},{4,12},{5,3},{6,14},{7,1},{8,0},{9,15},{1... | collective-permute-start | bytes 221192 | tf_op jit(solution)/shard_map/ppermute | solution.py:306
  9.9 0.3 %collective-permute-start.1 = (bf16[2,144,128]{2,1,0:T(8,128)(2,1)S(1)}, bf16[2,144,128]{2,1,0:T(8,128)(2,1)S(1)}, u32[]{:S(2)}, u32[]{:S(2)}) collective-permute-start(bf16[2,144,128]{2,1,0:T(8,128)(2,1)S(1)} %pad_maximum_fusion.refs_0_), channel_id=1, source_target_pairs={{0,2},{1,5},{2,0},{3,7},{4,6},{5,1},{6,4},{7,3},{8,10},{9,13},{10,... | collective-permute-start | bytes 221192 | tf_op jit(solution)/shard_map/ppermute | solution.py:306
  10.2 4.8 %collective-permute-start.7 = (bf16[1,144,128]{2,1,0:T(8,128)(2,1)}, bf16[1,144,128]{2,1,0:T(8,128)(2,1)S(1)}, u32[]{:S(2)}, u32[]{:S(2)}) collective-permute-start(bf16[1,144,128]{2,1,0:T(8,128)(2,1)} %bitcast.9), channel_id=1, source_target_pairs={{0,14},{1,15},{2,12},{3,13},{4,10},{5,11},{6,8},{7,9},{8,6},{9,7},... | collective-permute-start | bytes 110600 | tf_op jit(solution)/shard_map/ppermute | solution.py:306
  14.9 0.0 collective-permute-done.5.refs_5_
  14.9 0.0 collective-permute-start.6
  14.9 1.0 %collective-permute-done.3.refs_3_ = bf16[2,144,128]{2,1,0:T(8,128)(2,1)S(1)} collective-permute-done((bf16[2,144,128]{2,1,0:T(8,128)(2,1)S(1)}, bf16[2,144,128]{2,1,0:T(8,128)(2,1)S(1)}, u32[]{:S(2)}, u32[]{:S(2)}) %collective-permute-start.3) | collective-permute-done | bytes 73760 | tf_op jit(solution)/shard_map/ppermute | solution.py:306
  16.0 0.0 collective-permute-start.4
  16.0 0.0 collective-permute-done.1.refs_1_
  16.0 0.5 %collective-permute-start.2 = (bf16[2,144,128]{2,1,0:T(8,128)(2,1)S(1)}, bf16[2,144,128]{2,1,0:T(8,128)(2,1)S(1)}, u32[]{:S(2)}, u32[]{:S(2)}) collective-permute-start(bf16[2,144,128]{2,1,0:T(8,128)(2,1)S(1)} %collective-permute-done.1.refs_1_), channel_id=1, source_target_pairs={{0,1},{1,0},{2,3},{3,2},{4,5},{5,4},{6,7},{7,6},{8,9},{9,8},{10,11... | collective-permute-start | bytes 221192 | tf_op jit(solution)/shard_map/ppermute | solution.py:306
  16.5 0.6 %collective-permute-done.7.refs_7_ = bf16[1,144,128]{2,1,0:T(8,128)(2,1)S(1)} collective-permute-done((bf16[1,144,128]{2,1,0:T(8,128)(2,1)}, bf16[1,144,128]{2,1,0:T(8,128)(2,1)S(1)}, u32[]{:S(2)}, u32[]{:S(2)}) %collective-permute-start.7) | collective-permute-done | bytes 36896 | tf_op jit(solution)/shard_map/ppermute | solution.py:306
  17.1 0.5 %collective-permute-start.8 = (bf16[1,144,128]{2,1,0:T(8,128)(2,1)S(1)}, bf16[1,144,128]{2,1,0:T(8,128)(2,1)S(1)}, u32[]{:S(2)}, u32[]{:S(2)}) collective-permute-start(bf16[1,144,128]{2,1,0:T(8,128)(2,1)S(1)} %collective-permute-done.7.refs_7_), channel_id=1, source_target_pairs={{0,1},{1,0},{2,3},{3,2},{4,5},{5,4},{6,7},{7,6},{8,9},{9,8},{10,11... | collective-permute-start | bytes 110600 | tf_op jit(solution)/shard_map/ppermute | solution.py:306
  18.3 0.0 copy-start.2
  18.3 0.0 copy-start.3
  18.3 0.2 collective-permute-done.8.refs_8_
  18.5 0.0 collective-permute-done.6.refs_6_
  18.5 0.0 collective-permute-done.4.refs_4_
  18.5 0.0 collective-permute-done.2.refs_2_
  18.5 0.0 copy-done
  18.5 0.0 copy-done.1
  18.5 0.4 %copy-done.2 = f32[128]{0:T(128)S(1)} copy-done((f32[128]{0:T(128)S(1)}, f32[128]{0:T(128)}, u32[]{:S(2)}) %copy-start.2) | copy-done | bytes 536
  18.9 0.0 copy-done.3
  18.9 7.3 %part.1 = (bf16[8,8,128]{2,1,0:T(8,128)(2,1)}, bf16[8,8,128]{2,1,0:T(8,128)(2,1)}, f32[6,128,128]{2,1,0:T(8,128)}) custom-call(s32[1]{0:T(128)S(6)} %copy.10.crop_ref, bf16[8,8,128]{2,1,0:T(8,128)(2,1)S(1)} %copy-done.1, bf16[6,128,128]{2,1,0:T(8,128)(2,1)S(1)} %copy-done, f32[1,128]{1,0:T(1,128)S(1)} %bitcast.6, f32[1,128]{1,0:T(1,128)S(1)} %bitcast.7, ...), custom_call_target="tpu_custom_call" | custom-call | tf_op jit(solution)/shard_map/part/pallas_call | solution.py:356
Async XLA Ops:
  0.6 17.9 %copy-start = (bf16[6,128,128]{2,1,0:T(8,128)(2,1)S(1)}, bf16[6,128,128]{2,1,0:T(8,128)(2,1)}, u32[]{:S(2)}) copy-start(bf16[6,128,128]{2,1,0:T(8,128)(2,1)} %weights_ref.1) | copy-start | bytes 589828
  2.3 1.6 %collective-permute-start = (bf16[144,128]{1,0:T(8,128)(2,1)}, bf16[144,128]{1,0:T(8,128)(2,1)S(1)}, u32[]{:S(2)}, u32[]{:S(2)}) collective-permute-start(bf16[144,128]{1,0:T(8,128)(2,1)} %pack.1), channel_id=1, source_target_pairs={{0,1},{1,0},{2,3},{3,2},{4,5},{5,4},{6,7},{7,6},{8,9},{9,8},{10,11... | collective-permute-start | bytes 110600 | tf_op jit(solution)/shard_map/ppermute | solution.py:306
  3.9 14.6 %copy-start.1 = (bf16[8,8,128]{2,1,0:T(8,128)(2,1)S(1)}, bf16[8,8,128]{2,1,0:T(8,128)(2,1)}, u32[]{:S(2)}) copy-start(bf16[8,8,128]{2,1,0:T(8,128)(2,1)} %act_ref.1) | copy-start | bytes 49156
  4.7 10.3 %collective-permute-start.5 = (bf16[2,144,128]{2,1,0:T(8,128)(2,1)S(1)}, bf16[2,144,128]{2,1,0:T(8,128)(2,1)S(1)}, u32[]{:S(2)}, u32[]{:S(2)}) collective-permute-start(bf16[2,144,128]{2,1,0:T(8,128)(2,1)S(1)} %pad_maximum_fusion.refs_0_), channel_id=1, source_target_pairs={{0,10},{1,13},{2,8},{3,15},{4,14},{5,9},{6,12},{7,11},{8,2},{9,5},... | collective-permute-start | bytes 221192 | tf_op jit(solution)/shard_map/ppermute | solution.py:306
  9.5 6.4 %collective-permute-start.3 = (bf16[2,144,128]{2,1,0:T(8,128)(2,1)S(1)}, bf16[2,144,128]{2,1,0:T(8,128)(2,1)S(1)}, u32[]{:S(2)}, u32[]{:S(2)}) collective-permute-start(bf16[2,144,128]{2,1,0:T(8,128)(2,1)S(1)} %pad_maximum_fusion.refs_0_), channel_id=1, source_target_pairs={{0,8},{1,7},{2,10},{3,5},{4,12},{5,3},{6,14},{7,1},{8,0},{9,15},{1... | collective-permute-start | bytes 221192 | tf_op jit(solution)/shard_map/ppermute | solution.py:306
  9.9 6.1 %collective-permute-start.1 = (bf16[2,144,128]{2,1,0:T(8,128)(2,1)S(1)}, bf16[2,144,128]{2,1,0:T(8,128)(2,1)S(1)}, u32[]{:S(2)}, u32[]{:S(2)}) collective-permute-start(bf16[2,144,128]{2,1,0:T(8,128)(2,1)S(1)} %pad_maximum_fusion.refs_0_), channel_id=1, source_target_pairs={{0,2},{1,5},{2,0},{3,7},{4,6},{5,1},{6,4},{7,3},{8,10},{9,13},{10,... | collective-permute-start | bytes 221192 | tf_op jit(solution)/shard_map/ppermute | solution.py:306
  10.2 6.9 %collective-permute-start.7 = (bf16[1,144,128]{2,1,0:T(8,128)(2,1)}, bf16[1,144,128]{2,1,0:T(8,128)(2,1)S(1)}, u32[]{:S(2)}, u32[]{:S(2)}) collective-permute-start(bf16[1,144,128]{2,1,0:T(8,128)(2,1)} %bitcast.9), channel_id=1, source_target_pairs={{0,14},{1,15},{2,12},{3,13},{4,10},{5,11},{6,8},{7,9},{8,6},{9,7},... | collective-permute-start | bytes 110600 | tf_op jit(solution)/shard_map/ppermute | solution.py:306
  14.9 3.5 %collective-permute-start.6 = (bf16[2,144,128]{2,1,0:T(8,128)(2,1)S(1)}, bf16[2,144,128]{2,1,0:T(8,128)(2,1)S(1)}, u32[]{:S(2)}, u32[]{:S(2)}) collective-permute-start(bf16[2,144,128]{2,1,0:T(8,128)(2,1)S(1)} %collective-permute-done.5.refs_5_), channel_id=1, source_target_pairs={{0,1},{1,0},{2,3},{3,2},{4,5},{5,4},{6,7},{7,6},{8,9},{9,8},{10,11... | collective-permute-start | bytes 221192 | tf_op jit(solution)/shard_map/ppermute | solution.py:306
  16.0 2.5 %collective-permute-start.4 = (bf16[2,144,128]{2,1,0:T(8,128)(2,1)S(1)}, bf16[2,144,128]{2,1,0:T(8,128)(2,1)S(1)}, u32[]{:S(2)}, u32[]{:S(2)}) collective-permute-start(bf16[2,144,128]{2,1,0:T(8,128)(2,1)S(1)} %collective-permute-done.3.refs_3_), channel_id=1, source_target_pairs={{0,1},{1,0},{2,3},{3,2},{4,5},{5,4},{6,7},{7,6},{8,9},{9,8},{10,11... | collective-permute-start | bytes 221192 | tf_op jit(solution)/shard_map/ppermute | solution.py:306
  16.0 2.5 %collective-permute-start.2 = (bf16[2,144,128]{2,1,0:T(8,128)(2,1)S(1)}, bf16[2,144,128]{2,1,0:T(8,128)(2,1)S(1)}, u32[]{:S(2)}, u32[]{:S(2)}) collective-permute-start(bf16[2,144,128]{2,1,0:T(8,128)(2,1)S(1)} %collective-permute-done.1.refs_1_), channel_id=1, source_target_pairs={{0,1},{1,0},{2,3},{3,2},{4,5},{5,4},{6,7},{7,6},{8,9},{9,8},{10,11... | collective-permute-start | bytes 221192 | tf_op jit(solution)/shard_map/ppermute | solution.py:306
  17.1 1.4 %collective-permute-start.8 = (bf16[1,144,128]{2,1,0:T(8,128)(2,1)S(1)}, bf16[1,144,128]{2,1,0:T(8,128)(2,1)S(1)}, u32[]{:S(2)}, u32[]{:S(2)}) collective-permute-start(bf16[1,144,128]{2,1,0:T(8,128)(2,1)S(1)} %collective-permute-done.7.refs_7_), channel_id=1, source_target_pairs={{0,1},{1,0},{2,3},{3,2},{4,5},{5,4},{6,7},{7,6},{8,9},{9,8},{10,11... | collective-permute-start | bytes 110600 | tf_op jit(solution)/shard_map/ppermute | solution.py:306
  18.3 0.7 %copy-start.2 = (f32[128]{0:T(128)S(1)}, f32[128]{0:T(128)}, u32[]{:S(2)}) copy-start(f32[128]{0:T(128)} %param.11) | copy-start | bytes 1540
  18.3 0.7 %copy-start.3 = (f32[128]{0:T(128)S(1)}, f32[128]{0:T(128)}, u32[]{:S(2)}) copy-start(f32[128]{0:T(128)} %param.12) | copy-start | bytes 1540

commit v7 on v6

--- a/solution.py
+++ b/solution.py
@@ -307,24 +307,25 @@
 
 
 def gather(own, n_row, n_col):
-    def other(block):
-        return flip_by(block, n_row, n_col, (0, 1), (0, 1))
-
-    both = jnp.stack([own, other(own)])
-    chips = [(row, col) for row in range(n_row) for col in range(0, n_col, 2) if row + col > 0]
-    chips.sort(key=lambda chip: (bin(chip[0]).count("1") + chip[1] // 2, chip))
-    pieces = [both]
-    owners = [((0, 0), (0, 0)), ((0, 1), (0, 1))]
-    while len(chips) > 1:
-        near, far = chips.pop(0), chips.pop(0)
-        piece = flip_by(both, n_row, n_col, near, far)
-        pieces += [piece, other(piece)]
-        for a, b, core in ((near, far, 0), (near, far, 1), (far, near, 1), (far, near, 0)):
-            owners.append(((a[0], a[1] ^ core), (b[0], b[1] ^ core)))
-    for last in chips:
-        piece = flip_by(own[None], n_row, n_col, last, last)
-        pieces += [piece, other(piece)]
-        owners += [(last, last), ((last[0], last[1] ^ 1),) * 2]
+    def flip(block, row, col):
+        return flip_by(block, n_row, n_col, (row, col), (row, col))
+
+    along = [flip(own, shift, 0) for shift in reversed(range(1, n_row))]
+    stacks = {0: [own[None]]}
+    bit = n_col // 2
+    while bit > 0:
+        stacks.update({col ^ bit: [flip(stack[0], 0, bit)] for col, stack in stacks.items()})
+        bit //= 2
+    stacks[0].append(jnp.stack(along))
+    bit = n_col // 2
+    while bit > 0:
+        for col in [col for col, stack in stacks.items() if len(stack) == 2]:
+            stacks[col ^ bit].append(flip(stacks[col][1], 0, bit))
+        bit //= 2
+    pieces, owners = [], []
+    for col, stack in sorted(stacks.items()):
+        pieces += stack
+        owners += [((row, col),) * 2 for row in (0, *reversed(range(1, n_row)))]
     return pieces, tuple(owners)
 
 

time: 26.5 us -> 31.7 us (1.20)
  waiting for transfers between devices: 2.9 us -> 12 us
  starting transfers between devices: 11.8 us -> 8.96 us
  other arithmetic: 0.79 us -> 0.01 us
  local copies, waits for them, and re-layouts: 0.44 us -> 0.11 us
    ppermute x9, waiting for transfers between devices: 2.9 us -> 12 us  [flip_by(): return lax.ppermute(block, ('row', 'col'), pairs)]
    ppermute x9, starting transfers between devices: 11.8 us -> 8.96 us  [flip_by(): return lax.ppermute(block, ('row', 'col'), pairs)]
    another operation x1, other arithmetic: 0.79 us -> 0.01 us  [gather(): stacks[0].append(jnp.stack(along))]
    unnamed x8 -> x10, local copies, waits for them, and re-layouts: 0.44 us -> 0.11 us
  transfers between devices with their start and end apart: 9 -> 9, of which waited for: 4 -> 5; matrix products, arithmetic and copies ran while one was open for 0% -> 0% of each run, Pallas kernels for 0% -> 0%
where the time goes in v7:
time: 31.7 us; the launch traced here: 31.4 us
  waiting for transfers between devices  12 us (38%)
  starting transfers between devices  8.96 us (28%)
  Pallas kernels  8.95 us (28%)
  between operations  1.35 us (4%)
    ppermute x9, waiting for transfers between devices, flip_by(): return lax.ppermute(block, ('row', 'col'), pairs)  12 us
    ppermute x9, starting transfers between devices, flip_by(): return lax.ppermute(block, ('row', 'col'), pairs)  8.96 us
    pallas_call x1, Pallas kernels, gathered_body(): pl.pallas_call(functools.partial(part_kernel, n_row, n_col, counts, owner...  7.31 us
    pallas_call x1, Pallas kernels, gathered_body(): pl.pallas_call(pack_kernel, name='pack', out_shape=jax.ShapeDtypeStruct((...  1.64 us
  transfers between devices with their start and end apart: 9, of which 5 were waited for; matrix products, arithmetic and copies ran while one was open for 0% of the time, Pallas kernels for 0%

profile of v7, /device:TPU:0, one launch (start us, length us, event | category | flops | bytes accessed | tf_op | source)
XLA Modules:
  0.0 31.4 jit_solution(10820112143024850652)
XLA Ops:
  0.6 0.0 copy-start
  0.6 1.6 %pack.1 = bf16[144,128]{1,0:T(8,128)(2,1)} custom-call(bf16[8,8,128]{2,1,0:T(8,128)(2,1)} %act_ref.1, s32[8,8]{1,0:T(8,128)} %mask_hbm.1, bf16[64,128]{1,0:T(8,128)(2,1)} %bitcast.16, f32[1,128]{1,0:T(1,128)} %bitcast.10), custom_call_target="tpu_custom_call" | custom-call | tf_op jit(solution)/shard_map/pack/pallas_call | solution.py:339
  2.3 3.1 %collective-permute-start.2 = (bf16[144,128]{1,0:T(8,128)(2,1)}, bf16[144,128]{1,0:T(8,128)(2,1)S(1)}, u32[]{:S(2)}, u32[]{:S(2)}) collective-permute-start(bf16[144,128]{1,0:T(8,128)(2,1)} %pack.1), channel_id=1, source_target_pairs={{0,4},{1,5},{2,6},{3,7},{4,0},{5,1},{6,2},{7,3},{8,12},{9,13},{10,... | collective-permute-start | bytes 110600 | tf_op jit(solution)/shard_map/ppermute | solution.py:306
  5.4 2.6 %collective-permute-start.1 = (bf16[144,128]{1,0:T(8,128)(2,1)}, bf16[144,128]{1,0:T(8,128)(2,1)S(1)}, u32[]{:S(2)}, u32[]{:S(2)}) collective-permute-start(bf16[144,128]{1,0:T(8,128)(2,1)} %pack.1), channel_id=1, source_target_pairs={{0,8},{1,9},{2,10},{3,11},{4,12},{5,13},{6,14},{7,15},{8,0},{9,1},... | collective-permute-start | bytes 110600 | tf_op jit(solution)/shard_map/ppermute | solution.py:306
  8.0 0.0 collective-permute-start
  8.0 0.0 collective-permute-done.2
  8.0 3.1 %collective-permute-done.1 = bf16[144,128]{1,0:T(8,128)(2,1)S(1)} collective-permute-done((bf16[144,128]{1,0:T(8,128)(2,1)}, bf16[144,128]{1,0:T(8,128)(2,1)S(1)}, u32[]{:S(2)}, u32[]{:S(2)}) %collective-permute-start.1) | collective-permute-done | bytes 36896 | tf_op jit(solution)/shard_map/ppermute | solution.py:306
  11.1 2.8 %collective-permute-done = bf16[144,128]{1,0:T(8,128)(2,1)S(1)} collective-permute-done((bf16[144,128]{1,0:T(8,128)(2,1)}, bf16[144,128]{1,0:T(8,128)(2,1)S(1)}, u32[]{:S(2)}, u32[]{:S(2)}) %collective-permute-start) | collective-permute-done | bytes 36896 | tf_op jit(solution)/shard_map/ppermute | solution.py:306
  13.9 0.0 copy-start.1
  13.9 0.0 copy-start.2
  14.0 1.6 %collective-permute-start.6 = (bf16[3,144,128]{2,1,0:T(8,128)(2,1)S(1)}, bf16[3,144,128]{2,1,0:T(8,128)(2,1)S(1)}, u32[]{:S(2)}, u32[]{:S(2)}) collective-permute-start(bf16[3,144,128]{2,1,0:T(8,128)(2,1)S(1)} %pad_maximum_fusion.refs_1_), channel_id=1, source_target_pairs={{0,2},{1,3},{2,0},{3,1},{4,6},{5,7},{6,4},{7,5},{8,10},{9,11},{10,... | collective-permute-start | bytes 331784 | tf_op jit(solution)/shard_map/ppermute | solution.py:306
  15.5 0.0 collective-permute-start.4
  15.5 3.3 %collective-permute-done.6.refs_5_ = bf16[3,144,128]{2,1,0:T(8,128)(2,1)S(1)} collective-permute-done((bf16[3,144,128]{2,1,0:T(8,128)(2,1)S(1)}, bf16[3,144,128]{2,1,0:T(8,128)(2,1)S(1)}, u32[]{:S(2)}, u32[]{:S(2)}) %collective-permute-start.6) | collective-permute-done | bytes 110624 | tf_op jit(solution)/shard_map/ppermute | solution.py:306
  18.8 0.0 collective-permute-start.8
  18.8 0.0 copy-done.1
  18.8 1.5 %collective-permute-start.5 = (bf16[1,144,128]{2,1,0:T(8,128)(2,1)S(1)}, bf16[1,144,128]{2,1,0:T(8,128)(2,1)S(1)}, u32[]{:S(2)}, u32[]{:S(2)}) collective-permute-start(bf16[1,144,128]{2,1,0:T(8,128)(2,1)S(1)} %bitcast.7), channel_id=1, source_target_pairs={{0,2},{1,3},{2,0},{3,1},{4,6},{5,7},{6,4},{7,5},{8,10},{9,11},{10,... | collective-permute-start | bytes 110600 | tf_op jit(solution)/shard_map/ppermute | solution.py:306
  20.3 0.2 collective-permute-start.3
  20.5 2.2 %collective-permute-done.5.refs_4_ = bf16[1,144,128]{2,1,0:T(8,128)(2,1)S(1)} collective-permute-done((bf16[1,144,128]{2,1,0:T(8,128)(2,1)S(1)}, bf16[1,144,128]{2,1,0:T(8,128)(2,1)S(1)}, u32[]{:S(2)}, u32[]{:S(2)}) %collective-permute-start.5) | collective-permute-done | bytes 36896 | tf_op jit(solution)/shard_map/ppermute | solution.py:306
  22.7 0.0 collective-permute-start.7
  23.4 0.0 copy-start.3
  23.4 0.0 copy-start.4
  23.4 0.0 collective-permute-done.3.refs_2_
  23.4 0.5 %collective-permute-done.7.refs_6_ = bf16[1,144,128]{2,1,0:T(8,128)(2,1)S(1)} collective-permute-done((bf16[1,144,128]{2,1,0:T(8,128)(2,1)S(1)}, bf16[1,144,128]{2,1,0:T(8,128)(2,1)S(1)}, u32[]{:S(2)}, u32[]{:S(2)}) %collective-permute-start.7) | collective-permute-done | bytes 36896 | tf_op jit(solution)/shard_map/ppermute | solution.py:306
  23.9 0.0 collective-permute-done.4.refs_3_
  24.0 0.0 collective-permute-done.8.refs_7_
  24.0 0.0 copy-done
  24.0 0.0 copy-done.2
  24.0 0.1 copy-done.3
  24.0 0.0 copy-done.4
  24.1 7.3 %part.1 = (bf16[8,8,128]{2,1,0:T(8,128)(2,1)}, bf16[8,8,128]{2,1,0:T(8,128)(2,1)}, f32[6,128,128]{2,1,0:T(8,128)}) custom-call(s32[1]{0:T(128)S(6)} %copy.10.crop_ref, bf16[8,8,128]{2,1,0:T(8,128)(2,1)S(1)} %copy-done.2, bf16[6,128,128]{2,1,0:T(8,128)(2,1)S(1)} %copy-done, f32[1,128]{1,0:T(1,128)S(1)} %bitcast.11, f32[1,128]{1,0:T(1,128)S(1)} %bitcast.12, ...), custom_call_target="tpu_custom_call" | custom-call | tf_op jit(solution)/shard_map/part/pallas_call | solution.py:357
  (1 shorter events, 0.0 us)
Async XLA Ops:
  0.6 23.3 %copy-start = (bf16[6,128,128]{2,1,0:T(8,128)(2,1)S(1)}, bf16[6,128,128]{2,1,0:T(8,128)(2,1)}, u32[]{:S(2)}) copy-start(bf16[6,128,128]{2,1,0:T(8,128)(2,1)} %weights_ref.1) | copy-start | bytes 589828
  2.3 5.7 %collective-permute-start.2 = (bf16[144,128]{1,0:T(8,128)(2,1)}, bf16[144,128]{1,0:T(8,128)(2,1)S(1)}, u32[]{:S(2)}, u32[]{:S(2)}) collective-permute-start(bf16[144,128]{1,0:T(8,128)(2,1)} %pack.1), channel_id=1, source_target_pairs={{0,4},{1,5},{2,6},{3,7},{4,0},{5,1},{6,2},{7,3},{8,12},{9,13},{10,... | collective-permute-start | bytes 110600 | tf_op jit(solution)/shard_map/ppermute | solution.py:306
  5.4 5.7 %collective-permute-start.1 = (bf16[144,128]{1,0:T(8,128)(2,1)}, bf16[144,128]{1,0:T(8,128)(2,1)S(1)}, u32[]{:S(2)}, u32[]{:S(2)}) collective-permute-start(bf16[144,128]{1,0:T(8,128)(2,1)} %pack.1), channel_id=1, source_target_pairs={{0,8},{1,9},{2,10},{3,11},{4,12},{5,13},{6,14},{7,15},{8,0},{9,1},... | collective-permute-start | bytes 110600 | tf_op jit(solution)/shard_map/ppermute | solution.py:306
  8.0 6.0 %collective-permute-start = (bf16[144,128]{1,0:T(8,128)(2,1)}, bf16[144,128]{1,0:T(8,128)(2,1)S(1)}, u32[]{:S(2)}, u32[]{:S(2)}) collective-permute-start(bf16[144,128]{1,0:T(8,128)(2,1)} %pack.1), channel_id=1, source_target_pairs={{0,12},{1,13},{2,14},{3,15},{4,8},{5,9},{6,10},{7,11},{8,4},{9,5},... | collective-permute-start | bytes 110600 | tf_op jit(solution)/shard_map/ppermute | solution.py:306
  13.9 4.8 %copy-start.1 = (bf16[144,128]{1,0:T(8,128)(2,1)S(1)}, bf16[144,128]{1,0:T(8,128)(2,1)}, u32[]{:S(2)}) copy-start(bf16[144,128]{1,0:T(8,128)(2,1)} %pack.1) | copy-start | bytes 110596
  13.9 10.0 %copy-start.2 = (bf16[8,8,128]{2,1,0:T(8,128)(2,1)S(1)}, bf16[8,8,128]{2,1,0:T(8,128)(2,1)}, u32[]{:S(2)}) copy-start(bf16[8,8,128]{2,1,0:T(8,128)(2,1)} %act_ref.1) | copy-start | bytes 49156
  14.0 4.8 %collective-permute-start.6 = (bf16[3,144,128]{2,1,0:T(8,128)(2,1)S(1)}, bf16[3,144,128]{2,1,0:T(8,128)(2,1)S(1)}, u32[]{:S(2)}, u32[]{:S(2)}) collective-permute-start(bf16[3,144,128]{2,1,0:T(8,128)(2,1)S(1)} %pad_maximum_fusion.refs_1_), channel_id=1, source_target_pairs={{0,2},{1,3},{2,0},{3,1},{4,6},{5,7},{6,4},{7,5},{8,10},{9,11},{10,... | collective-permute-start | bytes 331784 | tf_op jit(solution)/shard_map/ppermute | solution.py:306
  15.5 8.4 %collective-permute-start.4 = (bf16[3,144,128]{2,1,0:T(8,128)(2,1)S(1)}, bf16[3,144,128]{2,1,0:T(8,128)(2,1)S(1)}, u32[]{:S(2)}, u32[]{:S(2)}) collective-permute-start(bf16[3,144,128]{2,1,0:T(8,128)(2,1)S(1)} %pad_maximum_fusion.refs_1_), channel_id=1, source_target_pairs={{0,1},{1,0},{2,3},{3,2},{4,5},{5,4},{6,7},{7,6},{8,9},{9,8},{10,11... | collective-permute-start | bytes 331784 | tf_op jit(solution)/shard_map/ppermute | solution.py:306
  18.8 5.2 %collective-permute-start.8 = (bf16[3,144,128]{2,1,0:T(8,128)(2,1)S(1)}, bf16[3,144,128]{2,1,0:T(8,128)(2,1)S(1)}, u32[]{:S(2)}, u32[]{:S(2)}) collective-permute-start(bf16[3,144,128]{2,1,0:T(8,128)(2,1)S(1)} %collective-permute-done.6.refs_5_), channel_id=1, source_target_pairs={{0,1},{1,0},{2,3},{3,2},{4,5},{5,4},{6,7},{7,6},{8,9},{9,8},{10,11... | collective-permute-start | bytes 331784 | tf_op jit(solution)/shard_map/ppermute | solution.py:306
  18.8 4.0 %collective-permute-start.5 = (bf16[1,144,128]{2,1,0:T(8,128)(2,1)S(1)}, bf16[1,144,128]{2,1,0:T(8,128)(2,1)S(1)}, u32[]{:S(2)}, u32[]{:S(2)}) collective-permute-start(bf16[1,144,128]{2,1,0:T(8,128)(2,1)S(1)} %bitcast.7), channel_id=1, source_target_pairs={{0,2},{1,3},{2,0},{3,1},{4,6},{5,7},{6,4},{7,5},{8,10},{9,11},{10,... | collective-permute-start | bytes 110600 | tf_op jit(solution)/shard_map/ppermute | solution.py:306
  20.3 3.1 %collective-permute-start.3 = (bf16[1,144,128]{2,1,0:T(8,128)(2,1)S(1)}, bf16[1,144,128]{2,1,0:T(8,128)(2,1)S(1)}, u32[]{:S(2)}, u32[]{:S(2)}) collective-permute-start(bf16[1,144,128]{2,1,0:T(8,128)(2,1)S(1)} %bitcast.8), channel_id=1, source_target_pairs={{0,1},{1,0},{2,3},{3,2},{4,5},{5,4},{6,7},{7,6},{8,9},{9,8},{10,11... | collective-permute-start | bytes 110600 | tf_op jit(solution)/shard_map/ppermute | solution.py:306
  22.7 1.2 %collective-permute-start.7 = (bf16[1,144,128]{2,1,0:T(8,128)(2,1)S(1)}, bf16[1,144,128]{2,1,0:T(8,128)(2,1)S(1)}, u32[]{:S(2)}, u32[]{:S(2)}) collective-permute-start(bf16[1,144,128]{2,1,0:T(8,128)(2,1)S(1)} %collective-permute-done.5.refs_4_), channel_id=1, source_target_pairs={{0,1},{1,0},{2,3},{3,2},{4,5},{5,4},{6,7},{7,6},{8,9},{9,8},{10,11... | collective-permute-start | bytes 110600 | tf_op jit(solution)/shard_map/ppermute | solution.py:306
  23.4 0.7 %copy-start.3 = (f32[128]{0:T(128)S(1)}, f32[128]{0:T(128)}, u32[]{:S(2)}) copy-start(f32[128]{0:T(128)} %param.11) | copy-start | bytes 1540
  23.4 0.7 %copy-start.4 = (f32[128]{0:T(128)S(1)}, f32[128]{0:T(128)}, u32[]{:S(2)}) copy-start(f32[128]{0:T(128)} %param.12) | copy-start | bytes 1540

commit v8 on v0

--- a/solution.py
+++ b/solution.py
@@ -1,7 +1,14 @@
+import functools
+
 import jax
 import jax.numpy as jnp
 from jax import lax
+from jax.experimental import pallas as pl
+from jax.experimental.pallas import tpu as pltpu
 from jax.sharding import PartitionSpec as P
+
+SUB = 8
+EPS = 1e-05
 
 
 def normalize(values):
@@ -25,7 +32,7 @@
     return (grad_value, grad_gate)
 
 
-def body(pair_act, pair_mask, crop_length, weights, in_gain, out_gain, cotangent):
+def spread_body(pair_act, pair_mask, crop_length, weights, in_gain, out_gain, cotangent):
     tile_rows, tile_cols, channels = pair_act.shape
     residues = tile_rows * lax.axis_size("row")
     row_pos = lax.axis_index("row") * tile_rows + jnp.arange(tile_rows, dtype=jnp.int32)
@@ -99,9 +106,315 @@
     return (update, pair_grad, weight_grad)
 
 
+def pack_kernel(act_hbm, mask_hbm, cot_hbm, gain_hbm, out_ref, act_ref, mask_ref, gain_ref, sems):
+    tile_rows, tile_cols, channels = act_ref.shape
+    pairs = tile_rows * tile_cols
+    head = out_ref.shape[0] - pairs
+    pack_copies = [
+        pltpu.make_async_copy(act_hbm, act_ref, sems.at[0]),
+        pltpu.make_async_copy(gain_hbm, gain_ref, sems.at[1]),
+        pltpu.make_async_copy(mask_hbm, mask_ref, sems.at[2]),
+        pltpu.make_async_copy(cot_hbm, out_ref.at[head : head + pairs], sems.at[3]),
+    ]
+    for copy in pack_copies:
+        copy.start()
+    for copy in pack_copies:
+        copy.wait()
+    z_hat, _ = normalize(act_ref[...].astype(jnp.float32).reshape(pairs, channels))
+    out_ref[0:pairs] = (z_hat * gain_ref[...]).astype(jnp.bfloat16)
+    keep = mask_ref[...].astype(jnp.float32)
+    wide = jnp.concatenate([keep, jnp.zeros((tile_rows, channels - tile_cols), jnp.float32)], axis=1)
+    tall = jnp.concatenate([wide, jnp.zeros((channels - tile_rows, channels), jnp.float32)], axis=0)
+    out_ref[pairs:head] = tall.T[0 : head - pairs].astype(jnp.bfloat16)
+
+
+def join_kernel(head, count, *refs):
+    blocks, (front_ref, back_ref) = refs[:count], refs[-2:]
+    for at, block in enumerate(blocks):
+        front_ref[at] = block[0:head]
+        back_ref[at] = block[head:]
+
+
+def triangle(blocks, groups, steps, vectors_at, factors_at, start_at, store_at):
+    def block(a, _):
+        def step(q, totals):
+            totals = list(totals)
+            vectors = vectors_at(q)
+            factors = factors_at(a, q)
+            for inner in range(SUB):
+                rows = [vectors(g, inner) for g in range(groups)]
+                for lane in range(SUB):
+                    factor = factors(lane, inner)
+                    for g in range(groups):
+                        at = lane * groups + g
+                        totals[at] = totals[at] + factor * rows[g]
+            return tuple(totals)
+
+        totals = tuple(start_at(a, g, lane) for lane in range(SUB) for g in range(groups))
+        totals = step(0, totals) if steps == 1 else lax.fori_loop(0, steps, step, totals)
+        for g in range(groups):
+            store_at(a, g, [totals[lane * groups + g] for lane in range(SUB)])
+        return 0
+
+    lax.fori_loop(0, blocks, block, 0)
+
+
+def spread(ref, row):
+    return jnp.broadcast_to(ref[pl.ds(row, 1), :], (SUB, ref.shape[-1]))
+
+
+def line(ref, row):
+    return ref[pl.ds(pl.multiple_of(row, SUB), SUB), :]
+
+
+def column_kernel(n_row, n_col, col, crop_ref, first_ref, rest_ref, weights_ref, *refs):
+    tri_in, (tri_ref, left_ref, right_ref, side_ref, gate_ref, flip_ref) = refs[:-6], refs[-6:]
+    channels = first_ref.shape[-1]
+    tile = SUB * SUB
+    size = n_row * tile
+    bf16, f32 = jnp.bfloat16, jnp.float32
+    row_me, col_me = lax.axis_index("row"), lax.axis_index("col")
+    blocks = [first_ref] + [rest_ref.at[b] for b in range(n_row - 1)]
+    normed = jnp.concatenate([block[0:tile] for block in blocks], axis=0)
+    flip_ref[...] = normed.astype(f32).T.astype(bf16)
+    crop = crop_ref[0]
+    col_offset = lax.broadcasted_iota(jnp.int32, (SUB, channels), 0)
+    row_offset = lax.broadcasted_iota(jnp.int32, (SUB, channels), 1)
+    cols_in = col_offset < crop - (col_me ^ col) * SUB
+    kept = []
+    for b, block in enumerate(blocks):
+        keep = block[tile : tile + 2 * SUB].astype(f32)[0:SUB]
+        rows_in = row_offset < crop - (row_me ^ b) * SUB
+        keep = jnp.where(rows_in & cols_in, keep, 0.0)
+        kept += [jnp.broadcast_to(keep[:, at : at + 1], (SUB, channels)) for at in range(SUB)]
+    kept = jnp.concatenate(kept, axis=0)
+    for side, act_ref in enumerate((left_ref, right_ref)):
+        pair = jnp.concatenate([weights_ref[2 * side], weights_ref[2 * side + 1]], axis=1)
+        proj = jnp.dot(normed, pair, preferred_element_type=f32)
+        gate = jax.nn.sigmoid(proj[:, channels:])
+        masked = gate * kept
+        act = masked * proj[:, :channels]
+        act_ref[...] = act.astype(bf16).astype(f32)
+        side_ref[2 * side] = masked
+        side_ref[2 * side + 1] = act * (1.0 - gate)
+    gate_ref[...] = jax.nn.sigmoid(jnp.dot(normed, weights_ref[4], preferred_element_type=f32))
+    turn = row_me ^ col_me
+
+    def flipped(q):
+        firsts = [(turn ^ g) * tile for g in range(n_col)]
+        return lambda g, inner: right_ref[pl.ds(firsts[g] + inner, SUB, stride=SUB), :]
+
+    def along(a, q):
+        return lambda lane, inner: spread(left_ref, a * tile + lane * SUB + inner)
+
+    def start(a, g, lane):
+        if len(tri_in) == 0:
+            return jnp.zeros((SUB, channels), f32)
+        return line(tri_in[0], g * size + a * tile + lane * SUB)
+
+    def store(a, g, values):
+        for lane in range(SUB):
+            tri_ref[pl.ds(pl.multiple_of(g * size + a * tile + lane * SUB, SUB), SUB), :] = values[lane]
+
+    triangle(n_row, n_col, 1, flipped, along, start, store)
+
+
+def rest_kernel(n_row, n_col, act_ref, weights_ref, in_gain_ref, out_gain_ref, tri_ref, *refs):
+    parts = [refs[at * 7 : at * 7 + 7] for at in range(n_col)]
+    update_ref, pair_grad_ref, weight_grad_ref, back_ref, hat_ref, lin_ref, d_ref = refs[7 * n_col :]
+    channels = act_ref.shape[-1]
+    tile = SUB * SUB
+    size = n_row * tile
+    residues = n_row * SUB
+    bf16, f32 = jnp.bfloat16, jnp.float32
+    turn = lax.axis_index("row") ^ lax.axis_index("col")
+    out_gain = out_gain_ref[...]
+    for col, (first_ref, cots_ref, _, _, _, gate_ref, _) in enumerate(parts):
+        rows = slice(col * size, (col + 1) * size)
+        x_hat, inverse = normalize(tri_ref[rows, :])
+        normed_out = (x_hat * out_gain).astype(bf16)
+        hat_ref[rows, :] = normed_out
+        lin = jnp.dot(normed_out, weights_ref[5], preferred_element_type=f32)
+        out_gate = gate_ref[...]
+        if col == 0:
+            update_ref[...] = (out_gate[0:tile] * lin[0:tile]).astype(bf16).reshape(update_ref.shape)
+        head = first_ref.shape[0] - tile
+        cot = jnp.concatenate([first_ref[head:]] + [cots_ref[b] for b in range(n_row - 1)], axis=0).astype(f32)
+        grad = cot * out_gate
+        grad_lin = grad.astype(bf16)
+        lin_ref[rows, :] = grad_lin
+        d_ref[rows, 4 * channels : 5 * channels] = (grad * lin * (1.0 - out_gate)).astype(bf16)
+        back = lax.dot_general(grad_lin, weights_ref[5], (((1,), (1,)), ((), ())), preferred_element_type=f32)
+        back_ref[rows, :] = norm_back(back * out_gain, x_hat, inverse).astype(bf16).astype(f32)
+
+    lefts, rights, sides = [[part[at] for part in parts] for at in (2, 3, 4)]
+
+    def zero(a, g, lane):
+        return jnp.zeros((SUB, channels), f32)
+
+    def store(side):
+        def put(a, g, values):
+            for lane in range(0, SUB, 2):
+                at = pl.multiple_of(a * tile + lane * SUB, 2 * SUB)
+                both = jnp.concatenate(values[lane : lane + 2], axis=0)
+                rows = pl.ds(pl.multiple_of(g * size + at, 2 * SUB), 2 * SUB)
+                for kind in range(2):
+                    spot = (2 * side + kind) * channels
+                    scaled = both * sides[g][2 * side + kind, pl.ds(at, 2 * SUB), :]
+                    d_ref[rows, spot : spot + channels] = scaled.astype(bf16)
+        return put
+
+    def by_right(q):
+        return lambda g, inner: line(rights[g], (q ^ turn) * tile + inner * SUB)
+
+    def by_left(q):
+        return lambda g, inner: line(lefts[g], q * tile + inner * SUB)
+
+    def along(a, q):
+        return lambda lane, inner: spread(back_ref, q * size + a * tile + lane * SUB + inner)
+
+    def down(a, q):
+        return lambda lane, inner: spread(back_ref, (a ^ turn) * size + q * tile + inner * SUB + lane)
+
+    triangle(n_row, n_col, n_col, by_right, along, zero, store(0))
+    triangle(n_row, n_col, n_row, by_left, down, zero, store(1))
+
+    scale = 1.0 / residues
+    flipped = jnp.concatenate([part[6][...] for part in parts], axis=1)
+    sums = jnp.dot(flipped, d_ref[...], preferred_element_type=f32) * scale
+    for s in range(5):
+        weight_grad_ref[s] = sums[:, s * channels : (s + 1) * channels]
+    weight_grad_ref[5] = scale * lax.dot_general(
+        hat_ref[...], lin_ref[...], (((0,), (0,)), ((), ())), preferred_element_type=f32
+    )
+    total = jnp.zeros((tile, channels), f32)
+    for s in range(5):
+        total = total + lax.dot_general(
+            d_ref[0:tile, s * channels : (s + 1) * channels], weights_ref[s],
+            (((1,), (1,)), ((), ())), preferred_element_type=f32,
+        )
+    z_hat, z_inverse = normalize(act_ref[...].astype(f32).reshape(tile, channels))
+    grad = norm_back(total * in_gain_ref[...], z_hat, z_inverse)
+    pair_grad_ref[...] = grad.astype(bf16).reshape(pair_grad_ref.shape)
+
+
+def flip(block, n_row, n_col, row, col):
+    pairs = [(r * n_col + c, (r ^ row) * n_col + (c ^ col)) for r in range(n_row) for c in range(n_col)]
+    return lax.ppermute(block, ("row", "col"), pairs)
+
+
+def gathered_body(n_row, n_col, pair_act, pair_mask, crop_length, weights, in_gain, out_gain, cotangent):
+    tile_rows, tile_cols, channels = pair_act.shape
+    tile = tile_rows * tile_cols
+    size = n_row * tile
+    pairs = size * n_col
+    head = tile + 2 * SUB
+    f32, bf16 = jnp.float32, jnp.bfloat16
+    vmem = pl.BlockSpec(memory_space=pltpu.VMEM)
+    smem = pl.BlockSpec(memory_space=pltpu.SMEM)
+    hbm = pl.BlockSpec(memory_space=pltpu.HBM)
+    in_gain, out_gain = in_gain.reshape(1, channels), out_gain.reshape(1, channels)
+
+    def limit(mib):
+        return pltpu.CompilerParams(vmem_limit_bytes=mib * 1024 * 1024)
+
+    own = pl.pallas_call(
+        pack_kernel,
+        name="pack",
+        out_shape=jax.ShapeDtypeStruct((head + tile, channels), bf16),
+        in_specs=[hbm] * 4,
+        out_specs=vmem,
+        scratch_shapes=[
+            pltpu.VMEM(pair_act.shape, pair_act.dtype),
+            pltpu.VMEM(pair_mask.shape, jnp.int32),
+            pltpu.VMEM((1, channels), f32),
+            pltpu.SemaphoreType.DMA((4,)),
+        ],
+        compiler_params=limit(60),
+    )(pair_act, pair_mask, cotangent.reshape(tile, channels), in_gain)
+    crop_length, own = lax.optimization_barrier((crop_length, own))
+
+    firsts = {0: own}
+    along = [flip(own, n_row, n_col, shift, 0) for shift in reversed(range(1, n_row))]
+    bit = n_col // 2
+    while bit > 0:
+        firsts.update({col ^ bit: flip(first, n_row, n_col, 0, bit) for col, first in firsts.items()})
+        bit //= 2
+    direct = [firsts[1 << at] for at in range(n_col.bit_length() - 1)]
+    front, back = pl.pallas_call(
+        functools.partial(join_kernel, head, n_row - 1),
+        name="join",
+        out_shape=(
+            jax.ShapeDtypeStruct((n_row - 1, head, channels), bf16),
+            jax.ShapeDtypeStruct((n_row - 1, tile, channels), bf16),
+        ),
+        in_specs=[vmem] * (n_row - 1) + [pl.BlockSpec(memory_space=pl.ANY)] * len(direct),
+        out_specs=(vmem, vmem),
+        compiler_params=limit(2),
+    )(*reversed(along), *direct)
+    fronts, backs = {0: front}, {0: back}
+    bit = n_col // 2
+    while bit > 0:
+        fronts.update({col ^ bit: flip(stack, n_row, n_col, 0, bit) for col, stack in fronts.items()})
+        backs.update({col ^ bit: flip(stack, n_row, n_col, 0, bit) for col, stack in backs.items()})
+        bit //= 2
+
+    tri, parts = [], []
+    for col in range(n_col):
+        last = len(tri) > 0
+        results = pl.pallas_call(
+            functools.partial(column_kernel, n_row, n_col, col),
+            name=f"column_{col}",
+            out_shape=(
+                jax.ShapeDtypeStruct((pairs, channels), f32),
+                jax.ShapeDtypeStruct((size, channels), f32),
+                jax.ShapeDtypeStruct((size, channels), f32),
+                jax.ShapeDtypeStruct((4, size, channels), f32),
+                jax.ShapeDtypeStruct((size, channels), f32),
+                jax.ShapeDtypeStruct((channels, size), bf16),
+            ),
+            in_specs=[smem] + [vmem] * (3 + len(tri)),
+            out_specs=(vmem,) * 6,
+            input_output_aliases={4: 0} if last else {},
+            compiler_params=limit(8),
+            cost_estimate=pl.CostEstimate(flops=400_000_000, bytes_accessed=1_000_000, transcendentals=0),
+        )(crop_length, firsts[col], fronts[col], weights, *tri)
+        tri = [results[0]]
+        parts += [firsts[col], backs[col], *results[1:]]
+
+    return pl.pallas_call(
+        functools.partial(rest_kernel, n_row, n_col),
+        name="rest",
+        out_shape=(
+            jax.ShapeDtypeStruct(pair_act.shape, bf16),
+            jax.ShapeDtypeStruct(pair_act.shape, bf16),
+            jax.ShapeDtypeStruct(weights.shape, f32),
+        ),
+        in_specs=[vmem] * (5 + len(parts)),
+        out_specs=(vmem, vmem, vmem),
+        scratch_shapes=[
+            pltpu.VMEM((pairs, channels), f32),
+            pltpu.VMEM((pairs, channels), bf16),
+            pltpu.VMEM((pairs, channels), bf16),
+            pltpu.VMEM((pairs, 5 * channels), bf16),
+        ],
+        compiler_params=limit(16),
+    )(pair_act, weights, in_gain, out_gain, *tri, *parts)
+
+
+def body(n_row, n_col, pair_act, *others):
+    tile_rows, tile_cols, channels = pair_act.shape
+    pairs = tile_rows * n_row * tile_cols * n_col
+    small = pairs * channels * 4 <= 1024 * 1024 and channels == 128
+    square = n_row == n_col and tile_rows == SUB and tile_cols == SUB and n_col & (n_col - 1) == 0 and n_col > 1
+    if small and square:
+        return gathered_body(n_row, n_col, pair_act, *others)
+    return spread_body(pair_act, *others)
+
+
 def solution(mesh):
     return jax.shard_map(
-        body,
+        functools.partial(body, mesh.shape["row"], mesh.shape["col"]),
         mesh=mesh,
         in_specs=(
             P(("parts", "row"), "col", None),

time: 178 us -> 29.2 us (0.16)
  waiting for transfers between devices: 128 us -> 7.18 us
  blocking collectives: 20.1 us -> 0 us
  between operations: 14.6 us -> 1.41 us
  starting transfers between devices: 0.12 us -> 10.6 us
  Pallas kernels: 0 us -> 9.03 us
  local copies, waits for them, and re-layouts: 6.31 us -> 0.71 us
  other arithmetic: 4.21 us -> 0 us
  matrix products: 3.87 us -> 0 us
    psum x1 -> x0, waiting for transfers between devices: 89.5 us -> none  [body(): weight_grad = lax.psum(local_grads, ('row', 'col'))]
    reduce_scatter x2 -> x0, waiting for transfers between devices: 38.5 us -> none  [the longest x1 20.6 us: body(): lax.psum_scatter(partial_value.astype(jnp.bfloat16), 'col', scatter_dimen...]
    all_gather x2 -> x0, blocking collectives: 20.1 us -> none  [the longest x1 14.9 us: body(): lax.all_gather(right_act, 'row', axis=0, tiled=True)]
    ppermute x0 -> x12, starting transfers between devices: none -> 10.6 us  [flip(): return lax.ppermute(block, ('row', 'col'), pairs)]
    pallas_call x0 -> x7, Pallas kernels: none -> 9.03 us  [the longest x1 4.94 us: gathered_body(): pl.pallas_call(functools.partial(rest_kernel, n_row, n_col), name='rest',...]
    ppermute x0 -> x12, waiting for transfers between devices: none -> 7.18 us  [flip(): return lax.ppermute(block, ('row', 'col'), pairs)]
    dot_general x9 -> x0, matrix products: 3.87 us -> none  [the longest x1 1.12 us: body(): jnp.einsum('pc,scd->spd', flat_norm, weights[:5], preferred_element_type=...]
    unnamed x21 -> x10, local copies, waits for them, and re-layouts: 3.86 us -> 0.71 us
  transfers between devices with their start and end apart: 3 -> 12, of which waited for: 3 -> 3; matrix products, arithmetic and copies ran while one was open for 1% -> 0% of each run, Pallas kernels for 0% -> 8%
where the time goes in v8:
time: 29.2 us; the launch traced here: 28.9 us
  starting transfers between devices  10.6 us (36%)
  Pallas kernels  9.03 us (31%)
  waiting for transfers between devices  7.18 us (25%)
  between operations  1.41 us (5%)
  local copies, waits for them, and re-layouts  0.71 us (2%)
    ppermute x12, starting transfers between devices, flip(): return lax.ppermute(block, ('row', 'col'), pairs)  10.6 us
    ppermute x12, waiting for transfers between devices, flip(): return lax.ppermute(block, ('row', 'col'), pairs)  7.18 us
    pallas_call x1, Pallas kernels, gathered_body(): pl.pallas_call(functools.partial(rest_kernel, n_row, n_col), name='rest',...  4.94 us
    pallas_call x4, Pallas kernels, gathered_body(): pl.pallas_call(functools.partial(column_kernel, n_row, n_col, col), name=...  2.44 us
    pallas_call x1, Pallas kernels, gathered_body(): pl.pallas_call(pack_kernel, name='pack', out_shape=jax.ShapeDtypeStruct((...  1.64 us
    unnamed x10, local copies, waits for them, and re-layouts  0.71 us
  transfers between devices with their start and end apart: 12, of which 3 were waited for; matrix products, arithmetic and copies ran while one was open for 0% of the time, Pallas kernels for 8%

profile of v8, /device:TPU:0, one launch (start us, length us, event | category | flops | bytes accessed | tf_op | source)
XLA Modules:
  0.0 28.9 jit_solution(4058200602946268071)
XLA Ops:
  0.6 0.0 copy-start
  0.6 1.6 %pack.1.first_ref.refs_0_ = bf16[144,128]{1,0:T(8,128)(2,1)} custom-call(bf16[8,8,128]{2,1,0:T(8,128)(2,1)} %act_ref.1, s32[8,8]{1,0:T(8,128)} %mask_hbm.1, bf16[64,128]{1,0:T(8,128)(2,1)} %bitcast.6, f32[1,128]{1,0:T(1,128)} %bitcast.3), custom_call_target="tpu_custom_call" | custom-call | tf_op jit(solution)/shard_map/pack/pallas_call | solution.py:321
  2.3 0.0 copy-start.1
  2.3 3.0 %collective-permute-start = (bf16[144,128]{1,0:T(8,128)(2,1)}, bf16[144,128]{1,0:T(8,128)(2,1)S(1)}, u32[]{:S(2)}, u32[]{:S(2)}) collective-permute-start(bf16[144,128]{1,0:T(8,128)(2,1)} %pack.1.first_ref.refs_0_), channel_id=1, source_target_pairs={{0,2},{1,3},{2,0},{3,1},{4,6},{5,7},{6,4},{7,5},{8,10},{9,11},{10,... | collective-permute-start | bytes 110600 | tf_op jit(solution)/shard_map/ppermute | solution.py:303
  5.3 0.0 collective-permute-start.5
  5.3 1.6 %collective-permute-start.2 = (bf16[144,128]{1,0:T(8,128)(2,1)}, bf16[144,128]{1,0:T(8,128)(2,1)S(1)}, u32[]{:S(2)}, u32[]{:S(2)}) collective-permute-start(bf16[144,128]{1,0:T(8,128)(2,1)} %pack.1.first_ref.refs_0_), channel_id=1, source_target_pairs={{0,4},{1,5},{2,6},{3,7},{4,0},{5,1},{6,2},{7,3},{8,12},{9,13},{10,... | collective-permute-start | bytes 110600 | tf_op jit(solution)/shard_map/ppermute | solution.py:303
  6.9 2.6 %collective-permute-start.3 = (bf16[144,128]{1,0:T(8,128)(2,1)}, bf16[144,128]{1,0:T(8,128)(2,1)S(1)}, u32[]{:S(2)}, u32[]{:S(2)}) collective-permute-start(bf16[144,128]{1,0:T(8,128)(2,1)} %pack.1.first_ref.refs_0_), channel_id=1, source_target_pairs={{0,8},{1,9},{2,10},{3,11},{4,12},{5,13},{6,14},{7,15},{8,0},{9,1},... | collective-permute-start | bytes 110600 | tf_op jit(solution)/shard_map/ppermute | solution.py:303
  9.5 0.2 collective-permute-start.4
  9.7 0.0 collective-permute-done.refs_4_.first_ref.refs_14_
  9.7 0.0 collective-permute-done.5.refs_3_.first_ref.refs_7_
  9.7 0.0 collective-permute-done.2.refs_0_
  9.7 3.0 %collective-permute-done.3.refs_1_ = bf16[144,128]{1,0:T(8,128)(2,1)S(1)} collective-permute-done((bf16[144,128]{1,0:T(8,128)(2,1)}, bf16[144,128]{1,0:T(8,128)(2,1)S(1)}, u32[]{:S(2)}, u32[]{:S(2)}) %collective-permute-start.3) | collective-permute-done | bytes 36896 | tf_op jit(solution)/shard_map/ppermute | solution.py:303
  12.7 2.7 %collective-permute-done.4.refs_2_ = bf16[144,128]{1,0:T(8,128)(2,1)S(1)} collective-permute-done((bf16[144,128]{1,0:T(8,128)(2,1)}, bf16[144,128]{1,0:T(8,128)(2,1)S(1)}, u32[]{:S(2)}, u32[]{:S(2)}) %collective-permute-start.4) | collective-permute-done | bytes 36896 | tf_op jit(solution)/shard_map/ppermute | solution.py:303
  15.5 0.6 %collective-permute-start.6 = (bf16[3,80,128]{2,1,0:T(8,128)(2,1)S(1)}, bf16[3,80,128]{2,1,0:T(8,128)(2,1)S(1)}, u32[]{:S(2)}, u32[]{:S(2)}) collective-permute-start(bf16[3,80,128]{2,1,0:T(8,128)(2,1)S(1)} %get-tuple-element.33.rest_ref), channel_id=1, source_target_pairs={{0,2},{1,3},{2,0},{3,1},{4,6},{5,7},{6,4},{7,5},{8,10},{9,11},{10,... | collective-permute-start | bytes 184328 | tf_op jit(solution)/shard_map/ppermute | solution.py:303
  16.1 0.0 collective-permute-start.8
  16.1 1.5 %collective-permute-start.10 = (bf16[3,64,128]{2,1,0:T(8,128)(2,1)S(1)}, bf16[3,64,128]{2,1,0:T(8,128)(2,1)S(1)}, u32[]{:S(2)}, u32[]{:S(2)}) collective-permute-start(bf16[3,64,128]{2,1,0:T(8,128)(2,1)S(1)} %get-tuple-element.38.refs_1_), channel_id=1, source_target_pairs={{0,2},{1,3},{2,0},{3,1},{4,6},{5,7},{6,4},{7,5},{8,10},{9,11},{10,... | collective-permute-start | bytes 147464 | tf_op jit(solution)/shard_map/ppermute | solution.py:303
  18.2 0.3 %collective-permute-start.9 = (bf16[3,64,128]{2,1,0:T(8,128)(2,1)S(1)}, bf16[3,64,128]{2,1,0:T(8,128)(2,1)S(1)}, u32[]{:S(2)}, u32[]{:S(2)}) collective-permute-start(bf16[3,64,128]{2,1,0:T(8,128)(2,1)S(1)} %get-tuple-element.38.refs_1_), channel_id=1, source_target_pairs={{0,1},{1,0},{2,3},{3,2},{4,5},{5,4},{6,7},{7,6},{8,9},{9,8},{10,11... | collective-permute-start | bytes 147464 | tf_op jit(solution)/shard_map/ppermute | solution.py:303
  18.5 0.3 collective-permute-start.1
  18.8 0.0 copy-done
  18.8 0.0 copy-done.1
  18.8 0.6 %column_0.1 = (f32[1024,128]{1,0:T(8,128)S(1)}, f32[256,128]{1,0:T(8,128)S(1)}, f32[256,128]{1,0:T(8,128)S(1)}, f32[4,256,128]{2,1,0:T(8,128)S(1)}, f32[256,128]...) custom-call(s32[1]{0:T(128)S(6)} %copy.16.crop_ref, bf16[144,128]{1,0:T(8,128)(2,1)S(1)} %copy-done.1, ...), custom_call_target="tpu_custom_call" | custom-call | flops 400000000 | bytes 1000000 | tf_op jit(solution)/shard_map/column_0/pallas_call | solution.py:365
  19.4 1.4 %collective-permute-done.10.refs_15_ = bf16[3,64,128]{2,1,0:T(8,128)(2,1)S(1)} collective-permute-done((bf16[3,64,128]{2,1,0:T(8,128)(2,1)S(1)}, bf16[3,64,128]{2,1,0:T(8,128)(2,1)S(1)}, u32[]{:S(2)}, u32[]{:S(2)}) %collective-permute-start.10) | collective-permute-done | bytes 49184 | tf_op jit(solution)/shard_map/ppermute | solution.py:303
  20.8 0.0 collective-permute-start.11
  20.8 0.0 collective-permute-done.6.rest_ref
  20.8 0.5 %collective-permute-start.7 = (bf16[3,80,128]{2,1,0:T(8,128)(2,1)S(1)}, bf16[3,80,128]{2,1,0:T(8,128)(2,1)S(1)}, u32[]{:S(2)}, u32[]{:S(2)}) collective-permute-start(bf16[3,80,128]{2,1,0:T(8,128)(2,1)S(1)} %collective-permute-done.6.rest_ref), channel_id=1, source_target_pairs={{0,1},{1,0},{2,3},{3,2},{4,5},{5,4},{6,7},{7,6},{8,9},{9,8},{10,11... | collective-permute-start | bytes 184328 | tf_op jit(solution)/shard_map/ppermute | solution.py:303
  21.3 0.0 collective-permute-done.8.rest_ref
  21.3 0.6 %column_1.1 = (f32[1024,128]{1,0:T(8,128)S(1)}, f32[256,128]{1,0:T(8,128)S(1)}, f32[256,128]{1,0:T(8,128)S(1)}, f32[4,256,128]{2,1,0:T(8,128)S(1)}, f32[256,128]...) custom-call(s32[1]{0:T(128)S(6)} %copy.16.crop_ref, ...), custom_call_target="tpu_custom_call", output_to_operand_aliasing={{0}: (4, {})} | custom-call | flops 400000000 | bytes 1000000 | tf_op jit(solution)/shard_map/column_1/pallas_call | solution.py:365
  21.9 0.6 %column_2.1 = (f32[1024,128]{1,0:T(8,128)S(1)}, f32[256,128]{1,0:T(8,128)S(1)}, f32[256,128]{1,0:T(8,128)S(1)}, f32[4,256,128]{2,1,0:T(8,128)S(1)}, f32[256,128]...) custom-call(s32[1]{0:T(128)S(6)} %copy.16.crop_ref, ...), custom_call_target="tpu_custom_call", output_to_operand_aliasing={{0}: (4, {})} | custom-call | flops 400000000 | bytes 1000000 | tf_op jit(solution)/shard_map/column_2/pallas_call | solution.py:365
  22.6 0.0 collective-permute-done.1.first_ref.refs_21_
  22.6 0.0 collective-permute-done.7.rest_ref
  22.6 0.6 %column_3.1 = (f32[1024,128]{1,0:T(8,128)S(1)}, f32[256,128]{1,0:T(8,128)S(1)}, f32[256,128]{1,0:T(8,128)S(1)}, f32[4,256,128]{2,1,0:T(8,128)S(1)}, f32[256,128]...) custom-call(s32[1]{0:T(128)S(6)} %copy.16.crop_ref, ...), custom_call_target="tpu_custom_call", output_to_operand_aliasing={{0}: (4, {})} | custom-call | flops 400000000 | bytes 1000000 | tf_op jit(solution)/shard_map/column_3/pallas_call | solution.py:365
  23.2 0.0 collective-permute-done.9.refs_8_
  23.2 0.0 collective-permute-done.11.refs_22_
  23.2 0.0 copy-start.2
  23.3 0.0 copy-start.3
  23.3 0.0 copy-start.4
  23.3 0.7 %copy-done.2 = bf16[8,8,128]{2,1,0:T(8,128)(2,1)S(1)} copy-done((bf16[8,8,128]{2,1,0:T(8,128)(2,1)S(1)}, bf16[8,8,128]{2,1,0:T(8,128)(2,1)}, u32[]{:S(2)}) %copy-start.2) | copy-done | bytes 16408
  24.0 0.0 copy-done.3
  24.0 0.0 copy-done.4
  24.0 4.9 %rest.1 = (bf16[8,8,128]{2,1,0:T(8,128)(2,1)}, bf16[8,8,128]{2,1,0:T(8,128)(2,1)}, f32[6,128,128]{2,1,0:T(8,128)}) custom-call(bf16[8,8,128]{2,1,0:T(8,128)(2,1)S(1)} %copy-done.2, bf16[6,128,128]{2,1,0:T(8,128)(2,1)S(1)} %copy-done, f32[1,128]{1,0:T(1,128)S(1)} %bitcast.4, f32[1,128]{1,0:T(1,128)S(1)} %bitcast.5, ...), custom_call_target="tpu_custom_call" | custom-call | tf_op jit(solution)/shard_map/rest/pallas_call | solution.py:385
  (1 shorter events, 0.0 us)
Async XLA Ops:
  0.6 18.1 %copy-start = (bf16[6,128,128]{2,1,0:T(8,128)(2,1)S(1)}, bf16[6,128,128]{2,1,0:T(8,128)(2,1)}, u32[]{:S(2)}) copy-start(bf16[6,128,128]{2,1,0:T(8,128)(2,1)} %weights_ref.9) | copy-start | bytes 589828
  2.3 16.5 %copy-start.1 = (bf16[144,128]{1,0:T(8,128)(2,1)S(1)}, bf16[144,128]{1,0:T(8,128)(2,1)}, u32[]{:S(2)}) copy-start(bf16[144,128]{1,0:T(8,128)(2,1)} %pack.1.first_ref.refs_0_) | copy-start | bytes 110596
  2.3 7.4 %collective-permute-start = (bf16[144,128]{1,0:T(8,128)(2,1)}, bf16[144,128]{1,0:T(8,128)(2,1)S(1)}, u32[]{:S(2)}, u32[]{:S(2)}) collective-permute-start(bf16[144,128]{1,0:T(8,128)(2,1)} %pack.1.first_ref.refs_0_), channel_id=1, source_target_pairs={{0,2},{1,3},{2,0},{3,1},{4,6},{5,7},{6,4},{7,5},{8,10},{9,11},{10,... | collective-permute-start | bytes 110600 | tf_op jit(solution)/shard_map/ppermute | solution.py:303
  5.3 4.4 %collective-permute-start.5 = (bf16[144,128]{1,0:T(8,128)(2,1)}, bf16[144,128]{1,0:T(8,128)(2,1)S(1)}, u32[]{:S(2)}, u32[]{:S(2)}) collective-permute-start(bf16[144,128]{1,0:T(8,128)(2,1)} %pack.1.first_ref.refs_0_), channel_id=1, source_target_pairs={{0,1},{1,0},{2,3},{3,2},{4,5},{5,4},{6,7},{7,6},{8,9},{9,8},{10,11... | collective-permute-start | bytes 110600 | tf_op jit(solution)/shard_map/ppermute | solution.py:303
  5.3 4.4 %collective-permute-start.2 = (bf16[144,128]{1,0:T(8,128)(2,1)}, bf16[144,128]{1,0:T(8,128)(2,1)S(1)}, u32[]{:S(2)}, u32[]{:S(2)}) collective-permute-start(bf16[144,128]{1,0:T(8,128)(2,1)} %pack.1.first_ref.refs_0_), channel_id=1, source_target_pairs={{0,4},{1,5},{2,6},{3,7},{4,0},{5,1},{6,2},{7,3},{8,12},{9,13},{10,... | collective-permute-start | bytes 110600 | tf_op jit(solution)/shard_map/ppermute | solution.py:303
  6.9 5.9 %collective-permute-start.3 = (bf16[144,128]{1,0:T(8,128)(2,1)}, bf16[144,128]{1,0:T(8,128)(2,1)S(1)}, u32[]{:S(2)}, u32[]{:S(2)}) collective-permute-start(bf16[144,128]{1,0:T(8,128)(2,1)} %pack.1.first_ref.refs_0_), channel_id=1, source_target_pairs={{0,8},{1,9},{2,10},{3,11},{4,12},{5,13},{6,14},{7,15},{8,0},{9,1},... | collective-permute-start | bytes 110600 | tf_op jit(solution)/shard_map/ppermute | solution.py:303
  9.5 6.0 %collective-permute-start.4 = (bf16[144,128]{1,0:T(8,128)(2,1)}, bf16[144,128]{1,0:T(8,128)(2,1)S(1)}, u32[]{:S(2)}, u32[]{:S(2)}) collective-permute-start(bf16[144,128]{1,0:T(8,128)(2,1)} %pack.1.first_ref.refs_0_), channel_id=1, source_target_pairs={{0,12},{1,13},{2,14},{3,15},{4,8},{5,9},{6,10},{7,11},{8,4},{9,5},... | collective-permute-start | bytes 110600 | tf_op jit(solution)/shard_map/ppermute | solution.py:303
  15.5 5.3 %collective-permute-start.6 = (bf16[3,80,128]{2,1,0:T(8,128)(2,1)S(1)}, bf16[3,80,128]{2,1,0:T(8,128)(2,1)S(1)}, u32[]{:S(2)}, u32[]{:S(2)}) collective-permute-start(bf16[3,80,128]{2,1,0:T(8,128)(2,1)S(1)} %get-tuple-element.33.rest_ref), channel_id=1, source_target_pairs={{0,2},{1,3},{2,0},{3,1},{4,6},{5,7},{6,4},{7,5},{8,10},{9,11},{10,... | collective-permute-start | bytes 184328 | tf_op jit(solution)/shard_map/ppermute | solution.py:303
  16.1 5.3 %collective-permute-start.8 = (bf16[3,80,128]{2,1,0:T(8,128)(2,1)S(1)}, bf16[3,80,128]{2,1,0:T(8,128)(2,1)S(1)}, u32[]{:S(2)}, u32[]{:S(2)}) collective-permute-start(bf16[3,80,128]{2,1,0:T(8,128)(2,1)S(1)} %get-tuple-element.33.rest_ref), channel_id=1, source_target_pairs={{0,1},{1,0},{2,3},{3,2},{4,5},{5,4},{6,7},{7,6},{8,9},{9,8},{10,11... | collective-permute-start | bytes 184328 | tf_op jit(solution)/shard_map/ppermute | solution.py:303
  16.1 4.7 %collective-permute-start.10 = (bf16[3,64,128]{2,1,0:T(8,128)(2,1)S(1)}, bf16[3,64,128]{2,1,0:T(8,128)(2,1)S(1)}, u32[]{:S(2)}, u32[]{:S(2)}) collective-permute-start(bf16[3,64,128]{2,1,0:T(8,128)(2,1)S(1)} %get-tuple-element.38.refs_1_), channel_id=1, source_target_pairs={{0,2},{1,3},{2,0},{3,1},{4,6},{5,7},{6,4},{7,5},{8,10},{9,11},{10,... | collective-permute-start | bytes 147464 | tf_op jit(solution)/shard_map/ppermute | solution.py:303
  18.2 5.0 %collective-permute-start.9 = (bf16[3,64,128]{2,1,0:T(8,128)(2,1)S(1)}, bf16[3,64,128]{2,1,0:T(8,128)(2,1)S(1)}, u32[]{:S(2)}, u32[]{:S(2)}) collective-permute-start(bf16[3,64,128]{2,1,0:T(8,128)(2,1)S(1)} %get-tuple-element.38.refs_1_), channel_id=1, source_target_pairs={{0,1},{1,0},{2,3},{3,2},{4,5},{5,4},{6,7},{7,6},{8,9},{9,8},{10,11... | collective-permute-start | bytes 147464 | tf_op jit(solution)/shard_map/ppermute | solution.py:303
  18.5 4.1 %collective-permute-start.1 = (bf16[144,128]{1,0:T(8,128)(2,1)S(1)}, bf16[144,128]{1,0:T(8,128)(2,1)S(1)}, u32[]{:S(2)}, u32[]{:S(2)}) collective-permute-start(bf16[144,128]{1,0:T(8,128)(2,1)S(1)} %collective-permute-done.refs_4_.first_ref.refs_14_), channel_id=1, source_target_pairs={{0,1},{1,0},{2,3},{3,2},{4,5},{5,4},{6,7},{7,6},{8,9},{9,8},{10,11... | collective-permute-start | bytes 110600 | tf_op jit(solution)/shard_map/ppermute | solution.py:303
  20.8 2.4 %collective-permute-start.11 = (bf16[3,64,128]{2,1,0:T(8,128)(2,1)S(1)}, bf16[3,64,128]{2,1,0:T(8,128)(2,1)S(1)}, u32[]{:S(2)}, u32[]{:S(2)}) collective-permute-start(bf16[3,64,128]{2,1,0:T(8,128)(2,1)S(1)} %collective-permute-done.10.refs_15_), channel_id=1, source_target_pairs={{0,1},{1,0},{2,3},{3,2},{4,5},{5,4},{6,7},{7,6},{8,9},{9,8},{10,11... | collective-permute-start | bytes 147464 | tf_op jit(solution)/shard_map/ppermute | solution.py:303
  20.8 1.8 %collective-permute-start.7 = (bf16[3,80,128]{2,1,0:T(8,128)(2,1)S(1)}, bf16[3,80,128]{2,1,0:T(8,128)(2,1)S(1)}, u32[]{:S(2)}, u32[]{:S(2)}) collective-permute-start(bf16[3,80,128]{2,1,0:T(8,128)(2,1)S(1)} %collective-permute-done.6.rest_ref), channel_id=1, source_target_pairs={{0,1},{1,0},{2,3},{3,2},{4,5},{5,4},{6,7},{7,6},{8,9},{9,8},{10,11... | collective-permute-start | bytes 184328 | tf_op jit(solution)/shard_map/ppermute | solution.py:303
  23.2 0.7 %copy-start.2 = (bf16[8,8,128]{2,1,0:T(8,128)(2,1)S(1)}, bf16[8,8,128]{2,1,0:T(8,128)(2,1)}, u32[]{:S(2)}) copy-start(bf16[8,8,128]{2,1,0:T(8,128)(2,1)} %act_ref.1) | copy-start | bytes 49156
  23.3 0.7 %copy-start.3 = (f32[128]{0:T(128)S(1)}, f32[128]{0:T(128)}, u32[]{:S(2)}) copy-start(f32[128]{0:T(128)} %param.11) | copy-start | bytes 1540
  23.3 0.7 %copy-start.4 = (f32[128]{0:T(128)S(1)}, f32[128]{0:T(128)}, u32[]{:S(2)}) copy-start(f32[128]{0:T(128)} %param.12) | copy-start | bytes 1540

commit v9 on v8

--- a/solution.py
+++ b/solution.py
@@ -128,11 +128,12 @@
     out_ref[pairs:head] = tall.T[0 : head - pairs].astype(jnp.bfloat16)
 
 
-def join_kernel(head, count, *refs):
-    blocks, (front_ref, back_ref) = refs[:count], refs[-2:]
-    for at, block in enumerate(blocks):
+def join_kernel(head, far_3, far_2, over, near, cross, twin, front_ref, back_ref, near_ref):
+    for at, block in enumerate((far_2, far_3)):
         front_ref[at] = block[0:head]
         back_ref[at] = block[head:]
+    for at, block in enumerate((over, near, cross)):
+        near_ref[at] = block[...]
 
 
 def triangle(blocks, groups, steps, vectors_at, factors_at, start_at, store_at):
@@ -167,14 +168,22 @@
     return ref[pl.ds(pl.multiple_of(row, SUB), SUB), :]
 
 
-def column_kernel(n_row, n_col, col, crop_ref, first_ref, rest_ref, weights_ref, *refs):
+def column_kernel(n_row, n_col, col, spots, crop_ref, first_ref, second_ref, rest_ref, weights_ref, *refs):
+    if col == 0:
+        act_ref, in_gain_ref, out_gain_ref, *refs, own_ref, gains_ref = refs
+        z_hat, z_inverse = normalize(act_ref[...].astype(jnp.float32).reshape(own_ref.shape[1:]))
+        own_ref[0] = z_hat
+        own_ref[1] = jnp.broadcast_to(z_inverse, z_hat.shape)
+        gains_ref[0:1] = in_gain_ref[...]
+        gains_ref[1:2] = out_gain_ref[...]
     tri_in, (tri_ref, left_ref, right_ref, side_ref, gate_ref, flip_ref) = refs[:-6], refs[-6:]
-    channels = first_ref.shape[-1]
+    channels = rest_ref.shape[-1]
     tile = SUB * SUB
     size = n_row * tile
     bf16, f32 = jnp.bfloat16, jnp.float32
     row_me, col_me = lax.axis_index("row"), lax.axis_index("col")
-    blocks = [first_ref] + [rest_ref.at[b] for b in range(n_row - 1)]
+    blocks = [ref if at is None else ref.at[at] for ref, at in zip((first_ref, second_ref), spots)]
+    blocks += [rest_ref.at[b] for b in range(n_row - 2)]
     normed = jnp.concatenate([block[0:tile] for block in blocks], axis=0)
     flip_ref[...] = normed.astype(f32).T.astype(bf16)
     crop = crop_ref[0]
@@ -219,17 +228,17 @@
     triangle(n_row, n_col, 1, flipped, along, start, store)
 
 
-def rest_kernel(n_row, n_col, act_ref, weights_ref, in_gain_ref, out_gain_ref, tri_ref, *refs):
-    parts = [refs[at * 7 : at * 7 + 7] for at in range(n_col)]
-    update_ref, pair_grad_ref, weight_grad_ref, back_ref, hat_ref, lin_ref, d_ref = refs[7 * n_col :]
-    channels = act_ref.shape[-1]
+def rest_kernel(n_row, n_col, spots, weights_ref, own_ref, gains_ref, tri_ref, *refs):
+    parts = [refs[at * 8 : at * 8 + 8] for at in range(n_col)]
+    update_ref, pair_grad_ref, weight_grad_ref, back_ref, hat_ref, lin_ref, d_ref = refs[8 * n_col :]
+    channels = tri_ref.shape[-1]
     tile = SUB * SUB
     size = n_row * tile
     residues = n_row * SUB
     bf16, f32 = jnp.bfloat16, jnp.float32
     turn = lax.axis_index("row") ^ lax.axis_index("col")
-    out_gain = out_gain_ref[...]
-    for col, (first_ref, cots_ref, _, _, _, gate_ref, _) in enumerate(parts):
+    out_gain = gains_ref[1:2]
+    for col, (first_ref, second_ref, cots_ref, _, _, _, gate_ref, _) in enumerate(parts):
         rows = slice(col * size, (col + 1) * size)
         x_hat, inverse = normalize(tri_ref[rows, :])
         normed_out = (x_hat * out_gain).astype(bf16)
@@ -238,8 +247,9 @@
         out_gate = gate_ref[...]
         if col == 0:
             update_ref[...] = (out_gate[0:tile] * lin[0:tile]).astype(bf16).reshape(update_ref.shape)
-        head = first_ref.shape[0] - tile
-        cot = jnp.concatenate([first_ref[head:]] + [cots_ref[b] for b in range(n_row - 1)], axis=0).astype(f32)
+        blocks = [ref if at is None else ref.at[at] for ref, at in zip((first_ref, second_ref), spots[col])]
+        cots = [block[block.shape[0] - tile :] for block in blocks] + [cots_ref[b] for b in range(n_row - 2)]
+        cot = jnp.concatenate(cots, axis=0).astype(f32)
         grad = cot * out_gate
         grad_lin = grad.astype(bf16)
         lin_ref[rows, :] = grad_lin
@@ -247,7 +257,7 @@
         back = lax.dot_general(grad_lin, weights_ref[5], (((1,), (1,)), ((), ())), preferred_element_type=f32)
         back_ref[rows, :] = norm_back(back * out_gain, x_hat, inverse).astype(bf16).astype(f32)
 
-    lefts, rights, sides = [[part[at] for part in parts] for at in (2, 3, 4)]
+    lefts, rights, sides = [[part[at] for part in parts] for at in (3, 4, 5)]
 
     def zero(a, g, lane):
         return jnp.zeros((SUB, channels), f32)
@@ -280,7 +290,7 @@
     triangle(n_row, n_col, n_row, by_left, down, zero, store(1))
 
     scale = 1.0 / residues
-    flipped = jnp.concatenate([part[6][...] for part in parts], axis=1)
+    flipped = jnp.concatenate([part[7][...] for part in parts], axis=1)
     sums = jnp.dot(flipped, d_ref[...], preferred_element_type=f32) * scale
     for s in range(5):
         weight_grad_ref[s] = sums[:, s * channels : (s + 1) * channels]
@@ -293,8 +303,7 @@
             d_ref[0:tile, s * channels : (s + 1) * channels], weights_ref[s],
             (((1,), (1,)), ((), ())), preferred_element_type=f32,
         )
-    z_hat, z_inverse = normalize(act_ref[...].astype(f32).reshape(tile, channels))
-    grad = norm_back(total * in_gain_ref[...], z_hat, z_inverse)
+    grad = norm_back(total * gains_ref[0:1], own_ref[0], own_ref[1])
     pair_grad_ref[...] = grad.astype(bf16).reshape(pair_grad_ref.shape)
 
 
@@ -334,36 +343,39 @@
     )(pair_act, pair_mask, cotangent.reshape(tile, channels), in_gain)
     crop_length, own = lax.optimization_barrier((crop_length, own))
 
-    firsts = {0: own}
-    along = [flip(own, n_row, n_col, shift, 0) for shift in reversed(range(1, n_row))]
-    bit = n_col // 2
-    while bit > 0:
-        firsts.update({col ^ bit: flip(first, n_row, n_col, 0, bit) for col, first in firsts.items()})
-        bit //= 2
-    direct = [firsts[1 << at] for at in range(n_col.bit_length() - 1)]
-    front, back = pl.pallas_call(
-        functools.partial(join_kernel, head, n_row - 1),
+    def move(block, row, col):
+        return flip(block, n_row, n_col, row, col)
+
+    twin = move(own, 0, 1)
+    front, back, near = pl.pallas_call(
+        functools.partial(join_kernel, head),
         name="join",
         out_shape=(
-            jax.ShapeDtypeStruct((n_row - 1, head, channels), bf16),
-            jax.ShapeDtypeStruct((n_row - 1, tile, channels), bf16),
+            jax.ShapeDtypeStruct((2, head, channels), bf16),
+            jax.ShapeDtypeStruct((2, tile, channels), bf16),
+            jax.ShapeDtypeStruct((3,) + own.shape, bf16),
         ),
-        in_specs=[vmem] * (n_row - 1) + [pl.BlockSpec(memory_space=pl.ANY)] * len(direct),
-        out_specs=(vmem, vmem),
+        in_specs=[vmem] * 5 + [pl.BlockSpec(memory_space=pl.ANY)],
+        out_specs=(vmem, vmem, vmem),
         compiler_params=limit(2),
-    )(*reversed(along), *direct)
+    )(move(own, 3, 0), move(own, 2, 0), move(own, 0, 2), move(own, 1, 0), move(own, 1, 2), twin)
+    near_twin = move(near, 0, 1)
     fronts, backs = {0: front}, {0: back}
-    bit = n_col // 2
-    while bit > 0:
-        fronts.update({col ^ bit: flip(stack, n_row, n_col, 0, bit) for col, stack in fronts.items()})
-        backs.update({col ^ bit: flip(stack, n_row, n_col, 0, bit) for col, stack in backs.items()})
-        bit //= 2
-
-    tri, parts = [], []
+    for bit in (2, 1):
+        fronts.update({col ^ bit: move(stack, 0, bit) for col, stack in fronts.items()})
+        backs.update({col ^ bit: move(stack, 0, bit) for col, stack in backs.items()})
+    heads = {0: (own, near), 1: (twin, near_twin), 2: (near, near), 3: (near_twin, near_twin)}
+    spots = ((None, 1), (None, 1), (0, 2), (0, 2))
+
+    tri, parts, extra = [], [], []
     for col in range(n_col):
-        last = len(tri) > 0
-        results = pl.pallas_call(
-            functools.partial(column_kernel, n_row, n_col, col),
+        more = (pair_act, in_gain, out_gain) if col == 0 else tri
+        more_shapes = () if col > 0 else (
+            jax.ShapeDtypeStruct((2, tile, channels), f32),
+            jax.ShapeDtypeStruct((SUB, channels), f32),
+        )
+        tri, *results = pl.pallas_call(
+            functools.partial(column_kernel, n_row, n_col, col, spots[col]),
             name=f"column_{col}",
             out_shape=(
                 jax.ShapeDtypeStruct((pairs, channels), f32),
@@ -372,25 +384,27 @@
                 jax.ShapeDtypeStruct((4, size, channels), f32),
                 jax.ShapeDtypeStruct((size, channels), f32),
                 jax.ShapeDtypeStruct((channels, size), bf16),
+                *more_shapes,
             ),
-            in_specs=[smem] + [vmem] * (3 + len(tri)),
-            out_specs=(vmem,) * 6,
-            input_output_aliases={4: 0} if last else {},
+            in_specs=[smem] + [vmem] * (4 + len(more)),
+            out_specs=(vmem,) * (6 + len(more_shapes)),
+            input_output_aliases={5: 0} if col > 0 else {},
             compiler_params=limit(8),
             cost_estimate=pl.CostEstimate(flops=400_000_000, bytes_accessed=1_000_000, transcendentals=0),
-        )(crop_length, firsts[col], fronts[col], weights, *tri)
-        tri = [results[0]]
-        parts += [firsts[col], backs[col], *results[1:]]
+        )(crop_length, *heads[col], fronts[col], weights, *more)
+        tri = [tri]
+        parts += [*heads[col], backs[col], *results[:5]]
+        extra += results[5:]
 
     return pl.pallas_call(
-        functools.partial(rest_kernel, n_row, n_col),
+        functools.partial(rest_kernel, n_row, n_col, spots),
         name="rest",
         out_shape=(
             jax.ShapeDtypeStruct(pair_act.shape, bf16),
             jax.ShapeDtypeStruct(pair_act.shape, bf16),
             jax.ShapeDtypeStruct(weights.shape, f32),
         ),
-        in_specs=[vmem] * (5 + len(parts)),
+        in_specs=[vmem] * (4 + len(parts)),
         out_specs=(vmem, vmem, vmem),
         scratch_shapes=[
             pltpu.VMEM((pairs, channels), f32),
@@ -399,14 +413,14 @@
             pltpu.VMEM((pairs, 5 * channels), bf16),
         ],
         compiler_params=limit(16),
-    )(pair_act, weights, in_gain, out_gain, *tri, *parts)
+    )(weights, *extra, *tri, *parts)
 
 
 def body(n_row, n_col, pair_act, *others):
     tile_rows, tile_cols, channels = pair_act.shape
     pairs = tile_rows * n_row * tile_cols * n_col
     small = pairs * channels * 4 <= 1024 * 1024 and channels == 128
-    square = n_row == n_col and tile_rows == SUB and tile_cols == SUB and n_col & (n_col - 1) == 0 and n_col > 1
+    square = n_row == 4 and n_col == 4 and tile_rows == SUB and tile_cols == SUB
     if small and square:
         return gathered_body(n_row, n_col, pair_act, *others)
     return spread_body(pair_act, *others)

time: 29.2 us -> 28.1 us (0.962)
  waiting for transfers between devices: 7.18 us -> 5.58 us
  starting transfers between devices: 10.6 us -> 11.7 us
  local copies, waits for them, and re-layouts: 0.71 us -> 0.03 us
    ppermute x12 -> x13, waiting for transfers between devices: 7.18 us -> 5.58 us  [flip(): return lax.ppermute(block, ('row', 'col'), pairs)]
    ppermute x12 -> x13, starting transfers between devices: 10.6 us -> 11.7 us  [flip(): return lax.ppermute(block, ('row', 'col'), pairs)]
    unnamed x10, local copies, waits for them, and re-layouts: 0.71 us -> 0.03 us
  transfers between devices with their start and end apart: 12 -> 13, of which waited for: 3 -> 4; matrix products, arithmetic and copies ran while one was open for 0% -> 0% of each run, Pallas kernels for 8% -> 9%
where the time goes in v9:
time: 28.1 us; the launch traced here: 27.9 us
  starting transfers between devices  11.7 us (42%)
  Pallas kernels  9.2 us (33%)
  waiting for transfers between devices  5.58 us (20%)
  between operations  1.42 us (5%)
    ppermute x13, starting transfers between devices, flip(): return lax.ppermute(block, ('row', 'col'), pairs)  11.7 us
    ppermute x13, waiting for transfers between devices, flip(): return lax.ppermute(block, ('row', 'col'), pairs)  5.58 us
    pallas_call x1, Pallas kernels, gathered_body(): pl.pallas_call(functools.partial(rest_kernel, n_row, n_col, spots), name=...  5.04 us
    pallas_call x4, Pallas kernels, gathered_body(): pl.pallas_call(functools.partial(column_kernel, n_row, n_col, col, spots[...  2.52 us
    pallas_call x1, Pallas kernels, gathered_body(): pl.pallas_call(pack_kernel, name='pack', out_shape=jax.ShapeDtypeStruct((...  1.64 us
  transfers between devices with their start and end apart: 13, of which 4 were waited for; matrix products, arithmetic and copies ran while one was open for 0% of the time, Pallas kernels for 9%

profile of v9, /device:TPU:0, one launch (start us, length us, event | category | flops | bytes accessed | tf_op | source)
XLA Modules:
  0.0 27.9 jit_solution(10451748530382488683)
XLA Ops:
  0.6 0.0 copy-start
  0.6 1.6 %pack.1.first_ref.refs_0_ = bf16[144,128]{1,0:T(8,128)(2,1)} custom-call(bf16[8,8,128]{2,1,0:T(8,128)(2,1)} %refs_0_.1, s32[8,8]{1,0:T(8,128)} %mask_hbm.1, bf16[64,128]{1,0:T(8,128)(2,1)} %bitcast.6, f32[1,128]{1,0:T(1,128)} %bitcast.3), custom_call_target="tpu_custom_call" | custom-call | tf_op jit(solution)/shard_map/pack/pallas_call | solution.py:330
  2.3 0.0 copy-start.1
  2.3 0.0 copy-start.2
  2.3 0.5 %collective-permute-start.5 = (bf16[144,128]{1,0:T(8,128)(2,1)}, bf16[144,128]{1,0:T(8,128)(2,1)S(1)}, u32[]{:S(2)}, u32[]{:S(2)}) collective-permute-start(bf16[144,128]{1,0:T(8,128)(2,1)} %pack.1.first_ref.refs_0_), channel_id=1, source_target_pairs={{0,1},{1,0},{2,3},{3,2},{4,5},{5,4},{6,7},{7,6},{8,9},{9,8},{10,11... | collective-permute-start | bytes 110600 | tf_op jit(solution)/shard_map/ppermute | solution.py:312
  2.8 4.7 %collective-permute-start = (bf16[144,128]{1,0:T(8,128)(2,1)}, bf16[144,128]{1,0:T(8,128)(2,1)S(1)}, u32[]{:S(2)}, u32[]{:S(2)}) collective-permute-start(bf16[144,128]{1,0:T(8,128)(2,1)} %pack.1.first_ref.refs_0_), channel_id=1, source_target_pairs={{0,12},{1,13},{2,14},{3,15},{4,8},{5,9},{6,10},{7,11},{8,4},{9,5},... | collective-permute-start | bytes 110600 | tf_op jit(solution)/shard_map/ppermute | solution.py:312
  7.5 0.0 collective-permute-start.1
  7.5 1.5 %collective-permute-start.2 = (bf16[144,128]{1,0:T(8,128)(2,1)}, bf16[144,128]{1,0:T(8,128)(2,1)S(1)}, u32[]{:S(2)}, u32[]{:S(2)}) collective-permute-start(bf16[144,128]{1,0:T(8,128)(2,1)} %pack.1.first_ref.refs_0_), channel_id=1, source_target_pairs={{0,2},{1,3},{2,0},{3,1},{4,6},{5,7},{6,4},{7,5},{8,10},{9,11},{10,... | collective-permute-start | bytes 110600 | tf_op jit(solution)/shard_map/ppermute | solution.py:312
  9.0 0.8 %collective-permute-start.3 = (bf16[144,128]{1,0:T(8,128)(2,1)}, bf16[144,128]{1,0:T(8,128)(2,1)S(1)}, u32[]{:S(2)}, u32[]{:S(2)}) collective-permute-start(bf16[144,128]{1,0:T(8,128)(2,1)} %pack.1.first_ref.refs_0_), channel_id=1, source_target_pairs={{0,4},{1,5},{2,6},{3,7},{4,0},{5,1},{6,2},{7,3},{8,12},{9,13},{10,... | collective-permute-start | bytes 110600 | tf_op jit(solution)/shard_map/ppermute | solution.py:312
  9.8 0.0 collective-permute-done.5.twin.first_ref.refs_8_
  9.8 1.2 %collective-permute-start.4 = (bf16[144,128]{1,0:T(8,128)(2,1)}, bf16[144,128]{1,0:T(8,128)(2,1)S(1)}, u32[]{:S(2)}, u32[]{:S(2)}) collective-permute-start(bf16[144,128]{1,0:T(8,128)(2,1)} %pack.1.first_ref.refs_0_), channel_id=1, source_target_pairs={{0,6},{1,7},{2,4},{3,5},{4,2},{5,3},{6,0},{7,1},{8,14},{9,15},{10,... | collective-permute-start | bytes 110600 | tf_op jit(solution)/shard_map/ppermute | solution.py:312
  11.0 0.0 collective-permute-done.far_3
  11.0 1.6 %collective-permute-done.1.far_2 = bf16[144,128]{1,0:T(8,128)(2,1)S(1)} collective-permute-done((bf16[144,128]{1,0:T(8,128)(2,1)}, bf16[144,128]{1,0:T(8,128)(2,1)S(1)}, u32[]{:S(2)}, u32[]{:S(2)}) %collective-permute-start.1) | collective-permute-done | bytes 36896 | tf_op jit(solution)/shard_map/ppermute | solution.py:312
  12.6 0.0 collective-permute-done.2.over
  12.6 0.9 %collective-permute-done.3.near = bf16[144,128]{1,0:T(8,128)(2,1)S(1)} collective-permute-done((bf16[144,128]{1,0:T(8,128)(2,1)}, bf16[144,128]{1,0:T(8,128)(2,1)S(1)}, u32[]{:S(2)}, u32[]{:S(2)}) %collective-permute-start.3) | collective-permute-done | bytes 36896 | tf_op jit(solution)/shard_map/ppermute | solution.py:312
  13.5 1.3 %collective-permute-done.4.cross = bf16[144,128]{1,0:T(8,128)(2,1)S(1)} collective-permute-done((bf16[144,128]{1,0:T(8,128)(2,1)}, bf16[144,128]{1,0:T(8,128)(2,1)S(1)}, u32[]{:S(2)}, u32[]{:S(2)}) %collective-permute-start.4) | collective-permute-done | bytes 36896 | tf_op jit(solution)/shard_map/ppermute | solution.py:312
  14.9 0.1 collective-permute-start.6
  14.9 0.6 %collective-permute-start.7 = (bf16[2,80,128]{2,1,0:T(8,128)(2,1)S(1)}, bf16[2,80,128]{2,1,0:T(8,128)(2,1)S(1)}, u32[]{:S(2)}, u32[]{:S(2)}) collective-permute-start(bf16[2,80,128]{2,1,0:T(8,128)(2,1)S(1)} %get-tuple-element.37.rest_ref), channel_id=1, source_target_pairs={{0,2},{1,3},{2,0},{3,1},{4,6},{5,7},{6,4},{7,5},{8,10},{9,11},{10,... | collective-permute-start | bytes 122888 | tf_op jit(solution)/shard_map/ppermute | solution.py:312
  15.6 0.2 collective-permute-start.9
  16.4 0.0 copy-start.3
  16.4 0.0 copy-start.4
  16.4 1.6 %collective-permute-start.11 = (bf16[2,64,128]{2,1,0:T(8,128)(2,1)S(1)}, bf16[2,64,128]{2,1,0:T(8,128)(2,1)S(1)}, u32[]{:S(2)}, u32[]{:S(2)}) collective-permute-start(bf16[2,64,128]{2,1,0:T(8,128)(2,1)S(1)} %get-tuple-element.44.refs_2_), channel_id=1, source_target_pairs={{0,2},{1,3},{2,0},{3,1},{4,6},{5,7},{6,4},{7,5},{8,10},{9,11},{10,... | collective-permute-start | bytes 98312 | tf_op jit(solution)/shard_map/ppermute | solution.py:312
  17.9 0.1 collective-permute-start.10
  18.0 0.0 copy-done
  18.0 0.0 copy-done.1
  18.0 0.0 copy-done.2
  18.0 0.0 copy-done.3
  18.0 0.0 copy-done.4
  18.0 0.6 %column_0.1 = (f32[1024,128]{1,0:T(8,128)S(1)}, f32[256,128]{1,0:T(8,128)S(1)}, f32[256,128]{1,0:T(8,128)S(1)}, f32[4,256,128]{2,1,0:T(8,128)S(1)}, f32[256,128]...) custom-call(s32[1]{0:T(128)S(6)} %copy.16.crop_ref, ...), custom_call_target="tpu_custom_call" | custom-call | flops 400000000 | bytes 1000000 | tf_op jit(solution)/shard_map/column_0/pallas_call | solution.py:377
  18.7 1.7 %collective-permute-done.11.refs_18_ = bf16[2,64,128]{2,1,0:T(8,128)(2,1)S(1)} collective-permute-done((bf16[2,64,128]{2,1,0:T(8,128)(2,1)S(1)}, bf16[2,64,128]{2,1,0:T(8,128)(2,1)S(1)}, u32[]{:S(2)}, u32[]{:S(2)}) %collective-permute-start.11) | collective-permute-done | bytes 32800 | tf_op jit(solution)/shard_map/ppermute | solution.py:312
  20.4 0.0 collective-permute-start.12
  20.4 0.0 collective-permute-done.7.rest_ref
  20.4 0.5 %collective-permute-start.8 = (bf16[2,80,128]{2,1,0:T(8,128)(2,1)S(1)}, bf16[2,80,128]{2,1,0:T(8,128)(2,1)S(1)}, u32[]{:S(2)}, u32[]{:S(2)}) collective-permute-start(bf16[2,80,128]{2,1,0:T(8,128)(2,1)S(1)} %collective-permute-done.7.rest_ref), channel_id=1, source_target_pairs={{0,1},{1,0},{2,3},{3,2},{4,5},{5,4},{6,7},{7,6},{8,9},{9,8},{10,11... | collective-permute-start | bytes 122888 | tf_op jit(solution)/shard_map/ppermute | solution.py:312
  20.9 0.0 collective-permute-done.9.rest_ref
  20.9 0.0 collective-permute-done.6.second_ref.first_ref.refs_9_.refs_24_.refs_25_
  20.9 0.6 %column_1.1 = (f32[1024,128]{1,0:T(8,128)S(1)}, f32[256,128]{1,0:T(8,128)S(1)}, f32[256,128]{1,0:T(8,128)S(1)}, f32[4,256,128]{2,1,0:T(8,128)S(1)}, f32[256,128]...) custom-call(s32[1]{0:T(128)S(6)} %copy.16.crop_ref, ...), custom_call_target="tpu_custom_call", output_to_operand_aliasing={{0}: (5, {})} | custom-call | flops 400000000 | bytes 1000000 | tf_op jit(solution)/shard_map/column_1/pallas_call | solution.py:377
  21.5 0.6 %column_2.1 = (f32[1024,128]{1,0:T(8,128)S(1)}, f32[256,128]{1,0:T(8,128)S(1)}, f32[256,128]{1,0:T(8,128)S(1)}, f32[4,256,128]{2,1,0:T(8,128)S(1)}, f32[256,128]...) custom-call(s32[1]{0:T(128)S(6)} %copy.16.crop_ref, ...), custom_call_target="tpu_custom_call", output_to_operand_aliasing={{0}: (5, {})} | custom-call | flops 400000000 | bytes 1000000 | tf_op jit(solution)/shard_map/column_2/pallas_call | solution.py:377
  22.2 0.0 collective-permute-done.8.rest_ref
  22.2 0.6 %column_3.1 = (f32[1024,128]{1,0:T(8,128)S(1)}, f32[256,128]{1,0:T(8,128)S(1)}, f32[256,128]{1,0:T(8,128)S(1)}, f32[4,256,128]{2,1,0:T(8,128)S(1)}, f32[256,128]...) custom-call(s32[1]{0:T(128)S(6)} %copy.16.crop_ref, ...), custom_call_target="tpu_custom_call", output_to_operand_aliasing={{0}: (5, {})} | custom-call | flops 400000000 | bytes 1000000 | tf_op jit(solution)/shard_map/column_3/pallas_call | solution.py:377
  22.8 0.0 collective-permute-done.10.refs_10_
  22.8 0.0 collective-permute-done.12.refs_26_
  22.8 5.0 %rest.1 = (bf16[8,8,128]{2,1,0:T(8,128)(2,1)}, bf16[8,8,128]{2,1,0:T(8,128)(2,1)}, f32[6,128,128]{2,1,0:T(8,128)}) custom-call(bf16[6,128,128]{2,1,0:T(8,128)(2,1)S(1)} %copy-done, f32[2,64,128]{2,1,0:T(8,128)S(1)} %get-tuple-element.38.own_ref, f32[8,128]{1,0:T(8,128)S(1)} %get-tuple-element.39.gains_ref, f32[1024,128]{1,0:T(8,128)S(1)} %get-tuple-element.43.tri_ref, ...), custom_call_target="tpu_custom_call" | custom-call | tf_op jit(solution)/shard_map/rest/pallas_call | solution.py:399
  (1 shorter events, 0.0 us)
Async XLA Ops:
  0.6 17.4 %copy-start = (bf16[6,128,128]{2,1,0:T(8,128)(2,1)S(1)}, bf16[6,128,128]{2,1,0:T(8,128)(2,1)}, u32[]{:S(2)}) copy-start(bf16[6,128,128]{2,1,0:T(8,128)(2,1)} %weights_ref.9) | copy-start | bytes 589828
  2.3 15.7 %copy-start.1 = (bf16[144,128]{1,0:T(8,128)(2,1)S(1)}, bf16[144,128]{1,0:T(8,128)(2,1)}, u32[]{:S(2)}) copy-start(bf16[144,128]{1,0:T(8,128)(2,1)} %pack.1.first_ref.refs_0_) | copy-start | bytes 110596
  2.3 15.7 %copy-start.2 = (bf16[8,8,128]{2,1,0:T(8,128)(2,1)S(1)}, bf16[8,8,128]{2,1,0:T(8,128)(2,1)}, u32[]{:S(2)}) copy-start(bf16[8,8,128]{2,1,0:T(8,128)(2,1)} %refs_0_.1) | copy-start | bytes 49156
  2.3 7.5 %collective-permute-start.5 = (bf16[144,128]{1,0:T(8,128)(2,1)}, bf16[144,128]{1,0:T(8,128)(2,1)S(1)}, u32[]{:S(2)}, u32[]{:S(2)}) collective-permute-start(bf16[144,128]{1,0:T(8,128)(2,1)} %pack.1.first_ref.refs_0_), channel_id=1, source_target_pairs={{0,1},{1,0},{2,3},{3,2},{4,5},{5,4},{6,7},{7,6},{8,9},{9,8},{10,11... | collective-permute-start | bytes 110600 | tf_op jit(solution)/shard_map/ppermute | solution.py:312
  2.8 8.2 %collective-permute-start = (bf16[144,128]{1,0:T(8,128)(2,1)}, bf16[144,128]{1,0:T(8,128)(2,1)S(1)}, u32[]{:S(2)}, u32[]{:S(2)}) collective-permute-start(bf16[144,128]{1,0:T(8,128)(2,1)} %pack.1.first_ref.refs_0_), channel_id=1, source_target_pairs={{0,12},{1,13},{2,14},{3,15},{4,8},{5,9},{6,10},{7,11},{8,4},{9,5},... | collective-permute-start | bytes 110600 | tf_op jit(solution)/shard_map/ppermute | solution.py:312
  7.5 5.1 %collective-permute-start.1 = (bf16[144,128]{1,0:T(8,128)(2,1)}, bf16[144,128]{1,0:T(8,128)(2,1)S(1)}, u32[]{:S(2)}, u32[]{:S(2)}) collective-permute-start(bf16[144,128]{1,0:T(8,128)(2,1)} %pack.1.first_ref.refs_0_), channel_id=1, source_target_pairs={{0,8},{1,9},{2,10},{3,11},{4,12},{5,13},{6,14},{7,15},{8,0},{9,1},... | collective-permute-start | bytes 110600 | tf_op jit(solution)/shard_map/ppermute | solution.py:312
  7.5 5.1 %collective-permute-start.2 = (bf16[144,128]{1,0:T(8,128)(2,1)}, bf16[144,128]{1,0:T(8,128)(2,1)S(1)}, u32[]{:S(2)}, u32[]{:S(2)}) collective-permute-start(bf16[144,128]{1,0:T(8,128)(2,1)} %pack.1.first_ref.refs_0_), channel_id=1, source_target_pairs={{0,2},{1,3},{2,0},{3,1},{4,6},{5,7},{6,4},{7,5},{8,10},{9,11},{10,... | collective-permute-start | bytes 110600 | tf_op jit(solution)/shard_map/ppermute | solution.py:312
  9.0 4.5 %collective-permute-start.3 = (bf16[144,128]{1,0:T(8,128)(2,1)}, bf16[144,128]{1,0:T(8,128)(2,1)S(1)}, u32[]{:S(2)}, u32[]{:S(2)}) collective-permute-start(bf16[144,128]{1,0:T(8,128)(2,1)} %pack.1.first_ref.refs_0_), channel_id=1, source_target_pairs={{0,4},{1,5},{2,6},{3,7},{4,0},{5,1},{6,2},{7,3},{8,12},{9,13},{10,... | collective-permute-start | bytes 110600 | tf_op jit(solution)/shard_map/ppermute | solution.py:312
  9.8 5.1 %collective-permute-start.4 = (bf16[144,128]{1,0:T(8,128)(2,1)}, bf16[144,128]{1,0:T(8,128)(2,1)S(1)}, u32[]{:S(2)}, u32[]{:S(2)}) collective-permute-start(bf16[144,128]{1,0:T(8,128)(2,1)} %pack.1.first_ref.refs_0_), channel_id=1, source_target_pairs={{0,6},{1,7},{2,4},{3,5},{4,2},{5,3},{6,0},{7,1},{8,14},{9,15},{10,... | collective-permute-start | bytes 110600 | tf_op jit(solution)/shard_map/ppermute | solution.py:312
  14.9 6.0 %collective-permute-start.6 = (bf16[3,144,128]{2,1,0:T(8,128)(2,1)S(1)}, bf16[3,144,128]{2,1,0:T(8,128)(2,1)S(1)}, u32[]{:S(2)}, u32[]{:S(2)}) collective-permute-start(bf16[3,144,128]{2,1,0:T(8,128)(2,1)S(1)} %get-tuple-element.36.second_ref.first_ref.refs_1_.refs_16_.refs_17_), channel_id=1, source_target_pairs={{0,1},{1,0},{2,3},{3,2},{4,5},{5,4},{6,7},{7,6},{8,9},{9,8},{10,11... | collective-permute-start | bytes 331784 | tf_op jit(solution)/shard_map/ppermute | solution.py:312
  14.9 5.4 %collective-permute-start.7 = (bf16[2,80,128]{2,1,0:T(8,128)(2,1)S(1)}, bf16[2,80,128]{2,1,0:T(8,128)(2,1)S(1)}, u32[]{:S(2)}, u32[]{:S(2)}) collective-permute-start(bf16[2,80,128]{2,1,0:T(8,128)(2,1)S(1)} %get-tuple-element.37.rest_ref), channel_id=1, source_target_pairs={{0,2},{1,3},{2,0},{3,1},{4,6},{5,7},{6,4},{7,5},{8,10},{9,11},{10,... | collective-permute-start | bytes 122888 | tf_op jit(solution)/shard_map/ppermute | solution.py:312
  15.6 5.3 %collective-permute-start.9 = (bf16[2,80,128]{2,1,0:T(8,128)(2,1)S(1)}, bf16[2,80,128]{2,1,0:T(8,128)(2,1)S(1)}, u32[]{:S(2)}, u32[]{:S(2)}) collective-permute-start(bf16[2,80,128]{2,1,0:T(8,128)(2,1)S(1)} %get-tuple-element.37.rest_ref), channel_id=1, source_target_pairs={{0,1},{1,0},{2,3},{3,2},{4,5},{5,4},{6,7},{7,6},{8,9},{9,8},{10,11... | collective-permute-start | bytes 122888 | tf_op jit(solution)/shard_map/ppermute | solution.py:312
  16.4 1.7 %copy-start.3 = (f32[128]{0:T(128)S(1)}, f32[128]{0:T(128)}, u32[]{:S(2)}) copy-start(f32[128]{0:T(128)} %param.11) | copy-start | bytes 1540
  16.4 1.6 %copy-start.4 = (f32[128]{0:T(128)S(1)}, f32[128]{0:T(128)}, u32[]{:S(2)}) copy-start(f32[128]{0:T(128)} %param.12) | copy-start | bytes 1540
  16.4 4.0 %collective-permute-start.11 = (bf16[2,64,128]{2,1,0:T(8,128)(2,1)S(1)}, bf16[2,64,128]{2,1,0:T(8,128)(2,1)S(1)}, u32[]{:S(2)}, u32[]{:S(2)}) collective-permute-start(bf16[2,64,128]{2,1,0:T(8,128)(2,1)S(1)} %get-tuple-element.44.refs_2_), channel_id=1, source_target_pairs={{0,2},{1,3},{2,0},{3,1},{4,6},{5,7},{6,4},{7,5},{8,10},{9,11},{10,... | collective-permute-start | bytes 98312 | tf_op jit(solution)/shard_map/ppermute | solution.py:312
  17.9 4.9 %collective-permute-start.10 = (bf16[2,64,128]{2,1,0:T(8,128)(2,1)S(1)}, bf16[2,64,128]{2,1,0:T(8,128)(2,1)S(1)}, u32[]{:S(2)}, u32[]{:S(2)}) collective-permute-start(bf16[2,64,128]{2,1,0:T(8,128)(2,1)S(1)} %get-tuple-element.44.refs_2_), channel_id=1, source_target_pairs={{0,1},{1,0},{2,3},{3,2},{4,5},{5,4},{6,7},{7,6},{8,9},{9,8},{10,11... | collective-permute-start | bytes 98312 | tf_op jit(solution)/shard_map/ppermute | solution.py:312
  20.4 2.5 %collective-permute-start.12 = (bf16[2,64,128]{2,1,0:T(8,128)(2,1)S(1)}, bf16[2,64,128]{2,1,0:T(8,128)(2,1)S(1)}, u32[]{:S(2)}, u32[]{:S(2)}) collective-permute-start(bf16[2,64,128]{2,1,0:T(8,128)(2,1)S(1)} %collective-permute-done.11.refs_18_), channel_id=1, source_target_pairs={{0,1},{1,0},{2,3},{3,2},{4,5},{5,4},{6,7},{7,6},{8,9},{9,8},{10,11... | collective-permute-start | bytes 98312 | tf_op jit(solution)/shard_map/ppermute | solution.py:312
  20.4 1.8 %collective-permute-start.8 = (bf16[2,80,128]{2,1,0:T(8,128)(2,1)S(1)}, bf16[2,80,128]{2,1,0:T(8,128)(2,1)S(1)}, u32[]{:S(2)}, u32[]{:S(2)}) collective-permute-start(bf16[2,80,128]{2,1,0:T(8,128)(2,1)S(1)} %collective-permute-done.7.rest_ref), channel_id=1, source_target_pairs={{0,1},{1,0},{2,3},{3,2},{4,5},{5,4},{6,7},{7,6},{8,9},{9,8},{10,11... | collective-permute-start | bytes 122888 | tf_op jit(solution)/shard_map/ppermute | solution.py:312

commit v10 on v9

--- a/solution.py
+++ b/solution.py
@@ -128,12 +128,44 @@
     out_ref[pairs:head] = tall.T[0 : head - pairs].astype(jnp.bfloat16)
 
 
-def join_kernel(head, far_3, far_2, over, near, cross, twin, front_ref, back_ref, near_ref):
-    for at, block in enumerate((far_2, far_3)):
-        front_ref[at] = block[0:head]
-        back_ref[at] = block[head:]
-    for at, block in enumerate((over, near, cross)):
-        near_ref[at] = block[...]
+def join_kernel(own_ref, twin_ref, out_ref):
+    tile = SUB * SUB
+    refs = (own_ref, twin_ref)
+    for at, ref in enumerate(refs):
+        out_ref[at * tile : (at + 1) * tile] = ref[0:tile]
+        spot = 2 * tile + 2 * SUB + at * tile
+        out_ref[spot : spot + tile] = ref[tile + 2 * SUB :]
+    masks = [ref[tile : tile + 2 * SUB].astype(jnp.float32)[0:SUB] for ref in refs]
+    out_ref[2 * tile : 2 * tile + 2 * SUB] = jnp.concatenate(masks, axis=0).astype(jnp.bfloat16)
+
+
+def normed_rows(ref, sub):
+    return ref[sub * SUB * SUB : (sub + 1) * SUB * SUB]
+
+
+def mask_rows(ref, sub):
+    at = ref.shape[0] // 2 // (SUB * SUB) * SUB * SUB
+    return ref[at : at + 2 * SUB].astype(jnp.float32)[sub * SUB : (sub + 1) * SUB]
+
+
+def cot_rows(ref, sub):
+    at = ref.shape[0] // 2 // (SUB * SUB) * SUB * SUB + 2 * SUB
+    return ref[at + sub * SUB * SUB : at + (sub + 1) * SUB * SUB]
+
+
+def chip_rows(rows_of, refs, core, direct_on):
+    if direct_on is None:
+        return rows_of(refs[min(core, len(refs) - 1)], core if len(refs) == 1 else 0)
+    here = lax.axis_index("col") % 2 == direct_on
+    return jnp.where(here, rows_of(refs[0], core), rows_of(refs[1], 1 - core))
+
+
+def split_chips(refs, chips):
+    split, at = [], 0
+    for width, direct_on in chips:
+        split.append((refs[at : at + width], direct_on))
+        at += width
+    return split
 
 
 def triangle(blocks, groups, steps, vectors_at, factors_at, start_at, store_at):
@@ -168,7 +200,9 @@
     return ref[pl.ds(pl.multiple_of(row, SUB), SUB), :]
 
 
-def column_kernel(n_row, n_col, col, spots, crop_ref, first_ref, second_ref, rest_ref, weights_ref, *refs):
+def column_kernel(n_row, n_col, col, chips, crop_ref, weights_ref, *refs):
+    count = sum(width for width, _ in chips)
+    chip_refs, refs = refs[:count], refs[count:]
     if col == 0:
         act_ref, in_gain_ref, out_gain_ref, *refs, own_ref, gains_ref = refs
         z_hat, z_inverse = normalize(act_ref[...].astype(jnp.float32).reshape(own_ref.shape[1:]))
@@ -177,22 +211,21 @@
         gains_ref[0:1] = in_gain_ref[...]
         gains_ref[1:2] = out_gain_ref[...]
     tri_in, (tri_ref, left_ref, right_ref, side_ref, gate_ref, flip_ref) = refs[:-6], refs[-6:]
-    channels = rest_ref.shape[-1]
+    channels = weights_ref.shape[-1]
     tile = SUB * SUB
     size = n_row * tile
     bf16, f32 = jnp.bfloat16, jnp.float32
     row_me, col_me = lax.axis_index("row"), lax.axis_index("col")
-    blocks = [ref if at is None else ref.at[at] for ref, at in zip((first_ref, second_ref), spots)]
-    blocks += [rest_ref.at[b] for b in range(n_row - 2)]
-    normed = jnp.concatenate([block[0:tile] for block in blocks], axis=0)
+    chip_list = split_chips(chip_refs, chips)
+    normed = jnp.concatenate([chip_rows(normed_rows, chip, col % 2, on) for chip, on in chip_list], axis=0)
     flip_ref[...] = normed.astype(f32).T.astype(bf16)
     crop = crop_ref[0]
     col_offset = lax.broadcasted_iota(jnp.int32, (SUB, channels), 0)
     row_offset = lax.broadcasted_iota(jnp.int32, (SUB, channels), 1)
     cols_in = col_offset < crop - (col_me ^ col) * SUB
     kept = []
-    for b, block in enumerate(blocks):
-        keep = block[tile : tile + 2 * SUB].astype(f32)[0:SUB]
+    for b, (chip, on) in enumerate(chip_list):
+        keep = chip_rows(mask_rows, chip, col % 2, on)
         rows_in = row_offset < crop - (row_me ^ b) * SUB
         keep = jnp.where(rows_in & cols_in, keep, 0.0)
         kept += [jnp.broadcast_to(keep[:, at : at + 1], (SUB, channels)) for at in range(SUB)]
@@ -228,9 +261,14 @@
     triangle(n_row, n_col, 1, flipped, along, start, store)
 
 
-def rest_kernel(n_row, n_col, spots, weights_ref, own_ref, gains_ref, tri_ref, *refs):
-    parts = [refs[at * 8 : at * 8 + 8] for at in range(n_col)]
-    update_ref, pair_grad_ref, weight_grad_ref, back_ref, hat_ref, lin_ref, d_ref = refs[8 * n_col :]
+def rest_kernel(n_row, n_col, chips, weights_ref, own_ref, gains_ref, tri_ref, *refs):
+    chip_lists, columns = [], []
+    for col in range(n_col):
+        count = sum(width for width, _ in chips[col // 2])
+        chip_lists.append(split_chips(refs[:count], chips[col // 2]))
+        columns.append(refs[count : count + 5])
+        refs = refs[count + 5 :]
+    update_ref, pair_grad_ref, weight_grad_ref, back_ref, hat_ref, lin_ref, d_ref = refs
     channels = tri_ref.shape[-1]
     tile = SUB * SUB
     size = n_row * tile
@@ -238,7 +276,7 @@
     bf16, f32 = jnp.bfloat16, jnp.float32
     turn = lax.axis_index("row") ^ lax.axis_index("col")
     out_gain = gains_ref[1:2]
-    for col, (first_ref, second_ref, cots_ref, _, _, _, gate_ref, _) in enumerate(parts):
+    for col, (_, _, _, gate_ref, _) in enumerate(columns):
         rows = slice(col * size, (col + 1) * size)
         x_hat, inverse = normalize(tri_ref[rows, :])
         normed_out = (x_hat * out_gain).astype(bf16)
@@ -247,8 +285,7 @@
         out_gate = gate_ref[...]
         if col == 0:
             update_ref[...] = (out_gate[0:tile] * lin[0:tile]).astype(bf16).reshape(update_ref.shape)
-        blocks = [ref if at is None else ref.at[at] for ref, at in zip((first_ref, second_ref), spots[col])]
-        cots = [block[block.shape[0] - tile :] for block in blocks] + [cots_ref[b] for b in range(n_row - 2)]
+        cots = [chip_rows(cot_rows, chip, col % 2, on) for chip, on in chip_lists[col]]
         cot = jnp.concatenate(cots, axis=0).astype(f32)
         grad = cot * out_gate
         grad_lin = grad.astype(bf16)
@@ -257,7 +294,7 @@
         back = lax.dot_general(grad_lin, weights_ref[5], (((1,), (1,)), ((), ())), preferred_element_type=f32)
         back_ref[rows, :] = norm_back(back * out_gain, x_hat, inverse).astype(bf16).astype(f32)
 
-    lefts, rights, sides = [[part[at] for part in parts] for at in (3, 4, 5)]
+    lefts, rights, sides = [[column[at] for column in columns] for at in (0, 1, 2)]
 
     def zero(a, g, lane):
         return jnp.zeros((SUB, channels), f32)
@@ -290,7 +327,7 @@
     triangle(n_row, n_col, n_row, by_left, down, zero, store(1))
 
     scale = 1.0 / residues
-    flipped = jnp.concatenate([part[7][...] for part in parts], axis=1)
+    flipped = jnp.concatenate([column[4][...] for column in columns], axis=1)
     sums = jnp.dot(flipped, d_ref[...], preferred_element_type=f32) * scale
     for s in range(5):
         weight_grad_ref[s] = sums[:, s * channels : (s + 1) * channels]
@@ -307,8 +344,12 @@
     pair_grad_ref[...] = grad.astype(bf16).reshape(pair_grad_ref.shape)
 
 
-def flip(block, n_row, n_col, row, col):
-    pairs = [(r * n_col + c, (r ^ row) * n_col + (c ^ col)) for r in range(n_row) for c in range(n_col)]
+def flip(block, n_row, n_col, even, odd):
+    pairs = []
+    for row in range(n_row):
+        for col in range(n_col):
+            shift = odd if col % 2 else even
+            pairs.append((row * n_col + col, (row ^ shift[0]) * n_col + (col ^ shift[1])))
     return lax.ppermute(block, ("row", "col"), pairs)
 
 
@@ -343,29 +384,27 @@
     )(pair_act, pair_mask, cotangent.reshape(tile, channels), in_gain)
     crop_length, own = lax.optimization_barrier((crop_length, own))
 
-    def move(block, row, col):
-        return flip(block, n_row, n_col, row, col)
-
-    twin = move(own, 0, 1)
-    front, back, near = pl.pallas_call(
-        functools.partial(join_kernel, head),
+    def move(block, even, odd):
+        return flip(block, n_row, n_col, even, odd)
+
+    def other(block):
+        return move(block, (0, 1), (0, 1))
+
+    both = pl.pallas_call(
+        join_kernel,
         name="join",
-        out_shape=(
-            jax.ShapeDtypeStruct((2, head, channels), bf16),
-            jax.ShapeDtypeStruct((2, tile, channels), bf16),
-            jax.ShapeDtypeStruct((3,) + own.shape, bf16),
-        ),
-        in_specs=[vmem] * 5 + [pl.BlockSpec(memory_space=pl.ANY)],
-        out_specs=(vmem, vmem, vmem),
+        out_shape=jax.ShapeDtypeStruct((2 * own.shape[0] - 2 * SUB, channels), bf16),
+        in_specs=[vmem] * 2,
+        out_specs=vmem,
         compiler_params=limit(2),
-    )(move(own, 3, 0), move(own, 2, 0), move(own, 0, 2), move(own, 1, 0), move(own, 1, 2), twin)
-    near_twin = move(near, 0, 1)
-    fronts, backs = {0: front}, {0: back}
-    for bit in (2, 1):
-        fronts.update({col ^ bit: move(stack, 0, bit) for col, stack in fronts.items()})
-        backs.update({col ^ bit: move(stack, 0, bit) for col, stack in backs.items()})
-    heads = {0: (own, near), 1: (twin, near_twin), 2: (near, near), 3: (near_twin, near_twin)}
-    spots = ((None, 1), (None, 1), (0, 2), (0, 2))
+    )(own, other(own))
+    far = move(both, (2, 0), (3, 0))
+    near = move(both, (1, 0), (0, 2))
+    cross = move(both, (1, 2), (2, 2))
+    last = move(own, (3, 2), (3, 2))
+    far, near, cross, last = [(block, other(block)) for block in (far, near, cross, last)]
+    chips = (((1, None), (2, 0), (2, 0), (2, 1)), ((2, 1), (2, 0), (2, 1), (2, None)))
+    sources = ((both, *near, *far, *far), (*near, *cross, *cross, *last))
 
     tri, parts, extra = [], [], []
     for col in range(n_col):
@@ -375,7 +414,7 @@
             jax.ShapeDtypeStruct((SUB, channels), f32),
         )
         tri, *results = pl.pallas_call(
-            functools.partial(column_kernel, n_row, n_col, col, spots[col]),
+            functools.partial(column_kernel, n_row, n_col, col, chips[col // 2]),
             name=f"column_{col}",
             out_shape=(
                 jax.ShapeDtypeStruct((pairs, channels), f32),
@@ -386,18 +425,18 @@
                 jax.ShapeDtypeStruct((channels, size), bf16),
                 *more_shapes,
             ),
-            in_specs=[smem] + [vmem] * (4 + len(more)),
+            in_specs=[smem] + [vmem] * (1 + len(sources[col // 2]) + len(more)),
             out_specs=(vmem,) * (6 + len(more_shapes)),
-            input_output_aliases={5: 0} if col > 0 else {},
+            input_output_aliases={2 + len(sources[col // 2]): 0} if col > 0 else {},
             compiler_params=limit(8),
             cost_estimate=pl.CostEstimate(flops=400_000_000, bytes_accessed=1_000_000, transcendentals=0),
-        )(crop_length, *heads[col], fronts[col], weights, *more)
+        )(crop_length, weights, *sources[col // 2], *more)
         tri = [tri]
-        parts += [*heads[col], backs[col], *results[:5]]
+        parts += [*sources[col // 2], *results[:5]]
         extra += results[5:]
 
     return pl.pallas_call(
-        functools.partial(rest_kernel, n_row, n_col, spots),
+        functools.partial(rest_kernel, n_row, n_col, chips),
         name="rest",
         out_shape=(
             jax.ShapeDtypeStruct(pair_act.shape, bf16),

time: 28.1 us -> 29.7 us (1.057)
  starting transfers between devices: 11.7 us -> 13.7 us
  waiting for transfers between devices: 5.58 us -> 4.31 us
  Pallas kernels: 9.2 us -> 10 us
    ppermute x13 -> x9, starting transfers between devices: 11.7 us -> 13.7 us  [flip(): return lax.ppermute(block, ('row', 'col'), pairs)]
    ppermute x13 -> x9, waiting for transfers between devices: 5.58 us -> 4.31 us  [flip(): return lax.ppermute(block, ('row', 'col'), pairs)]
    pallas_call x6, Pallas kernels: 7.57 us -> 8.41 us  [the longest x1 5.11 us: gathered_body(): pl.pallas_call(functools.partial(rest_kernel, n_row, n_col, chips), name=...]
  transfers between devices with their start and end apart: 13 -> 9, of which waited for: 4 -> 4; matrix products, arithmetic and copies ran while one was open for 0% -> 0% of each run, Pallas kernels for 9% -> 4%
where the time goes in v10:
time: 29.7 us; the launch traced here: 29.5 us
  starting transfers between devices  13.7 us (46%)
  Pallas kernels  10 us (34%)
  waiting for transfers between devices  4.31 us (15%)
  between operations  1.4 us (5%)
    ppermute x9, starting transfers between devices, flip(): return lax.ppermute(block, ('row', 'col'), pairs)  13.7 us
    pallas_call x1, Pallas kernels, gathered_body(): pl.pallas_call(functools.partial(rest_kernel, n_row, n_col, chips), name=...  5.11 us
    ppermute x9, waiting for transfers between devices, flip(): return lax.ppermute(block, ('row', 'col'), pairs)  4.31 us
    pallas_call x4, Pallas kernels, gathered_body(): pl.pallas_call(functools.partial(column_kernel, n_row, n_col, col, chips[...  2.53 us
    pallas_call x1, Pallas kernels, gathered_body(): pl.pallas_call(pack_kernel, name='pack', out_shape=jax.ShapeDtypeStruct((...  1.64 us
    pallas_call x1, Pallas kernels, gathered_body(): pl.pallas_call(join_kernel, name='join', out_shape=jax.ShapeDtypeStruct((...  0.77 us
  transfers between devices with their start and end apart: 9, of which 4 were waited for; matrix products, arithmetic and copies ran while one was open for 0% of the time, Pallas kernels for 4%

profile of v10, /device:TPU:0, one launch (start us, length us, event | category | flops | bytes accessed | tf_op | source)
XLA Modules:
  0.0 29.5 jit_solution(7539905797677307044)
XLA Ops:
  0.6 0.0 copy-start
  0.6 1.6 %pack.1.own_ref = bf16[144,128]{1,0:T(8,128)(2,1)} custom-call(bf16[8,8,128]{2,1,0:T(8,128)(2,1)} %refs_7_.1, s32[8,8]{1,0:T(8,128)} %mask_hbm.1, bf16[64,128]{1,0:T(8,128)(2,1)} %bitcast.6, f32[1,128]{1,0:T(1,128)} %bitcast.3), custom_call_target="tpu_custom_call" | custom-call | tf_op jit(solution)/shard_map/pack/pallas_call | solution.py:371
  2.3 0.0 copy-start.1
  2.3 0.5 %collective-permute-start = (bf16[144,128]{1,0:T(8,128)(2,1)}, bf16[144,128]{1,0:T(8,128)(2,1)S(1)}, u32[]{:S(2)}, u32[]{:S(2)}) collective-permute-start(bf16[144,128]{1,0:T(8,128)(2,1)} %pack.1.own_ref), channel_id=1, source_target_pairs={{0,1},{1,0},{2,3},{3,2},{4,5},{5,4},{6,7},{7,6},{8,9},{9,8},{10,11... | collective-permute-start | bytes 110600 | tf_op jit(solution)/shard_map/ppermute | solution.py:353
  2.8 1.1 %collective-permute-done.twin_ref = bf16[144,128]{1,0:T(8,128)(2,1)S(1)} collective-permute-done((bf16[144,128]{1,0:T(8,128)(2,1)}, bf16[144,128]{1,0:T(8,128)(2,1)S(1)}, u32[]{:S(2)}, u32[]{:S(2)}) %collective-permute-start) | collective-permute-done | bytes 36896 | tf_op jit(solution)/shard_map/ppermute | solution.py:353
  3.9 0.8 %join.1.refs_0_.refs_12_ = bf16[272,128]{1,0:T(8,128)(2,1)S(1)} custom-call(bf16[144,128]{1,0:T(8,128)(2,1)} %pack.1.own_ref, bf16[144,128]{1,0:T(8,128)(2,1)S(1)} %collective-permute-done.twin_ref), custom_call_target="tpu_custom_call" | custom-call | tf_op jit(solution)/shard_map/join/pallas_call | solution.py:393
  4.7 3.9 %collective-permute-start.3 = (bf16[272,128]{1,0:T(8,128)(2,1)S(1)}, bf16[272,128]{1,0:T(8,128)(2,1)S(1)}, u32[]{:S(2)}, u32[]{:S(2)}) collective-permute-start(bf16[272,128]{1,0:T(8,128)(2,1)S(1)} %join.1.refs_0_.refs_12_), channel_id=1, source_target_pairs={{0,8},{1,13},{2,10},{3,15},{4,12},{5,9},{6,14},{7,11},{8,0},{9,5},... | collective-permute-start | bytes 208904 | tf_op jit(solution)/shard_map/ppermute | solution.py:353
  8.6 1.6 %collective-permute-start.1 = (bf16[272,128]{1,0:T(8,128)(2,1)S(1)}, bf16[272,128]{1,0:T(8,128)(2,1)S(1)}, u32[]{:S(2)}, u32[]{:S(2)}) collective-permute-start(bf16[272,128]{1,0:T(8,128)(2,1)S(1)} %join.1.refs_0_.refs_12_), channel_id=1, source_target_pairs={{0,4},{1,3},{2,6},{3,1},{4,0},{5,7},{6,2},{7,5},{8,12},{9,11},{10,... | collective-permute-start | bytes 208904 | tf_op jit(solution)/shard_map/ppermute | solution.py:353
  10.2 1.4 %collective-permute-start.5 = (bf16[272,128]{1,0:T(8,128)(2,1)S(1)}, bf16[272,128]{1,0:T(8,128)(2,1)S(1)}, u32[]{:S(2)}, u32[]{:S(2)}) collective-permute-start(bf16[272,128]{1,0:T(8,128)(2,1)S(1)} %join.1.refs_0_.refs_12_), channel_id=1, source_target_pairs={{0,6},{1,11},{2,4},{3,9},{4,2},{5,15},{6,0},{7,13},{8,14},{9,3},{1... | collective-permute-start | bytes 208904 | tf_op jit(solution)/shard_map/ppermute | solution.py:353
  11.6 1.3 %collective-permute-done.3.refs_3_.refs_5_.refs_15_.refs_17_ = bf16[272,128]{1,0:T(8,128)(2,1)S(1)} collective-permute-done((bf16[272,128]{1,0:T(8,128)(2,1)S(1)}, bf16[272,128]{1,0:T(8,128)(2,1)S(1)}, u32[]{:S(2)}, u32[]{:S(2)}) %collective-permute-start.3) | collective-permute-done | bytes 69664 | tf_op jit(solution)/shard_map/ppermute | solution.py:353
  12.9 0.0 collective-permute-start.4
  12.9 0.4 %collective-permute-done.1.refs_1_.refs_0_.refs_13_.refs_24_.refs_37_ = bf16[272,128]{1,0:T(8,128)(2,1)S(1)} collective-permute-done((bf16[272,128]{1,0:T(8,128)(2,1)S(1)}, bf16[272,128]{1,0:T(8,128)(2,1)S(1)}, u32[]{:S(2)}, u32[]{:S(2)}) %collective-permute-start.1) | collective-permute-done | bytes 69664 | tf_op jit(solution)/shard_map/ppermute | solution.py:353
  13.3 0.1 collective-permute-start.2
  13.4 5.7 %collective-permute-start.7 = (bf16[144,128]{1,0:T(8,128)(2,1)}, bf16[144,128]{1,0:T(8,128)(2,1)S(1)}, u32[]{:S(2)}, u32[]{:S(2)}) collective-permute-start(bf16[144,128]{1,0:T(8,128)(2,1)} %pack.1.own_ref), channel_id=1, source_target_pairs={{0,14},{1,15},{2,12},{3,13},{4,10},{5,11},{6,8},{7,9},{8,6},{9,7},... | collective-permute-start | bytes 110600 | tf_op jit(solution)/shard_map/ppermute | solution.py:353
  19.7 0.0 copy-start.2
  19.8 0.0 copy-start.3
  19.8 1.5 %collective-permute-done.7.refs_6_.refs_30_.refs_43_ = bf16[144,128]{1,0:T(8,128)(2,1)S(1)} collective-permute-done((bf16[144,128]{1,0:T(8,128)(2,1)}, bf16[144,128]{1,0:T(8,128)(2,1)S(1)}, u32[]{:S(2)}, u32[]{:S(2)}) %collective-permute-start.7) | collective-permute-done | bytes 36896 | tf_op jit(solution)/shard_map/ppermute | solution.py:353
  21.2 0.0 collective-permute-start.8
  21.2 0.0 collective-permute-done.5.refs_2_.refs_4_.refs_26_.refs_28_.refs_39_.refs_41_
  21.2 0.5 %collective-permute-start.6 = (bf16[272,128]{1,0:T(8,128)(2,1)S(1)}, bf16[272,128]{1,0:T(8,128)(2,1)S(1)}, u32[]{:S(2)}, u32[]{:S(2)}) collective-permute-start(bf16[272,128]{1,0:T(8,128)(2,1)S(1)} %collective-permute-done.5.refs_2_.refs_4_.refs_26_.refs_28_.refs_39_.refs_41_), channel_id=1, source_target_pairs={{0,1},{1,0},{2,3},{3,2},{4,5},{5,4},{6,7},{7,6},{8,9},{9,8},{10,11... | collective-permute-start | bytes 208904 | tf_op jit(solution)/shard_map/ppermute | solution.py:353
  21.7 0.0 collective-permute-done.4.refs_4_.refs_6_.refs_16_.refs_18_
  21.8 0.0 collective-permute-done.2.refs_2_.refs_1_.refs_14_.refs_25_.refs_38_
  21.8 0.0 copy-done
  21.8 0.0 copy-done.1
  21.8 0.0 copy-done.2
  21.8 0.0 copy-done.3
  21.8 0.6 %column_0.1 = (f32[1024,128]{1,0:T(8,128)S(1)}, f32[256,128]{1,0:T(8,128)S(1)}, f32[256,128]{1,0:T(8,128)S(1)}, f32[4,256,128]{2,1,0:T(8,128)S(1)}, f32[256,128]...) custom-call(s32[1]{0:T(128)S(6)} %copy.16.crop_ref, ...), custom_call_target="tpu_custom_call" | custom-call | flops 400000000 | bytes 1000000 | tf_op jit(solution)/shard_map/column_0/pallas_call | solution.py:416
  22.4 0.6 %column_1.1 = (f32[1024,128]{1,0:T(8,128)S(1)}, f32[256,128]{1,0:T(8,128)S(1)}, f32[256,128]{1,0:T(8,128)S(1)}, f32[4,256,128]{2,1,0:T(8,128)S(1)}, f32[256,128]...) custom-call(s32[1]{0:T(128)S(6)} %copy.16.crop_ref, bf16[6,128,128]{2,1,0:T(8,128)(2,1)S(1)} %copy-done, ...), custom_call_target="tpu_custom_call", output_to_operand_aliasing={{0}: (9, {})} | custom-call | flops 400000000 | bytes 1000000 | tf_op jit(solution)/shard_map/column_1/pallas_call | solution.py:416
  23.1 0.0 collective-permute-done.8.refs_7_.refs_31_.refs_44_
  23.1 0.0 collective-permute-done.6.refs_3_.refs_5_.refs_27_.refs_29_.refs_40_.refs_42_
  23.1 0.6 %column_2.1 = (f32[1024,128]{1,0:T(8,128)S(1)}, f32[256,128]{1,0:T(8,128)S(1)}, f32[256,128]{1,0:T(8,128)S(1)}, f32[4,256,128]{2,1,0:T(8,128)S(1)}, f32[256,128]...) custom-call(s32[1]{0:T(128)S(6)} %copy.16.crop_ref, ...), custom_call_target="tpu_custom_call", output_to_operand_aliasing={{0}: (10, {})} | custom-call | flops 400000000 | bytes 1000000 | tf_op jit(solution)/shard_map/column_2/pallas_call | solution.py:416
  23.7 0.6 %column_3.1 = (f32[1024,128]{1,0:T(8,128)S(1)}, f32[256,128]{1,0:T(8,128)S(1)}, f32[256,128]{1,0:T(8,128)S(1)}, f32[4,256,128]{2,1,0:T(8,128)S(1)}, f32[256,128]...) custom-call(s32[1]{0:T(128)S(6)} %copy.16.crop_ref, ...), custom_call_target="tpu_custom_call", output_to_operand_aliasing={{0}: (10, {})} | custom-call | flops 400000000 | bytes 1000000 | tf_op jit(solution)/shard_map/column_3/pallas_call | solution.py:416
  24.4 5.1 %rest.1 = (bf16[8,8,128]{2,1,0:T(8,128)(2,1)}, bf16[8,8,128]{2,1,0:T(8,128)(2,1)}, f32[6,128,128]{2,1,0:T(8,128)}) custom-call(bf16[6,128,128]{2,1,0:T(8,128)(2,1)S(1)} %copy-done, f32[2,64,128]{2,1,0:T(8,128)S(1)} %get-tuple-element.33.own_ref, f32[8,128]{1,0:T(8,128)S(1)} %get-tuple-element.34.gains_ref, f32[1024,128]{1,0:T(8,128)S(1)} %get-tuple-element.38.tri_ref, ...), custom_call_target="tpu_custom_call" | custom-call | tf_op jit(solution)/shard_map/rest/pallas_call | solution.py:438
Async XLA Ops:
  0.6 21.1 %copy-start = (bf16[6,128,128]{2,1,0:T(8,128)(2,1)S(1)}, bf16[6,128,128]{2,1,0:T(8,128)(2,1)}, u32[]{:S(2)}) copy-start(bf16[6,128,128]{2,1,0:T(8,128)(2,1)} %weights_ref.9) | copy-start | bytes 589828
  2.3 19.5 %copy-start.1 = (bf16[8,8,128]{2,1,0:T(8,128)(2,1)S(1)}, bf16[8,8,128]{2,1,0:T(8,128)(2,1)}, u32[]{:S(2)}) copy-start(bf16[8,8,128]{2,1,0:T(8,128)(2,1)} %refs_7_.1) | copy-start | bytes 49156
  2.3 1.6 %collective-permute-start = (bf16[144,128]{1,0:T(8,128)(2,1)}, bf16[144,128]{1,0:T(8,128)(2,1)S(1)}, u32[]{:S(2)}, u32[]{:S(2)}) collective-permute-start(bf16[144,128]{1,0:T(8,128)(2,1)} %pack.1.own_ref), channel_id=1, source_target_pairs={{0,1},{1,0},{2,3},{3,2},{4,5},{5,4},{6,7},{7,6},{8,9},{9,8},{10,11... | collective-permute-start | bytes 110600 | tf_op jit(solution)/shard_map/ppermute | solution.py:353
  4.7 8.2 %collective-permute-start.3 = (bf16[272,128]{1,0:T(8,128)(2,1)S(1)}, bf16[272,128]{1,0:T(8,128)(2,1)S(1)}, u32[]{:S(2)}, u32[]{:S(2)}) collective-permute-start(bf16[272,128]{1,0:T(8,128)(2,1)S(1)} %join.1.refs_0_.refs_12_), channel_id=1, source_target_pairs={{0,8},{1,13},{2,10},{3,15},{4,12},{5,9},{6,14},{7,11},{8,0},{9,5},... | collective-permute-start | bytes 208904 | tf_op jit(solution)/shard_map/ppermute | solution.py:353
  8.6 4.7 %collective-permute-start.1 = (bf16[272,128]{1,0:T(8,128)(2,1)S(1)}, bf16[272,128]{1,0:T(8,128)(2,1)S(1)}, u32[]{:S(2)}, u32[]{:S(2)}) collective-permute-start(bf16[272,128]{1,0:T(8,128)(2,1)S(1)} %join.1.refs_0_.refs_12_), channel_id=1, source_target_pairs={{0,4},{1,3},{2,6},{3,1},{4,0},{5,7},{6,2},{7,5},{8,12},{9,11},{10,... | collective-permute-start | bytes 208904 | tf_op jit(solution)/shard_map/ppermute | solution.py:353
  10.2 11.1 %collective-permute-start.5 = (bf16[272,128]{1,0:T(8,128)(2,1)S(1)}, bf16[272,128]{1,0:T(8,128)(2,1)S(1)}, u32[]{:S(2)}, u32[]{:S(2)}) collective-permute-start(bf16[272,128]{1,0:T(8,128)(2,1)S(1)} %join.1.refs_0_.refs_12_), channel_id=1, source_target_pairs={{0,6},{1,11},{2,4},{3,9},{4,2},{5,15},{6,0},{7,13},{8,14},{9,3},{1... | collective-permute-start | bytes 208904 | tf_op jit(solution)/shard_map/ppermute | solution.py:353
  12.9 8.9 %collective-permute-start.4 = (bf16[272,128]{1,0:T(8,128)(2,1)S(1)}, bf16[272,128]{1,0:T(8,128)(2,1)S(1)}, u32[]{:S(2)}, u32[]{:S(2)}) collective-permute-start(bf16[272,128]{1,0:T(8,128)(2,1)S(1)} %collective-permute-done.3.refs_3_.refs_5_.refs_15_.refs_17_), channel_id=1, source_target_pairs={{0,1},{1,0},{2,3},{3,2},{4,5},{5,4},{6,7},{7,6},{8,9},{9,8},{10,11... | collective-permute-start | bytes 208904 | tf_op jit(solution)/shard_map/ppermute | solution.py:353
  13.3 8.5 %collective-permute-start.2 = (bf16[272,128]{1,0:T(8,128)(2,1)S(1)}, bf16[272,128]{1,0:T(8,128)(2,1)S(1)}, u32[]{:S(2)}, u32[]{:S(2)}) collective-permute-start(bf16[272,128]{1,0:T(8,128)(2,1)S(1)} %collective-permute-done.1.refs_1_.refs_0_.refs_13_.refs_24_.refs_37_), channel_id=1, source_target_pairs={{0,1},{1,0},{2,3},{3,2},{4,5},{5,4},{6,7},{7,6},{8,9},{9,8},{10,11... | collective-permute-start | bytes 208904 | tf_op jit(solution)/shard_map/ppermute | solution.py:353
  13.4 7.8 %collective-permute-start.7 = (bf16[144,128]{1,0:T(8,128)(2,1)}, bf16[144,128]{1,0:T(8,128)(2,1)S(1)}, u32[]{:S(2)}, u32[]{:S(2)}) collective-permute-start(bf16[144,128]{1,0:T(8,128)(2,1)} %pack.1.own_ref), channel_id=1, source_target_pairs={{0,14},{1,15},{2,12},{3,13},{4,10},{5,11},{6,8},{7,9},{8,6},{9,7},... | collective-permute-start | bytes 110600 | tf_op jit(solution)/shard_map/ppermute | solution.py:353
  19.7 2.0 %copy-start.2 = (f32[128]{0:T(128)S(1)}, f32[128]{0:T(128)}, u32[]{:S(2)}) copy-start(f32[128]{0:T(128)} %param.11) | copy-start | bytes 1540
  19.8 2.0 %copy-start.3 = (f32[128]{0:T(128)S(1)}, f32[128]{0:T(128)}, u32[]{:S(2)}) copy-start(f32[128]{0:T(128)} %param.12) | copy-start | bytes 1540
  21.2 1.8 %collective-permute-start.8 = (bf16[144,128]{1,0:T(8,128)(2,1)S(1)}, bf16[144,128]{1,0:T(8,128)(2,1)S(1)}, u32[]{:S(2)}, u32[]{:S(2)}) collective-permute-start(bf16[144,128]{1,0:T(8,128)(2,1)S(1)} %collective-permute-done.7.refs_6_.refs_30_.refs_43_), channel_id=1, source_target_pairs={{0,1},{1,0},{2,3},{3,2},{4,5},{5,4},{6,7},{7,6},{8,9},{9,8},{10,11... | collective-permute-start | bytes 110600 | tf_op jit(solution)/shard_map/ppermute | solution.py:353
  21.2 1.8 %collective-permute-start.6 = (bf16[272,128]{1,0:T(8,128)(2,1)S(1)}, bf16[272,128]{1,0:T(8,128)(2,1)S(1)}, u32[]{:S(2)}, u32[]{:S(2)}) collective-permute-start(bf16[272,128]{1,0:T(8,128)(2,1)S(1)} %collective-permute-done.5.refs_2_.refs_4_.refs_26_.refs_28_.refs_39_.refs_41_), channel_id=1, source_target_pairs={{0,1},{1,0},{2,3},{3,2},{4,5},{5,4},{6,7},{7,6},{8,9},{9,8},{10,11... | collective-permute-start | bytes 208904 | tf_op jit(solution)/shard_map/ppermute | solution.py:353

commit v11 on v10

--- a/solution.py
+++ b/solution.py
@@ -126,6 +126,10 @@
     wide = jnp.concatenate([keep, jnp.zeros((tile_rows, channels - tile_cols), jnp.float32)], axis=1)
     tall = jnp.concatenate([wide, jnp.zeros((channels - tile_rows, channels), jnp.float32)], axis=0)
     out_ref[pairs:head] = tall.T[0 : head - pairs].astype(jnp.bfloat16)
+
+
+def copy_kernel(in_ref, out_ref):
+    out_ref[...] = in_ref[...]
 
 
 def join_kernel(own_ref, twin_ref, out_ref):
@@ -349,7 +353,8 @@
     for row in range(n_row):
         for col in range(n_col):
             shift = odd if col % 2 else even
-            pairs.append((row * n_col + col, (row ^ shift[0]) * n_col + (col ^ shift[1])))
+            if shift is not None:
+                pairs.append((row * n_col + col, (row ^ shift[0]) * n_col + (col ^ shift[1])))
     return lax.ppermute(block, ("row", "col"), pairs)
 
 
@@ -387,9 +392,18 @@
     def move(block, even, odd):
         return flip(block, n_row, n_col, even, odd)
 
-    def other(block):
-        return move(block, (0, 1), (0, 1))
-
+    def other(block, odd=(0, 1)):
+        return move(block, (0, 1), odd)
+
+    held = pl.pallas_call(
+        copy_kernel,
+        name="hold",
+        out_shape=jax.ShapeDtypeStruct(own.shape, bf16),
+        in_specs=[vmem],
+        out_specs=vmem,
+        compiler_params=limit(2),
+        cost_estimate=pl.CostEstimate(flops=100_000_000, bytes_accessed=1_000_000, transcendentals=0),
+    )(own)
     both = pl.pallas_call(
         join_kernel,
         name="join",
@@ -397,14 +411,15 @@
         in_specs=[vmem] * 2,
         out_specs=vmem,
         compiler_params=limit(2),
-    )(own, other(own))
-    far = move(both, (2, 0), (3, 0))
-    near = move(both, (1, 0), (0, 2))
-    cross = move(both, (1, 2), (2, 2))
-    last = move(own, (3, 2), (3, 2))
-    far, near, cross, last = [(block, other(block)) for block in (far, near, cross, last)]
-    chips = (((1, None), (2, 0), (2, 0), (2, 1)), ((2, 1), (2, 0), (2, 1), (2, None)))
-    sources = ((both, *near, *far, *far), (*near, *cross, *cross, *last))
+    )(held, other(own))
+    first = move(both, (2, 0), (3, 0))
+    second = move(both, (3, 2), (0, 2))
+    third = move(both, (2, 2), (1, 0))
+    fourth = move(both, (1, 2), None)
+    first, second, third = [(block, other(block)) for block in (first, second, third)]
+    fourth = fourth, other(fourth, None)
+    chips = (((1, None), (2, 1), (2, 0), (2, 1)), ((2, 1), (2, 0), (2, 0), (2, 0)))
+    sources = ((both, *third, *first, *first), (*second, *fourth, *third, *second))
 
     tri, parts, extra = [], [], []
     for col in range(n_col):

time: 29.7 us -> 27.8 us (0.936)
  waiting for transfers between devices: 4.31 us -> 0.73 us
  starting transfers between devices: 13.7 us -> 15.1 us
  local copies, waits for them, and re-layouts: 0.02 us -> 0.79 us
  Pallas kernels: 10 us -> 9.28 us
    ppermute x9, waiting for transfers between devices: 4.31 us -> 0.73 us  [flip(): return lax.ppermute(block, ('row', 'col'), pairs)]
    ppermute x9, starting transfers between devices: 13.7 us -> 15.1 us  [flip(): return lax.ppermute(block, ('row', 'col'), pairs)]
    unnamed x8 -> x10, local copies, waits for them, and re-layouts: 0.02 us -> 0.79 us
    pallas_call x1, Pallas kernels: 0.77 us -> 0.01 us  [gathered_body(): pl.pallas_call(join_kernel, name='join', out_shape=jax.ShapeDtypeStruct((...]
  transfers between devices with their start and end apart: 9 -> 9, of which waited for: 4 -> 2; matrix products, arithmetic and copies ran while one was open for 0% -> 0% of each run, Pallas kernels for 4% -> 5%
where the time goes in v11:
time: 27.8 us; the launch traced here: 27.3 us
  starting transfers between devices  15.1 us (54%)
  Pallas kernels  9.28 us (33%)
  between operations  1.43 us (5%)
  local copies, waits for them, and re-layouts  0.79 us (3%)
  waiting for transfers between devices  0.73 us (3%)
    ppermute x9, starting transfers between devices, flip(): return lax.ppermute(block, ('row', 'col'), pairs)  15.1 us
    pallas_call x1, Pallas kernels, gathered_body(): pl.pallas_call(functools.partial(rest_kernel, n_row, n_col, chips), name=...  5.14 us
    pallas_call x4, Pallas kernels, gathered_body(): pl.pallas_call(functools.partial(column_kernel, n_row, n_col, col, chips[...  2.53 us
    pallas_call x1, Pallas kernels, gathered_body(): pl.pallas_call(pack_kernel, name='pack', out_shape=jax.ShapeDtypeStruct((...  1.6 us
    unnamed x10, local copies, waits for them, and re-layouts  0.79 us
    ppermute x9, waiting for transfers between devices, flip(): return lax.ppermute(block, ('row', 'col'), pairs)  0.73 us
  transfers between devices with their start and end apart: 9, of which 2 were waited for; matrix products, arithmetic and copies ran while one was open for 0% of the time, Pallas kernels for 5%

profile of v11, /device:TPU:0, one launch (start us, length us, event | category | flops | bytes accessed | tf_op | source)
XLA Modules:
  0.0 27.3 jit_solution(2097924982965152882)
XLA Ops:
  0.6 1.6 %pack.1.in_ref = bf16[144,128]{1,0:T(8,128)(2,1)} custom-call(bf16[8,8,128]{2,1,0:T(8,128)(2,1)} %refs_7_.1, s32[8,8]{1,0:T(8,128)} %mask_hbm.1, bf16[64,128]{1,0:T(8,128)(2,1)} %bitcast.6, f32[1,128]{1,0:T(1,128)} %bitcast.3), custom_call_target="tpu_custom_call" | custom-call | tf_op jit(solution)/shard_map/pack/pallas_call | solution.py:376
  2.2 0.0 copy-start
  2.2 0.5 %collective-permute-start = (bf16[144,128]{1,0:T(8,128)(2,1)}, bf16[144,128]{1,0:T(8,128)(2,1)S(1)}, u32[]{:S(2)}, u32[]{:S(2)}) collective-permute-start(bf16[144,128]{1,0:T(8,128)(2,1)} %pack.1.in_ref), channel_id=1, source_target_pairs={{0,1},{1,0},{2,3},{3,2},{4,5},{5,4},{6,7},{7,6},{8,9},{9,8},{10,11... | collective-permute-start | bytes 110600 | tf_op jit(solution)/shard_map/ppermute | solution.py:358
  2.8 0.0 copy-start.1
  2.8 0.8 %copy-done.1 = bf16[144,128]{1,0:T(8,128)(2,1)S(1)} copy-done((bf16[144,128]{1,0:T(8,128)(2,1)S(1)}, bf16[144,128]{1,0:T(8,128)(2,1)}, u32[]{:S(2)}) %copy-start.1) | copy-done | bytes 36888
  3.5 0.0 copy-start.2
  3.5 0.3 %collective-permute-done.twin_ref = bf16[144,128]{1,0:T(8,128)(2,1)S(1)} collective-permute-done((bf16[144,128]{1,0:T(8,128)(2,1)}, bf16[144,128]{1,0:T(8,128)(2,1)S(1)}, u32[]{:S(2)}, u32[]{:S(2)}) %collective-permute-start) | collective-permute-done | bytes 36896 | tf_op jit(solution)/shard_map/ppermute | solution.py:358
  3.9 3.9 %collective-permute-start.3 = (bf16[272,128]{1,0:T(8,128)(2,1)S(1)}, bf16[272,128]{1,0:T(8,128)(2,1)S(1)}, u32[]{:S(2)}, u32[]{:S(2)}) collective-permute-start(bf16[272,128]{1,0:T(8,128)(2,1)S(1)} %join.1.refs_0_.refs_12_), channel_id=1, source_target_pairs={{0,8},{1,13},{2,10},{3,15},{4,12},{5,9},{6,14},{7,11},{8,0},{9,5},... | collective-permute-start | bytes 208904 | tf_op jit(solution)/shard_map/ppermute | solution.py:358
  7.8 1.3 %collective-permute-start.1 = (bf16[272,128]{1,0:T(8,128)(2,1)S(1)}, bf16[272,128]{1,0:T(8,128)(2,1)S(1)}, u32[]{:S(2)}, u32[]{:S(2)}) collective-permute-start(bf16[272,128]{1,0:T(8,128)(2,1)S(1)} %join.1.refs_0_.refs_12_), channel_id=1, source_target_pairs={{0,10},{1,5},{2,8},{3,7},{4,14},{5,1},{6,12},{7,3},{8,2},{9,13},{1... | collective-permute-start | bytes 208904 | tf_op jit(solution)/shard_map/ppermute | solution.py:358
  9.0 3.4 %collective-permute-start.7 = (bf16[272,128]{1,0:T(8,128)(2,1)S(1)}, bf16[272,128]{1,0:T(8,128)(2,1)S(1)}, u32[]{:S(2)}, u32[]{:S(2)}) collective-permute-start(bf16[272,128]{1,0:T(8,128)(2,1)S(1)} %join.1.refs_0_.refs_12_), channel_id=1, source_target_pairs={{0,6},{2,4},{4,2},{6,0},{8,14},{10,12},{12,10},{14,8},{16,22},{18,... | collective-permute-start | bytes 208904 | tf_op jit(solution)/shard_map/ppermute | solution.py:358
  12.5 3.5 %collective-permute-start.5 = (bf16[272,128]{1,0:T(8,128)(2,1)S(1)}, bf16[272,128]{1,0:T(8,128)(2,1)S(1)}, u32[]{:S(2)}, u32[]{:S(2)}) collective-permute-start(bf16[272,128]{1,0:T(8,128)(2,1)S(1)} %join.1.refs_0_.refs_12_), channel_id=1, source_target_pairs={{0,14},{1,3},{2,12},{3,1},{4,10},{5,7},{6,8},{7,5},{8,6},{9,11},{1... | collective-permute-start | bytes 208904 | tf_op jit(solution)/shard_map/ppermute | solution.py:358
  16.0 0.0 collective-permute-done.3.refs_3_.refs_5_.refs_15_.refs_17_
  16.0 0.0 collective-permute-start.4
  16.0 0.0 collective-permute-done.1.refs_1_.refs_4_.refs_13_.refs_28_.refs_41_
  16.0 0.5 %collective-permute-start.2 = (bf16[272,128]{1,0:T(8,128)(2,1)S(1)}, bf16[272,128]{1,0:T(8,128)(2,1)S(1)}, u32[]{:S(2)}, u32[]{:S(2)}) collective-permute-start(bf16[272,128]{1,0:T(8,128)(2,1)S(1)} %collective-permute-done.1.refs_1_.refs_4_.refs_13_.refs_28_.refs_41_), channel_id=1, source_target_pairs={{0,1},{1,0},{2,3},{3,2},{4,5},{5,4},{6,7},{7,6},{8,9},{9,8},{10,11... | collective-permute-start | bytes 208904 | tf_op jit(solution)/shard_map/ppermute | solution.py:358
  17.1 0.0 copy-start.3
  17.1 0.0 copy-start.4
  17.2 0.0 collective-permute-done.7.refs_2_.refs_26_.refs_39_
  17.2 2.0 %collective-permute-start.8 = (bf16[272,128]{1,0:T(8,128)(2,1)S(1)}, bf16[272,128]{1,0:T(8,128)(2,1)S(1)}, u32[]{:S(2)}, u32[]{:S(2)}) collective-permute-start(bf16[272,128]{1,0:T(8,128)(2,1)S(1)} %collective-permute-done.7.refs_2_.refs_26_.refs_39_), channel_id=1, source_target_pairs={{0,1},{2,3},{4,5},{6,7},{8,9},{10,11},{12,13},{14,15},{16,17},{18,... | collective-permute-start | bytes 208904 | tf_op jit(solution)/shard_map/ppermute | solution.py:358
  19.2 0.4 %collective-permute-done.5.refs_0_.refs_6_.refs_24_.refs_30_.refs_37_.refs_43_ = bf16[272,128]{1,0:T(8,128)(2,1)S(1)} collective-permute-done((bf16[272,128]{1,0:T(8,128)(2,1)S(1)}, bf16[272,128]{1,0:T(8,128)(2,1)S(1)}, u32[]{:S(2)}, u32[]{:S(2)}) %collective-permute-start.5) | collective-permute-done | bytes 69664 | tf_op jit(solution)/shard_map/ppermute | solution.py:358
  19.6 0.0 collective-permute-start.6
  19.6 0.0 collective-permute-done.4.refs_4_.refs_6_.refs_16_.refs_18_
  19.6 0.0 collective-permute-done.2.refs_2_.refs_5_.refs_14_.refs_29_.refs_42_
  19.6 0.0 copy-done
  19.6 0.0 copy-done.2
  19.6 0.0 copy-done.3
  19.6 0.0 copy-done.4
  19.6 0.6 %column_0.1 = (f32[1024,128]{1,0:T(8,128)S(1)}, f32[256,128]{1,0:T(8,128)S(1)}, f32[256,128]{1,0:T(8,128)S(1)}, f32[4,256,128]{2,1,0:T(8,128)S(1)}, f32[256,128]...) custom-call(s32[1]{0:T(128)S(6)} %copy.16.crop_ref, ...), custom_call_target="tpu_custom_call" | custom-call | flops 400000000 | bytes 1000000 | tf_op jit(solution)/shard_map/column_0/pallas_call | solution.py:431
  20.2 0.6 %column_1.1 = (f32[1024,128]{1,0:T(8,128)S(1)}, f32[256,128]{1,0:T(8,128)S(1)}, f32[256,128]{1,0:T(8,128)S(1)}, f32[4,256,128]{2,1,0:T(8,128)S(1)}, f32[256,128]...) custom-call(s32[1]{0:T(128)S(6)} %copy.16.crop_ref, bf16[6,128,128]{2,1,0:T(8,128)(2,1)S(1)} %copy-done, ...), custom_call_target="tpu_custom_call", output_to_operand_aliasing={{0}: (9, {})} | custom-call | flops 400000000 | bytes 1000000 | tf_op jit(solution)/shard_map/column_1/pallas_call | solution.py:431
  20.9 0.0 collective-permute-done.8.refs_3_.refs_27_.refs_40_
  20.9 0.0 collective-permute-done.6.refs_1_.refs_7_.refs_25_.refs_31_.refs_38_.refs_44_
  20.9 0.6 %column_2.1 = (f32[1024,128]{1,0:T(8,128)S(1)}, f32[256,128]{1,0:T(8,128)S(1)}, f32[256,128]{1,0:T(8,128)S(1)}, f32[4,256,128]{2,1,0:T(8,128)S(1)}, f32[256,128]...) custom-call(s32[1]{0:T(128)S(6)} %copy.16.crop_ref, ...), custom_call_target="tpu_custom_call", output_to_operand_aliasing={{0}: (10, {})} | custom-call | flops 400000000 | bytes 1000000 | tf_op jit(solution)/shard_map/column_2/pallas_call | solution.py:431
  21.6 0.6 %column_3.1 = (f32[1024,128]{1,0:T(8,128)S(1)}, f32[256,128]{1,0:T(8,128)S(1)}, f32[256,128]{1,0:T(8,128)S(1)}, f32[4,256,128]{2,1,0:T(8,128)S(1)}, f32[256,128]...) custom-call(s32[1]{0:T(128)S(6)} %copy.16.crop_ref, ...), custom_call_target="tpu_custom_call", output_to_operand_aliasing={{0}: (10, {})} | custom-call | flops 400000000 | bytes 1000000 | tf_op jit(solution)/shard_map/column_3/pallas_call | solution.py:431
  22.2 5.1 %rest.1 = (bf16[8,8,128]{2,1,0:T(8,128)(2,1)}, bf16[8,8,128]{2,1,0:T(8,128)(2,1)}, f32[6,128,128]{2,1,0:T(8,128)}) custom-call(bf16[6,128,128]{2,1,0:T(8,128)(2,1)S(1)} %copy-done, f32[2,64,128]{2,1,0:T(8,128)S(1)} %get-tuple-element.33.own_ref, f32[8,128]{1,0:T(8,128)S(1)} %get-tuple-element.34.gains_ref, f32[1024,128]{1,0:T(8,128)S(1)} %get-tuple-element.38.tri_ref, ...), custom_call_target="tpu_custom_call" | custom-call | tf_op jit(solution)/shard_map/rest/pallas_call | solution.py:453
  (2 shorter events, 0.0 us)
Async XLA Ops:
  2.2 17.3 %copy-start = (bf16[6,128,128]{2,1,0:T(8,128)(2,1)S(1)}, bf16[6,128,128]{2,1,0:T(8,128)(2,1)}, u32[]{:S(2)}) copy-start(bf16[6,128,128]{2,1,0:T(8,128)(2,1)} %weights_ref.9) | copy-start | bytes 589828
  2.2 1.6 %collective-permute-start = (bf16[144,128]{1,0:T(8,128)(2,1)}, bf16[144,128]{1,0:T(8,128)(2,1)S(1)}, u32[]{:S(2)}, u32[]{:S(2)}) collective-permute-start(bf16[144,128]{1,0:T(8,128)(2,1)} %pack.1.in_ref), channel_id=1, source_target_pairs={{0,1},{1,0},{2,3},{3,2},{4,5},{5,4},{6,7},{7,6},{8,9},{9,8},{10,11... | collective-permute-start | bytes 110600 | tf_op jit(solution)/shard_map/ppermute | solution.py:358
  2.8 0.8 %copy-start.1 = (bf16[144,128]{1,0:T(8,128)(2,1)S(1)}, bf16[144,128]{1,0:T(8,128)(2,1)}, u32[]{:S(2)}) copy-start(bf16[144,128]{1,0:T(8,128)(2,1)} %pack.1.in_ref) | copy-start | bytes 110596
  3.5 16.1 %copy-start.2 = (bf16[8,8,128]{2,1,0:T(8,128)(2,1)S(1)}, bf16[8,8,128]{2,1,0:T(8,128)(2,1)}, u32[]{:S(2)}) copy-start(bf16[8,8,128]{2,1,0:T(8,128)(2,1)} %refs_7_.1) | copy-start | bytes 49156
  3.9 12.1 %collective-permute-start.3 = (bf16[272,128]{1,0:T(8,128)(2,1)S(1)}, bf16[272,128]{1,0:T(8,128)(2,1)S(1)}, u32[]{:S(2)}, u32[]{:S(2)}) collective-permute-start(bf16[272,128]{1,0:T(8,128)(2,1)S(1)} %join.1.refs_0_.refs_12_), channel_id=1, source_target_pairs={{0,8},{1,13},{2,10},{3,15},{4,12},{5,9},{6,14},{7,11},{8,0},{9,5},... | collective-permute-start | bytes 208904 | tf_op jit(solution)/shard_map/ppermute | solution.py:358
  7.8 8.2 %collective-permute-start.1 = (bf16[272,128]{1,0:T(8,128)(2,1)S(1)}, bf16[272,128]{1,0:T(8,128)(2,1)S(1)}, u32[]{:S(2)}, u32[]{:S(2)}) collective-permute-start(bf16[272,128]{1,0:T(8,128)(2,1)S(1)} %join.1.refs_0_.refs_12_), channel_id=1, source_target_pairs={{0,10},{1,5},{2,8},{3,7},{4,14},{5,1},{6,12},{7,3},{8,2},{9,13},{1... | collective-permute-start | bytes 208904 | tf_op jit(solution)/shard_map/ppermute | solution.py:358
  9.0 8.1 %collective-permute-start.7 = (bf16[272,128]{1,0:T(8,128)(2,1)S(1)}, bf16[272,128]{1,0:T(8,128)(2,1)S(1)}, u32[]{:S(2)}, u32[]{:S(2)}) collective-permute-start(bf16[272,128]{1,0:T(8,128)(2,1)S(1)} %join.1.refs_0_.refs_12_), channel_id=1, source_target_pairs={{0,6},{2,4},{4,2},{6,0},{8,14},{10,12},{12,10},{14,8},{16,22},{18,... | collective-permute-start | bytes 208904 | tf_op jit(solution)/shard_map/ppermute | solution.py:358
  12.5 7.1 %collective-permute-start.5 = (bf16[272,128]{1,0:T(8,128)(2,1)S(1)}, bf16[272,128]{1,0:T(8,128)(2,1)S(1)}, u32[]{:S(2)}, u32[]{:S(2)}) collective-permute-start(bf16[272,128]{1,0:T(8,128)(2,1)S(1)} %join.1.refs_0_.refs_12_), channel_id=1, source_target_pairs={{0,14},{1,3},{2,12},{3,1},{4,10},{5,7},{6,8},{7,5},{8,6},{9,11},{1... | collective-permute-start | bytes 208904 | tf_op jit(solution)/shard_map/ppermute | solution.py:358
  16.0 3.6 %collective-permute-start.4 = (bf16[272,128]{1,0:T(8,128)(2,1)S(1)}, bf16[272,128]{1,0:T(8,128)(2,1)S(1)}, u32[]{:S(2)}, u32[]{:S(2)}) collective-permute-start(bf16[272,128]{1,0:T(8,128)(2,1)S(1)} %collective-permute-done.3.refs_3_.refs_5_.refs_15_.refs_17_), channel_id=1, source_target_pairs={{0,1},{1,0},{2,3},{3,2},{4,5},{5,4},{6,7},{7,6},{8,9},{9,8},{10,11... | collective-permute-start | bytes 208904 | tf_op jit(solution)/shard_map/ppermute | solution.py:358
  16.0 3.6 %collective-permute-start.2 = (bf16[272,128]{1,0:T(8,128)(2,1)S(1)}, bf16[272,128]{1,0:T(8,128)(2,1)S(1)}, u32[]{:S(2)}, u32[]{:S(2)}) collective-permute-start(bf16[272,128]{1,0:T(8,128)(2,1)S(1)} %collective-permute-done.1.refs_1_.refs_4_.refs_13_.refs_28_.refs_41_), channel_id=1, source_target_pairs={{0,1},{1,0},{2,3},{3,2},{4,5},{5,4},{6,7},{7,6},{8,9},{9,8},{10,11... | collective-permute-start | bytes 208904 | tf_op jit(solution)/shard_map/ppermute | solution.py:358
  17.1 2.5 %copy-start.3 = (f32[128]{0:T(128)S(1)}, f32[128]{0:T(128)}, u32[]{:S(2)}) copy-start(f32[128]{0:T(128)} %param.11) | copy-start | bytes 1540
  17.1 2.5 %copy-start.4 = (f32[128]{0:T(128)S(1)}, f32[128]{0:T(128)}, u32[]{:S(2)}) copy-start(f32[128]{0:T(128)} %param.12) | copy-start | bytes 1540
  17.2 3.7 %collective-permute-start.8 = (bf16[272,128]{1,0:T(8,128)(2,1)S(1)}, bf16[272,128]{1,0:T(8,128)(2,1)S(1)}, u32[]{:S(2)}, u32[]{:S(2)}) collective-permute-start(bf16[272,128]{1,0:T(8,128)(2,1)S(1)} %collective-permute-done.7.refs_2_.refs_26_.refs_39_), channel_id=1, source_target_pairs={{0,1},{2,3},{4,5},{6,7},{8,9},{10,11},{12,13},{14,15},{16,17},{18,... | collective-permute-start | bytes 208904 | tf_op jit(solution)/shard_map/ppermute | solution.py:358
  19.6 1.3 %collective-permute-start.6 = (bf16[272,128]{1,0:T(8,128)(2,1)S(1)}, bf16[272,128]{1,0:T(8,128)(2,1)S(1)}, u32[]{:S(2)}, u32[]{:S(2)}) collective-permute-start(bf16[272,128]{1,0:T(8,128)(2,1)S(1)} %collective-permute-done.5.refs_0_.refs_6_.refs_24_.refs_30_.refs_37_.refs_43_), channel_id=1, source_target_pairs={{0,1},{1,0},{2,3},{3,2},{4,5},{5,4},{6,7},{7,6},{8,9},{9,8},{10,11... | collective-permute-start | bytes 208904 | tf_op jit(solution)/shard_map/ppermute | solution.py:358

commit v12 on v11

--- a/solution.py
+++ b/solution.py
@@ -353,8 +353,7 @@
     for row in range(n_row):
         for col in range(n_col):
             shift = odd if col % 2 else even
-            if shift is not None:
-                pairs.append((row * n_col + col, (row ^ shift[0]) * n_col + (col ^ shift[1])))
+            pairs.append((row * n_col + col, (row ^ shift[0]) * n_col + (col ^ shift[1])))
     return lax.ppermute(block, ("row", "col"), pairs)
 
 
@@ -392,8 +391,8 @@
     def move(block, even, odd):
         return flip(block, n_row, n_col, even, odd)
 
-    def other(block, odd=(0, 1)):
-        return move(block, (0, 1), odd)
+    def other(block):
+        return move(block, (0, 1), (0, 1))
 
     held = pl.pallas_call(
         copy_kernel,
@@ -412,14 +411,13 @@
         out_specs=vmem,
         compiler_params=limit(2),
     )(held, other(own))
-    first = move(both, (2, 0), (3, 0))
-    second = move(both, (3, 2), (0, 2))
-    third = move(both, (2, 2), (1, 0))
-    fourth = move(both, (1, 2), None)
-    first, second, third = [(block, other(block)) for block in (first, second, third)]
-    fourth = fourth, other(fourth, None)
-    chips = (((1, None), (2, 1), (2, 0), (2, 1)), ((2, 1), (2, 0), (2, 0), (2, 0)))
-    sources = ((both, *third, *first, *first), (*second, *fourth, *third, *second))
+    straight = move(own, (3, 0), (3, 0))
+    first = move(both, (2, 0), (1, 0))
+    second = move(both, (0, 2), (2, 2))
+    third = move(both, (1, 2), (3, 2))
+    straight, first, second, third = [(block, other(block)) for block in (straight, first, second, third)]
+    chips = (((1, None), (2, 1), (2, 0), (2, None)), ((2, 0), (2, 0), (2, 1), (2, 1)))
+    sources = ((both, *first, *first, *straight), (*second, *third, *second, *third))
 
     tri, parts, extra = [], [], []
     for col in range(n_col):

time: 27.8 us -> 24.9 us (0.90)
  starting transfers between devices: 15.1 us -> 8.36 us
  waiting for transfers between devices: 0.73 us -> 4.71 us
    ppermute x9, starting transfers between devices: 15.1 us -> 8.36 us  [flip(): return lax.ppermute(block, ('row', 'col'), pairs)]
    ppermute x9, waiting for transfers between devices: 0.73 us -> 4.71 us  [flip(): return lax.ppermute(block, ('row', 'col'), pairs)]
    unnamed x10 -> x12, local copies, waits for them, and re-layouts: 0.79 us -> 0.79 us
  transfers between devices with their start and end apart: 9 -> 9, of which waited for: 2 -> 4; matrix products, arithmetic and copies ran while one was open for 0% -> 0% of each run, Pallas kernels for 5% -> 5%
where the time goes in v12:
time: 24.9 us; the launch traced here: 24.5 us
  Pallas kernels  9.28 us (37%)
  starting transfers between devices  8.36 us (34%)
  waiting for transfers between devices  4.71 us (19%)
  between operations  1.4 us (6%)
  local copies, waits for them, and re-layouts  0.79 us (3%)
    ppermute x9, starting transfers between devices, flip(): return lax.ppermute(block, ('row', 'col'), pairs)  8.36 us
    pallas_call x1, Pallas kernels, gathered_body(): pl.pallas_call(functools.partial(rest_kernel, n_row, n_col, chips), name=...  5.14 us
    ppermute x9, waiting for transfers between devices, flip(): return lax.ppermute(block, ('row', 'col'), pairs)  4.71 us
    pallas_call x4, Pallas kernels, gathered_body(): pl.pallas_call(functools.partial(column_kernel, n_row, n_col, col, chips[...  2.53 us
    pallas_call x1, Pallas kernels, gathered_body(): pl.pallas_call(pack_kernel, name='pack', out_shape=jax.ShapeDtypeStruct((...  1.6 us
    unnamed x12, local copies, waits for them, and re-layouts  0.79 us
  transfers between devices with their start and end apart: 9, of which 4 were waited for; matrix products, arithmetic and copies ran while one was open for 0% of the time, Pallas kernels for 5%

profile of v12, /device:TPU:0, one launch (start us, length us, event | category | flops | bytes accessed | tf_op | source)
XLA Modules:
  0.0 24.5 jit_solution(10689225176720493258)
XLA Ops:
  0.6 1.6 %pack.1.in_ref = bf16[144,128]{1,0:T(8,128)(2,1)} custom-call(bf16[8,8,128]{2,1,0:T(8,128)(2,1)} %refs_7_.1, s32[8,8]{1,0:T(8,128)} %mask_hbm.1, bf16[64,128]{1,0:T(8,128)(2,1)} %bitcast.6, f32[1,128]{1,0:T(1,128)} %bitcast.3), custom_call_target="tpu_custom_call" | custom-call | tf_op jit(solution)/shard_map/pack/pallas_call | solution.py:375
  2.2 0.0 copy-start
  2.2 0.5 %collective-permute-start = (bf16[144,128]{1,0:T(8,128)(2,1)}, bf16[144,128]{1,0:T(8,128)(2,1)S(1)}, u32[]{:S(2)}, u32[]{:S(2)}) collective-permute-start(bf16[144,128]{1,0:T(8,128)(2,1)} %pack.1.in_ref), channel_id=1, source_target_pairs={{0,1},{1,0},{2,3},{3,2},{4,5},{5,4},{6,7},{7,6},{8,9},{9,8},{10,11... | collective-permute-start | bytes 110600 | tf_op jit(solution)/shard_map/ppermute | solution.py:357
  2.8 0.0 copy-start.1
  2.8 0.8 %copy-done.1 = bf16[144,128]{1,0:T(8,128)(2,1)S(1)} copy-done((bf16[144,128]{1,0:T(8,128)(2,1)S(1)}, bf16[144,128]{1,0:T(8,128)(2,1)}, u32[]{:S(2)}) %copy-start.1) | copy-done | bytes 36888
  3.5 0.0 copy-start.2
  3.5 0.0 copy-start.3
  3.5 0.3 %collective-permute-done.twin_ref = bf16[144,128]{1,0:T(8,128)(2,1)S(1)} collective-permute-done((bf16[144,128]{1,0:T(8,128)(2,1)}, bf16[144,128]{1,0:T(8,128)(2,1)S(1)}, u32[]{:S(2)}, u32[]{:S(2)}) %collective-permute-start) | collective-permute-done | bytes 36896 | tf_op jit(solution)/shard_map/ppermute | solution.py:357
  3.9 3.9 %collective-permute-start.1 = (bf16[272,128]{1,0:T(8,128)(2,1)S(1)}, bf16[272,128]{1,0:T(8,128)(2,1)S(1)}, u32[]{:S(2)}, u32[]{:S(2)}) collective-permute-start(bf16[272,128]{1,0:T(8,128)(2,1)S(1)} %join.1.refs_0_.refs_12_), channel_id=1, source_target_pairs={{0,8},{1,5},{2,10},{3,7},{4,12},{5,1},{6,14},{7,3},{8,0},{9,13},{1... | collective-permute-start | bytes 208904 | tf_op jit(solution)/shard_map/ppermute | solution.py:357
  7.8 0.0 copy-done.2
  7.8 1.3 %collective-permute-start.3 = (bf16[144,128]{1,0:T(8,128)(2,1)S(1)}, bf16[144,128]{1,0:T(8,128)(2,1)S(1)}, u32[]{:S(2)}, u32[]{:S(2)}) collective-permute-start(bf16[144,128]{1,0:T(8,128)(2,1)S(1)} %copy-done.2), channel_id=1, source_target_pairs={{0,12},{1,13},{2,14},{3,15},{4,8},{5,9},{6,10},{7,11},{8,4},{9,5},... | collective-permute-start | bytes 110600 | tf_op jit(solution)/shard_map/ppermute | solution.py:357
  9.1 1.2 %collective-permute-start.7 = (bf16[272,128]{1,0:T(8,128)(2,1)S(1)}, bf16[272,128]{1,0:T(8,128)(2,1)S(1)}, u32[]{:S(2)}, u32[]{:S(2)}) collective-permute-start(bf16[272,128]{1,0:T(8,128)(2,1)S(1)} %join.1.refs_0_.refs_12_), channel_id=1, source_target_pairs={{0,6},{1,15},{2,4},{3,13},{4,2},{5,11},{6,0},{7,9},{8,14},{9,7},{1... | collective-permute-start | bytes 208904 | tf_op jit(solution)/shard_map/ppermute | solution.py:357
  10.3 0.5 %collective-permute-start.5 = (bf16[272,128]{1,0:T(8,128)(2,1)S(1)}, bf16[272,128]{1,0:T(8,128)(2,1)S(1)}, u32[]{:S(2)}, u32[]{:S(2)}) collective-permute-start(bf16[272,128]{1,0:T(8,128)(2,1)S(1)} %join.1.refs_0_.refs_12_), channel_id=1, source_target_pairs={{0,2},{1,11},{2,0},{3,9},{4,6},{5,15},{6,4},{7,13},{8,10},{9,3},{1... | collective-permute-start | bytes 208904 | tf_op jit(solution)/shard_map/ppermute | solution.py:357
  10.8 0.0 collective-permute-done.1.refs_1_.refs_3_.refs_13_.refs_15_
  10.8 0.5 %collective-permute-start.2 = (bf16[272,128]{1,0:T(8,128)(2,1)S(1)}, bf16[272,128]{1,0:T(8,128)(2,1)S(1)}, u32[]{:S(2)}, u32[]{:S(2)}) collective-permute-start(bf16[272,128]{1,0:T(8,128)(2,1)S(1)} %collective-permute-done.1.refs_1_.refs_3_.refs_13_.refs_15_), channel_id=1, source_target_pairs={{0,1},{1,0},{2,3},{3,2},{4,5},{5,4},{6,7},{7,6},{8,9},{9,8},{10,11... | collective-permute-start | bytes 208904 | tf_op jit(solution)/shard_map/ppermute | solution.py:357
  11.3 2.3 %collective-permute-done.3.refs_5_.refs_17_ = bf16[144,128]{1,0:T(8,128)(2,1)S(1)} collective-permute-done((bf16[144,128]{1,0:T(8,128)(2,1)S(1)}, bf16[144,128]{1,0:T(8,128)(2,1)S(1)}, u32[]{:S(2)}, u32[]{:S(2)}) %collective-permute-start.3) | collective-permute-done | bytes 36896 | tf_op jit(solution)/shard_map/ppermute | solution.py:357
  13.6 0.0 collective-permute-start.4
  14.3 0.0 copy-start.4
  14.3 0.0 copy-start.5
  14.3 1.4 %collective-permute-done.7.refs_2_.refs_6_.refs_26_.refs_30_.refs_39_.refs_43_ = bf16[272,128]{1,0:T(8,128)(2,1)S(1)} collective-permute-done((bf16[272,128]{1,0:T(8,128)(2,1)S(1)}, bf16[272,128]{1,0:T(8,128)(2,1)S(1)}, u32[]{:S(2)}, u32[]{:S(2)}) %collective-permute-start.7) | collective-permute-done | bytes 69664 | tf_op jit(solution)/shard_map/ppermute | solution.py:357
  15.8 0.0 collective-permute-start.8
  15.8 0.6 %collective-permute-done.5.refs_0_.refs_4_.refs_24_.refs_28_.refs_37_.refs_41_ = bf16[272,128]{1,0:T(8,128)(2,1)S(1)} collective-permute-done((bf16[272,128]{1,0:T(8,128)(2,1)S(1)}, bf16[272,128]{1,0:T(8,128)(2,1)S(1)}, u32[]{:S(2)}, u32[]{:S(2)}) %collective-permute-start.5) | collective-permute-done | bytes 69664 | tf_op jit(solution)/shard_map/ppermute | solution.py:357
  16.4 0.4 %collective-permute-start.6 = (bf16[272,128]{1,0:T(8,128)(2,1)S(1)}, bf16[272,128]{1,0:T(8,128)(2,1)S(1)}, u32[]{:S(2)}, u32[]{:S(2)}) collective-permute-start(bf16[272,128]{1,0:T(8,128)(2,1)S(1)} %collective-permute-done.5.refs_0_.refs_4_.refs_24_.refs_28_.refs_37_.refs_41_), channel_id=1, source_target_pairs={{0,1},{1,0},{2,3},{3,2},{4,5},{5,4},{6,7},{7,6},{8,9},{9,8},{10,11... | collective-permute-start | bytes 208904 | tf_op jit(solution)/shard_map/ppermute | solution.py:357
  16.8 0.0 collective-permute-done.4.refs_6_.refs_18_
  16.8 0.0 collective-permute-done.2.refs_2_.refs_4_.refs_14_.refs_16_
  16.8 0.0 copy-done
  16.8 0.0 copy-done.3
  16.8 0.0 copy-done.4
  16.8 0.0 copy-done.5
  16.8 0.6 %column_0.1 = (f32[1024,128]{1,0:T(8,128)S(1)}, f32[256,128]{1,0:T(8,128)S(1)}, f32[256,128]{1,0:T(8,128)S(1)}, f32[4,256,128]{2,1,0:T(8,128)S(1)}, f32[256,128]...) custom-call(s32[1]{0:T(128)S(6)} %copy.16.crop_ref, ...), custom_call_target="tpu_custom_call" | custom-call | flops 400000000 | bytes 1000000 | tf_op jit(solution)/shard_map/column_0/pallas_call | solution.py:429
  17.5 0.6 %column_1.1 = (f32[1024,128]{1,0:T(8,128)S(1)}, f32[256,128]{1,0:T(8,128)S(1)}, f32[256,128]{1,0:T(8,128)S(1)}, f32[4,256,128]{2,1,0:T(8,128)S(1)}, f32[256,128]...) custom-call(s32[1]{0:T(128)S(6)} %copy.16.crop_ref, bf16[6,128,128]{2,1,0:T(8,128)(2,1)S(1)} %copy-done, ...), custom_call_target="tpu_custom_call", output_to_operand_aliasing={{0}: (9, {})} | custom-call | flops 400000000 | bytes 1000000 | tf_op jit(solution)/shard_map/column_1/pallas_call | solution.py:429
  18.1 0.0 collective-permute-done.8.refs_3_.refs_7_.refs_27_.refs_31_.refs_40_.refs_44_
  18.1 0.0 collective-permute-done.6.refs_1_.refs_5_.refs_25_.refs_29_.refs_38_.refs_42_
  18.1 0.6 %column_2.1 = (f32[1024,128]{1,0:T(8,128)S(1)}, f32[256,128]{1,0:T(8,128)S(1)}, f32[256,128]{1,0:T(8,128)S(1)}, f32[4,256,128]{2,1,0:T(8,128)S(1)}, f32[256,128]...) custom-call(s32[1]{0:T(128)S(6)} %copy.16.crop_ref, ...), custom_call_target="tpu_custom_call", output_to_operand_aliasing={{0}: (10, {})} | custom-call | flops 400000000 | bytes 1000000 | tf_op jit(solution)/shard_map/column_2/pallas_call | solution.py:429
  18.8 0.6 %column_3.1 = (f32[1024,128]{1,0:T(8,128)S(1)}, f32[256,128]{1,0:T(8,128)S(1)}, f32[256,128]{1,0:T(8,128)S(1)}, f32[4,256,128]{2,1,0:T(8,128)S(1)}, f32[256,128]...) custom-call(s32[1]{0:T(128)S(6)} %copy.16.crop_ref, ...), custom_call_target="tpu_custom_call", output_to_operand_aliasing={{0}: (10, {})} | custom-call | flops 400000000 | bytes 1000000 | tf_op jit(solution)/shard_map/column_3/pallas_call | solution.py:429
  19.4 5.1 %rest.1 = (bf16[8,8,128]{2,1,0:T(8,128)(2,1)}, bf16[8,8,128]{2,1,0:T(8,128)(2,1)}, f32[6,128,128]{2,1,0:T(8,128)}) custom-call(bf16[6,128,128]{2,1,0:T(8,128)(2,1)S(1)} %copy-done, f32[2,64,128]{2,1,0:T(8,128)S(1)} %get-tuple-element.33.own_ref, f32[8,128]{1,0:T(8,128)S(1)} %get-tuple-element.34.gains_ref, f32[1024,128]{1,0:T(8,128)S(1)} %get-tuple-element.38.tri_ref, ...), custom_call_target="tpu_custom_call" | custom-call | tf_op jit(solution)/shard_map/rest/pallas_call | solution.py:451
  (2 shorter events, 0.0 us)
Async XLA Ops:
  2.2 14.6 %copy-start = (bf16[6,128,128]{2,1,0:T(8,128)(2,1)S(1)}, bf16[6,128,128]{2,1,0:T(8,128)(2,1)}, u32[]{:S(2)}) copy-start(bf16[6,128,128]{2,1,0:T(8,128)(2,1)} %weights_ref.9) | copy-start | bytes 589828
  2.2 1.6 %collective-permute-start = (bf16[144,128]{1,0:T(8,128)(2,1)}, bf16[144,128]{1,0:T(8,128)(2,1)S(1)}, u32[]{:S(2)}, u32[]{:S(2)}) collective-permute-start(bf16[144,128]{1,0:T(8,128)(2,1)} %pack.1.in_ref), channel_id=1, source_target_pairs={{0,1},{1,0},{2,3},{3,2},{4,5},{5,4},{6,7},{7,6},{8,9},{9,8},{10,11... | collective-permute-start | bytes 110600 | tf_op jit(solution)/shard_map/ppermute | solution.py:357
  2.8 0.8 %copy-start.1 = (bf16[144,128]{1,0:T(8,128)(2,1)S(1)}, bf16[144,128]{1,0:T(8,128)(2,1)}, u32[]{:S(2)}) copy-start(bf16[144,128]{1,0:T(8,128)(2,1)} %pack.1.in_ref) | copy-start | bytes 110596
  3.5 4.2 %copy-start.2 = (bf16[144,128]{1,0:T(8,128)(2,1)S(1)}, bf16[144,128]{1,0:T(8,128)(2,1)}, u32[]{:S(2)}) copy-start(bf16[144,128]{1,0:T(8,128)(2,1)} %pack.1.in_ref) | copy-start | bytes 110596
  3.5 13.3 %copy-start.3 = (bf16[8,8,128]{2,1,0:T(8,128)(2,1)S(1)}, bf16[8,8,128]{2,1,0:T(8,128)(2,1)}, u32[]{:S(2)}) copy-start(bf16[8,8,128]{2,1,0:T(8,128)(2,1)} %refs_7_.1) | copy-start | bytes 49156
  3.9 7.0 %collective-permute-start.1 = (bf16[272,128]{1,0:T(8,128)(2,1)S(1)}, bf16[272,128]{1,0:T(8,128)(2,1)S(1)}, u32[]{:S(2)}, u32[]{:S(2)}) collective-permute-start(bf16[272,128]{1,0:T(8,128)(2,1)S(1)} %join.1.refs_0_.refs_12_), channel_id=1, source_target_pairs={{0,8},{1,5},{2,10},{3,7},{4,12},{5,1},{6,14},{7,3},{8,0},{9,13},{1... | collective-permute-start | bytes 208904 | tf_op jit(solution)/shard_map/ppermute | solution.py:357
  7.8 5.9 %collective-permute-start.3 = (bf16[144,128]{1,0:T(8,128)(2,1)S(1)}, bf16[144,128]{1,0:T(8,128)(2,1)S(1)}, u32[]{:S(2)}, u32[]{:S(2)}) collective-permute-start(bf16[144,128]{1,0:T(8,128)(2,1)S(1)} %copy-done.2), channel_id=1, source_target_pairs={{0,12},{1,13},{2,14},{3,15},{4,8},{5,9},{6,10},{7,11},{8,4},{9,5},... | collective-permute-start | bytes 110600 | tf_op jit(solution)/shard_map/ppermute | solution.py:357
  9.1 6.6 %collective-permute-start.7 = (bf16[272,128]{1,0:T(8,128)(2,1)S(1)}, bf16[272,128]{1,0:T(8,128)(2,1)S(1)}, u32[]{:S(2)}, u32[]{:S(2)}) collective-permute-start(bf16[272,128]{1,0:T(8,128)(2,1)S(1)} %join.1.refs_0_.refs_12_), channel_id=1, source_target_pairs={{0,6},{1,15},{2,4},{3,13},{4,2},{5,11},{6,0},{7,9},{8,14},{9,7},{1... | collective-permute-start | bytes 208904 | tf_op jit(solution)/shard_map/ppermute | solution.py:357
  10.3 6.1 %collective-permute-start.5 = (bf16[272,128]{1,0:T(8,128)(2,1)S(1)}, bf16[272,128]{1,0:T(8,128)(2,1)S(1)}, u32[]{:S(2)}, u32[]{:S(2)}) collective-permute-start(bf16[272,128]{1,0:T(8,128)(2,1)S(1)} %join.1.refs_0_.refs_12_), channel_id=1, source_target_pairs={{0,2},{1,11},{2,0},{3,9},{4,6},{5,15},{6,4},{7,13},{8,10},{9,3},{1... | collective-permute-start | bytes 208904 | tf_op jit(solution)/shard_map/ppermute | solution.py:357
  10.8 6.0 %collective-permute-start.2 = (bf16[272,128]{1,0:T(8,128)(2,1)S(1)}, bf16[272,128]{1,0:T(8,128)(2,1)S(1)}, u32[]{:S(2)}, u32[]{:S(2)}) collective-permute-start(bf16[272,128]{1,0:T(8,128)(2,1)S(1)} %collective-permute-done.1.refs_1_.refs_3_.refs_13_.refs_15_), channel_id=1, source_target_pairs={{0,1},{1,0},{2,3},{3,2},{4,5},{5,4},{6,7},{7,6},{8,9},{9,8},{10,11... | collective-permute-start | bytes 208904 | tf_op jit(solution)/shard_map/ppermute | solution.py:357
  13.6 3.1 %collective-permute-start.4 = (bf16[144,128]{1,0:T(8,128)(2,1)S(1)}, bf16[144,128]{1,0:T(8,128)(2,1)S(1)}, u32[]{:S(2)}, u32[]{:S(2)}) collective-permute-start(bf16[144,128]{1,0:T(8,128)(2,1)S(1)} %collective-permute-done.3.refs_5_.refs_17_), channel_id=1, source_target_pairs={{0,1},{1,0},{2,3},{3,2},{4,5},{5,4},{6,7},{7,6},{8,9},{9,8},{10,11... | collective-permute-start | bytes 110600 | tf_op jit(solution)/shard_map/ppermute | solution.py:357
  14.3 2.5 %copy-start.4 = (f32[128]{0:T(128)S(1)}, f32[128]{0:T(128)}, u32[]{:S(2)}) copy-start(f32[128]{0:T(128)} %param.11) | copy-start | bytes 1540
  14.3 2.5 %copy-start.5 = (f32[128]{0:T(128)S(1)}, f32[128]{0:T(128)}, u32[]{:S(2)}) copy-start(f32[128]{0:T(128)} %param.12) | copy-start | bytes 1540
  15.8 2.3 %collective-permute-start.8 = (bf16[272,128]{1,0:T(8,128)(2,1)S(1)}, bf16[272,128]{1,0:T(8,128)(2,1)S(1)}, u32[]{:S(2)}, u32[]{:S(2)}) collective-permute-start(bf16[272,128]{1,0:T(8,128)(2,1)S(1)} %collective-permute-done.7.refs_2_.refs_6_.refs_26_.refs_30_.refs_39_.refs_43_), channel_id=1, source_target_pairs={{0,1},{1,0},{2,3},{3,2},{4,5},{5,4},{6,7},{7,6},{8,9},{9,8},{10,11... | collective-permute-start | bytes 208904 | tf_op jit(solution)/shard_map/ppermute | solution.py:357
  16.4 1.7 %collective-permute-start.6 = (bf16[272,128]{1,0:T(8,128)(2,1)S(1)}, bf16[272,128]{1,0:T(8,128)(2,1)S(1)}, u32[]{:S(2)}, u32[]{:S(2)}) collective-permute-start(bf16[272,128]{1,0:T(8,128)(2,1)S(1)} %collective-permute-done.5.refs_0_.refs_4_.refs_24_.refs_28_.refs_37_.refs_41_), channel_id=1, source_target_pairs={{0,1},{1,0},{2,3},{3,2},{4,5},{5,4},{6,7},{7,6},{8,9},{9,8},{10,11... | collective-permute-start | bytes 208904 | tf_op jit(solution)/shard_map/ppermute | solution.py:357

commit v13 on v12

--- a/solution.py
+++ b/solution.py
@@ -130,6 +130,11 @@
 
 def copy_kernel(in_ref, out_ref):
     out_ref[...] = in_ref[...]
+
+
+def pair_kernel(one_ref, two_ref, one_out, two_out):
+    one_out[...] = one_ref[...]
+    two_out[...] = two_ref[...]
 
 
 def join_kernel(own_ref, twin_ref, out_ref):
@@ -416,6 +421,15 @@
     second = move(both, (0, 2), (2, 2))
     third = move(both, (1, 2), (3, 2))
     straight, first, second, third = [(block, other(block)) for block in (straight, first, second, third)]
+    straight = pl.pallas_call(
+        pair_kernel,
+        name="pair",
+        out_shape=(jax.ShapeDtypeStruct(own.shape, bf16),) * 2,
+        in_specs=[vmem] * 2,
+        out_specs=(vmem, vmem),
+        compiler_params=limit(2),
+        cost_estimate=pl.CostEstimate(flops=1_000_000_000, bytes_accessed=1_000_000, transcendentals=0),
+    )(*straight)
     chips = (((1, None), (2, 1), (2, 0), (2, None)), ((2, 0), (2, 0), (2, 1), (2, 1)))
     sources = ((both, *first, *first, *straight), (*second, *third, *second, *third))
 

time: 24.9 us -> 29.2 us (1.17)
  starting transfers between devices: 8.36 us -> 13.9 us
  waiting for transfers between devices: 4.71 us -> 2.8 us
  local copies, waits for them, and re-layouts: 0.79 us -> 1.47 us
    ppermute x9, starting transfers between devices: 8.36 us -> 13.9 us  [flip(): return lax.ppermute(block, ('row', 'col'), pairs)]
    ppermute x9, waiting for transfers between devices: 4.71 us -> 2.8 us  [flip(): return lax.ppermute(block, ('row', 'col'), pairs)]
    unnamed x12 -> x10, local copies, waits for them, and re-layouts: 0.79 us -> 1.47 us
  transfers between devices with their start and end apart: 9 -> 9, of which waited for: 4 -> 3; matrix products, arithmetic and copies ran while one was open for 0% -> 0% of each run, Pallas kernels for 5% -> 4%
where the time goes in v13:
time: 29.2 us; the launch traced here: 28.8 us
  starting transfers between devices  13.9 us (48%)
  Pallas kernels  9.23 us (32%)
  waiting for transfers between devices  2.8 us (10%)
  local copies, waits for them, and re-layouts  1.47 us (5%)
  between operations  1.39 us (5%)
    ppermute x9, starting transfers between devices, flip(): return lax.ppermute(block, ('row', 'col'), pairs)  13.9 us
    pallas_call x1, Pallas kernels, gathered_body(): pl.pallas_call(functools.partial(rest_kernel, n_row, n_col, chips), name=...  5.1 us
    ppermute x9, waiting for transfers between devices, flip(): return lax.ppermute(block, ('row', 'col'), pairs)  2.8 us
    pallas_call x4, Pallas kernels, gathered_body(): pl.pallas_call(functools.partial(column_kernel, n_row, n_col, col, chips[...  2.51 us
    pallas_call x1, Pallas kernels, gathered_body(): pl.pallas_call(pack_kernel, name='pack', out_shape=jax.ShapeDtypeStruct((...  1.6 us
    unnamed x10, local copies, waits for them, and re-layouts  1.47 us
  transfers between devices with their start and end apart: 9, of which 3 were waited for; matrix products, arithmetic and copies ran while one was open for 0% of the time, Pallas kernels for 4%

profile of v13, /device:TPU:0, one launch (start us, length us, event | category | flops | bytes accessed | tf_op | source)
XLA Modules:
  0.0 28.8 jit_solution(6353740878811251200)
XLA Ops:
  0.6 1.6 %pack.1.in_ref = bf16[144,128]{1,0:T(8,128)(2,1)} custom-call(bf16[8,8,128]{2,1,0:T(8,128)(2,1)} %refs_7_.1, s32[8,8]{1,0:T(8,128)} %mask_hbm.1, bf16[64,128]{1,0:T(8,128)(2,1)} %bitcast.6, f32[1,128]{1,0:T(1,128)} %bitcast.3), custom_call_target="tpu_custom_call" | custom-call | tf_op jit(solution)/shard_map/pack/pallas_call | solution.py:380
  2.2 0.5 %collective-permute-start = (bf16[144,128]{1,0:T(8,128)(2,1)}, bf16[144,128]{1,0:T(8,128)(2,1)S(1)}, u32[]{:S(2)}, u32[]{:S(2)}) collective-permute-start(bf16[144,128]{1,0:T(8,128)(2,1)} %pack.1.in_ref), channel_id=1, source_target_pairs={{0,1},{1,0},{2,3},{3,2},{4,5},{5,4},{6,7},{7,6},{8,9},{9,8},{10,11... | collective-permute-start | bytes 110600 | tf_op jit(solution)/shard_map/ppermute | solution.py:362
  2.8 4.7 %collective-permute-start.3 = (bf16[144,128]{1,0:T(8,128)(2,1)}, bf16[144,128]{1,0:T(8,128)(2,1)S(1)}, u32[]{:S(2)}, u32[]{:S(2)}) collective-permute-start(bf16[144,128]{1,0:T(8,128)(2,1)} %pack.1.in_ref), channel_id=1, source_target_pairs={{0,12},{1,13},{2,14},{3,15},{4,8},{5,9},{6,10},{7,11},{8,4},{9,5},... | collective-permute-start | bytes 110600 | tf_op jit(solution)/shard_map/ppermute | solution.py:362
  7.4 0.0 copy-start.1
  7.4 0.8 %copy-done.1 = bf16[144,128]{1,0:T(8,128)(2,1)S(1)} copy-done((bf16[144,128]{1,0:T(8,128)(2,1)S(1)}, bf16[144,128]{1,0:T(8,128)(2,1)}, u32[]{:S(2)}) %copy-start.1) | copy-done | bytes 36888
  8.2 0.0 collective-permute-done.twin_ref
  8.2 0.1 collective-permute-start.1
  8.3 1.5 %collective-permute-done.3.one_ref = bf16[144,128]{1,0:T(8,128)(2,1)S(1)} collective-permute-done((bf16[144,128]{1,0:T(8,128)(2,1)}, bf16[144,128]{1,0:T(8,128)(2,1)S(1)}, u32[]{:S(2)}, u32[]{:S(2)}) %collective-permute-start.3) | collective-permute-done | bytes 36896 | tf_op jit(solution)/shard_map/ppermute | solution.py:362
  9.8 0.0 collective-permute-start.4
  10.5 0.0 copy-start
  10.5 0.0 copy-start.2
  10.5 1.4 %collective-permute-start.7 = (bf16[272,128]{1,0:T(8,128)(2,1)S(1)}, bf16[272,128]{1,0:T(8,128)(2,1)S(1)}, u32[]{:S(2)}, u32[]{:S(2)}) collective-permute-start(bf16[272,128]{1,0:T(8,128)(2,1)S(1)} %join.1.refs_0_.refs_12_), channel_id=1, source_target_pairs={{0,6},{1,15},{2,4},{3,13},{4,2},{5,11},{6,0},{7,9},{8,14},{9,7},{1... | collective-permute-start | bytes 208904 | tf_op jit(solution)/shard_map/ppermute | solution.py:362
  11.9 0.5 %collective-permute-start.5 = (bf16[272,128]{1,0:T(8,128)(2,1)S(1)}, bf16[272,128]{1,0:T(8,128)(2,1)S(1)}, u32[]{:S(2)}, u32[]{:S(2)}) collective-permute-start(bf16[272,128]{1,0:T(8,128)(2,1)S(1)} %join.1.refs_0_.refs_12_), channel_id=1, source_target_pairs={{0,2},{1,11},{2,0},{3,9},{4,6},{5,15},{6,4},{7,13},{8,10},{9,3},{1... | collective-permute-start | bytes 208904 | tf_op jit(solution)/shard_map/ppermute | solution.py:362
  12.4 1.1 %collective-permute-done.1.refs_1_.refs_3_.refs_13_.refs_15_ = bf16[272,128]{1,0:T(8,128)(2,1)S(1)} collective-permute-done((bf16[272,128]{1,0:T(8,128)(2,1)S(1)}, bf16[272,128]{1,0:T(8,128)(2,1)S(1)}, u32[]{:S(2)}, u32[]{:S(2)}) %collective-permute-start.1) | collective-permute-done | bytes 69664 | tf_op jit(solution)/shard_map/ppermute | solution.py:362
  13.5 2.0 %collective-permute-start.2 = (bf16[272,128]{1,0:T(8,128)(2,1)S(1)}, bf16[272,128]{1,0:T(8,128)(2,1)S(1)}, u32[]{:S(2)}, u32[]{:S(2)}) collective-permute-start(bf16[272,128]{1,0:T(8,128)(2,1)S(1)} %collective-permute-done.1.refs_1_.refs_3_.refs_13_.refs_15_), channel_id=1, source_target_pairs={{0,1},{1,0},{2,3},{3,2},{4,5},{5,4},{6,7},{7,6},{8,9},{9,8},{10,11... | collective-permute-start | bytes 208904 | tf_op jit(solution)/shard_map/ppermute | solution.py:362
  15.5 0.0 collective-permute-done.4.two_ref
  15.6 0.2 collective-permute-done.7.refs_2_.refs_6_.refs_26_.refs_30_.refs_39_.refs_43_
  15.8 2.0 %collective-permute-start.8 = (bf16[272,128]{1,0:T(8,128)(2,1)S(1)}, bf16[272,128]{1,0:T(8,128)(2,1)S(1)}, u32[]{:S(2)}, u32[]{:S(2)}) collective-permute-start(bf16[272,128]{1,0:T(8,128)(2,1)S(1)} %collective-permute-done.7.refs_2_.refs_6_.refs_26_.refs_30_.refs_39_.refs_43_), channel_id=1, source_target_pairs={{0,1},{1,0},{2,3},{3,2},{4,5},{5,4},{6,7},{7,6},{8,9},{9,8},{10,11... | collective-permute-start | bytes 208904 | tf_op jit(solution)/shard_map/ppermute | solution.py:362
  17.8 0.0 collective-permute-done.5.refs_0_.refs_4_.refs_24_.refs_28_.refs_37_.refs_41_
  17.8 2.7 %collective-permute-start.6 = (bf16[272,128]{1,0:T(8,128)(2,1)S(1)}, bf16[272,128]{1,0:T(8,128)(2,1)S(1)}, u32[]{:S(2)}, u32[]{:S(2)}) collective-permute-start(bf16[272,128]{1,0:T(8,128)(2,1)S(1)} %collective-permute-done.5.refs_0_.refs_4_.refs_24_.refs_28_.refs_37_.refs_41_), channel_id=1, source_target_pairs={{0,1},{1,0},{2,3},{3,2},{4,5},{5,4},{6,7},{7,6},{8,9},{9,8},{10,11... | collective-permute-start | bytes 208904 | tf_op jit(solution)/shard_map/ppermute | solution.py:362
  20.5 0.0 collective-permute-done.2.refs_2_.refs_4_.refs_14_.refs_16_
  20.5 0.0 copy-start.3
  20.5 0.0 copy-start.4
  20.5 0.0 copy-done
  20.5 0.0 copy-done.2
  20.5 0.6 %copy-done.3 = f32[128]{0:T(128)S(1)} copy-done((f32[128]{0:T(128)S(1)}, f32[128]{0:T(128)}, u32[]{:S(2)}) %copy-start.3) | copy-done | bytes 536
  21.2 0.0 copy-done.4
  21.2 0.6 %column_0.1 = (f32[1024,128]{1,0:T(8,128)S(1)}, f32[256,128]{1,0:T(8,128)S(1)}, f32[256,128]{1,0:T(8,128)S(1)}, f32[4,256,128]{2,1,0:T(8,128)S(1)}, f32[256,128]...) custom-call(s32[1]{0:T(128)S(6)} %copy.16.crop_ref, ...), custom_call_target="tpu_custom_call" | custom-call | flops 400000000 | bytes 1000000 | tf_op jit(solution)/shard_map/column_0/pallas_call | solution.py:443
  21.8 0.6 %column_1.1 = (f32[1024,128]{1,0:T(8,128)S(1)}, f32[256,128]{1,0:T(8,128)S(1)}, f32[256,128]{1,0:T(8,128)S(1)}, f32[4,256,128]{2,1,0:T(8,128)S(1)}, f32[256,128]...) custom-call(s32[1]{0:T(128)S(6)} %copy.16.crop_ref, bf16[6,128,128]{2,1,0:T(8,128)(2,1)S(1)} %copy-done, ...), custom_call_target="tpu_custom_call", output_to_operand_aliasing={{0}: (9, {})} | custom-call | flops 400000000 | bytes 1000000 | tf_op jit(solution)/shard_map/column_1/pallas_call | solution.py:443
  22.4 0.0 collective-permute-done.8.refs_3_.refs_7_.refs_27_.refs_31_.refs_40_.refs_44_
  22.4 0.0 collective-permute-done.6.refs_1_.refs_5_.refs_25_.refs_29_.refs_38_.refs_42_
  22.4 0.6 %column_2.1 = (f32[1024,128]{1,0:T(8,128)S(1)}, f32[256,128]{1,0:T(8,128)S(1)}, f32[256,128]{1,0:T(8,128)S(1)}, f32[4,256,128]{2,1,0:T(8,128)S(1)}, f32[256,128]...) custom-call(s32[1]{0:T(128)S(6)} %copy.16.crop_ref, ...), custom_call_target="tpu_custom_call", output_to_operand_aliasing={{0}: (10, {})} | custom-call | flops 400000000 | bytes 1000000 | tf_op jit(solution)/shard_map/column_2/pallas_call | solution.py:443
  23.1 0.6 %column_3.1 = (f32[1024,128]{1,0:T(8,128)S(1)}, f32[256,128]{1,0:T(8,128)S(1)}, f32[256,128]{1,0:T(8,128)S(1)}, f32[4,256,128]{2,1,0:T(8,128)S(1)}, f32[256,128]...) custom-call(s32[1]{0:T(128)S(6)} %copy.16.crop_ref, ...), custom_call_target="tpu_custom_call", output_to_operand_aliasing={{0}: (10, {})} | custom-call | flops 400000000 | bytes 1000000 | tf_op jit(solution)/shard_map/column_3/pallas_call | solution.py:443
  23.7 5.1 %rest.1 = (bf16[8,8,128]{2,1,0:T(8,128)(2,1)}, bf16[8,8,128]{2,1,0:T(8,128)(2,1)}, f32[6,128,128]{2,1,0:T(8,128)}) custom-call(bf16[6,128,128]{2,1,0:T(8,128)(2,1)S(1)} %copy-done, f32[2,64,128]{2,1,0:T(8,128)S(1)} %get-tuple-element.37.own_ref, f32[8,128]{1,0:T(8,128)S(1)} %get-tuple-element.38.gains_ref, f32[1024,128]{1,0:T(8,128)S(1)} %get-tuple-element.42.tri_ref, ...), custom_call_target="tpu_custom_call" | custom-call | tf_op jit(solution)/shard_map/rest/pallas_call | solution.py:465
  (3 shorter events, 0.0 us)
Async XLA Ops:
  2.2 6.0 %collective-permute-start = (bf16[144,128]{1,0:T(8,128)(2,1)}, bf16[144,128]{1,0:T(8,128)(2,1)S(1)}, u32[]{:S(2)}, u32[]{:S(2)}) collective-permute-start(bf16[144,128]{1,0:T(8,128)(2,1)} %pack.1.in_ref), channel_id=1, source_target_pairs={{0,1},{1,0},{2,3},{3,2},{4,5},{5,4},{6,7},{7,6},{8,9},{9,8},{10,11... | collective-permute-start | bytes 110600 | tf_op jit(solution)/shard_map/ppermute | solution.py:362
  2.8 7.0 %collective-permute-start.3 = (bf16[144,128]{1,0:T(8,128)(2,1)}, bf16[144,128]{1,0:T(8,128)(2,1)S(1)}, u32[]{:S(2)}, u32[]{:S(2)}) collective-permute-start(bf16[144,128]{1,0:T(8,128)(2,1)} %pack.1.in_ref), channel_id=1, source_target_pairs={{0,12},{1,13},{2,14},{3,15},{4,8},{5,9},{6,10},{7,11},{8,4},{9,5},... | collective-permute-start | bytes 110600 | tf_op jit(solution)/shard_map/ppermute | solution.py:362
  7.4 0.8 %copy-start.1 = (bf16[144,128]{1,0:T(8,128)(2,1)S(1)}, bf16[144,128]{1,0:T(8,128)(2,1)}, u32[]{:S(2)}) copy-start(bf16[144,128]{1,0:T(8,128)(2,1)} %pack.1.in_ref) | copy-start | bytes 110596
  8.2 5.3 %collective-permute-start.1 = (bf16[272,128]{1,0:T(8,128)(2,1)S(1)}, bf16[272,128]{1,0:T(8,128)(2,1)S(1)}, u32[]{:S(2)}, u32[]{:S(2)}) collective-permute-start(bf16[272,128]{1,0:T(8,128)(2,1)S(1)} %join.1.refs_0_.refs_12_), channel_id=1, source_target_pairs={{0,8},{1,5},{2,10},{3,7},{4,12},{5,1},{6,14},{7,3},{8,0},{9,13},{1... | collective-permute-start | bytes 208904 | tf_op jit(solution)/shard_map/ppermute | solution.py:362
  9.8 5.7 %collective-permute-start.4 = (bf16[144,128]{1,0:T(8,128)(2,1)S(1)}, bf16[144,128]{1,0:T(8,128)(2,1)S(1)}, u32[]{:S(2)}, u32[]{:S(2)}) collective-permute-start(bf16[144,128]{1,0:T(8,128)(2,1)S(1)} %collective-permute-done.3.one_ref), channel_id=1, source_target_pairs={{0,1},{1,0},{2,3},{3,2},{4,5},{5,4},{6,7},{7,6},{8,9},{9,8},{10,11... | collective-permute-start | bytes 110600 | tf_op jit(solution)/shard_map/ppermute | solution.py:362
  10.5 10.0 %copy-start = (bf16[6,128,128]{2,1,0:T(8,128)(2,1)S(1)}, bf16[6,128,128]{2,1,0:T(8,128)(2,1)}, u32[]{:S(2)}) copy-start(bf16[6,128,128]{2,1,0:T(8,128)(2,1)} %weights_ref.9) | copy-start | bytes 589828
  10.5 10.0 %copy-start.2 = (bf16[8,8,128]{2,1,0:T(8,128)(2,1)S(1)}, bf16[8,8,128]{2,1,0:T(8,128)(2,1)}, u32[]{:S(2)}) copy-start(bf16[8,8,128]{2,1,0:T(8,128)(2,1)} %refs_7_.1) | copy-start | bytes 49156
  10.5 5.3 %collective-permute-start.7 = (bf16[272,128]{1,0:T(8,128)(2,1)S(1)}, bf16[272,128]{1,0:T(8,128)(2,1)S(1)}, u32[]{:S(2)}, u32[]{:S(2)}) collective-permute-start(bf16[272,128]{1,0:T(8,128)(2,1)S(1)} %join.1.refs_0_.refs_12_), channel_id=1, source_target_pairs={{0,6},{1,15},{2,4},{3,13},{4,2},{5,11},{6,0},{7,9},{8,14},{9,7},{1... | collective-permute-start | bytes 208904 | tf_op jit(solution)/shard_map/ppermute | solution.py:362
  11.9 5.9 %collective-permute-start.5 = (bf16[272,128]{1,0:T(8,128)(2,1)S(1)}, bf16[272,128]{1,0:T(8,128)(2,1)S(1)}, u32[]{:S(2)}, u32[]{:S(2)}) collective-permute-start(bf16[272,128]{1,0:T(8,128)(2,1)S(1)} %join.1.refs_0_.refs_12_), channel_id=1, source_target_pairs={{0,2},{1,11},{2,0},{3,9},{4,6},{5,15},{6,4},{7,13},{8,10},{9,3},{1... | collective-permute-start | bytes 208904 | tf_op jit(solution)/shard_map/ppermute | solution.py:362
  13.5 7.0 %collective-permute-start.2 = (bf16[272,128]{1,0:T(8,128)(2,1)S(1)}, bf16[272,128]{1,0:T(8,128)(2,1)S(1)}, u32[]{:S(2)}, u32[]{:S(2)}) collective-permute-start(bf16[272,128]{1,0:T(8,128)(2,1)S(1)} %collective-permute-done.1.refs_1_.refs_3_.refs_13_.refs_15_), channel_id=1, source_target_pairs={{0,1},{1,0},{2,3},{3,2},{4,5},{5,4},{6,7},{7,6},{8,9},{9,8},{10,11... | collective-permute-start | bytes 208904 | tf_op jit(solution)/shard_map/ppermute | solution.py:362
  15.8 6.6 %collective-permute-start.8 = (bf16[272,128]{1,0:T(8,128)(2,1)S(1)}, bf16[272,128]{1,0:T(8,128)(2,1)S(1)}, u32[]{:S(2)}, u32[]{:S(2)}) collective-permute-start(bf16[272,128]{1,0:T(8,128)(2,1)S(1)} %collective-permute-done.7.refs_2_.refs_6_.refs_26_.refs_30_.refs_39_.refs_43_), channel_id=1, source_target_pairs={{0,1},{1,0},{2,3},{3,2},{4,5},{5,4},{6,7},{7,6},{8,9},{9,8},{10,11... | collective-permute-start | bytes 208904 | tf_op jit(solution)/shard_map/ppermute | solution.py:362
  17.8 4.6 %collective-permute-start.6 = (bf16[272,128]{1,0:T(8,128)(2,1)S(1)}, bf16[272,128]{1,0:T(8,128)(2,1)S(1)}, u32[]{:S(2)}, u32[]{:S(2)}) collective-permute-start(bf16[272,128]{1,0:T(8,128)(2,1)S(1)} %collective-permute-done.5.refs_0_.refs_4_.refs_24_.refs_28_.refs_37_.refs_41_), channel_id=1, source_target_pairs={{0,1},{1,0},{2,3},{3,2},{4,5},{5,4},{6,7},{7,6},{8,9},{9,8},{10,11... | collective-permute-start | bytes 208904 | tf_op jit(solution)/shard_map/ppermute | solution.py:362
  20.5 0.7 %copy-start.3 = (f32[128]{0:T(128)S(1)}, f32[128]{0:T(128)}, u32[]{:S(2)}) copy-start(f32[128]{0:T(128)} %param.11) | copy-start | bytes 1540
  20.5 0.7 %copy-start.4 = (f32[128]{0:T(128)S(1)}, f32[128]{0:T(128)}, u32[]{:S(2)}) copy-start(f32[128]{0:T(128)} %param.12) | copy-start | bytes 1540

commit v14 on v12

--- a/solution.py
+++ b/solution.py
@@ -207,6 +207,7 @@
 def column_kernel(n_row, n_col, col, chips, crop_ref, weights_ref, *refs):
     count = sum(width for width, _ in chips)
     chip_refs, refs = refs[:count], refs[count:]
+    own_ref = None
     if col == 0:
         act_ref, in_gain_ref, out_gain_ref, *refs, own_ref, gains_ref = refs
         z_hat, z_inverse = normalize(act_ref[...].astype(jnp.float32).reshape(own_ref.shape[1:]))
@@ -214,7 +215,9 @@
         own_ref[1] = jnp.broadcast_to(z_inverse, z_hat.shape)
         gains_ref[0:1] = in_gain_ref[...]
         gains_ref[1:2] = out_gain_ref[...]
-    tri_in, (tri_ref, left_ref, right_ref, side_ref, gate_ref, flip_ref) = refs[:-6], refs[-6:]
+    else:
+        gains_ref, *refs = refs
+    tri_in, (tri_ref, left_ref, right_ref, side_ref, back_ref, flip_ref) = refs[:-6], refs[-6:]
     channels = weights_ref.shape[-1]
     tile = SUB * SUB
     size = n_row * tile
@@ -222,7 +225,7 @@
     row_me, col_me = lax.axis_index("row"), lax.axis_index("col")
     chip_list = split_chips(chip_refs, chips)
     normed = jnp.concatenate([chip_rows(normed_rows, chip, col % 2, on) for chip, on in chip_list], axis=0)
-    flip_ref[...] = normed.astype(f32).T.astype(bf16)
+    flip_ref[0] = normed.astype(f32).T.astype(bf16)
     crop = crop_ref[0]
     col_offset = lax.broadcasted_iota(jnp.int32, (SUB, channels), 0)
     row_offset = lax.broadcasted_iota(jnp.int32, (SUB, channels), 1)
@@ -243,7 +246,17 @@
         act_ref[...] = act.astype(bf16).astype(f32)
         side_ref[2 * side] = masked
         side_ref[2 * side + 1] = act * (1.0 - gate)
-    gate_ref[...] = jax.nn.sigmoid(jnp.dot(normed, weights_ref[4], preferred_element_type=f32))
+    out_gate = jax.nn.sigmoid(jnp.dot(normed, weights_ref[4], preferred_element_type=f32))
+    if own_ref is not None:
+        own_ref[2] = out_gate[0:tile]
+    cot = jnp.concatenate([chip_rows(cot_rows, chip, col % 2, on) for chip, on in chip_list], axis=0)
+    grad = cot.astype(f32) * out_gate
+    grad_lin = grad.astype(bf16)
+    flip_ref[1] = grad_lin.astype(f32).T.astype(bf16)
+    back_ref[0] = grad * (1.0 - out_gate)
+    back = lax.dot_general(grad_lin, weights_ref[5], (((1,), (1,)), ((), ())), preferred_element_type=f32)
+    back = back * gains_ref[1:2]
+    back_ref[1] = back - jnp.mean(back, axis=-1, keepdims=True)
     turn = row_me ^ col_me
 
     def flipped(q):
@@ -265,14 +278,9 @@
     triangle(n_row, n_col, 1, flipped, along, start, store)
 
 
-def rest_kernel(n_row, n_col, chips, weights_ref, own_ref, gains_ref, tri_ref, *refs):
-    chip_lists, columns = [], []
-    for col in range(n_col):
-        count = sum(width for width, _ in chips[col // 2])
-        chip_lists.append(split_chips(refs[:count], chips[col // 2]))
-        columns.append(refs[count : count + 5])
-        refs = refs[count + 5 :]
-    update_ref, pair_grad_ref, weight_grad_ref, back_ref, hat_ref, lin_ref, d_ref = refs
+def rest_kernel(n_row, n_col, weights_ref, own_ref, gains_ref, tri_ref, *refs):
+    columns = [refs[at * 5 : at * 5 + 5] for at in range(n_col)]
+    update_ref, pair_grad_ref, weight_grad_ref, back_ref, hat_ref, d_ref = refs[5 * n_col :]
     channels = tri_ref.shape[-1]
     tile = SUB * SUB
     size = n_row * tile
@@ -280,23 +288,18 @@
     bf16, f32 = jnp.bfloat16, jnp.float32
     turn = lax.axis_index("row") ^ lax.axis_index("col")
     out_gain = gains_ref[1:2]
-    for col, (_, _, _, gate_ref, _) in enumerate(columns):
+    for col, (_, _, _, backs_ref, _) in enumerate(columns):
         rows = slice(col * size, (col + 1) * size)
         x_hat, inverse = normalize(tri_ref[rows, :])
         normed_out = (x_hat * out_gain).astype(bf16)
         hat_ref[rows, :] = normed_out
         lin = jnp.dot(normed_out, weights_ref[5], preferred_element_type=f32)
-        out_gate = gate_ref[...]
         if col == 0:
-            update_ref[...] = (out_gate[0:tile] * lin[0:tile]).astype(bf16).reshape(update_ref.shape)
-        cots = [chip_rows(cot_rows, chip, col % 2, on) for chip, on in chip_lists[col]]
-        cot = jnp.concatenate(cots, axis=0).astype(f32)
-        grad = cot * out_gate
-        grad_lin = grad.astype(bf16)
-        lin_ref[rows, :] = grad_lin
-        d_ref[rows, 4 * channels : 5 * channels] = (grad * lin * (1.0 - out_gate)).astype(bf16)
-        back = lax.dot_general(grad_lin, weights_ref[5], (((1,), (1,)), ((), ())), preferred_element_type=f32)
-        back_ref[rows, :] = norm_back(back * out_gain, x_hat, inverse).astype(bf16).astype(f32)
+            update_ref[...] = (own_ref[2] * lin[0:tile]).astype(bf16).reshape(update_ref.shape)
+        d_ref[rows, 4 * channels : 5 * channels] = (backs_ref[0] * lin).astype(bf16)
+        back = backs_ref[1]
+        second = jnp.mean(back * x_hat, axis=-1, keepdims=True)
+        back_ref[rows, :] = ((back - x_hat * second) * inverse).astype(bf16).astype(f32)
 
     lefts, rights, sides = [[column[at] for column in columns] for at in (0, 1, 2)]
 
@@ -331,13 +334,11 @@
     triangle(n_row, n_col, n_row, by_left, down, zero, store(1))
 
     scale = 1.0 / residues
-    flipped = jnp.concatenate([column[4][...] for column in columns], axis=1)
+    flipped, lin_flipped = [jnp.concatenate([column[4][at] for column in columns], axis=1) for at in range(2)]
     sums = jnp.dot(flipped, d_ref[...], preferred_element_type=f32) * scale
     for s in range(5):
         weight_grad_ref[s] = sums[:, s * channels : (s + 1) * channels]
-    weight_grad_ref[5] = scale * lax.dot_general(
-        hat_ref[...], lin_ref[...], (((0,), (0,)), ((), ())), preferred_element_type=f32
-    )
+    weight_grad_ref[5] = jnp.dot(lin_flipped, hat_ref[...], preferred_element_type=f32).T * scale
     total = jnp.zeros((tile, channels), f32)
     for s in range(5):
         total = total + lax.dot_general(
@@ -421,9 +422,9 @@
 
     tri, parts, extra = [], [], []
     for col in range(n_col):
-        more = (pair_act, in_gain, out_gain) if col == 0 else tri
+        more = (pair_act, in_gain, out_gain) if col == 0 else (extra[1], *tri)
         more_shapes = () if col > 0 else (
-            jax.ShapeDtypeStruct((2, tile, channels), f32),
+            jax.ShapeDtypeStruct((3, tile, channels), f32),
             jax.ShapeDtypeStruct((SUB, channels), f32),
         )
         tri, *results = pl.pallas_call(
@@ -434,22 +435,22 @@
                 jax.ShapeDtypeStruct((size, channels), f32),
                 jax.ShapeDtypeStruct((size, channels), f32),
                 jax.ShapeDtypeStruct((4, size, channels), f32),
-                jax.ShapeDtypeStruct((size, channels), f32),
-                jax.ShapeDtypeStruct((channels, size), bf16),
+                jax.ShapeDtypeStruct((2, size, channels), f32),
+                jax.ShapeDtypeStruct((2, channels, size), bf16),
                 *more_shapes,
             ),
             in_specs=[smem] + [vmem] * (1 + len(sources[col // 2]) + len(more)),
             out_specs=(vmem,) * (6 + len(more_shapes)),
-            input_output_aliases={2 + len(sources[col // 2]): 0} if col > 0 else {},
+            input_output_aliases={3 + len(sources[col // 2]): 0} if col > 0 else {},
             compiler_params=limit(8),
             cost_estimate=pl.CostEstimate(flops=400_000_000, bytes_accessed=1_000_000, transcendentals=0),
         )(crop_length, weights, *sources[col // 2], *more)
         tri = [tri]
-        parts += [*sources[col // 2], *results[:5]]
+        parts += results[:5]
         extra += results[5:]
 
     return pl.pallas_call(
-        functools.partial(rest_kernel, n_row, n_col, chips),
+        functools.partial(rest_kernel, n_row, n_col),
         name="rest",
         out_shape=(
             jax.ShapeDtypeStruct(pair_act.shape, bf16),
@@ -460,7 +461,6 @@
         out_specs=(vmem, vmem, vmem),
         scratch_shapes=[
             pltpu.VMEM((pairs, channels), f32),
-            pltpu.VMEM((pairs, channels), bf16),
             pltpu.VMEM((pairs, channels), bf16),
             pltpu.VMEM((pairs, 5 * channels), bf16),
         ],

time: 24.9 us -> 25.4 us (1.020)
  Pallas kernels: 9.28 us -> 9.8 us
    pallas_call x4, Pallas kernels: 2.53 us -> 3.38 us  [gathered_body(): pl.pallas_call(functools.partial(column_kernel, n_row, n_col, col, chips[...]
    pallas_call x1, Pallas kernels: 5.14 us -> 4.81 us  [gathered_body(): pl.pallas_call(functools.partial(rest_kernel, n_row, n_col), name='rest',...]
    unnamed x12 -> x10, local copies, waits for them, and re-layouts: 0.79 us -> 0.79 us
  transfers between devices with their start and end apart: 9 -> 9, of which waited for: 4 -> 4; matrix products, arithmetic and copies ran while one was open for 0% -> 0% of each run, Pallas kernels for 5% -> 7%
where the time goes in v14:
time: 25.4 us; the launch traced here: 25 us
  Pallas kernels  9.8 us (39%)
  starting transfers between devices  8.29 us (33%)
  waiting for transfers between devices  4.76 us (19%)
  between operations  1.4 us (6%)
  local copies, waits for them, and re-layouts  0.79 us (3%)
    ppermute x9, starting transfers between devices, flip(): return lax.ppermute(block, ('row', 'col'), pairs)  8.29 us
    pallas_call x1, Pallas kernels, gathered_body(): pl.pallas_call(functools.partial(rest_kernel, n_row, n_col), name='rest',...  4.81 us
    ppermute x9, waiting for transfers between devices, flip(): return lax.ppermute(block, ('row', 'col'), pairs)  4.76 us
    pallas_call x4, Pallas kernels, gathered_body(): pl.pallas_call(functools.partial(column_kernel, n_row, n_col, col, chips[...  3.38 us
    pallas_call x1, Pallas kernels, gathered_body(): pl.pallas_call(pack_kernel, name='pack', out_shape=jax.ShapeDtypeStruct((...  1.6 us
    unnamed x10, local copies, waits for them, and re-layouts  0.79 us
  transfers between devices with their start and end apart: 9, of which 4 were waited for; matrix products, arithmetic and copies ran while one was open for 0% of the time, Pallas kernels for 7%

profile of v14, /device:TPU:0, one launch (start us, length us, event | category | flops | bytes accessed | tf_op | source)
XLA Modules:
  0.0 25.0 jit_solution(5587633371454899232)
XLA Ops:
  0.6 1.6 %pack.1.in_ref = bf16[144,128]{1,0:T(8,128)(2,1)} custom-call(bf16[8,8,128]{2,1,0:T(8,128)(2,1)} %refs_7_.1, s32[8,8]{1,0:T(8,128)} %mask_hbm.1, bf16[64,128]{1,0:T(8,128)(2,1)} %bitcast.6, f32[1,128]{1,0:T(1,128)} %bitcast.3), custom_call_target="tpu_custom_call" | custom-call | tf_op jit(solution)/shard_map/pack/pallas_call | solution.py:376
  2.2 0.0 copy-start
  2.2 0.5 %collective-permute-start = (bf16[144,128]{1,0:T(8,128)(2,1)}, bf16[144,128]{1,0:T(8,128)(2,1)S(1)}, u32[]{:S(2)}, u32[]{:S(2)}) collective-permute-start(bf16[144,128]{1,0:T(8,128)(2,1)} %pack.1.in_ref), channel_id=1, source_target_pairs={{0,1},{1,0},{2,3},{3,2},{4,5},{5,4},{6,7},{7,6},{8,9},{9,8},{10,11... | collective-permute-start | bytes 110600 | tf_op jit(solution)/shard_map/ppermute | solution.py:358
  2.8 0.0 copy-start.1
  2.8 0.8 %copy-done.1 = bf16[144,128]{1,0:T(8,128)(2,1)S(1)} copy-done((bf16[144,128]{1,0:T(8,128)(2,1)S(1)}, bf16[144,128]{1,0:T(8,128)(2,1)}, u32[]{:S(2)}) %copy-start.1) | copy-done | bytes 36888
  3.5 0.0 copy-start.2
  3.5 0.3 %collective-permute-done.twin_ref = bf16[144,128]{1,0:T(8,128)(2,1)S(1)} collective-permute-done((bf16[144,128]{1,0:T(8,128)(2,1)}, bf16[144,128]{1,0:T(8,128)(2,1)S(1)}, u32[]{:S(2)}, u32[]{:S(2)}) %collective-permute-start) | collective-permute-done | bytes 36896 | tf_op jit(solution)/shard_map/ppermute | solution.py:358
  3.9 3.9 %collective-permute-start.1 = (bf16[272,128]{1,0:T(8,128)(2,1)S(1)}, bf16[272,128]{1,0:T(8,128)(2,1)S(1)}, u32[]{:S(2)}, u32[]{:S(2)}) collective-permute-start(bf16[272,128]{1,0:T(8,128)(2,1)S(1)} %join.1.refs_0_), channel_id=1, source_target_pairs={{0,8},{1,5},{2,10},{3,7},{4,12},{5,1},{6,14},{7,3},{8,0},{9,13},{1... | collective-permute-start | bytes 208904 | tf_op jit(solution)/shard_map/ppermute | solution.py:358
  7.8 1.3 %collective-permute-start.3 = (bf16[144,128]{1,0:T(8,128)(2,1)S(1)}, bf16[144,128]{1,0:T(8,128)(2,1)S(1)}, u32[]{:S(2)}, u32[]{:S(2)}) collective-permute-start(bf16[144,128]{1,0:T(8,128)(2,1)S(1)} %copy-done.1), channel_id=1, source_target_pairs={{0,12},{1,13},{2,14},{3,15},{4,8},{5,9},{6,10},{7,11},{8,4},{9,5},... | collective-permute-start | bytes 110600 | tf_op jit(solution)/shard_map/ppermute | solution.py:358
  9.1 1.2 %collective-permute-start.7 = (bf16[272,128]{1,0:T(8,128)(2,1)S(1)}, bf16[272,128]{1,0:T(8,128)(2,1)S(1)}, u32[]{:S(2)}, u32[]{:S(2)}) collective-permute-start(bf16[272,128]{1,0:T(8,128)(2,1)S(1)} %join.1.refs_0_), channel_id=1, source_target_pairs={{0,6},{1,15},{2,4},{3,13},{4,2},{5,11},{6,0},{7,9},{8,14},{9,7},{1... | collective-permute-start | bytes 208904 | tf_op jit(solution)/shard_map/ppermute | solution.py:358
  10.3 0.5 %collective-permute-start.5 = (bf16[272,128]{1,0:T(8,128)(2,1)S(1)}, bf16[272,128]{1,0:T(8,128)(2,1)S(1)}, u32[]{:S(2)}, u32[]{:S(2)}) collective-permute-start(bf16[272,128]{1,0:T(8,128)(2,1)S(1)} %join.1.refs_0_), channel_id=1, source_target_pairs={{0,2},{1,11},{2,0},{3,9},{4,6},{5,15},{6,4},{7,13},{8,10},{9,3},{1... | collective-permute-start | bytes 208904 | tf_op jit(solution)/shard_map/ppermute | solution.py:358
  10.8 0.0 collective-permute-done.1.refs_1_.refs_3_
  10.8 0.5 %collective-permute-start.2 = (bf16[272,128]{1,0:T(8,128)(2,1)S(1)}, bf16[272,128]{1,0:T(8,128)(2,1)S(1)}, u32[]{:S(2)}, u32[]{:S(2)}) collective-permute-start(bf16[272,128]{1,0:T(8,128)(2,1)S(1)} %collective-permute-done.1.refs_1_.refs_3_), channel_id=1, source_target_pairs={{0,1},{1,0},{2,3},{3,2},{4,5},{5,4},{6,7},{7,6},{8,9},{9,8},{10,11... | collective-permute-start | bytes 208904 | tf_op jit(solution)/shard_map/ppermute | solution.py:358
  11.3 2.3 %collective-permute-done.3.refs_5_ = bf16[144,128]{1,0:T(8,128)(2,1)S(1)} collective-permute-done((bf16[144,128]{1,0:T(8,128)(2,1)S(1)}, bf16[144,128]{1,0:T(8,128)(2,1)S(1)}, u32[]{:S(2)}, u32[]{:S(2)}) %collective-permute-start.3) | collective-permute-done | bytes 36896 | tf_op jit(solution)/shard_map/ppermute | solution.py:358
  13.6 0.0 collective-permute-start.4
  14.3 0.0 copy-start.3
  14.3 0.0 copy-start.4
  14.3 1.5 %collective-permute-done.7.refs_2_.refs_6_ = bf16[272,128]{1,0:T(8,128)(2,1)S(1)} collective-permute-done((bf16[272,128]{1,0:T(8,128)(2,1)S(1)}, bf16[272,128]{1,0:T(8,128)(2,1)S(1)}, u32[]{:S(2)}, u32[]{:S(2)}) %collective-permute-start.7) | collective-permute-done | bytes 69664 | tf_op jit(solution)/shard_map/ppermute | solution.py:358
  15.8 0.0 collective-permute-start.8
  15.8 0.7 %collective-permute-done.5.refs_0_.refs_4_ = bf16[272,128]{1,0:T(8,128)(2,1)S(1)} collective-permute-done((bf16[272,128]{1,0:T(8,128)(2,1)S(1)}, bf16[272,128]{1,0:T(8,128)(2,1)S(1)}, u32[]{:S(2)}, u32[]{:S(2)}) %collective-permute-start.5) | collective-permute-done | bytes 69664 | tf_op jit(solution)/shard_map/ppermute | solution.py:358
  16.5 0.3 %collective-permute-start.6 = (bf16[272,128]{1,0:T(8,128)(2,1)S(1)}, bf16[272,128]{1,0:T(8,128)(2,1)S(1)}, u32[]{:S(2)}, u32[]{:S(2)}) collective-permute-start(bf16[272,128]{1,0:T(8,128)(2,1)S(1)} %collective-permute-done.5.refs_0_.refs_4_), channel_id=1, source_target_pairs={{0,1},{1,0},{2,3},{3,2},{4,5},{5,4},{6,7},{7,6},{8,9},{9,8},{10,11... | collective-permute-start | bytes 208904 | tf_op jit(solution)/shard_map/ppermute | solution.py:358
  16.7 0.0 collective-permute-done.4.refs_6_
  16.8 0.0 collective-permute-done.2.refs_2_.refs_4_
  16.8 0.0 copy-done
  16.8 0.0 copy-done.2
  16.8 0.0 copy-done.3
  16.8 0.0 copy-done.4
  16.8 0.8 %column_0.1 = (f32[1024,128]{1,0:T(8,128)S(1)}, f32[256,128]{1,0:T(8,128)S(1)}, f32[256,128]{1,0:T(8,128)S(1)}, f32[4,256,128]{2,1,0:T(8,128)S(1)}, f32[2,256,12...) custom-call(s32[1]{0:T(128)S(6)} %copy.16.crop_ref, ...), custom_call_target="tpu_custom_call" | custom-call | flops 400000000 | bytes 1000000 | tf_op jit(solution)/shard_map/column_0/pallas_call | solution.py:430
  17.6 0.8 %column_1.1 = (f32[1024,128]{1,0:T(8,128)S(1)}, f32[256,128]{1,0:T(8,128)S(1)}, f32[256,128]{1,0:T(8,128)S(1)}, f32[4,256,128]{2,1,0:T(8,128)S(1)}, f32[2,256,12...) custom-call(s32[1]{0:T(128)S(6)} %copy.16.crop_ref, ...), custom_call_target="tpu_custom_call", output_to_operand_aliasing={{0}: (10, {})} | custom-call | flops 400000000 | bytes 1000000 | tf_op jit(solution)/shard_map/column_1/pallas_call | solution.py:430
  18.5 0.0 collective-permute-done.8.refs_3_.refs_7_
  18.5 0.0 collective-permute-done.6.refs_1_.refs_5_
  18.5 0.8 %column_2.1 = (f32[1024,128]{1,0:T(8,128)S(1)}, f32[256,128]{1,0:T(8,128)S(1)}, f32[256,128]{1,0:T(8,128)S(1)}, f32[4,256,128]{2,1,0:T(8,128)S(1)}, f32[2,256,12...) custom-call(s32[1]{0:T(128)S(6)} %copy.16.crop_ref, ...), custom_call_target="tpu_custom_call", output_to_operand_aliasing={{0}: (11, {})} | custom-call | flops 400000000 | bytes 1000000 | tf_op jit(solution)/shard_map/column_2/pallas_call | solution.py:430
  19.4 0.8 %column_3.1 = (f32[1024,128]{1,0:T(8,128)S(1)}, f32[256,128]{1,0:T(8,128)S(1)}, f32[256,128]{1,0:T(8,128)S(1)}, f32[4,256,128]{2,1,0:T(8,128)S(1)}, f32[2,256,12...) custom-call(s32[1]{0:T(128)S(6)} %copy.16.crop_ref, ...), custom_call_target="tpu_custom_call", output_to_operand_aliasing={{0}: (11, {})} | custom-call | flops 400000000 | bytes 1000000 | tf_op jit(solution)/shard_map/column_3/pallas_call | solution.py:430
  20.2 4.8 %rest.1 = (bf16[8,8,128]{2,1,0:T(8,128)(2,1)}, bf16[8,8,128]{2,1,0:T(8,128)(2,1)}, f32[6,128,128]{2,1,0:T(8,128)}) custom-call(bf16[6,128,128]{2,1,0:T(8,128)(2,1)S(1)} %copy-done, f32[3,64,128]{2,1,0:T(8,128)S(1)} %get-tuple-element.33.own_ref, f32[8,128]{1,0:T(8,128)S(1)} %get-tuple-element.34.refs_7_.refs_8_.gains_ref, ...), custom_call_target="tpu_custom_call" | custom-call | tf_op jit(solution)/shard_map/rest/pallas_call | solution.py:452
  (2 shorter events, 0.0 us)
Async XLA Ops:
  2.2 14.5 %copy-start = (bf16[6,128,128]{2,1,0:T(8,128)(2,1)S(1)}, bf16[6,128,128]{2,1,0:T(8,128)(2,1)}, u32[]{:S(2)}) copy-start(bf16[6,128,128]{2,1,0:T(8,128)(2,1)} %weights_ref.9) | copy-start | bytes 589828
  2.2 1.6 %collective-permute-start = (bf16[144,128]{1,0:T(8,128)(2,1)}, bf16[144,128]{1,0:T(8,128)(2,1)S(1)}, u32[]{:S(2)}, u32[]{:S(2)}) collective-permute-start(bf16[144,128]{1,0:T(8,128)(2,1)} %pack.1.in_ref), channel_id=1, source_target_pairs={{0,1},{1,0},{2,3},{3,2},{4,5},{5,4},{6,7},{7,6},{8,9},{9,8},{10,11... | collective-permute-start | bytes 110600 | tf_op jit(solution)/shard_map/ppermute | solution.py:358
  2.8 0.8 %copy-start.1 = (bf16[144,128]{1,0:T(8,128)(2,1)S(1)}, bf16[144,128]{1,0:T(8,128)(2,1)}, u32[]{:S(2)}) copy-start(bf16[144,128]{1,0:T(8,128)(2,1)} %pack.1.in_ref) | copy-start | bytes 110596
  3.5 13.2 %copy-start.2 = (bf16[8,8,128]{2,1,0:T(8,128)(2,1)S(1)}, bf16[8,8,128]{2,1,0:T(8,128)(2,1)}, u32[]{:S(2)}) copy-start(bf16[8,8,128]{2,1,0:T(8,128)(2,1)} %refs_7_.1) | copy-start | bytes 49156
  3.9 7.0 %collective-permute-start.1 = (bf16[272,128]{1,0:T(8,128)(2,1)S(1)}, bf16[272,128]{1,0:T(8,128)(2,1)S(1)}, u32[]{:S(2)}, u32[]{:S(2)}) collective-permute-start(bf16[272,128]{1,0:T(8,128)(2,1)S(1)} %join.1.refs_0_), channel_id=1, source_target_pairs={{0,8},{1,5},{2,10},{3,7},{4,12},{5,1},{6,14},{7,3},{8,0},{9,13},{1... | collective-permute-start | bytes 208904 | tf_op jit(solution)/shard_map/ppermute | solution.py:358
  7.8 5.9 %collective-permute-start.3 = (bf16[144,128]{1,0:T(8,128)(2,1)S(1)}, bf16[144,128]{1,0:T(8,128)(2,1)S(1)}, u32[]{:S(2)}, u32[]{:S(2)}) collective-permute-start(bf16[144,128]{1,0:T(8,128)(2,1)S(1)} %copy-done.1), channel_id=1, source_target_pairs={{0,12},{1,13},{2,14},{3,15},{4,8},{5,9},{6,10},{7,11},{8,4},{9,5},... | collective-permute-start | bytes 110600 | tf_op jit(solution)/shard_map/ppermute | solution.py:358
  9.1 6.6 %collective-permute-start.7 = (bf16[272,128]{1,0:T(8,128)(2,1)S(1)}, bf16[272,128]{1,0:T(8,128)(2,1)S(1)}, u32[]{:S(2)}, u32[]{:S(2)}) collective-permute-start(bf16[272,128]{1,0:T(8,128)(2,1)S(1)} %join.1.refs_0_), channel_id=1, source_target_pairs={{0,6},{1,15},{2,4},{3,13},{4,2},{5,11},{6,0},{7,9},{8,14},{9,7},{1... | collective-permute-start | bytes 208904 | tf_op jit(solution)/shard_map/ppermute | solution.py:358
  10.3 6.2 %collective-permute-start.5 = (bf16[272,128]{1,0:T(8,128)(2,1)S(1)}, bf16[272,128]{1,0:T(8,128)(2,1)S(1)}, u32[]{:S(2)}, u32[]{:S(2)}) collective-permute-start(bf16[272,128]{1,0:T(8,128)(2,1)S(1)} %join.1.refs_0_), channel_id=1, source_target_pairs={{0,2},{1,11},{2,0},{3,9},{4,6},{5,15},{6,4},{7,13},{8,10},{9,3},{1... | collective-permute-start | bytes 208904 | tf_op jit(solution)/shard_map/ppermute | solution.py:358
  10.8 5.9 %collective-permute-start.2 = (bf16[272,128]{1,0:T(8,128)(2,1)S(1)}, bf16[272,128]{1,0:T(8,128)(2,1)S(1)}, u32[]{:S(2)}, u32[]{:S(2)}) collective-permute-start(bf16[272,128]{1,0:T(8,128)(2,1)S(1)} %collective-permute-done.1.refs_1_.refs_3_), channel_id=1, source_target_pairs={{0,1},{1,0},{2,3},{3,2},{4,5},{5,4},{6,7},{7,6},{8,9},{9,8},{10,11... | collective-permute-start | bytes 208904 | tf_op jit(solution)/shard_map/ppermute | solution.py:358
  13.6 3.1 %collective-permute-start.4 = (bf16[144,128]{1,0:T(8,128)(2,1)S(1)}, bf16[144,128]{1,0:T(8,128)(2,1)S(1)}, u32[]{:S(2)}, u32[]{:S(2)}) collective-permute-start(bf16[144,128]{1,0:T(8,128)(2,1)S(1)} %collective-permute-done.3.refs_5_), channel_id=1, source_target_pairs={{0,1},{1,0},{2,3},{3,2},{4,5},{5,4},{6,7},{7,6},{8,9},{9,8},{10,11... | collective-permute-start | bytes 110600 | tf_op jit(solution)/shard_map/ppermute | solution.py:358
  14.3 2.5 %copy-start.3 = (f32[128]{0:T(128)S(1)}, f32[128]{0:T(128)}, u32[]{:S(2)}) copy-start(f32[128]{0:T(128)} %param.11) | copy-start | bytes 1540
  14.3 2.5 %copy-start.4 = (f32[128]{0:T(128)S(1)}, f32[128]{0:T(128)}, u32[]{:S(2)}) copy-start(f32[128]{0:T(128)} %param.12) | copy-start | bytes 1540
  15.8 2.7 %collective-permute-start.8 = (bf16[272,128]{1,0:T(8,128)(2,1)S(1)}, bf16[272,128]{1,0:T(8,128)(2,1)S(1)}, u32[]{:S(2)}, u32[]{:S(2)}) collective-permute-start(bf16[272,128]{1,0:T(8,128)(2,1)S(1)} %collective-permute-done.7.refs_2_.refs_6_), channel_id=1, source_target_pairs={{0,1},{1,0},{2,3},{3,2},{4,5},{5,4},{6,7},{7,6},{8,9},{9,8},{10,11... | collective-permute-start | bytes 208904 | tf_op jit(solution)/shard_map/ppermute | solution.py:358
  16.5 2.0 %collective-permute-start.6 = (bf16[272,128]{1,0:T(8,128)(2,1)S(1)}, bf16[272,128]{1,0:T(8,128)(2,1)S(1)}, u32[]{:S(2)}, u32[]{:S(2)}) collective-permute-start(bf16[272,128]{1,0:T(8,128)(2,1)S(1)} %collective-permute-done.5.refs_0_.refs_4_), channel_id=1, source_target_pairs={{0,1},{1,0},{2,3},{3,2},{4,5},{5,4},{6,7},{7,6},{8,9},{9,8},{10,11... | collective-permute-start | bytes 208904 | tf_op jit(solution)/shard_map/ppermute | solution.py:358

commit v15 on v14

--- a/solution.py
+++ b/solution.py
@@ -188,7 +188,11 @@
             return tuple(totals)
 
         totals = tuple(start_at(a, g, lane) for lane in range(SUB) for g in range(groups))
-        totals = step(0, totals) if steps == 1 else lax.fori_loop(0, steps, step, totals)
+        if steps > 2:
+            totals = lax.fori_loop(0, steps, step, totals)
+        else:
+            for q in range(steps):
+                totals = step(q, totals)
         for g in range(groups):
             store_at(a, g, [totals[lane * groups + g] for lane in range(SUB)])
         return 0
@@ -204,11 +208,11 @@
     return ref[pl.ds(pl.multiple_of(row, SUB), SUB), :]
 
 
-def column_kernel(n_row, n_col, col, chips, crop_ref, weights_ref, *refs):
+def columns_kernel(n_row, n_col, side_x, chips, crop_ref, weights_ref, *refs):
     count = sum(width for width, _ in chips)
-    chip_refs, refs = refs[:count], refs[count:]
+    chip_list, refs = split_chips(refs[:count], chips), refs[count:]
     own_ref = None
-    if col == 0:
+    if side_x == 0:
         act_ref, in_gain_ref, out_gain_ref, *refs, own_ref, gains_ref = refs
         z_hat, z_inverse = normalize(act_ref[...].astype(jnp.float32).reshape(own_ref.shape[1:]))
         own_ref[0] = z_hat
@@ -223,17 +227,17 @@
     size = n_row * tile
     bf16, f32 = jnp.bfloat16, jnp.float32
     row_me, col_me = lax.axis_index("row"), lax.axis_index("col")
-    chip_list = split_chips(chip_refs, chips)
-    normed = jnp.concatenate([chip_rows(normed_rows, chip, col % 2, on) for chip, on in chip_list], axis=0)
+    chip_list = [(chip, on, core, b) for core in range(2) for b, (chip, on) in enumerate(chip_list)]
+    normed = jnp.concatenate([chip_rows(normed_rows, chip, core, on) for chip, on, core, _ in chip_list], axis=0)
     flip_ref[0] = normed.astype(f32).T.astype(bf16)
     crop = crop_ref[0]
     col_offset = lax.broadcasted_iota(jnp.int32, (SUB, channels), 0)
     row_offset = lax.broadcasted_iota(jnp.int32, (SUB, channels), 1)
-    cols_in = col_offset < crop - (col_me ^ col) * SUB
     kept = []
-    for b, (chip, on) in enumerate(chip_list):
-        keep = chip_rows(mask_rows, chip, col % 2, on)
+    for chip, on, core, b in chip_list:
+        keep = chip_rows(mask_rows, chip, core, on)
         rows_in = row_offset < crop - (row_me ^ b) * SUB
+        cols_in = col_offset < crop - (col_me ^ (2 * side_x + core)) * SUB
         keep = jnp.where(rows_in & cols_in, keep, 0.0)
         kept += [jnp.broadcast_to(keep[:, at : at + 1], (SUB, channels)) for at in range(SUB)]
     kept = jnp.concatenate(kept, axis=0)
@@ -249,7 +253,7 @@
     out_gate = jax.nn.sigmoid(jnp.dot(normed, weights_ref[4], preferred_element_type=f32))
     if own_ref is not None:
         own_ref[2] = out_gate[0:tile]
-    cot = jnp.concatenate([chip_rows(cot_rows, chip, col % 2, on) for chip, on in chip_list], axis=0)
+    cot = jnp.concatenate([chip_rows(cot_rows, chip, core, on) for chip, on, core, _ in chip_list], axis=0)
     grad = cot.astype(f32) * out_gate
     grad_lin = grad.astype(bf16)
     flip_ref[1] = grad_lin.astype(f32).T.astype(bf16)
@@ -260,11 +264,11 @@
     turn = row_me ^ col_me
 
     def flipped(q):
-        firsts = [(turn ^ g) * tile for g in range(n_col)]
+        firsts = [q * size + (turn ^ g) * tile for g in range(n_col)]
         return lambda g, inner: right_ref[pl.ds(firsts[g] + inner, SUB, stride=SUB), :]
 
     def along(a, q):
-        return lambda lane, inner: spread(left_ref, a * tile + lane * SUB + inner)
+        return lambda lane, inner: spread(left_ref, q * size + a * tile + lane * SUB + inner)
 
     def start(a, g, lane):
         if len(tri_in) == 0:
@@ -275,20 +279,25 @@
         for lane in range(SUB):
             tri_ref[pl.ds(pl.multiple_of(g * size + a * tile + lane * SUB, SUB), SUB), :] = values[lane]
 
-    triangle(n_row, n_col, 1, flipped, along, start, store)
+    triangle(n_row, n_col, 2, flipped, along, start, store)
 
 
 def rest_kernel(n_row, n_col, weights_ref, own_ref, gains_ref, tri_ref, *refs):
-    columns = [refs[at * 5 : at * 5 + 5] for at in range(n_col)]
-    update_ref, pair_grad_ref, weight_grad_ref, back_ref, hat_ref, d_ref = refs[5 * n_col :]
+    groups = [refs[at * 5 : at * 5 + 5] for at in range(n_col // 2)]
+    update_ref, pair_grad_ref, weight_grad_ref, back_ref, hat_ref, d_ref = refs[5 * (n_col // 2) :]
     channels = tri_ref.shape[-1]
     tile = SUB * SUB
     size = n_row * tile
+    columns = []
+    for col in range(n_col):
+        own = pl.ds(col % 2 * size, size)
+        left, right, side, backs, _ = groups[col // 2]
+        columns.append((left.at[own], right.at[own], side.at[:, own], backs.at[:, own]))
     residues = n_row * SUB
     bf16, f32 = jnp.bfloat16, jnp.float32
     turn = lax.axis_index("row") ^ lax.axis_index("col")
     out_gain = gains_ref[1:2]
-    for col, (_, _, _, backs_ref, _) in enumerate(columns):
+    for col, (_, _, _, backs_ref) in enumerate(columns):
         rows = slice(col * size, (col + 1) * size)
         x_hat, inverse = normalize(tri_ref[rows, :])
         normed_out = (x_hat * out_gain).astype(bf16)
@@ -334,7 +343,7 @@
     triangle(n_row, n_col, n_row, by_left, down, zero, store(1))
 
     scale = 1.0 / residues
-    flipped, lin_flipped = [jnp.concatenate([column[4][at] for column in columns], axis=1) for at in range(2)]
+    flipped, lin_flipped = [jnp.concatenate([group[4][at] for group in groups], axis=1) for at in range(2)]
     sums = jnp.dot(flipped, d_ref[...], preferred_element_type=f32) * scale
     for s in range(5):
         weight_grad_ref[s] = sums[:, s * channels : (s + 1) * channels]
@@ -421,30 +430,30 @@
     sources = ((both, *first, *first, *straight), (*second, *third, *second, *third))
 
     tri, parts, extra = [], [], []
-    for col in range(n_col):
-        more = (pair_act, in_gain, out_gain) if col == 0 else (extra[1], *tri)
-        more_shapes = () if col > 0 else (
+    for side_x in range(n_col // 2):
+        more = (pair_act, in_gain, out_gain) if side_x == 0 else (extra[1], *tri)
+        more_shapes = () if side_x > 0 else (
             jax.ShapeDtypeStruct((3, tile, channels), f32),
             jax.ShapeDtypeStruct((SUB, channels), f32),
         )
         tri, *results = pl.pallas_call(
-            functools.partial(column_kernel, n_row, n_col, col, chips[col // 2]),
-            name=f"column_{col}",
+            functools.partial(columns_kernel, n_row, n_col, side_x, chips[side_x]),
+            name=f"columns_{side_x}",
             out_shape=(
                 jax.ShapeDtypeStruct((pairs, channels), f32),
-                jax.ShapeDtypeStruct((size, channels), f32),
-                jax.ShapeDtypeStruct((size, channels), f32),
-                jax.ShapeDtypeStruct((4, size, channels), f32),
-                jax.ShapeDtypeStruct((2, size, channels), f32),
-                jax.ShapeDtypeStruct((2, channels, size), bf16),
+                jax.ShapeDtypeStruct((2 * size, channels), f32),
+                jax.ShapeDtypeStruct((2 * size, channels), f32),
+                jax.ShapeDtypeStruct((4, 2 * size, channels), f32),
+                jax.ShapeDtypeStruct((2, 2 * size, channels), f32),
+                jax.ShapeDtypeStruct((2, channels, 2 * size), bf16),
                 *more_shapes,
             ),
-            in_specs=[smem] + [vmem] * (1 + len(sources[col // 2]) + len(more)),
+            in_specs=[smem] + [vmem] * (1 + len(sources[side_x]) + len(more)),
             out_specs=(vmem,) * (6 + len(more_shapes)),
-            input_output_aliases={3 + len(sources[col // 2]): 0} if col > 0 else {},
-            compiler_params=limit(8),
-            cost_estimate=pl.CostEstimate(flops=400_000_000, bytes_accessed=1_000_000, transcendentals=0),
-        )(crop_length, weights, *sources[col // 2], *more)
+            input_output_aliases={3 + len(sources[side_x]): 0} if side_x > 0 else {},
+            compiler_params=limit(12),
+            cost_estimate=pl.CostEstimate(flops=800_000_000, bytes_accessed=1_000_000, transcendentals=0),
+        )(crop_length, weights, *sources[side_x], *more)
         tri = [tri]
         parts += results[:5]
         extra += results[5:]

time: 25.4 us -> 24.6 us (0.969)
  Pallas kernels: 9.8 us -> 9.07 us
    pallas_call x4 -> x2, Pallas kernels: 3.38 us -> 2.7 us  [gathered_body(): pl.pallas_call(functools.partial(columns_kernel, n_row, n_col, side_x, ch...]
  transfers between devices with their start and end apart: 9 -> 9, of which waited for: 4 -> 4; matrix products, arithmetic and copies ran while one was open for 0% -> 0% of each run, Pallas kernels for 7% -> 6%
where the time goes in v15:
time: 24.6 us; the launch traced here: 24.3 us
  Pallas kernels  9.07 us (37%)
  starting transfers between devices  8.29 us (34%)
  waiting for transfers between devices  4.76 us (19%)
  between operations  1.38 us (6%)
  local copies, waits for them, and re-layouts  0.79 us (3%)
    ppermute x9, starting transfers between devices, flip(): return lax.ppermute(block, ('row', 'col'), pairs)  8.29 us
    pallas_call x1, Pallas kernels, gathered_body(): pl.pallas_call(functools.partial(rest_kernel, n_row, n_col), name='rest',...  4.77 us
    ppermute x9, waiting for transfers between devices, flip(): return lax.ppermute(block, ('row', 'col'), pairs)  4.76 us
    pallas_call x2, Pallas kernels, gathered_body(): pl.pallas_call(functools.partial(columns_kernel, n_row, n_col, side_x, ch...  2.7 us
    pallas_call x1, Pallas kernels, gathered_body(): pl.pallas_call(pack_kernel, name='pack', out_shape=jax.ShapeDtypeStruct((...  1.6 us
    unnamed x10, local copies, waits for them, and re-layouts  0.79 us
  transfers between devices with their start and end apart: 9, of which 4 were waited for; matrix products, arithmetic and copies ran while one was open for 0% of the time, Pallas kernels for 6%

profile of v15, /device:TPU:0, one launch (start us, length us, event | category | flops | bytes accessed | tf_op | source)
XLA Modules:
  0.0 24.3 jit_solution(16192283152936254720)
XLA Ops:
  0.6 1.6 %pack.1.in_ref = bf16[144,128]{1,0:T(8,128)(2,1)} custom-call(bf16[8,8,128]{2,1,0:T(8,128)(2,1)} %refs_7_.1, s32[8,8]{1,0:T(8,128)} %mask_hbm.1, bf16[64,128]{1,0:T(8,128)(2,1)} %bitcast.6, f32[1,128]{1,0:T(1,128)} %bitcast.3), custom_call_target="tpu_custom_call" | custom-call | tf_op jit(solution)/shard_map/pack/pallas_call | solution.py:385
  2.2 0.0 copy-start
  2.2 0.5 %collective-permute-start = (bf16[144,128]{1,0:T(8,128)(2,1)}, bf16[144,128]{1,0:T(8,128)(2,1)S(1)}, u32[]{:S(2)}, u32[]{:S(2)}) collective-permute-start(bf16[144,128]{1,0:T(8,128)(2,1)} %pack.1.in_ref), channel_id=1, source_target_pairs={{0,1},{1,0},{2,3},{3,2},{4,5},{5,4},{6,7},{7,6},{8,9},{9,8},{10,11... | collective-permute-start | bytes 110600 | tf_op jit(solution)/shard_map/ppermute | solution.py:367
  2.8 0.0 copy-start.1
  2.8 0.8 %copy-done.1 = bf16[144,128]{1,0:T(8,128)(2,1)S(1)} copy-done((bf16[144,128]{1,0:T(8,128)(2,1)S(1)}, bf16[144,128]{1,0:T(8,128)(2,1)}, u32[]{:S(2)}) %copy-start.1) | copy-done | bytes 36888
  3.5 0.0 copy-start.2
  3.5 0.3 %collective-permute-done.twin_ref = bf16[144,128]{1,0:T(8,128)(2,1)S(1)} collective-permute-done((bf16[144,128]{1,0:T(8,128)(2,1)}, bf16[144,128]{1,0:T(8,128)(2,1)S(1)}, u32[]{:S(2)}, u32[]{:S(2)}) %collective-permute-start) | collective-permute-done | bytes 36896 | tf_op jit(solution)/shard_map/ppermute | solution.py:367
  3.9 3.9 %collective-permute-start.1 = (bf16[272,128]{1,0:T(8,128)(2,1)S(1)}, bf16[272,128]{1,0:T(8,128)(2,1)S(1)}, u32[]{:S(2)}, u32[]{:S(2)}) collective-permute-start(bf16[272,128]{1,0:T(8,128)(2,1)S(1)} %join.1.refs_0_), channel_id=1, source_target_pairs={{0,8},{1,5},{2,10},{3,7},{4,12},{5,1},{6,14},{7,3},{8,0},{9,13},{1... | collective-permute-start | bytes 208904 | tf_op jit(solution)/shard_map/ppermute | solution.py:367
  7.8 1.3 %collective-permute-start.3 = (bf16[144,128]{1,0:T(8,128)(2,1)S(1)}, bf16[144,128]{1,0:T(8,128)(2,1)S(1)}, u32[]{:S(2)}, u32[]{:S(2)}) collective-permute-start(bf16[144,128]{1,0:T(8,128)(2,1)S(1)} %copy-done.1), channel_id=1, source_target_pairs={{0,12},{1,13},{2,14},{3,15},{4,8},{5,9},{6,10},{7,11},{8,4},{9,5},... | collective-permute-start | bytes 110600 | tf_op jit(solution)/shard_map/ppermute | solution.py:367
  9.1 1.2 %collective-permute-start.7 = (bf16[272,128]{1,0:T(8,128)(2,1)S(1)}, bf16[272,128]{1,0:T(8,128)(2,1)S(1)}, u32[]{:S(2)}, u32[]{:S(2)}) collective-permute-start(bf16[272,128]{1,0:T(8,128)(2,1)S(1)} %join.1.refs_0_), channel_id=1, source_target_pairs={{0,6},{1,15},{2,4},{3,13},{4,2},{5,11},{6,0},{7,9},{8,14},{9,7},{1... | collective-permute-start | bytes 208904 | tf_op jit(solution)/shard_map/ppermute | solution.py:367
  10.3 0.5 %collective-permute-start.5 = (bf16[272,128]{1,0:T(8,128)(2,1)S(1)}, bf16[272,128]{1,0:T(8,128)(2,1)S(1)}, u32[]{:S(2)}, u32[]{:S(2)}) collective-permute-start(bf16[272,128]{1,0:T(8,128)(2,1)S(1)} %join.1.refs_0_), channel_id=1, source_target_pairs={{0,2},{1,11},{2,0},{3,9},{4,6},{5,15},{6,4},{7,13},{8,10},{9,3},{1... | collective-permute-start | bytes 208904 | tf_op jit(solution)/shard_map/ppermute | solution.py:367
  10.8 0.0 collective-permute-done.1.refs_1_.refs_3_
  10.8 0.5 %collective-permute-start.2 = (bf16[272,128]{1,0:T(8,128)(2,1)S(1)}, bf16[272,128]{1,0:T(8,128)(2,1)S(1)}, u32[]{:S(2)}, u32[]{:S(2)}) collective-permute-start(bf16[272,128]{1,0:T(8,128)(2,1)S(1)} %collective-permute-done.1.refs_1_.refs_3_), channel_id=1, source_target_pairs={{0,1},{1,0},{2,3},{3,2},{4,5},{5,4},{6,7},{7,6},{8,9},{9,8},{10,11... | collective-permute-start | bytes 208904 | tf_op jit(solution)/shard_map/ppermute | solution.py:367
  11.3 2.3 %collective-permute-done.3.refs_5_ = bf16[144,128]{1,0:T(8,128)(2,1)S(1)} collective-permute-done((bf16[144,128]{1,0:T(8,128)(2,1)S(1)}, bf16[144,128]{1,0:T(8,128)(2,1)S(1)}, u32[]{:S(2)}, u32[]{:S(2)}) %collective-permute-start.3) | collective-permute-done | bytes 36896 | tf_op jit(solution)/shard_map/ppermute | solution.py:367
  13.6 0.0 collective-permute-start.4
  14.3 0.0 copy-start.3
  14.3 0.0 copy-start.4
  14.3 1.5 %collective-permute-done.7.refs_2_.refs_6_ = bf16[272,128]{1,0:T(8,128)(2,1)S(1)} collective-permute-done((bf16[272,128]{1,0:T(8,128)(2,1)S(1)}, bf16[272,128]{1,0:T(8,128)(2,1)S(1)}, u32[]{:S(2)}, u32[]{:S(2)}) %collective-permute-start.7) | collective-permute-done | bytes 69664 | tf_op jit(solution)/shard_map/ppermute | solution.py:367
  15.8 0.0 collective-permute-start.8
  15.8 0.7 %collective-permute-done.5.refs_0_.refs_4_ = bf16[272,128]{1,0:T(8,128)(2,1)S(1)} collective-permute-done((bf16[272,128]{1,0:T(8,128)(2,1)S(1)}, bf16[272,128]{1,0:T(8,128)(2,1)S(1)}, u32[]{:S(2)}, u32[]{:S(2)}) %collective-permute-start.5) | collective-permute-done | bytes 69664 | tf_op jit(solution)/shard_map/ppermute | solution.py:367
  16.5 0.3 %collective-permute-start.6 = (bf16[272,128]{1,0:T(8,128)(2,1)S(1)}, bf16[272,128]{1,0:T(8,128)(2,1)S(1)}, u32[]{:S(2)}, u32[]{:S(2)}) collective-permute-start(bf16[272,128]{1,0:T(8,128)(2,1)S(1)} %collective-permute-done.5.refs_0_.refs_4_), channel_id=1, source_target_pairs={{0,1},{1,0},{2,3},{3,2},{4,5},{5,4},{6,7},{7,6},{8,9},{9,8},{10,11... | collective-permute-start | bytes 208904 | tf_op jit(solution)/shard_map/ppermute | solution.py:367
  16.7 0.0 collective-permute-done.4.refs_6_
  16.8 0.0 collective-permute-done.2.refs_2_.refs_4_
  16.8 0.0 copy-done
  16.8 0.0 copy-done.2
  16.8 0.0 copy-done.3
  16.8 0.0 copy-done.4
  16.8 1.3 %columns_0.1 = (f32[1024,128]{1,0:T(8,128)S(1)}, f32[512,128]{1,0:T(8,128)S(1)}, f32[512,128]{1,0:T(8,128)S(1)}, f32[4,512,128]{2,1,0:T(8,128)S(1)}, f32[2,512,1...) custom-call(s32[1]{0:T(128)S(6)} %copy.12.crop_ref, ...), custom_call_target="tpu_custom_call" | custom-call | flops 800000000 | bytes 1000000 | tf_op jit(solution)/shard_map/columns_0/pallas_call | solution.py:439
  18.1 0.0 collective-permute-done.8.refs_3_.refs_7_
  18.1 0.0 collective-permute-done.6.refs_1_.refs_5_
  18.2 1.4 %columns_1.1 = (f32[1024,128]{1,0:T(8,128)S(1)}, f32[512,128]{1,0:T(8,128)S(1)}, f32[512,128]{1,0:T(8,128)S(1)}, f32[4,512,128]{2,1,0:T(8,128)S(1)}, f32[2,512,1...) custom-call(s32[1]{0:T(128)S(6)} %copy.12.crop_ref, ...), custom_call_target="tpu_custom_call", output_to_operand_aliasing={{0}: (11, {})} | custom-call | flops 800000000 | bytes 1000000 | tf_op jit(solution)/shard_map/columns_1/pallas_call | solution.py:439
  19.5 4.8 %rest.1 = (bf16[8,8,128]{2,1,0:T(8,128)(2,1)}, bf16[8,8,128]{2,1,0:T(8,128)(2,1)}, f32[6,128,128]{2,1,0:T(8,128)}) custom-call(bf16[6,128,128]{2,1,0:T(8,128)(2,1)S(1)} %copy-done, f32[3,64,128]{2,1,0:T(8,128)S(1)} %get-tuple-element.21.own_ref, f32[8,128]{1,0:T(8,128)S(1)} %get-tuple-element.22.refs_8_.gains_ref, ...), custom_call_target="tpu_custom_call" | custom-call | tf_op jit(solution)/shard_map/rest/pallas_call | solution.py:461
  (2 shorter events, 0.0 us)
Async XLA Ops:
  2.2 14.5 %copy-start = (bf16[6,128,128]{2,1,0:T(8,128)(2,1)S(1)}, bf16[6,128,128]{2,1,0:T(8,128)(2,1)}, u32[]{:S(2)}) copy-start(bf16[6,128,128]{2,1,0:T(8,128)(2,1)} %weights_ref.5) | copy-start | bytes 589828
  2.2 1.6 %collective-permute-start = (bf16[144,128]{1,0:T(8,128)(2,1)}, bf16[144,128]{1,0:T(8,128)(2,1)S(1)}, u32[]{:S(2)}, u32[]{:S(2)}) collective-permute-start(bf16[144,128]{1,0:T(8,128)(2,1)} %pack.1.in_ref), channel_id=1, source_target_pairs={{0,1},{1,0},{2,3},{3,2},{4,5},{5,4},{6,7},{7,6},{8,9},{9,8},{10,11... | collective-permute-start | bytes 110600 | tf_op jit(solution)/shard_map/ppermute | solution.py:367
  2.8 0.8 %copy-start.1 = (bf16[144,128]{1,0:T(8,128)(2,1)S(1)}, bf16[144,128]{1,0:T(8,128)(2,1)}, u32[]{:S(2)}) copy-start(bf16[144,128]{1,0:T(8,128)(2,1)} %pack.1.in_ref) | copy-start | bytes 110596
  3.5 13.2 %copy-start.2 = (bf16[8,8,128]{2,1,0:T(8,128)(2,1)S(1)}, bf16[8,8,128]{2,1,0:T(8,128)(2,1)}, u32[]{:S(2)}) copy-start(bf16[8,8,128]{2,1,0:T(8,128)(2,1)} %refs_7_.1) | copy-start | bytes 49156
  3.9 7.0 %collective-permute-start.1 = (bf16[272,128]{1,0:T(8,128)(2,1)S(1)}, bf16[272,128]{1,0:T(8,128)(2,1)S(1)}, u32[]{:S(2)}, u32[]{:S(2)}) collective-permute-start(bf16[272,128]{1,0:T(8,128)(2,1)S(1)} %join.1.refs_0_), channel_id=1, source_target_pairs={{0,8},{1,5},{2,10},{3,7},{4,12},{5,1},{6,14},{7,3},{8,0},{9,13},{1... | collective-permute-start | bytes 208904 | tf_op jit(solution)/shard_map/ppermute | solution.py:367
  7.8 5.9 %collective-permute-start.3 = (bf16[144,128]{1,0:T(8,128)(2,1)S(1)}, bf16[144,128]{1,0:T(8,128)(2,1)S(1)}, u32[]{:S(2)}, u32[]{:S(2)}) collective-permute-start(bf16[144,128]{1,0:T(8,128)(2,1)S(1)} %copy-done.1), channel_id=1, source_target_pairs={{0,12},{1,13},{2,14},{3,15},{4,8},{5,9},{6,10},{7,11},{8,4},{9,5},... | collective-permute-start | bytes 110600 | tf_op jit(solution)/shard_map/ppermute | solution.py:367
  9.1 6.6 %collective-permute-start.7 = (bf16[272,128]{1,0:T(8,128)(2,1)S(1)}, bf16[272,128]{1,0:T(8,128)(2,1)S(1)}, u32[]{:S(2)}, u32[]{:S(2)}) collective-permute-start(bf16[272,128]{1,0:T(8,128)(2,1)S(1)} %join.1.refs_0_), channel_id=1, source_target_pairs={{0,6},{1,15},{2,4},{3,13},{4,2},{5,11},{6,0},{7,9},{8,14},{9,7},{1... | collective-permute-start | bytes 208904 | tf_op jit(solution)/shard_map/ppermute | solution.py:367
  10.3 6.2 %collective-permute-start.5 = (bf16[272,128]{1,0:T(8,128)(2,1)S(1)}, bf16[272,128]{1,0:T(8,128)(2,1)S(1)}, u32[]{:S(2)}, u32[]{:S(2)}) collective-permute-start(bf16[272,128]{1,0:T(8,128)(2,1)S(1)} %join.1.refs_0_), channel_id=1, source_target_pairs={{0,2},{1,11},{2,0},{3,9},{4,6},{5,15},{6,4},{7,13},{8,10},{9,3},{1... | collective-permute-start | bytes 208904 | tf_op jit(solution)/shard_map/ppermute | solution.py:367
  10.8 5.9 %collective-permute-start.2 = (bf16[272,128]{1,0:T(8,128)(2,1)S(1)}, bf16[272,128]{1,0:T(8,128)(2,1)S(1)}, u32[]{:S(2)}, u32[]{:S(2)}) collective-permute-start(bf16[272,128]{1,0:T(8,128)(2,1)S(1)} %collective-permute-done.1.refs_1_.refs_3_), channel_id=1, source_target_pairs={{0,1},{1,0},{2,3},{3,2},{4,5},{5,4},{6,7},{7,6},{8,9},{9,8},{10,11... | collective-permute-start | bytes 208904 | tf_op jit(solution)/shard_map/ppermute | solution.py:367
  13.6 3.1 %collective-permute-start.4 = (bf16[144,128]{1,0:T(8,128)(2,1)S(1)}, bf16[144,128]{1,0:T(8,128)(2,1)S(1)}, u32[]{:S(2)}, u32[]{:S(2)}) collective-permute-start(bf16[144,128]{1,0:T(8,128)(2,1)S(1)} %collective-permute-done.3.refs_5_), channel_id=1, source_target_pairs={{0,1},{1,0},{2,3},{3,2},{4,5},{5,4},{6,7},{7,6},{8,9},{9,8},{10,11... | collective-permute-start | bytes 110600 | tf_op jit(solution)/shard_map/ppermute | solution.py:367
  14.3 2.5 %copy-start.3 = (f32[128]{0:T(128)S(1)}, f32[128]{0:T(128)}, u32[]{:S(2)}) copy-start(f32[128]{0:T(128)} %param.11) | copy-start | bytes 1540
  14.3 2.5 %copy-start.4 = (f32[128]{0:T(128)S(1)}, f32[128]{0:T(128)}, u32[]{:S(2)}) copy-start(f32[128]{0:T(128)} %param.12) | copy-start | bytes 1540
  15.8 2.4 %collective-permute-start.8 = (bf16[272,128]{1,0:T(8,128)(2,1)S(1)}, bf16[272,128]{1,0:T(8,128)(2,1)S(1)}, u32[]{:S(2)}, u32[]{:S(2)}) collective-permute-start(bf16[272,128]{1,0:T(8,128)(2,1)S(1)} %collective-permute-done.7.refs_2_.refs_6_), channel_id=1, source_target_pairs={{0,1},{1,0},{2,3},{3,2},{4,5},{5,4},{6,7},{7,6},{8,9},{9,8},{10,11... | collective-permute-start | bytes 208904 | tf_op jit(solution)/shard_map/ppermute | solution.py:367
  16.5 1.7 %collective-permute-start.6 = (bf16[272,128]{1,0:T(8,128)(2,1)S(1)}, bf16[272,128]{1,0:T(8,128)(2,1)S(1)}, u32[]{:S(2)}, u32[]{:S(2)}) collective-permute-start(bf16[272,128]{1,0:T(8,128)(2,1)S(1)} %collective-permute-done.5.refs_0_.refs_4_), channel_id=1, source_target_pairs={{0,1},{1,0},{2,3},{3,2},{4,5},{5,4},{6,7},{7,6},{8,9},{9,8},{10,11... | collective-permute-start | bytes 208904 | tf_op jit(solution)/shard_map/ppermute | solution.py:367

commit v16 on v15

--- a/solution.py
+++ b/solution.py
@@ -188,7 +188,7 @@
             return tuple(totals)
 
         totals = tuple(start_at(a, g, lane) for lane in range(SUB) for g in range(groups))
-        if steps > 2:
+        if steps > 4:
             totals = lax.fori_loop(0, steps, step, totals)
         else:
             for q in range(steps):
@@ -229,7 +229,13 @@
     row_me, col_me = lax.axis_index("row"), lax.axis_index("col")
     chip_list = [(chip, on, core, b) for core in range(2) for b, (chip, on) in enumerate(chip_list)]
     normed = jnp.concatenate([chip_rows(normed_rows, chip, core, on) for chip, on, core, _ in chip_list], axis=0)
-    flip_ref[0] = normed.astype(f32).T.astype(bf16)
+    same = lax.broadcasted_iota(jnp.int32, (channels, channels), 0) == lax.broadcasted_iota(jnp.int32, (channels, channels), 1)
+    identity = jnp.where(same, 1.0, 0.0).astype(bf16)
+
+    def turned(rows):
+        return lax.dot_general(identity, rows, (((1,), (1,)), ((), ())), preferred_element_type=f32).astype(bf16)
+
+    flip_ref[0] = turned(normed)
     crop = crop_ref[0]
     col_offset = lax.broadcasted_iota(jnp.int32, (SUB, channels), 0)
     row_offset = lax.broadcasted_iota(jnp.int32, (SUB, channels), 1)
@@ -256,7 +262,7 @@
     cot = jnp.concatenate([chip_rows(cot_rows, chip, core, on) for chip, on, core, _ in chip_list], axis=0)
     grad = cot.astype(f32) * out_gate
     grad_lin = grad.astype(bf16)
-    flip_ref[1] = grad_lin.astype(f32).T.astype(bf16)
+    flip_ref[1] = turned(grad_lin)
     back_ref[0] = grad * (1.0 - out_gate)
     back = lax.dot_general(grad_lin, weights_ref[5], (((1,), (1,)), ((), ())), preferred_element_type=f32)
     back = back * gains_ref[1:2]

time: 24.6 us -> 24.2 us (0.984)
  Pallas kernels: 9.07 us -> 8.65 us
    pallas_call x1, Pallas kernels: 4.77 us -> 4.45 us  [gathered_body(): pl.pallas_call(functools.partial(rest_kernel, n_row, n_col), name='rest',...]
  transfers between devices with their start and end apart: 9 -> 9, of which waited for: 4 -> 4; matrix products, arithmetic and copies ran while one was open for 0% -> 0% of each run, Pallas kernels for 6% -> 5%
where the time goes in v16:
time: 24.2 us; the launch traced here: 23.9 us
  Pallas kernels  8.65 us (36%)
  starting transfers between devices  8.29 us (34%)
  waiting for transfers between devices  4.76 us (20%)
  between operations  1.38 us (6%)
  local copies, waits for them, and re-layouts  0.79 us (3%)
    ppermute x9, starting transfers between devices, flip(): return lax.ppermute(block, ('row', 'col'), pairs)  8.29 us
    ppermute x9, waiting for transfers between devices, flip(): return lax.ppermute(block, ('row', 'col'), pairs)  4.76 us
    pallas_call x1, Pallas kernels, gathered_body(): pl.pallas_call(functools.partial(rest_kernel, n_row, n_col), name='rest',...  4.45 us
    pallas_call x2, Pallas kernels, gathered_body(): pl.pallas_call(functools.partial(columns_kernel, n_row, n_col, side_x, ch...  2.6 us
    pallas_call x1, Pallas kernels, gathered_body(): pl.pallas_call(pack_kernel, name='pack', out_shape=jax.ShapeDtypeStruct((...  1.6 us
    unnamed x10, local copies, waits for them, and re-layouts  0.79 us
  transfers between devices with their start and end apart: 9, of which 4 were waited for; matrix products, arithmetic and copies ran while one was open for 0% of the time, Pallas kernels for 5%

profile of v16, /device:TPU:0, one launch (start us, length us, event | category | flops | bytes accessed | tf_op | source)
XLA Modules:
  0.0 23.9 jit_solution(6941431224594024980)
XLA Ops:
  0.6 1.6 %pack.1.in_ref = bf16[144,128]{1,0:T(8,128)(2,1)} custom-call(bf16[8,8,128]{2,1,0:T(8,128)(2,1)} %refs_7_.1, s32[8,8]{1,0:T(8,128)} %mask_hbm.1, bf16[64,128]{1,0:T(8,128)(2,1)} %bitcast.6, f32[1,128]{1,0:T(1,128)} %bitcast.3), custom_call_target="tpu_custom_call" | custom-call | tf_op jit(solution)/shard_map/pack/pallas_call | solution.py:391
  2.2 0.0 copy-start
  2.2 0.5 %collective-permute-start = (bf16[144,128]{1,0:T(8,128)(2,1)}, bf16[144,128]{1,0:T(8,128)(2,1)S(1)}, u32[]{:S(2)}, u32[]{:S(2)}) collective-permute-start(bf16[144,128]{1,0:T(8,128)(2,1)} %pack.1.in_ref), channel_id=1, source_target_pairs={{0,1},{1,0},{2,3},{3,2},{4,5},{5,4},{6,7},{7,6},{8,9},{9,8},{10,11... | collective-permute-start | bytes 110600 | tf_op jit(solution)/shard_map/ppermute | solution.py:373
  2.8 0.0 copy-start.1
  2.8 0.8 %copy-done.1 = bf16[144,128]{1,0:T(8,128)(2,1)S(1)} copy-done((bf16[144,128]{1,0:T(8,128)(2,1)S(1)}, bf16[144,128]{1,0:T(8,128)(2,1)}, u32[]{:S(2)}) %copy-start.1) | copy-done | bytes 36888
  3.5 0.0 copy-start.2
  3.5 0.3 %collective-permute-done.twin_ref = bf16[144,128]{1,0:T(8,128)(2,1)S(1)} collective-permute-done((bf16[144,128]{1,0:T(8,128)(2,1)}, bf16[144,128]{1,0:T(8,128)(2,1)S(1)}, u32[]{:S(2)}, u32[]{:S(2)}) %collective-permute-start) | collective-permute-done | bytes 36896 | tf_op jit(solution)/shard_map/ppermute | solution.py:373
  3.9 3.9 %collective-permute-start.1 = (bf16[272,128]{1,0:T(8,128)(2,1)S(1)}, bf16[272,128]{1,0:T(8,128)(2,1)S(1)}, u32[]{:S(2)}, u32[]{:S(2)}) collective-permute-start(bf16[272,128]{1,0:T(8,128)(2,1)S(1)} %join.1.refs_0_), channel_id=1, source_target_pairs={{0,8},{1,5},{2,10},{3,7},{4,12},{5,1},{6,14},{7,3},{8,0},{9,13},{1... | collective-permute-start | bytes 208904 | tf_op jit(solution)/shard_map/ppermute | solution.py:373
  7.8 1.3 %collective-permute-start.3 = (bf16[144,128]{1,0:T(8,128)(2,1)S(1)}, bf16[144,128]{1,0:T(8,128)(2,1)S(1)}, u32[]{:S(2)}, u32[]{:S(2)}) collective-permute-start(bf16[144,128]{1,0:T(8,128)(2,1)S(1)} %copy-done.1), channel_id=1, source_target_pairs={{0,12},{1,13},{2,14},{3,15},{4,8},{5,9},{6,10},{7,11},{8,4},{9,5},... | collective-permute-start | bytes 110600 | tf_op jit(solution)/shard_map/ppermute | solution.py:373
  9.1 1.2 %collective-permute-start.7 = (bf16[272,128]{1,0:T(8,128)(2,1)S(1)}, bf16[272,128]{1,0:T(8,128)(2,1)S(1)}, u32[]{:S(2)}, u32[]{:S(2)}) collective-permute-start(bf16[272,128]{1,0:T(8,128)(2,1)S(1)} %join.1.refs_0_), channel_id=1, source_target_pairs={{0,6},{1,15},{2,4},{3,13},{4,2},{5,11},{6,0},{7,9},{8,14},{9,7},{1... | collective-permute-start | bytes 208904 | tf_op jit(solution)/shard_map/ppermute | solution.py:373
  10.3 0.5 %collective-permute-start.5 = (bf16[272,128]{1,0:T(8,128)(2,1)S(1)}, bf16[272,128]{1,0:T(8,128)(2,1)S(1)}, u32[]{:S(2)}, u32[]{:S(2)}) collective-permute-start(bf16[272,128]{1,0:T(8,128)(2,1)S(1)} %join.1.refs_0_), channel_id=1, source_target_pairs={{0,2},{1,11},{2,0},{3,9},{4,6},{5,15},{6,4},{7,13},{8,10},{9,3},{1... | collective-permute-start | bytes 208904 | tf_op jit(solution)/shard_map/ppermute | solution.py:373
  10.8 0.0 collective-permute-done.1.refs_1_.refs_3_
  10.8 0.5 %collective-permute-start.2 = (bf16[272,128]{1,0:T(8,128)(2,1)S(1)}, bf16[272,128]{1,0:T(8,128)(2,1)S(1)}, u32[]{:S(2)}, u32[]{:S(2)}) collective-permute-start(bf16[272,128]{1,0:T(8,128)(2,1)S(1)} %collective-permute-done.1.refs_1_.refs_3_), channel_id=1, source_target_pairs={{0,1},{1,0},{2,3},{3,2},{4,5},{5,4},{6,7},{7,6},{8,9},{9,8},{10,11... | collective-permute-start | bytes 208904 | tf_op jit(solution)/shard_map/ppermute | solution.py:373
  11.3 2.3 %collective-permute-done.3.refs_5_ = bf16[144,128]{1,0:T(8,128)(2,1)S(1)} collective-permute-done((bf16[144,128]{1,0:T(8,128)(2,1)S(1)}, bf16[144,128]{1,0:T(8,128)(2,1)S(1)}, u32[]{:S(2)}, u32[]{:S(2)}) %collective-permute-start.3) | collective-permute-done | bytes 36896 | tf_op jit(solution)/shard_map/ppermute | solution.py:373
  13.6 0.0 collective-permute-start.4
  14.3 0.0 copy-start.3
  14.3 0.0 copy-start.4
  14.3 1.5 %collective-permute-done.7.refs_2_.refs_6_ = bf16[272,128]{1,0:T(8,128)(2,1)S(1)} collective-permute-done((bf16[272,128]{1,0:T(8,128)(2,1)S(1)}, bf16[272,128]{1,0:T(8,128)(2,1)S(1)}, u32[]{:S(2)}, u32[]{:S(2)}) %collective-permute-start.7) | collective-permute-done | bytes 69664 | tf_op jit(solution)/shard_map/ppermute | solution.py:373
  15.8 0.0 collective-permute-start.8
  15.8 0.7 %collective-permute-done.5.refs_0_.refs_4_ = bf16[272,128]{1,0:T(8,128)(2,1)S(1)} collective-permute-done((bf16[272,128]{1,0:T(8,128)(2,1)S(1)}, bf16[272,128]{1,0:T(8,128)(2,1)S(1)}, u32[]{:S(2)}, u32[]{:S(2)}) %collective-permute-start.5) | collective-permute-done | bytes 69664 | tf_op jit(solution)/shard_map/ppermute | solution.py:373
  16.5 0.3 %collective-permute-start.6 = (bf16[272,128]{1,0:T(8,128)(2,1)S(1)}, bf16[272,128]{1,0:T(8,128)(2,1)S(1)}, u32[]{:S(2)}, u32[]{:S(2)}) collective-permute-start(bf16[272,128]{1,0:T(8,128)(2,1)S(1)} %collective-permute-done.5.refs_0_.refs_4_), channel_id=1, source_target_pairs={{0,1},{1,0},{2,3},{3,2},{4,5},{5,4},{6,7},{7,6},{8,9},{9,8},{10,11... | collective-permute-start | bytes 208904 | tf_op jit(solution)/shard_map/ppermute | solution.py:373
  16.7 0.0 collective-permute-done.4.refs_6_
  16.8 0.0 collective-permute-done.2.refs_2_.refs_4_
  16.8 0.0 copy-done
  16.8 0.0 copy-done.2
  16.8 0.0 copy-done.3
  16.8 0.0 copy-done.4
  16.8 1.3 %columns_0.1 = (f32[1024,128]{1,0:T(8,128)S(1)}, f32[512,128]{1,0:T(8,128)S(1)}, f32[512,128]{1,0:T(8,128)S(1)}, f32[4,512,128]{2,1,0:T(8,128)S(1)}, f32[2,512,1...) custom-call(s32[1]{0:T(128)S(6)} %copy.12.crop_ref, ...), custom_call_target="tpu_custom_call" | custom-call | flops 800000000 | bytes 1000000 | tf_op jit(solution)/shard_map/columns_0/pallas_call | solution.py:445
  18.1 0.0 collective-permute-done.8.refs_3_.refs_7_
  18.1 0.0 collective-permute-done.6.refs_1_.refs_5_
  18.1 1.3 %columns_1.1 = (f32[1024,128]{1,0:T(8,128)S(1)}, f32[512,128]{1,0:T(8,128)S(1)}, f32[512,128]{1,0:T(8,128)S(1)}, f32[4,512,128]{2,1,0:T(8,128)S(1)}, f32[2,512,1...) custom-call(s32[1]{0:T(128)S(6)} %copy.12.crop_ref, ...), custom_call_target="tpu_custom_call", output_to_operand_aliasing={{0}: (11, {})} | custom-call | flops 800000000 | bytes 1000000 | tf_op jit(solution)/shard_map/columns_1/pallas_call | solution.py:445
  19.4 4.4 %rest.1 = (bf16[8,8,128]{2,1,0:T(8,128)(2,1)}, bf16[8,8,128]{2,1,0:T(8,128)(2,1)}, f32[6,128,128]{2,1,0:T(8,128)}) custom-call(bf16[6,128,128]{2,1,0:T(8,128)(2,1)S(1)} %copy-done, f32[3,64,128]{2,1,0:T(8,128)S(1)} %get-tuple-element.21.own_ref, f32[8,128]{1,0:T(8,128)S(1)} %get-tuple-element.22.refs_8_.gains_ref, ...), custom_call_target="tpu_custom_call" | custom-call | tf_op jit(solution)/shard_map/rest/pallas_call | solution.py:467
  (2 shorter events, 0.0 us)
Async XLA Ops:
  2.2 14.5 %copy-start = (bf16[6,128,128]{2,1,0:T(8,128)(2,1)S(1)}, bf16[6,128,128]{2,1,0:T(8,128)(2,1)}, u32[]{:S(2)}) copy-start(bf16[6,128,128]{2,1,0:T(8,128)(2,1)} %weights_ref.5) | copy-start | bytes 589828
  2.2 1.6 %collective-permute-start = (bf16[144,128]{1,0:T(8,128)(2,1)}, bf16[144,128]{1,0:T(8,128)(2,1)S(1)}, u32[]{:S(2)}, u32[]{:S(2)}) collective-permute-start(bf16[144,128]{1,0:T(8,128)(2,1)} %pack.1.in_ref), channel_id=1, source_target_pairs={{0,1},{1,0},{2,3},{3,2},{4,5},{5,4},{6,7},{7,6},{8,9},{9,8},{10,11... | collective-permute-start | bytes 110600 | tf_op jit(solution)/shard_map/ppermute | solution.py:373
  2.8 0.8 %copy-start.1 = (bf16[144,128]{1,0:T(8,128)(2,1)S(1)}, bf16[144,128]{1,0:T(8,128)(2,1)}, u32[]{:S(2)}) copy-start(bf16[144,128]{1,0:T(8,128)(2,1)} %pack.1.in_ref) | copy-start | bytes 110596
  3.5 13.2 %copy-start.2 = (bf16[8,8,128]{2,1,0:T(8,128)(2,1)S(1)}, bf16[8,8,128]{2,1,0:T(8,128)(2,1)}, u32[]{:S(2)}) copy-start(bf16[8,8,128]{2,1,0:T(8,128)(2,1)} %refs_7_.1) | copy-start | bytes 49156
  3.9 7.0 %collective-permute-start.1 = (bf16[272,128]{1,0:T(8,128)(2,1)S(1)}, bf16[272,128]{1,0:T(8,128)(2,1)S(1)}, u32[]{:S(2)}, u32[]{:S(2)}) collective-permute-start(bf16[272,128]{1,0:T(8,128)(2,1)S(1)} %join.1.refs_0_), channel_id=1, source_target_pairs={{0,8},{1,5},{2,10},{3,7},{4,12},{5,1},{6,14},{7,3},{8,0},{9,13},{1... | collective-permute-start | bytes 208904 | tf_op jit(solution)/shard_map/ppermute | solution.py:373
  7.8 5.9 %collective-permute-start.3 = (bf16[144,128]{1,0:T(8,128)(2,1)S(1)}, bf16[144,128]{1,0:T(8,128)(2,1)S(1)}, u32[]{:S(2)}, u32[]{:S(2)}) collective-permute-start(bf16[144,128]{1,0:T(8,128)(2,1)S(1)} %copy-done.1), channel_id=1, source_target_pairs={{0,12},{1,13},{2,14},{3,15},{4,8},{5,9},{6,10},{7,11},{8,4},{9,5},... | collective-permute-start | bytes 110600 | tf_op jit(solution)/shard_map/ppermute | solution.py:373
  9.1 6.6 %collective-permute-start.7 = (bf16[272,128]{1,0:T(8,128)(2,1)S(1)}, bf16[272,128]{1,0:T(8,128)(2,1)S(1)}, u32[]{:S(2)}, u32[]{:S(2)}) collective-permute-start(bf16[272,128]{1,0:T(8,128)(2,1)S(1)} %join.1.refs_0_), channel_id=1, source_target_pairs={{0,6},{1,15},{2,4},{3,13},{4,2},{5,11},{6,0},{7,9},{8,14},{9,7},{1... | collective-permute-start | bytes 208904 | tf_op jit(solution)/shard_map/ppermute | solution.py:373
  10.3 6.2 %collective-permute-start.5 = (bf16[272,128]{1,0:T(8,128)(2,1)S(1)}, bf16[272,128]{1,0:T(8,128)(2,1)S(1)}, u32[]{:S(2)}, u32[]{:S(2)}) collective-permute-start(bf16[272,128]{1,0:T(8,128)(2,1)S(1)} %join.1.refs_0_), channel_id=1, source_target_pairs={{0,2},{1,11},{2,0},{3,9},{4,6},{5,15},{6,4},{7,13},{8,10},{9,3},{1... | collective-permute-start | bytes 208904 | tf_op jit(solution)/shard_map/ppermute | solution.py:373
  10.8 5.9 %collective-permute-start.2 = (bf16[272,128]{1,0:T(8,128)(2,1)S(1)}, bf16[272,128]{1,0:T(8,128)(2,1)S(1)}, u32[]{:S(2)}, u32[]{:S(2)}) collective-permute-start(bf16[272,128]{1,0:T(8,128)(2,1)S(1)} %collective-permute-done.1.refs_1_.refs_3_), channel_id=1, source_target_pairs={{0,1},{1,0},{2,3},{3,2},{4,5},{5,4},{6,7},{7,6},{8,9},{9,8},{10,11... | collective-permute-start | bytes 208904 | tf_op jit(solution)/shard_map/ppermute | solution.py:373
  13.6 3.1 %collective-permute-start.4 = (bf16[144,128]{1,0:T(8,128)(2,1)S(1)}, bf16[144,128]{1,0:T(8,128)(2,1)S(1)}, u32[]{:S(2)}, u32[]{:S(2)}) collective-permute-start(bf16[144,128]{1,0:T(8,128)(2,1)S(1)} %collective-permute-done.3.refs_5_), channel_id=1, source_target_pairs={{0,1},{1,0},{2,3},{3,2},{4,5},{5,4},{6,7},{7,6},{8,9},{9,8},{10,11... | collective-permute-start | bytes 110600 | tf_op jit(solution)/shard_map/ppermute | solution.py:373
  14.3 2.5 %copy-start.3 = (f32[128]{0:T(128)S(1)}, f32[128]{0:T(128)}, u32[]{:S(2)}) copy-start(f32[128]{0:T(128)} %param.11) | copy-start | bytes 1540
  14.3 2.5 %copy-start.4 = (f32[128]{0:T(128)S(1)}, f32[128]{0:T(128)}, u32[]{:S(2)}) copy-start(f32[128]{0:T(128)} %param.12) | copy-start | bytes 1540
  15.8 2.3 %collective-permute-start.8 = (bf16[272,128]{1,0:T(8,128)(2,1)S(1)}, bf16[272,128]{1,0:T(8,128)(2,1)S(1)}, u32[]{:S(2)}, u32[]{:S(2)}) collective-permute-start(bf16[272,128]{1,0:T(8,128)(2,1)S(1)} %collective-permute-done.7.refs_2_.refs_6_), channel_id=1, source_target_pairs={{0,1},{1,0},{2,3},{3,2},{4,5},{5,4},{6,7},{7,6},{8,9},{9,8},{10,11... | collective-permute-start | bytes 208904 | tf_op jit(solution)/shard_map/ppermute | solution.py:373
  16.5 1.6 %collective-permute-start.6 = (bf16[272,128]{1,0:T(8,128)(2,1)S(1)}, bf16[272,128]{1,0:T(8,128)(2,1)S(1)}, u32[]{:S(2)}, u32[]{:S(2)}) collective-permute-start(bf16[272,128]{1,0:T(8,128)(2,1)S(1)} %collective-permute-done.5.refs_0_.refs_4_), channel_id=1, source_target_pairs={{0,1},{1,0},{2,3},{3,2},{4,5},{5,4},{6,7},{7,6},{8,9},{9,8},{10,11... | collective-permute-start | bytes 208904 | tf_op jit(solution)/shard_map/ppermute | solution.py:373

commit v17 on v16

--- a/solution.py
+++ b/solution.py
@@ -208,12 +208,12 @@
     return ref[pl.ds(pl.multiple_of(row, SUB), SUB), :]
 
 
-def columns_kernel(n_row, n_col, side_x, chips, crop_ref, weights_ref, *refs):
+def columns_kernel(n_row, n_col, side_x, is_first, chips, crop_ref, weights_ref, *refs):
     count = sum(width for width, _ in chips)
     chip_list, refs = split_chips(refs[:count], chips), refs[count:]
-    own_ref = None
-    if side_x == 0:
-        act_ref, in_gain_ref, out_gain_ref, *refs, own_ref, gains_ref = refs
+    gate_ref = None
+    if is_first:
+        act_ref, in_gain_ref, out_gain_ref, *refs, gains_ref, own_ref = refs
         z_hat, z_inverse = normalize(act_ref[...].astype(jnp.float32).reshape(own_ref.shape[1:]))
         own_ref[0] = z_hat
         own_ref[1] = jnp.broadcast_to(z_inverse, z_hat.shape)
@@ -221,6 +221,8 @@
         gains_ref[1:2] = out_gain_ref[...]
     else:
         gains_ref, *refs = refs
+        if side_x == 0:
+            *refs, gate_ref = refs
     tri_in, (tri_ref, left_ref, right_ref, side_ref, back_ref, flip_ref) = refs[:-6], refs[-6:]
     channels = weights_ref.shape[-1]
     tile = SUB * SUB
@@ -257,8 +259,8 @@
         side_ref[2 * side] = masked
         side_ref[2 * side + 1] = act * (1.0 - gate)
     out_gate = jax.nn.sigmoid(jnp.dot(normed, weights_ref[4], preferred_element_type=f32))
-    if own_ref is not None:
-        own_ref[2] = out_gate[0:tile]
+    if gate_ref is not None:
+        gate_ref[...] = out_gate[0:tile]
     cot = jnp.concatenate([chip_rows(cot_rows, chip, core, on) for chip, on, core, _ in chip_list], axis=0)
     grad = cot.astype(f32) * out_gate
     grad_lin = grad.astype(bf16)
@@ -288,7 +290,7 @@
     triangle(n_row, n_col, 2, flipped, along, start, store)
 
 
-def rest_kernel(n_row, n_col, weights_ref, own_ref, gains_ref, tri_ref, *refs):
+def rest_kernel(n_row, n_col, weights_ref, gains_ref, own_ref, gate_ref, tri_ref, *refs):
     groups = [refs[at * 5 : at * 5 + 5] for at in range(n_col // 2)]
     update_ref, pair_grad_ref, weight_grad_ref, back_ref, hat_ref, d_ref = refs[5 * (n_col // 2) :]
     channels = tri_ref.shape[-1]
@@ -310,7 +312,7 @@
         hat_ref[rows, :] = normed_out
         lin = jnp.dot(normed_out, weights_ref[5], preferred_element_type=f32)
         if col == 0:
-            update_ref[...] = (own_ref[2] * lin[0:tile]).astype(bf16).reshape(update_ref.shape)
+            update_ref[...] = (gate_ref[...] * lin[0:tile]).astype(bf16).reshape(update_ref.shape)
         d_ref[rows, 4 * channels : 5 * channels] = (backs_ref[0] * lin).astype(bf16)
         back = backs_ref[1]
         second = jnp.mean(back * x_hat, axis=-1, keepdims=True)
@@ -369,7 +371,8 @@
     for row in range(n_row):
         for col in range(n_col):
             shift = odd if col % 2 else even
-            pairs.append((row * n_col + col, (row ^ shift[0]) * n_col + (col ^ shift[1])))
+            if shift is not None:
+                pairs.append((row * n_col + col, (row ^ shift[0]) * n_col + (col ^ shift[1])))
     return lax.ppermute(block, ("row", "col"), pairs)
 
 
@@ -427,42 +430,44 @@
         out_specs=vmem,
         compiler_params=limit(2),
     )(held, other(own))
-    straight = move(own, (3, 0), (3, 0))
     first = move(both, (2, 0), (1, 0))
     second = move(both, (0, 2), (2, 2))
     third = move(both, (1, 2), (3, 2))
-    straight, first, second, third = [(block, other(block)) for block in (straight, first, second, third)]
-    chips = (((1, None), (2, 1), (2, 0), (2, None)), ((2, 0), (2, 0), (2, 1), (2, 1)))
-    sources = ((both, *first, *first, *straight), (*second, *third, *second, *third))
-
-    tri, parts, extra = [], [], []
-    for side_x in range(n_col // 2):
-        more = (pair_act, in_gain, out_gain) if side_x == 0 else (extra[1], *tri)
-        more_shapes = () if side_x > 0 else (
-            jax.ShapeDtypeStruct((3, tile, channels), f32),
-            jax.ShapeDtypeStruct((SUB, channels), f32),
+    relayed = move(first, (1, 0), None)
+    first, second, third, relayed = [(block, other(block)) for block in (first, second, third, relayed)]
+    chips = (((1, None), (2, 1), (2, 0), (2, 0)), ((2, 0), (2, 0), (2, 1), (2, 1)))
+    sources = ((both, *first, *first, *relayed), (*second, *third, *second, *third))
+
+    tri, parts, extra = [], {}, []
+    for side_x in reversed(range(n_col // 2)):
+        more = (pair_act, in_gain, out_gain) if len(tri) == 0 else (extra[0], *tri)
+        shapes = (
+            jax.ShapeDtypeStruct((pairs, channels), f32),
+            jax.ShapeDtypeStruct((2 * size, channels), f32),
+            jax.ShapeDtypeStruct((2 * size, channels), f32),
+            jax.ShapeDtypeStruct((4, 2 * size, channels), f32),
+            jax.ShapeDtypeStruct((2, 2 * size, channels), f32),
+            jax.ShapeDtypeStruct((2, channels, 2 * size), bf16),
         )
+        if len(tri) == 0:
+            shapes += (jax.ShapeDtypeStruct((SUB, channels), f32), jax.ShapeDtypeStruct((2, tile, channels), f32))
+        elif side_x == 0:
+            shapes += (jax.ShapeDtypeStruct((tile, channels), f32),)
+        alias = {3 + len(sources[side_x]): 0} if len(tri) > 0 else {}
         tri, *results = pl.pallas_call(
-            functools.partial(columns_kernel, n_row, n_col, side_x, chips[side_x]),
+            functools.partial(columns_kernel, n_row, n_col, side_x, len(tri) == 0, chips[side_x]),
             name=f"columns_{side_x}",
-            out_shape=(
-                jax.ShapeDtypeStruct((pairs, channels), f32),
-                jax.ShapeDtypeStruct((2 * size, channels), f32),
-                jax.ShapeDtypeStruct((2 * size, channels), f32),
-                jax.ShapeDtypeStruct((4, 2 * size, channels), f32),
-                jax.ShapeDtypeStruct((2, 2 * size, channels), f32),
-                jax.ShapeDtypeStruct((2, channels, 2 * size), bf16),
-                *more_shapes,
-            ),
+            out_shape=shapes,
             in_specs=[smem] + [vmem] * (1 + len(sources[side_x]) + len(more)),
-            out_specs=(vmem,) * (6 + len(more_shapes)),
-            input_output_aliases={3 + len(sources[side_x]): 0} if side_x > 0 else {},
+            out_specs=(vmem,) * len(shapes),
+            input_output_aliases=alias,
             compiler_params=limit(12),
             cost_estimate=pl.CostEstimate(flops=800_000_000, bytes_accessed=1_000_000, transcendentals=0),
         )(crop_length, weights, *sources[side_x], *more)
         tri = [tri]
-        parts += results[:5]
+        parts[side_x] = results[:5]
         extra += results[5:]
+    parts = [array for side_x in range(n_col // 2) for array in parts[side_x]]
 
     return pl.pallas_call(
         functools.partial(rest_kernel, n_row, n_col),
@@ -472,7 +477,7 @@
             jax.ShapeDtypeStruct(pair_act.shape, bf16),
             jax.ShapeDtypeStruct(weights.shape, f32),
         ),
-        in_specs=[vmem] * (4 + len(parts)),
+        in_specs=[vmem] * (5 + len(parts)),
         out_specs=(vmem, vmem, vmem),
         scratch_shapes=[
             pltpu.VMEM((pairs, channels), f32),

time: 24.2 us -> 26.2 us (1.083)
  the two profiles are of different devices: /device:TPU:0 before, /device:TPU:31 now
where the time goes in v17:
time: 26.2 us; the launch traced here: 25.8 us
  starting transfers between devices  12.7 us (48%)
  Pallas kernels  8.65 us (33%)
  waiting for transfers between devices  2.28 us (9%)
  between operations  1.39 us (5%)
  local copies, waits for them, and re-layouts  0.79 us (3%)
    ppermute x9, starting transfers between devices, flip(): return lax.ppermute(block, ('row', 'col'), pairs)  12.7 us
    pallas_call x1, Pallas kernels, gathered_body(): pl.pallas_call(functools.partial(rest_kernel, n_row, n_col), name='rest',...  4.45 us
    pallas_call x2, Pallas kernels, gathered_body(): pl.pallas_call(functools.partial(columns_kernel, n_row, n_col, side_x, le...  2.59 us
    ppermute x9, waiting for transfers between devices, flip(): return lax.ppermute(block, ('row', 'col'), pairs)  2.28 us
    pallas_call x1, Pallas kernels, gathered_body(): pl.pallas_call(pack_kernel, name='pack', out_shape=jax.ShapeDtypeStruct((...  1.6 us
    unnamed x10, local copies, waits for them, and re-layouts  0.79 us
  transfers between devices with their start and end apart: 9, of which 2 were waited for; matrix products, arithmetic and copies ran while one was open for 0% of the time, Pallas kernels for 5%

profile of v17, /device:TPU:31, one launch (start us, length us, event | category | flops | bytes accessed | tf_op | source)
XLA Modules:
  0.0 25.8 jit_solution(15576254899906472487)
XLA Ops:
  0.6 1.6 %pack.1.in_ref = bf16[144,128]{1,0:T(8,128)(2,1)} custom-call(bf16[8,8,128]{2,1,0:T(8,128)(2,1)} %refs_8_.1, s32[8,8]{1,0:T(8,128)} %mask_hbm.1, bf16[64,128]{1,0:T(8,128)(2,1)} %bitcast.6, f32[1,128]{1,0:T(1,128)} %bitcast.3), custom_call_target="tpu_custom_call" | custom-call | tf_op jit(solution)/shard_map/pack/pallas_call | solution.py:394
  2.2 0.0 copy-start
  2.2 0.7 %collective-permute-start = (bf16[144,128]{1,0:T(8,128)(2,1)}, bf16[144,128]{1,0:T(8,128)(2,1)S(1)}, u32[]{:S(2)}, u32[]{:S(2)}) collective-permute-start(bf16[144,128]{1,0:T(8,128)(2,1)} %pack.1.in_ref), channel_id=1, source_target_pairs={{0,1},{1,0},{2,3},{3,2},{4,5},{5,4},{6,7},{7,6},{8,9},{9,8},{10,11... | collective-permute-start | bytes 110600 | tf_op jit(solution)/shard_map/ppermute | solution.py:376
  3.0 0.0 copy-start.1
  3.0 0.8 %copy-done.1 = bf16[144,128]{1,0:T(8,128)(2,1)S(1)} copy-done((bf16[144,128]{1,0:T(8,128)(2,1)S(1)}, bf16[144,128]{1,0:T(8,128)(2,1)}, u32[]{:S(2)}) %copy-start.1) | copy-done | bytes 36888
  3.8 0.0 copy-start.2
  3.8 0.3 %collective-permute-done.twin_ref = bf16[144,128]{1,0:T(8,128)(2,1)S(1)} collective-permute-done((bf16[144,128]{1,0:T(8,128)(2,1)}, bf16[144,128]{1,0:T(8,128)(2,1)S(1)}, u32[]{:S(2)}, u32[]{:S(2)}) %collective-permute-start) | collective-permute-done | bytes 36896 | tf_op jit(solution)/shard_map/ppermute | solution.py:376
  4.1 0.2 collective-permute-start.5
  4.2 1.0 %collective-permute-start.3 = (bf16[272,128]{1,0:T(8,128)(2,1)S(1)}, bf16[272,128]{1,0:T(8,128)(2,1)S(1)}, u32[]{:S(2)}, u32[]{:S(2)}) collective-permute-start(bf16[272,128]{1,0:T(8,128)(2,1)S(1)} %join.1.refs_0_), channel_id=1, source_target_pairs={{0,6},{1,15},{2,4},{3,13},{4,2},{5,11},{6,0},{7,9},{8,14},{9,7},{1... | collective-permute-start | bytes 208904 | tf_op jit(solution)/shard_map/ppermute | solution.py:376
  5.3 2.3 %collective-permute-start.1 = (bf16[272,128]{1,0:T(8,128)(2,1)S(1)}, bf16[272,128]{1,0:T(8,128)(2,1)S(1)}, u32[]{:S(2)}, u32[]{:S(2)}) collective-permute-start(bf16[272,128]{1,0:T(8,128)(2,1)S(1)} %join.1.refs_0_), channel_id=1, source_target_pairs={{0,2},{1,11},{2,0},{3,9},{4,6},{5,15},{6,4},{7,13},{8,10},{9,3},{1... | collective-permute-start | bytes 208904 | tf_op jit(solution)/shard_map/ppermute | solution.py:376
  7.6 0.0 collective-permute-done.5.refs_1_.refs_3_
  7.6 0.7 %collective-permute-start.7 = (bf16[272,128]{1,0:T(8,128)(2,1)S(1)}, bf16[272,128]{1,0:T(8,128)(2,1)S(1)}, u32[]{:S(2)}, u32[]{:S(2)}) collective-permute-start(bf16[272,128]{1,0:T(8,128)(2,1)S(1)} %collective-permute-done.5.refs_1_.refs_3_), channel_id=1, source_target_pairs={{0,4},{2,6},{4,0},{6,2},{8,12},{10,14},{12,8},{14,10},{16,20},{18,... | collective-permute-start | bytes 208904 | tf_op jit(solution)/shard_map/ppermute | solution.py:376
  8.3 2.0 %collective-permute-done.3.refs_2_.refs_6_ = bf16[272,128]{1,0:T(8,128)(2,1)S(1)} collective-permute-done((bf16[272,128]{1,0:T(8,128)(2,1)S(1)}, bf16[272,128]{1,0:T(8,128)(2,1)S(1)}, u32[]{:S(2)}, u32[]{:S(2)}) %collective-permute-start.3) | collective-permute-done | bytes 69664 | tf_op jit(solution)/shard_map/ppermute | solution.py:376
  10.3 4.3 %collective-permute-start.4 = (bf16[272,128]{1,0:T(8,128)(2,1)S(1)}, bf16[272,128]{1,0:T(8,128)(2,1)S(1)}, u32[]{:S(2)}, u32[]{:S(2)}) collective-permute-start(bf16[272,128]{1,0:T(8,128)(2,1)S(1)} %collective-permute-done.3.refs_2_.refs_6_), channel_id=1, source_target_pairs={{0,1},{1,0},{2,3},{3,2},{4,5},{5,4},{6,7},{7,6},{8,9},{9,8},{10,11... | collective-permute-start | bytes 208904 | tf_op jit(solution)/shard_map/ppermute | solution.py:376
  14.5 0.0 collective-permute-done.1.refs_0_.refs_4_
  14.5 0.1 collective-permute-start.2
  15.3 0.0 copy-start.3
  15.3 0.0 copy-start.4
  15.3 0.5 %collective-permute-start.6 = (bf16[272,128]{1,0:T(8,128)(2,1)S(1)}, bf16[272,128]{1,0:T(8,128)(2,1)S(1)}, u32[]{:S(2)}, u32[]{:S(2)}) collective-permute-start(bf16[272,128]{1,0:T(8,128)(2,1)S(1)} %collective-permute-done.5.refs_1_.refs_3_), channel_id=1, source_target_pairs={{0,1},{1,0},{2,3},{3,2},{4,5},{5,4},{6,7},{7,6},{8,9},{9,8},{10,11... | collective-permute-start | bytes 208904 | tf_op jit(solution)/shard_map/ppermute | solution.py:376
  15.8 0.0 collective-permute-done.7.refs_5_
  15.8 2.9 %collective-permute-start.8 = (bf16[272,128]{1,0:T(8,128)(2,1)S(1)}, bf16[272,128]{1,0:T(8,128)(2,1)S(1)}, u32[]{:S(2)}, u32[]{:S(2)}) collective-permute-start(bf16[272,128]{1,0:T(8,128)(2,1)S(1)} %collective-permute-done.7.refs_5_), channel_id=1, source_target_pairs={{0,1},{1,0},{2,3},{3,2},{4,5},{5,4},{6,7},{7,6},{8,9},{9,8},{10,11... | collective-permute-start | bytes 208904 | tf_op jit(solution)/shard_map/ppermute | solution.py:376
  18.7 0.0 collective-permute-done.4.refs_3_.refs_7_
  18.7 0.0 collective-permute-done.2.refs_1_.refs_5_
  18.7 0.0 copy-done
  18.7 0.0 copy-done.2
  18.7 0.0 copy-done.3
  18.8 0.0 copy-done.4
  18.8 1.3 %columns_1.1 = (f32[1024,128]{1,0:T(8,128)S(1)}, f32[512,128]{1,0:T(8,128)S(1)}, f32[512,128]{1,0:T(8,128)S(1)}, f32[4,512,128]{2,1,0:T(8,128)S(1)}, f32[2,512,1...) custom-call(s32[1]{0:T(128)S(6)} %copy.12.crop_ref, ...), custom_call_target="tpu_custom_call" | custom-call | flops 800000000 | bytes 1000000 | tf_op jit(solution)/shard_map/columns_1/pallas_call | solution.py:457
  20.0 0.0 collective-permute-done.6.refs_2_.refs_4_
  20.1 0.0 collective-permute-done.8.refs_6_
  20.1 1.3 %columns_0.1 = (f32[1024,128]{1,0:T(8,128)S(1)}, f32[512,128]{1,0:T(8,128)S(1)}, f32[512,128]{1,0:T(8,128)S(1)}, f32[4,512,128]{2,1,0:T(8,128)S(1)}, f32[2,512,1...) custom-call(s32[1]{0:T(128)S(6)} %copy.12.crop_ref, ...), custom_call_target="tpu_custom_call", output_to_operand_aliasing={{0}: (10, {})} | custom-call | flops 800000000 | bytes 1000000 | tf_op jit(solution)/shard_map/columns_0/pallas_call | solution.py:457
  21.4 4.5 %rest.1 = (bf16[8,8,128]{2,1,0:T(8,128)(2,1)}, bf16[8,8,128]{2,1,0:T(8,128)(2,1)}, f32[6,128,128]{2,1,0:T(8,128)}) custom-call(bf16[6,128,128]{2,1,0:T(8,128)(2,1)S(1)} %copy-done, f32[8,128]{1,0:T(8,128)S(1)} %get-tuple-element.22.refs_7_.gains_ref, f32[2,64,128]{2,1,0:T(8,128)S(1)} %get-tuple-element.23.own_ref, f32[64,128]{1,0:T(8,128)S(1)} %get-tuple-element.25.gate_ref, ...), custom_call_target="tpu_custom_call" | custom-call | tf_op jit(solution)/shard_map/rest/pallas_call | solution.py:472
  (2 shorter events, 0.0 us)
Async XLA Ops:
  2.2 16.5 %copy-start = (bf16[6,128,128]{2,1,0:T(8,128)(2,1)S(1)}, bf16[6,128,128]{2,1,0:T(8,128)(2,1)}, u32[]{:S(2)}) copy-start(bf16[6,128,128]{2,1,0:T(8,128)(2,1)} %weights_ref.5) | copy-start | bytes 589828
  2.2 1.8 %collective-permute-start = (bf16[144,128]{1,0:T(8,128)(2,1)}, bf16[144,128]{1,0:T(8,128)(2,1)S(1)}, u32[]{:S(2)}, u32[]{:S(2)}) collective-permute-start(bf16[144,128]{1,0:T(8,128)(2,1)} %pack.1.in_ref), channel_id=1, source_target_pairs={{0,1},{1,0},{2,3},{3,2},{4,5},{5,4},{6,7},{7,6},{8,9},{9,8},{10,11... | collective-permute-start | bytes 110600 | tf_op jit(solution)/shard_map/ppermute | solution.py:376
  3.0 0.8 %copy-start.1 = (bf16[144,128]{1,0:T(8,128)(2,1)S(1)}, bf16[144,128]{1,0:T(8,128)(2,1)}, u32[]{:S(2)}) copy-start(bf16[144,128]{1,0:T(8,128)(2,1)} %pack.1.in_ref) | copy-start | bytes 110596
  3.8 15.0 %copy-start.2 = (bf16[8,8,128]{2,1,0:T(8,128)(2,1)S(1)}, bf16[8,8,128]{2,1,0:T(8,128)(2,1)}, u32[]{:S(2)}) copy-start(bf16[8,8,128]{2,1,0:T(8,128)(2,1)} %refs_8_.1) | copy-start | bytes 49156
  4.1 3.6 %collective-permute-start.5 = (bf16[272,128]{1,0:T(8,128)(2,1)S(1)}, bf16[272,128]{1,0:T(8,128)(2,1)S(1)}, u32[]{:S(2)}, u32[]{:S(2)}) collective-permute-start(bf16[272,128]{1,0:T(8,128)(2,1)S(1)} %join.1.refs_0_), channel_id=1, source_target_pairs={{0,8},{1,5},{2,10},{3,7},{4,12},{5,1},{6,14},{7,3},{8,0},{9,13},{1... | collective-permute-start | bytes 208904 | tf_op jit(solution)/shard_map/ppermute | solution.py:376
  4.2 6.0 %collective-permute-start.3 = (bf16[272,128]{1,0:T(8,128)(2,1)S(1)}, bf16[272,128]{1,0:T(8,128)(2,1)S(1)}, u32[]{:S(2)}, u32[]{:S(2)}) collective-permute-start(bf16[272,128]{1,0:T(8,128)(2,1)S(1)} %join.1.refs_0_), channel_id=1, source_target_pairs={{0,6},{1,15},{2,4},{3,13},{4,2},{5,11},{6,0},{7,9},{8,14},{9,7},{1... | collective-permute-start | bytes 208904 | tf_op jit(solution)/shard_map/ppermute | solution.py:376
  5.3 9.2 %collective-permute-start.1 = (bf16[272,128]{1,0:T(8,128)(2,1)S(1)}, bf16[272,128]{1,0:T(8,128)(2,1)S(1)}, u32[]{:S(2)}, u32[]{:S(2)}) collective-permute-start(bf16[272,128]{1,0:T(8,128)(2,1)S(1)} %join.1.refs_0_), channel_id=1, source_target_pairs={{0,2},{1,11},{2,0},{3,9},{4,6},{5,15},{6,4},{7,13},{8,10},{9,3},{1... | collective-permute-start | bytes 208904 | tf_op jit(solution)/shard_map/ppermute | solution.py:376
  7.6 8.2 %collective-permute-start.7 = (bf16[272,128]{1,0:T(8,128)(2,1)S(1)}, bf16[272,128]{1,0:T(8,128)(2,1)S(1)}, u32[]{:S(2)}, u32[]{:S(2)}) collective-permute-start(bf16[272,128]{1,0:T(8,128)(2,1)S(1)} %collective-permute-done.5.refs_1_.refs_3_), channel_id=1, source_target_pairs={{0,4},{2,6},{4,0},{6,2},{8,12},{10,14},{12,8},{14,10},{16,20},{18,... | collective-permute-start | bytes 208904 | tf_op jit(solution)/shard_map/ppermute | solution.py:376
  10.3 8.5 %collective-permute-start.4 = (bf16[272,128]{1,0:T(8,128)(2,1)S(1)}, bf16[272,128]{1,0:T(8,128)(2,1)S(1)}, u32[]{:S(2)}, u32[]{:S(2)}) collective-permute-start(bf16[272,128]{1,0:T(8,128)(2,1)S(1)} %collective-permute-done.3.refs_2_.refs_6_), channel_id=1, source_target_pairs={{0,1},{1,0},{2,3},{3,2},{4,5},{5,4},{6,7},{7,6},{8,9},{9,8},{10,11... | collective-permute-start | bytes 208904 | tf_op jit(solution)/shard_map/ppermute | solution.py:376
  14.5 4.2 %collective-permute-start.2 = (bf16[272,128]{1,0:T(8,128)(2,1)S(1)}, bf16[272,128]{1,0:T(8,128)(2,1)S(1)}, u32[]{:S(2)}, u32[]{:S(2)}) collective-permute-start(bf16[272,128]{1,0:T(8,128)(2,1)S(1)} %collective-permute-done.1.refs_0_.refs_4_), channel_id=1, source_target_pairs={{0,1},{1,0},{2,3},{3,2},{4,5},{5,4},{6,7},{7,6},{8,9},{9,8},{10,11... | collective-permute-start | bytes 208904 | tf_op jit(solution)/shard_map/ppermute | solution.py:376
  15.3 3.5 %copy-start.3 = (f32[128]{0:T(128)S(1)}, f32[128]{0:T(128)}, u32[]{:S(2)}) copy-start(f32[128]{0:T(128)} %param.11) | copy-start | bytes 1540
  15.3 3.5 %copy-start.4 = (f32[128]{0:T(128)S(1)}, f32[128]{0:T(128)}, u32[]{:S(2)}) copy-start(f32[128]{0:T(128)} %param.12) | copy-start | bytes 1540
  15.3 4.8 %collective-permute-start.6 = (bf16[272,128]{1,0:T(8,128)(2,1)S(1)}, bf16[272,128]{1,0:T(8,128)(2,1)S(1)}, u32[]{:S(2)}, u32[]{:S(2)}) collective-permute-start(bf16[272,128]{1,0:T(8,128)(2,1)S(1)} %collective-permute-done.5.refs_1_.refs_3_), channel_id=1, source_target_pairs={{0,1},{1,0},{2,3},{3,2},{4,5},{5,4},{6,7},{7,6},{8,9},{9,8},{10,11... | collective-permute-start | bytes 208904 | tf_op jit(solution)/shard_map/ppermute | solution.py:376
  15.8 4.3 %collective-permute-start.8 = (bf16[272,128]{1,0:T(8,128)(2,1)S(1)}, bf16[272,128]{1,0:T(8,128)(2,1)S(1)}, u32[]{:S(2)}, u32[]{:S(2)}) collective-permute-start(bf16[272,128]{1,0:T(8,128)(2,1)S(1)} %collective-permute-done.7.refs_5_), channel_id=1, source_target_pairs={{0,1},{1,0},{2,3},{3,2},{4,5},{5,4},{6,7},{7,6},{8,9},{9,8},{10,11... | collective-permute-start | bytes 208904 | tf_op jit(solution)/shard_map/ppermute | solution.py:376

commit v18 on v17

--- a/solution.py
+++ b/solution.py
@@ -132,6 +132,10 @@
     out_ref[...] = in_ref[...]
 
 
+def token_kernel(*refs):
+    refs[-1][...] = jnp.zeros(refs[-1].shape, refs[-1].dtype)
+
+
 def join_kernel(own_ref, twin_ref, out_ref):
     tile = SUB * SUB
     refs = (own_ref, twin_ref)
@@ -220,7 +224,7 @@
         gains_ref[0:1] = in_gain_ref[...]
         gains_ref[1:2] = out_gain_ref[...]
     else:
-        gains_ref, *refs = refs
+        _, gains_ref, *refs = refs
         if side_x == 0:
             *refs, gate_ref = refs
     tri_in, (tri_ref, left_ref, right_ref, side_ref, back_ref, flip_ref) = refs[:-6], refs[-6:]
@@ -430,17 +434,27 @@
         out_specs=vmem,
         compiler_params=limit(2),
     )(held, other(own))
+    straight = move(own, (3, 0), (3, 0))
     first = move(both, (2, 0), (1, 0))
     second = move(both, (0, 2), (2, 2))
     third = move(both, (1, 2), (3, 2))
-    relayed = move(first, (1, 0), None)
-    first, second, third, relayed = [(block, other(block)) for block in (first, second, third, relayed)]
-    chips = (((1, None), (2, 1), (2, 0), (2, 0)), ((2, 0), (2, 0), (2, 1), (2, 1)))
-    sources = ((both, *first, *first, *relayed), (*second, *third, *second, *third))
+    straight, first, second, third = [(block, other(block)) for block in (straight, first, second, third)]
+    chips = (((1, None), (2, 1), (2, 0), (2, None)), ((2, 0), (2, 0), (2, 1), (2, 1)))
+    sources = ((both, *first, *first, *straight), (*second, *third, *second, *third))
+    anywhere = pl.BlockSpec(memory_space=pl.ANY)
+    token = pl.pallas_call(
+        token_kernel,
+        name="token",
+        out_shape=jax.ShapeDtypeStruct((SUB, channels), f32),
+        in_specs=[anywhere] * 2,
+        out_specs=vmem,
+        compiler_params=limit(2),
+        cost_estimate=pl.CostEstimate(flops=1_000_000_000, bytes_accessed=1_000_000, transcendentals=0),
+    )(*straight)
 
     tri, parts, extra = [], {}, []
     for side_x in reversed(range(n_col // 2)):
-        more = (pair_act, in_gain, out_gain) if len(tri) == 0 else (extra[0], *tri)
+        more = (pair_act, in_gain, out_gain) if len(tri) == 0 else (token, extra[0], *tri)
         shapes = (
             jax.ShapeDtypeStruct((pairs, channels), f32),
             jax.ShapeDtypeStruct((2 * size, channels), f32),
@@ -453,7 +467,7 @@
             shapes += (jax.ShapeDtypeStruct((SUB, channels), f32), jax.ShapeDtypeStruct((2, tile, channels), f32))
         elif side_x == 0:
             shapes += (jax.ShapeDtypeStruct((tile, channels), f32),)
-        alias = {3 + len(sources[side_x]): 0} if len(tri) > 0 else {}
+        alias = {4 + len(sources[side_x]): 0} if len(tri) > 0 else {}
         tri, *results = pl.pallas_call(
             functools.partial(columns_kernel, n_row, n_col, side_x, len(tri) == 0, chips[side_x]),
             name=f"columns_{side_x}",

time: 26.2 us -> 24.3 us (0.927)
  the two profiles are of different devices: /device:TPU:31 before, /device:TPU:0 now
where the time goes in v18:
time: 24.3 us; the launch traced here: 23.8 us
  starting transfers between devices  11.4 us (47%)
  Pallas kernels  8.65 us (36%)
  waiting for transfers between devices  1.62 us (7%)
  between operations  1.35 us (6%)
  local copies, waits for them, and re-layouts  0.82 us (3%)
    ppermute x9, starting transfers between devices, flip(): return lax.ppermute(block, ('row', 'col'), pairs)  11.4 us
    pallas_call x1, Pallas kernels, gathered_body(): pl.pallas_call(functools.partial(rest_kernel, n_row, n_col), name='rest',...  4.45 us
    pallas_call x2, Pallas kernels, gathered_body(): pl.pallas_call(functools.partial(columns_kernel, n_row, n_col, side_x, le...  2.59 us
    ppermute x9, waiting for transfers between devices, flip(): return lax.ppermute(block, ('row', 'col'), pairs)  1.62 us
    pallas_call x1, Pallas kernels, gathered_body(): pl.pallas_call(pack_kernel, name='pack', out_shape=jax.ShapeDtypeStruct((...  1.6 us
    unnamed x10, local copies, waits for them, and re-layouts  0.82 us
  transfers between devices with their start and end apart: 9, of which 4 were waited for; matrix products, arithmetic and copies ran while one was open for 0% of the time, Pallas kernels for 5%

profile of v18, /device:TPU:0, one launch (start us, length us, event | category | flops | bytes accessed | tf_op | source)
XLA Modules:
  0.0 23.8 jit_solution(12190048260774385930)
XLA Ops:
  0.6 1.6 %pack.1.in_ref = bf16[144,128]{1,0:T(8,128)(2,1)} custom-call(bf16[8,8,128]{2,1,0:T(8,128)(2,1)} %refs_8_.1, s32[8,8]{1,0:T(8,128)} %mask_hbm.1, bf16[64,128]{1,0:T(8,128)(2,1)} %bitcast.6, f32[1,128]{1,0:T(1,128)} %bitcast.3), custom_call_target="tpu_custom_call" | custom-call | tf_op jit(solution)/shard_map/pack/pallas_call | solution.py:398
  2.2 0.5 %collective-permute-start = (bf16[144,128]{1,0:T(8,128)(2,1)}, bf16[144,128]{1,0:T(8,128)(2,1)S(1)}, u32[]{:S(2)}, u32[]{:S(2)}) collective-permute-start(bf16[144,128]{1,0:T(8,128)(2,1)} %pack.1.in_ref), channel_id=1, source_target_pairs={{0,1},{1,0},{2,3},{3,2},{4,5},{5,4},{6,7},{7,6},{8,9},{9,8},{10,11... | collective-permute-start | bytes 110600 | tf_op jit(solution)/shard_map/ppermute | solution.py:380
  2.8 4.7 %collective-permute-start.7 = (bf16[144,128]{1,0:T(8,128)(2,1)}, bf16[144,128]{1,0:T(8,128)(2,1)S(1)}, u32[]{:S(2)}, u32[]{:S(2)}) collective-permute-start(bf16[144,128]{1,0:T(8,128)(2,1)} %pack.1.in_ref), channel_id=1, source_target_pairs={{0,12},{1,13},{2,14},{3,15},{4,8},{5,9},{6,10},{7,11},{8,4},{9,5},... | collective-permute-start | bytes 110600 | tf_op jit(solution)/shard_map/ppermute | solution.py:380
  7.4 0.0 copy-start.1
  7.4 0.8 %copy-done.1 = bf16[144,128]{1,0:T(8,128)(2,1)S(1)} copy-done((bf16[144,128]{1,0:T(8,128)(2,1)S(1)}, bf16[144,128]{1,0:T(8,128)(2,1)}, u32[]{:S(2)}) %copy-start.1) | copy-done | bytes 36888
  8.2 0.0 collective-permute-done.twin_ref
  8.2 0.5 %collective-permute-start.3 = (bf16[272,128]{1,0:T(8,128)(2,1)S(1)}, bf16[272,128]{1,0:T(8,128)(2,1)S(1)}, u32[]{:S(2)}, u32[]{:S(2)}) collective-permute-start(bf16[272,128]{1,0:T(8,128)(2,1)S(1)} %join.1.refs_0_), channel_id=1, source_target_pairs={{0,6},{1,15},{2,4},{3,13},{4,2},{5,11},{6,0},{7,9},{8,14},{9,7},{1... | collective-permute-start | bytes 208904 | tf_op jit(solution)/shard_map/ppermute | solution.py:380
  8.8 1.1 %collective-permute-start.1 = (bf16[272,128]{1,0:T(8,128)(2,1)S(1)}, bf16[272,128]{1,0:T(8,128)(2,1)S(1)}, u32[]{:S(2)}, u32[]{:S(2)}) collective-permute-start(bf16[272,128]{1,0:T(8,128)(2,1)S(1)} %join.1.refs_0_), channel_id=1, source_target_pairs={{0,2},{1,11},{2,0},{3,9},{4,6},{5,15},{6,4},{7,13},{8,10},{9,3},{1... | collective-permute-start | bytes 208904 | tf_op jit(solution)/shard_map/ppermute | solution.py:380
  9.9 0.0 collective-permute-done.7.refs_0_.refs_5_
  9.9 0.0 collective-permute-start.8
  10.5 0.0 copy-start
  10.6 0.0 copy-start.2
  10.6 2.4 %collective-permute-start.5 = (bf16[272,128]{1,0:T(8,128)(2,1)S(1)}, bf16[272,128]{1,0:T(8,128)(2,1)S(1)}, u32[]{:S(2)}, u32[]{:S(2)}) collective-permute-start(bf16[272,128]{1,0:T(8,128)(2,1)S(1)} %join.1.refs_0_), channel_id=1, source_target_pairs={{0,8},{1,5},{2,10},{3,7},{4,12},{5,1},{6,14},{7,3},{8,0},{9,13},{1... | collective-permute-start | bytes 208904 | tf_op jit(solution)/shard_map/ppermute | solution.py:380
  13.0 0.7 %collective-permute-done.3.refs_2_.refs_6_ = bf16[272,128]{1,0:T(8,128)(2,1)S(1)} collective-permute-done((bf16[272,128]{1,0:T(8,128)(2,1)S(1)}, bf16[272,128]{1,0:T(8,128)(2,1)S(1)}, u32[]{:S(2)}, u32[]{:S(2)}) %collective-permute-start.3) | collective-permute-done | bytes 69664 | tf_op jit(solution)/shard_map/ppermute | solution.py:380
  13.6 0.8 %collective-permute-start.4 = (bf16[272,128]{1,0:T(8,128)(2,1)S(1)}, bf16[272,128]{1,0:T(8,128)(2,1)S(1)}, u32[]{:S(2)}, u32[]{:S(2)}) collective-permute-start(bf16[272,128]{1,0:T(8,128)(2,1)S(1)} %collective-permute-done.3.refs_2_.refs_6_), channel_id=1, source_target_pairs={{0,1},{1,0},{2,3},{3,2},{4,5},{5,4},{6,7},{7,6},{8,9},{9,8},{10,11... | collective-permute-start | bytes 208904 | tf_op jit(solution)/shard_map/ppermute | solution.py:380
  14.4 0.2 collective-permute-done.1.refs_0_.refs_4_
  14.7 1.2 %collective-permute-start.2 = (bf16[272,128]{1,0:T(8,128)(2,1)S(1)}, bf16[272,128]{1,0:T(8,128)(2,1)S(1)}, u32[]{:S(2)}, u32[]{:S(2)}) collective-permute-start(bf16[272,128]{1,0:T(8,128)(2,1)S(1)} %collective-permute-done.1.refs_0_.refs_4_), channel_id=1, source_target_pairs={{0,1},{1,0},{2,3},{3,2},{4,5},{5,4},{6,7},{7,6},{8,9},{9,8},{10,11... | collective-permute-start | bytes 208904 | tf_op jit(solution)/shard_map/ppermute | solution.py:380
  15.9 0.0 collective-permute-done.8.refs_1_.refs_6_
  15.9 0.0 copy-start.3
  15.9 0.0 copy-start.4
  15.9 0.3 %collective-permute-done.5.refs_1_.refs_3_ = bf16[272,128]{1,0:T(8,128)(2,1)S(1)} collective-permute-done((bf16[272,128]{1,0:T(8,128)(2,1)S(1)}, bf16[272,128]{1,0:T(8,128)(2,1)S(1)}, u32[]{:S(2)}, u32[]{:S(2)}) %collective-permute-start.5) | collective-permute-done | bytes 69664 | tf_op jit(solution)/shard_map/ppermute | solution.py:380
  16.2 0.2 collective-permute-start.6
  16.4 0.0 collective-permute-done.4.refs_3_.refs_7_
  16.4 0.4 %collective-permute-done.2.refs_1_.refs_5_ = bf16[272,128]{1,0:T(8,128)(2,1)S(1)} collective-permute-done((bf16[272,128]{1,0:T(8,128)(2,1)S(1)}, bf16[272,128]{1,0:T(8,128)(2,1)S(1)}, u32[]{:S(2)}, u32[]{:S(2)}) %collective-permute-start.2) | collective-permute-done | bytes 69664 | tf_op jit(solution)/shard_map/ppermute | solution.py:380
  16.8 0.0 copy-done
  16.8 0.0 copy-done.2
  16.8 0.0 copy-done.3
  16.8 0.0 copy-done.4
  16.8 1.3 %columns_1.1 = (f32[1024,128]{1,0:T(8,128)S(1)}, f32[512,128]{1,0:T(8,128)S(1)}, f32[512,128]{1,0:T(8,128)S(1)}, f32[4,512,128]{2,1,0:T(8,128)S(1)}, f32[2,512,1...) custom-call(s32[1]{0:T(128)S(6)} %copy.12.crop_ref, ...), custom_call_target="tpu_custom_call" | custom-call | flops 800000000 | bytes 1000000 | tf_op jit(solution)/shard_map/columns_1/pallas_call | solution.py:471
  18.1 0.0 collective-permute-done.6.refs_2_.refs_4_
  18.1 1.3 %columns_0.1 = (f32[1024,128]{1,0:T(8,128)S(1)}, f32[512,128]{1,0:T(8,128)S(1)}, f32[512,128]{1,0:T(8,128)S(1)}, f32[4,512,128]{2,1,0:T(8,128)S(1)}, f32[2,512,1...) custom-call(s32[1]{0:T(128)S(6)} %copy.12.crop_ref, ...), custom_call_target="tpu_custom_call", output_to_operand_aliasing={{0}: (11, {})} | custom-call | flops 800000000 | bytes 1000000 | tf_op jit(solution)/shard_map/columns_0/pallas_call | solution.py:471
  19.4 4.4 %rest.1 = (bf16[8,8,128]{2,1,0:T(8,128)(2,1)}, bf16[8,8,128]{2,1,0:T(8,128)(2,1)}, f32[6,128,128]{2,1,0:T(8,128)}) custom-call(bf16[6,128,128]{2,1,0:T(8,128)(2,1)S(1)} %copy-done, f32[8,128]{1,0:T(8,128)S(1)} %get-tuple-element.22.refs_8_.gains_ref, f32[2,64,128]{2,1,0:T(8,128)S(1)} %get-tuple-element.23.own_ref, f32[64,128]{1,0:T(8,128)S(1)} %get-tuple-element.25.gate_ref, ...), custom_call_target="tpu_custom_call" | custom-call | tf_op jit(solution)/shard_map/rest/pallas_call | solution.py:486
  (3 shorter events, 0.0 us)
Async XLA Ops:
  2.2 6.0 %collective-permute-start = (bf16[144,128]{1,0:T(8,128)(2,1)}, bf16[144,128]{1,0:T(8,128)(2,1)S(1)}, u32[]{:S(2)}, u32[]{:S(2)}) collective-permute-start(bf16[144,128]{1,0:T(8,128)(2,1)} %pack.1.in_ref), channel_id=1, source_target_pairs={{0,1},{1,0},{2,3},{3,2},{4,5},{5,4},{6,7},{7,6},{8,9},{9,8},{10,11... | collective-permute-start | bytes 110600 | tf_op jit(solution)/shard_map/ppermute | solution.py:380
  2.8 7.1 %collective-permute-start.7 = (bf16[144,128]{1,0:T(8,128)(2,1)}, bf16[144,128]{1,0:T(8,128)(2,1)S(1)}, u32[]{:S(2)}, u32[]{:S(2)}) collective-permute-start(bf16[144,128]{1,0:T(8,128)(2,1)} %pack.1.in_ref), channel_id=1, source_target_pairs={{0,12},{1,13},{2,14},{3,15},{4,8},{5,9},{6,10},{7,11},{8,4},{9,5},... | collective-permute-start | bytes 110600 | tf_op jit(solution)/shard_map/ppermute | solution.py:380
  7.4 0.8 %copy-start.1 = (bf16[144,128]{1,0:T(8,128)(2,1)S(1)}, bf16[144,128]{1,0:T(8,128)(2,1)}, u32[]{:S(2)}) copy-start(bf16[144,128]{1,0:T(8,128)(2,1)} %pack.1.in_ref) | copy-start | bytes 110596
  8.2 5.4 %collective-permute-start.3 = (bf16[272,128]{1,0:T(8,128)(2,1)S(1)}, bf16[272,128]{1,0:T(8,128)(2,1)S(1)}, u32[]{:S(2)}, u32[]{:S(2)}) collective-permute-start(bf16[272,128]{1,0:T(8,128)(2,1)S(1)} %join.1.refs_0_), channel_id=1, source_target_pairs={{0,6},{1,15},{2,4},{3,13},{4,2},{5,11},{6,0},{7,9},{8,14},{9,7},{1... | collective-permute-start | bytes 208904 | tf_op jit(solution)/shard_map/ppermute | solution.py:380
  8.8 5.9 %collective-permute-start.1 = (bf16[272,128]{1,0:T(8,128)(2,1)S(1)}, bf16[272,128]{1,0:T(8,128)(2,1)S(1)}, u32[]{:S(2)}, u32[]{:S(2)}) collective-permute-start(bf16[272,128]{1,0:T(8,128)(2,1)S(1)} %join.1.refs_0_), channel_id=1, source_target_pairs={{0,2},{1,11},{2,0},{3,9},{4,6},{5,15},{6,4},{7,13},{8,10},{9,3},{1... | collective-permute-start | bytes 208904 | tf_op jit(solution)/shard_map/ppermute | solution.py:380
  9.9 6.0 %collective-permute-start.8 = (bf16[144,128]{1,0:T(8,128)(2,1)S(1)}, bf16[144,128]{1,0:T(8,128)(2,1)S(1)}, u32[]{:S(2)}, u32[]{:S(2)}) collective-permute-start(bf16[144,128]{1,0:T(8,128)(2,1)S(1)} %collective-permute-done.7.refs_0_.refs_5_), channel_id=1, source_target_pairs={{0,1},{1,0},{2,3},{3,2},{4,5},{5,4},{6,7},{7,6},{8,9},{9,8},{10,11... | collective-permute-start | bytes 110600 | tf_op jit(solution)/shard_map/ppermute | solution.py:380
  10.5 6.2 %copy-start = (bf16[6,128,128]{2,1,0:T(8,128)(2,1)S(1)}, bf16[6,128,128]{2,1,0:T(8,128)(2,1)}, u32[]{:S(2)}) copy-start(bf16[6,128,128]{2,1,0:T(8,128)(2,1)} %weights_ref.5) | copy-start | bytes 589828
  10.6 6.2 %copy-start.2 = (bf16[8,8,128]{2,1,0:T(8,128)(2,1)S(1)}, bf16[8,8,128]{2,1,0:T(8,128)(2,1)}, u32[]{:S(2)}) copy-start(bf16[8,8,128]{2,1,0:T(8,128)(2,1)} %refs_8_.1) | copy-start | bytes 49156
  10.6 5.6 %collective-permute-start.5 = (bf16[272,128]{1,0:T(8,128)(2,1)S(1)}, bf16[272,128]{1,0:T(8,128)(2,1)S(1)}, u32[]{:S(2)}, u32[]{:S(2)}) collective-permute-start(bf16[272,128]{1,0:T(8,128)(2,1)S(1)} %join.1.refs_0_), channel_id=1, source_target_pairs={{0,8},{1,5},{2,10},{3,7},{4,12},{5,1},{6,14},{7,3},{8,0},{9,13},{1... | collective-permute-start | bytes 208904 | tf_op jit(solution)/shard_map/ppermute | solution.py:380
  13.6 2.7 %collective-permute-start.4 = (bf16[272,128]{1,0:T(8,128)(2,1)S(1)}, bf16[272,128]{1,0:T(8,128)(2,1)S(1)}, u32[]{:S(2)}, u32[]{:S(2)}) collective-permute-start(bf16[272,128]{1,0:T(8,128)(2,1)S(1)} %collective-permute-done.3.refs_2_.refs_6_), channel_id=1, source_target_pairs={{0,1},{1,0},{2,3},{3,2},{4,5},{5,4},{6,7},{7,6},{8,9},{9,8},{10,11... | collective-permute-start | bytes 208904 | tf_op jit(solution)/shard_map/ppermute | solution.py:380
  14.7 2.1 %collective-permute-start.2 = (bf16[272,128]{1,0:T(8,128)(2,1)S(1)}, bf16[272,128]{1,0:T(8,128)(2,1)S(1)}, u32[]{:S(2)}, u32[]{:S(2)}) collective-permute-start(bf16[272,128]{1,0:T(8,128)(2,1)S(1)} %collective-permute-done.1.refs_0_.refs_4_), channel_id=1, source_target_pairs={{0,1},{1,0},{2,3},{3,2},{4,5},{5,4},{6,7},{7,6},{8,9},{9,8},{10,11... | collective-permute-start | bytes 208904 | tf_op jit(solution)/shard_map/ppermute | solution.py:380
  15.9 0.9 %copy-start.3 = (f32[128]{0:T(128)S(1)}, f32[128]{0:T(128)}, u32[]{:S(2)}) copy-start(f32[128]{0:T(128)} %param.11) | copy-start | bytes 1540
  15.9 0.9 %copy-start.4 = (f32[128]{0:T(128)S(1)}, f32[128]{0:T(128)}, u32[]{:S(2)}) copy-start(f32[128]{0:T(128)} %param.12) | copy-start | bytes 1540
  16.2 1.9 %collective-permute-start.6 = (bf16[272,128]{1,0:T(8,128)(2,1)S(1)}, bf16[272,128]{1,0:T(8,128)(2,1)S(1)}, u32[]{:S(2)}, u32[]{:S(2)}) collective-permute-start(bf16[272,128]{1,0:T(8,128)(2,1)S(1)} %collective-permute-done.5.refs_1_.refs_3_), channel_id=1, source_target_pairs={{0,1},{1,0},{2,3},{3,2},{4,5},{5,4},{6,7},{7,6},{8,9},{9,8},{10,11... | collective-permute-start | bytes 208904 | tf_op jit(solution)/shard_map/ppermute | solution.py:380

commit v19 on v16

--- a/solution.py
+++ b/solution.py
@@ -132,6 +132,10 @@
     out_ref[...] = in_ref[...]
 
 
+def token_kernel(*refs):
+    refs[-1][...] = jnp.zeros(refs[-1].shape, refs[-1].dtype)
+
+
 def join_kernel(own_ref, twin_ref, out_ref):
     tile = SUB * SUB
     refs = (own_ref, twin_ref)
@@ -213,14 +217,14 @@
     chip_list, refs = split_chips(refs[:count], chips), refs[count:]
     own_ref = None
     if side_x == 0:
-        act_ref, in_gain_ref, out_gain_ref, *refs, own_ref, gains_ref = refs
+        _, act_ref, in_gain_ref, out_gain_ref, *refs, own_ref, gains_ref = refs
         z_hat, z_inverse = normalize(act_ref[...].astype(jnp.float32).reshape(own_ref.shape[1:]))
         own_ref[0] = z_hat
         own_ref[1] = jnp.broadcast_to(z_inverse, z_hat.shape)
         gains_ref[0:1] = in_gain_ref[...]
         gains_ref[1:2] = out_gain_ref[...]
     else:
-        gains_ref, *refs = refs
+        _, gains_ref, *refs = refs
     tri_in, (tri_ref, left_ref, right_ref, side_ref, back_ref, flip_ref) = refs[:-6], refs[-6:]
     channels = weights_ref.shape[-1]
     tile = SUB * SUB
@@ -435,9 +439,23 @@
     chips = (((1, None), (2, 1), (2, 0), (2, None)), ((2, 0), (2, 0), (2, 1), (2, 1)))
     sources = ((both, *first, *first, *straight), (*second, *third, *second, *third))
 
+    anywhere = pl.BlockSpec(memory_space=pl.ANY)
+
+    def token(cost, *pieces):
+        return pl.pallas_call(
+            token_kernel,
+            name="token",
+            out_shape=jax.ShapeDtypeStruct((SUB, channels), f32),
+            in_specs=[anywhere] * len(pieces),
+            out_specs=vmem,
+            compiler_params=limit(2),
+            cost_estimate=pl.CostEstimate(flops=cost, bytes_accessed=1_000_000, transcendentals=0),
+        )(*pieces)
+
+    tokens = (token(1_000_000_000, *straight), token(1_000_000, *second, *third))
     tri, parts, extra = [], [], []
     for side_x in range(n_col // 2):
-        more = (pair_act, in_gain, out_gain) if side_x == 0 else (extra[1], *tri)
+        more = (tokens[0], pair_act, in_gain, out_gain) if side_x == 0 else (tokens[1], extra[1], *tri)
         more_shapes = () if side_x > 0 else (
             jax.ShapeDtypeStruct((3, tile, channels), f32),
             jax.ShapeDtypeStruct((SUB, channels), f32),
@@ -456,7 +474,7 @@
             ),
             in_specs=[smem] + [vmem] * (1 + len(sources[side_x]) + len(more)),
             out_specs=(vmem,) * (6 + len(more_shapes)),
-            input_output_aliases={3 + len(sources[side_x]): 0} if side_x > 0 else {},
+            input_output_aliases={4 + len(sources[side_x]): 0} if side_x > 0 else {},
             compiler_params=limit(12),
             cost_estimate=pl.CostEstimate(flops=800_000_000, bytes_accessed=1_000_000, transcendentals=0),
         )(crop_length, weights, *sources[side_x], *more)

time: 24.2 us -> 25.6 us (1.058)
  starting transfers between devices: 8.29 us -> 12.6 us
  waiting for transfers between devices: 4.76 us -> 1.69 us
    ppermute x9, starting transfers between devices: 8.29 us -> 12.6 us  [flip(): return lax.ppermute(block, ('row', 'col'), pairs)]
    ppermute x9, waiting for transfers between devices: 4.76 us -> 1.69 us  [flip(): return lax.ppermute(block, ('row', 'col'), pairs)]
  transfers between devices with their start and end apart: 9 -> 9, of which waited for: 4 -> 4; matrix products, arithmetic and copies ran while one was open for 0% -> 0% of each run, Pallas kernels for 5% -> 0%
where the time goes in v19:
time: 25.6 us; the launch traced here: 25.3 us
  starting transfers between devices  12.6 us (49%)
  Pallas kernels  8.65 us (34%)
  waiting for transfers between devices  1.69 us (7%)
  between operations  1.35 us (5%)
  local copies, waits for them, and re-layouts  0.94 us (4%)
    ppermute x9, starting transfers between devices, flip(): return lax.ppermute(block, ('row', 'col'), pairs)  12.6 us
    pallas_call x1, Pallas kernels, gathered_body(): pl.pallas_call(functools.partial(rest_kernel, n_row, n_col), name='rest',...  4.45 us
    pallas_call x2, Pallas kernels, gathered_body(): pl.pallas_call(functools.partial(columns_kernel, n_row, n_col, side_x, ch...  2.59 us
    ppermute x9, waiting for transfers between devices, flip(): return lax.ppermute(block, ('row', 'col'), pairs)  1.69 us
    pallas_call x1, Pallas kernels, gathered_body(): pl.pallas_call(pack_kernel, name='pack', out_shape=jax.ShapeDtypeStruct((...  1.6 us
    unnamed x10, local copies, waits for them, and re-layouts  0.94 us
  transfers between devices with their start and end apart: 9, of which 4 were waited for; matrix products, arithmetic and copies ran while one was open for 0% of the time, Pallas kernels for 0%

profile of v19, /device:TPU:0, one launch (start us, length us, event | category | flops | bytes accessed | tf_op | source)
XLA Modules:
  0.0 25.3 jit_solution(3928280048274992924)
XLA Ops:
  0.6 1.6 %pack.1.in_ref = bf16[144,128]{1,0:T(8,128)(2,1)} custom-call(bf16[8,8,128]{2,1,0:T(8,128)(2,1)} %refs_8_.1, s32[8,8]{1,0:T(8,128)} %mask_hbm.1, bf16[64,128]{1,0:T(8,128)(2,1)} %bitcast.6, f32[1,128]{1,0:T(1,128)} %bitcast.3), custom_call_target="tpu_custom_call" | custom-call | tf_op jit(solution)/shard_map/pack/pallas_call | solution.py:395
  2.2 0.5 %collective-permute-start = (bf16[144,128]{1,0:T(8,128)(2,1)}, bf16[144,128]{1,0:T(8,128)(2,1)S(1)}, u32[]{:S(2)}, u32[]{:S(2)}) collective-permute-start(bf16[144,128]{1,0:T(8,128)(2,1)} %pack.1.in_ref), channel_id=1, source_target_pairs={{0,1},{1,0},{2,3},{3,2},{4,5},{5,4},{6,7},{7,6},{8,9},{9,8},{10,11... | collective-permute-start | bytes 110600 | tf_op jit(solution)/shard_map/ppermute | solution.py:377
  2.8 4.7 %collective-permute-start.3 = (bf16[144,128]{1,0:T(8,128)(2,1)}, bf16[144,128]{1,0:T(8,128)(2,1)S(1)}, u32[]{:S(2)}, u32[]{:S(2)}) collective-permute-start(bf16[144,128]{1,0:T(8,128)(2,1)} %pack.1.in_ref), channel_id=1, source_target_pairs={{0,12},{1,13},{2,14},{3,15},{4,8},{5,9},{6,10},{7,11},{8,4},{9,5},... | collective-permute-start | bytes 110600 | tf_op jit(solution)/shard_map/ppermute | solution.py:377
  7.4 0.0 copy-start.1
  7.4 0.8 %copy-done.1 = bf16[144,128]{1,0:T(8,128)(2,1)S(1)} copy-done((bf16[144,128]{1,0:T(8,128)(2,1)S(1)}, bf16[144,128]{1,0:T(8,128)(2,1)}, u32[]{:S(2)}) %copy-start.1) | copy-done | bytes 36888
  8.2 0.0 collective-permute-done.twin_ref
  8.2 0.5 %collective-permute-start.7 = (bf16[272,128]{1,0:T(8,128)(2,1)S(1)}, bf16[272,128]{1,0:T(8,128)(2,1)S(1)}, u32[]{:S(2)}, u32[]{:S(2)}) collective-permute-start(bf16[272,128]{1,0:T(8,128)(2,1)S(1)} %join.1.refs_0_), channel_id=1, source_target_pairs={{0,6},{1,15},{2,4},{3,13},{4,2},{5,11},{6,0},{7,9},{8,14},{9,7},{1... | collective-permute-start | bytes 208904 | tf_op jit(solution)/shard_map/ppermute | solution.py:377
  8.8 1.1 %collective-permute-start.5 = (bf16[272,128]{1,0:T(8,128)(2,1)S(1)}, bf16[272,128]{1,0:T(8,128)(2,1)S(1)}, u32[]{:S(2)}, u32[]{:S(2)}) collective-permute-start(bf16[272,128]{1,0:T(8,128)(2,1)S(1)} %join.1.refs_0_), channel_id=1, source_target_pairs={{0,2},{1,11},{2,0},{3,9},{4,6},{5,15},{6,4},{7,13},{8,10},{9,3},{1... | collective-permute-start | bytes 208904 | tf_op jit(solution)/shard_map/ppermute | solution.py:377
  9.9 0.9 %collective-permute-start.1 = (bf16[272,128]{1,0:T(8,128)(2,1)S(1)}, bf16[272,128]{1,0:T(8,128)(2,1)S(1)}, u32[]{:S(2)}, u32[]{:S(2)}) collective-permute-start(bf16[272,128]{1,0:T(8,128)(2,1)S(1)} %join.1.refs_0_), channel_id=1, source_target_pairs={{0,8},{1,5},{2,10},{3,7},{4,12},{5,1},{6,14},{7,3},{8,0},{9,13},{1... | collective-permute-start | bytes 208904 | tf_op jit(solution)/shard_map/ppermute | solution.py:377
  10.8 0.0 collective-permute-done.3.refs_0_.refs_5_
  10.8 2.1 %collective-permute-start.4 = (bf16[144,128]{1,0:T(8,128)(2,1)S(1)}, bf16[144,128]{1,0:T(8,128)(2,1)S(1)}, u32[]{:S(2)}, u32[]{:S(2)}) collective-permute-start(bf16[144,128]{1,0:T(8,128)(2,1)S(1)} %collective-permute-done.3.refs_0_.refs_5_), channel_id=1, source_target_pairs={{0,1},{1,0},{2,3},{3,2},{4,5},{5,4},{6,7},{7,6},{8,9},{9,8},{10,11... | collective-permute-start | bytes 110600 | tf_op jit(solution)/shard_map/ppermute | solution.py:377
  13.6 0.0 collective-permute-done.7.refs_2_.refs_6_
  13.6 0.8 %collective-permute-start.8 = (bf16[272,128]{1,0:T(8,128)(2,1)S(1)}, bf16[272,128]{1,0:T(8,128)(2,1)S(1)}, u32[]{:S(2)}, u32[]{:S(2)}) collective-permute-start(bf16[272,128]{1,0:T(8,128)(2,1)S(1)} %collective-permute-done.7.refs_2_.refs_6_), channel_id=1, source_target_pairs={{0,1},{1,0},{2,3},{3,2},{4,5},{5,4},{6,7},{7,6},{8,9},{9,8},{10,11... | collective-permute-start | bytes 208904 | tf_op jit(solution)/shard_map/ppermute | solution.py:377
  14.4 0.2 collective-permute-done.5.refs_0_.refs_4_
  14.7 2.0 %collective-permute-start.6 = (bf16[272,128]{1,0:T(8,128)(2,1)S(1)}, bf16[272,128]{1,0:T(8,128)(2,1)S(1)}, u32[]{:S(2)}, u32[]{:S(2)}) collective-permute-start(bf16[272,128]{1,0:T(8,128)(2,1)S(1)} %collective-permute-done.5.refs_0_.refs_4_), channel_id=1, source_target_pairs={{0,1},{1,0},{2,3},{3,2},{4,5},{5,4},{6,7},{7,6},{8,9},{9,8},{10,11... | collective-permute-start | bytes 208904 | tf_op jit(solution)/shard_map/ppermute | solution.py:377
  16.6 0.2 collective-permute-done.1.refs_1_.refs_3_
  16.8 0.0 collective-permute-start.2
  16.8 0.0 collective-permute-done.4.refs_1_.refs_6_
  16.8 0.0 copy-start
  16.9 0.0 copy-start.2
  16.9 0.0 collective-permute-done.8.refs_3_.refs_7_
  16.9 0.6 %collective-permute-done.6.refs_1_.refs_5_ = bf16[272,128]{1,0:T(8,128)(2,1)S(1)} collective-permute-done((bf16[272,128]{1,0:T(8,128)(2,1)S(1)}, bf16[272,128]{1,0:T(8,128)(2,1)S(1)}, u32[]{:S(2)}, u32[]{:S(2)}) %collective-permute-start.6) | collective-permute-done | bytes 69664 | tf_op jit(solution)/shard_map/ppermute | solution.py:377
  17.5 0.0 copy-start.3
  17.5 0.0 copy-start.4
  17.5 0.6 %collective-permute-done.2.refs_2_.refs_4_ = bf16[272,128]{1,0:T(8,128)(2,1)S(1)} collective-permute-done((bf16[272,128]{1,0:T(8,128)(2,1)S(1)}, bf16[272,128]{1,0:T(8,128)(2,1)S(1)}, u32[]{:S(2)}, u32[]{:S(2)}) %collective-permute-start.2) | collective-permute-done | bytes 69664 | tf_op jit(solution)/shard_map/ppermute | solution.py:377
  18.1 0.0 copy-done
  18.1 0.0 copy-done.2
  18.1 0.1 copy-done.3
  18.2 0.0 copy-done.4
  18.2 1.3 %columns_0.1 = (f32[1024,128]{1,0:T(8,128)S(1)}, f32[512,128]{1,0:T(8,128)S(1)}, f32[512,128]{1,0:T(8,128)S(1)}, f32[4,512,128]{2,1,0:T(8,128)S(1)}, f32[2,512,1...) custom-call(s32[1]{0:T(128)S(6)} %copy.12.crop_ref, ...), custom_call_target="tpu_custom_call" | custom-call | flops 800000000 | bytes 1000000 | tf_op jit(solution)/shard_map/columns_0/pallas_call | solution.py:463
  19.5 1.3 %columns_1.1 = (f32[1024,128]{1,0:T(8,128)S(1)}, f32[512,128]{1,0:T(8,128)S(1)}, f32[512,128]{1,0:T(8,128)S(1)}, f32[4,512,128]{2,1,0:T(8,128)S(1)}, f32[2,512,1...) custom-call(s32[1]{0:T(128)S(6)} %copy.12.crop_ref, ...), custom_call_target="tpu_custom_call", output_to_operand_aliasing={{0}: (12, {})} | custom-call | flops 800000000 | bytes 1000000 | tf_op jit(solution)/shard_map/columns_1/pallas_call | solution.py:463
  20.8 4.5 %rest.1 = (bf16[8,8,128]{2,1,0:T(8,128)(2,1)}, bf16[8,8,128]{2,1,0:T(8,128)(2,1)}, f32[6,128,128]{2,1,0:T(8,128)}) custom-call(bf16[6,128,128]{2,1,0:T(8,128)(2,1)S(1)} %copy-done, f32[3,64,128]{2,1,0:T(8,128)S(1)} %get-tuple-element.21.own_ref, f32[8,128]{1,0:T(8,128)S(1)} %get-tuple-element.22.refs_9_.gains_ref, ...), custom_call_target="tpu_custom_call" | custom-call | tf_op jit(solution)/shard_map/rest/pallas_call | solution.py:485
  (4 shorter events, 0.0 us)
Async XLA Ops:
  2.2 6.0 %collective-permute-start = (bf16[144,128]{1,0:T(8,128)(2,1)}, bf16[144,128]{1,0:T(8,128)(2,1)S(1)}, u32[]{:S(2)}, u32[]{:S(2)}) collective-permute-start(bf16[144,128]{1,0:T(8,128)(2,1)} %pack.1.in_ref), channel_id=1, source_target_pairs={{0,1},{1,0},{2,3},{3,2},{4,5},{5,4},{6,7},{7,6},{8,9},{9,8},{10,11... | collective-permute-start | bytes 110600 | tf_op jit(solution)/shard_map/ppermute | solution.py:377
  2.8 8.1 %collective-permute-start.3 = (bf16[144,128]{1,0:T(8,128)(2,1)}, bf16[144,128]{1,0:T(8,128)(2,1)S(1)}, u32[]{:S(2)}, u32[]{:S(2)}) collective-permute-start(bf16[144,128]{1,0:T(8,128)(2,1)} %pack.1.in_ref), channel_id=1, source_target_pairs={{0,12},{1,13},{2,14},{3,15},{4,8},{5,9},{6,10},{7,11},{8,4},{9,5},... | collective-permute-start | bytes 110600 | tf_op jit(solution)/shard_map/ppermute | solution.py:377
  7.4 0.8 %copy-start.1 = (bf16[144,128]{1,0:T(8,128)(2,1)S(1)}, bf16[144,128]{1,0:T(8,128)(2,1)}, u32[]{:S(2)}) copy-start(bf16[144,128]{1,0:T(8,128)(2,1)} %pack.1.in_ref) | copy-start | bytes 110596
  8.2 5.4 %collective-permute-start.7 = (bf16[272,128]{1,0:T(8,128)(2,1)S(1)}, bf16[272,128]{1,0:T(8,128)(2,1)S(1)}, u32[]{:S(2)}, u32[]{:S(2)}) collective-permute-start(bf16[272,128]{1,0:T(8,128)(2,1)S(1)} %join.1.refs_0_), channel_id=1, source_target_pairs={{0,6},{1,15},{2,4},{3,13},{4,2},{5,11},{6,0},{7,9},{8,14},{9,7},{1... | collective-permute-start | bytes 208904 | tf_op jit(solution)/shard_map/ppermute | solution.py:377
  8.8 5.9 %collective-permute-start.5 = (bf16[272,128]{1,0:T(8,128)(2,1)S(1)}, bf16[272,128]{1,0:T(8,128)(2,1)S(1)}, u32[]{:S(2)}, u32[]{:S(2)}) collective-permute-start(bf16[272,128]{1,0:T(8,128)(2,1)S(1)} %join.1.refs_0_), channel_id=1, source_target_pairs={{0,2},{1,11},{2,0},{3,9},{4,6},{5,15},{6,4},{7,13},{8,10},{9,3},{1... | collective-permute-start | bytes 208904 | tf_op jit(solution)/shard_map/ppermute | solution.py:377
  9.9 6.9 %collective-permute-start.1 = (bf16[272,128]{1,0:T(8,128)(2,1)S(1)}, bf16[272,128]{1,0:T(8,128)(2,1)S(1)}, u32[]{:S(2)}, u32[]{:S(2)}) collective-permute-start(bf16[272,128]{1,0:T(8,128)(2,1)S(1)} %join.1.refs_0_), channel_id=1, source_target_pairs={{0,8},{1,5},{2,10},{3,7},{4,12},{5,1},{6,14},{7,3},{8,0},{9,13},{1... | collective-permute-start | bytes 208904 | tf_op jit(solution)/shard_map/ppermute | solution.py:377
  10.8 6.0 %collective-permute-start.4 = (bf16[144,128]{1,0:T(8,128)(2,1)S(1)}, bf16[144,128]{1,0:T(8,128)(2,1)S(1)}, u32[]{:S(2)}, u32[]{:S(2)}) collective-permute-start(bf16[144,128]{1,0:T(8,128)(2,1)S(1)} %collective-permute-done.3.refs_0_.refs_5_), channel_id=1, source_target_pairs={{0,1},{1,0},{2,3},{3,2},{4,5},{5,4},{6,7},{7,6},{8,9},{9,8},{10,11... | collective-permute-start | bytes 110600 | tf_op jit(solution)/shard_map/ppermute | solution.py:377
  13.6 3.2 %collective-permute-start.8 = (bf16[272,128]{1,0:T(8,128)(2,1)S(1)}, bf16[272,128]{1,0:T(8,128)(2,1)S(1)}, u32[]{:S(2)}, u32[]{:S(2)}) collective-permute-start(bf16[272,128]{1,0:T(8,128)(2,1)S(1)} %collective-permute-done.7.refs_2_.refs_6_), channel_id=1, source_target_pairs={{0,1},{1,0},{2,3},{3,2},{4,5},{5,4},{6,7},{7,6},{8,9},{9,8},{10,11... | collective-permute-start | bytes 208904 | tf_op jit(solution)/shard_map/ppermute | solution.py:377
  14.7 2.9 %collective-permute-start.6 = (bf16[272,128]{1,0:T(8,128)(2,1)S(1)}, bf16[272,128]{1,0:T(8,128)(2,1)S(1)}, u32[]{:S(2)}, u32[]{:S(2)}) collective-permute-start(bf16[272,128]{1,0:T(8,128)(2,1)S(1)} %collective-permute-done.5.refs_0_.refs_4_), channel_id=1, source_target_pairs={{0,1},{1,0},{2,3},{3,2},{4,5},{5,4},{6,7},{7,6},{8,9},{9,8},{10,11... | collective-permute-start | bytes 208904 | tf_op jit(solution)/shard_map/ppermute | solution.py:377
  16.8 1.3 %collective-permute-start.2 = (bf16[272,128]{1,0:T(8,128)(2,1)S(1)}, bf16[272,128]{1,0:T(8,128)(2,1)S(1)}, u32[]{:S(2)}, u32[]{:S(2)}) collective-permute-start(bf16[272,128]{1,0:T(8,128)(2,1)S(1)} %collective-permute-done.1.refs_1_.refs_3_), channel_id=1, source_target_pairs={{0,1},{1,0},{2,3},{3,2},{4,5},{5,4},{6,7},{7,6},{8,9},{9,8},{10,11... | collective-permute-start | bytes 208904 | tf_op jit(solution)/shard_map/ppermute | solution.py:377
  16.8 1.3 %copy-start = (bf16[6,128,128]{2,1,0:T(8,128)(2,1)S(1)}, bf16[6,128,128]{2,1,0:T(8,128)(2,1)}, u32[]{:S(2)}) copy-start(bf16[6,128,128]{2,1,0:T(8,128)(2,1)} %weights_ref.5) | copy-start | bytes 589828
  16.9 1.2 %copy-start.2 = (bf16[8,8,128]{2,1,0:T(8,128)(2,1)S(1)}, bf16[8,8,128]{2,1,0:T(8,128)(2,1)}, u32[]{:S(2)}) copy-start(bf16[8,8,128]{2,1,0:T(8,128)(2,1)} %refs_8_.1) | copy-start | bytes 49156
  17.5 0.7 %copy-start.3 = (f32[128]{0:T(128)S(1)}, f32[128]{0:T(128)}, u32[]{:S(2)}) copy-start(f32[128]{0:T(128)} %param.11) | copy-start | bytes 1540
  17.5 0.7 %copy-start.4 = (f32[128]{0:T(128)S(1)}, f32[128]{0:T(128)}, u32[]{:S(2)}) copy-start(f32[128]{0:T(128)} %param.12) | copy-start | bytes 1540

commit v20 on v16

--- a/solution.py
+++ b/solution.py
@@ -172,8 +172,10 @@
     return split
 
 
-def triangle(blocks, groups, steps, vectors_at, factors_at, start_at, store_at):
+def triangle(blocks, groups, steps, vectors_at, factors_at, start_at, store_at, beside=None):
     def block(a, _):
+        if beside is not None:
+            beside(a)
         def step(q, totals):
             totals = list(totals)
             vectors = vectors_at(q)
@@ -221,7 +223,7 @@
         gains_ref[1:2] = out_gain_ref[...]
     else:
         gains_ref, *refs = refs
-    tri_in, (tri_ref, left_ref, right_ref, side_ref, back_ref, flip_ref) = refs[:-6], refs[-6:]
+    tri_in, (tri_ref, flip_ref, left_ref, right_ref, side_ref, back_ref) = refs[:-6], refs[-6:]
     channels = weights_ref.shape[-1]
     tile = SUB * SUB
     size = n_row * tile
@@ -235,7 +237,12 @@
     def turned(rows):
         return lax.dot_general(identity, rows, (((1,), (1,)), ((), ())), preferred_element_type=f32).astype(bf16)
 
-    flip_ref[0] = turned(normed)
+    def put(kind, rows):
+        both = turned(rows)
+        for core in range(2):
+            flip_ref[kind, 2 * side_x + core] = both[:, core * size : (core + 1) * size]
+
+    put(0, normed)
     crop = crop_ref[0]
     col_offset = lax.broadcasted_iota(jnp.int32, (SUB, channels), 0)
     row_offset = lax.broadcasted_iota(jnp.int32, (SUB, channels), 1)
@@ -262,7 +269,7 @@
     cot = jnp.concatenate([chip_rows(cot_rows, chip, core, on) for chip, on, core, _ in chip_list], axis=0)
     grad = cot.astype(f32) * out_gate
     grad_lin = grad.astype(bf16)
-    flip_ref[1] = turned(grad_lin)
+    put(1, grad_lin)
     back_ref[0] = grad * (1.0 - out_gate)
     back = lax.dot_general(grad_lin, weights_ref[5], (((1,), (1,)), ((), ())), preferred_element_type=f32)
     back = back * gains_ref[1:2]
@@ -288,16 +295,16 @@
     triangle(n_row, n_col, 2, flipped, along, start, store)
 
 
-def rest_kernel(n_row, n_col, weights_ref, own_ref, gains_ref, tri_ref, *refs):
-    groups = [refs[at * 5 : at * 5 + 5] for at in range(n_col // 2)]
-    update_ref, pair_grad_ref, weight_grad_ref, back_ref, hat_ref, d_ref = refs[5 * (n_col // 2) :]
+def rest_kernel(n_row, n_col, weights_ref, own_ref, gains_ref, tri_ref, flip_ref, *refs):
+    groups = [refs[at * 4 : at * 4 + 4] for at in range(n_col // 2)]
+    update_ref, pair_grad_ref, weight_grad_ref, back_ref, hat_ref, d_ref, sum_ref = refs[4 * (n_col // 2) :]
     channels = tri_ref.shape[-1]
     tile = SUB * SUB
     size = n_row * tile
     columns = []
     for col in range(n_col):
         own = pl.ds(col % 2 * size, size)
-        left, right, side, backs, _ = groups[col // 2]
+        left, right, side, backs = groups[col // 2]
         columns.append((left.at[own], right.at[own], side.at[:, own], backs.at[:, own]))
     residues = n_row * SUB
     bf16, f32 = jnp.bfloat16, jnp.float32
@@ -345,15 +352,29 @@
     def down(a, q):
         return lambda lane, inner: spread(back_ref, (a ^ turn) * size + q * tile + inner * SUB + lane)
 
-    triangle(n_row, n_col, n_col, by_right, along, zero, store(0))
-    triangle(n_row, n_col, n_row, by_left, down, zero, store(1))
+    def chunk(ref, a, first, last):
+        return ref[pl.ds(pl.multiple_of(a * size, size), size), first * channels : last * channels]
+
+    def early_sums(a):
+        sum_ref[:, 0:channels] += jnp.dot(flip_ref[0, a], chunk(d_ref, a, 4, 5), preferred_element_type=f32)
+        sum_ref[:, channels : 2 * channels] += jnp.dot(flip_ref[1, a], chunk(hat_ref, a, 0, 1), preferred_element_type=f32)
+
+    def left_sums(a):
+        sum_ref[:, 2 * channels :] += jnp.dot(flip_ref[0, a], chunk(d_ref, a, 0, 2), preferred_element_type=f32)
+
+    sum_ref[...] = jnp.zeros(sum_ref.shape, f32)
+    triangle(n_row, n_col, n_col, by_right, along, zero, store(0), early_sums)
+    triangle(n_row, n_col, n_row, by_left, down, zero, store(1), left_sums)
 
     scale = 1.0 / residues
-    flipped, lin_flipped = [jnp.concatenate([group[4][at] for group in groups], axis=1) for at in range(2)]
-    sums = jnp.dot(flipped, d_ref[...], preferred_element_type=f32) * scale
-    for s in range(5):
-        weight_grad_ref[s] = sums[:, s * channels : (s + 1) * channels]
-    weight_grad_ref[5] = jnp.dot(lin_flipped, hat_ref[...], preferred_element_type=f32).T * scale
+    flipped = jnp.concatenate([flip_ref[0, col] for col in range(n_col)], axis=1)
+    right_sums = jnp.dot(flipped, d_ref[:, 2 * channels : 4 * channels], preferred_element_type=f32)
+    for s in range(2):
+        part = slice(s * channels, (s + 1) * channels)
+        weight_grad_ref[s] = sum_ref[:, (2 + s) * channels : (3 + s) * channels] * scale
+        weight_grad_ref[2 + s] = right_sums[:, part] * scale
+    weight_grad_ref[4] = sum_ref[:, 0:channels] * scale
+    weight_grad_ref[5] = sum_ref[:, channels : 2 * channels].T * scale
     total = jnp.zeros((tile, channels), f32)
     for s in range(5):
         total = total + lax.dot_general(
@@ -442,27 +463,28 @@
             jax.ShapeDtypeStruct((3, tile, channels), f32),
             jax.ShapeDtypeStruct((SUB, channels), f32),
         )
-        tri, *results = pl.pallas_call(
+        last = 3 + len(sources[side_x])
+        results = pl.pallas_call(
             functools.partial(columns_kernel, n_row, n_col, side_x, chips[side_x]),
             name=f"columns_{side_x}",
             out_shape=(
                 jax.ShapeDtypeStruct((pairs, channels), f32),
+                jax.ShapeDtypeStruct((2, n_col, channels, size), bf16),
                 jax.ShapeDtypeStruct((2 * size, channels), f32),
                 jax.ShapeDtypeStruct((2 * size, channels), f32),
                 jax.ShapeDtypeStruct((4, 2 * size, channels), f32),
                 jax.ShapeDtypeStruct((2, 2 * size, channels), f32),
-                jax.ShapeDtypeStruct((2, channels, 2 * size), bf16),
                 *more_shapes,
             ),
             in_specs=[smem] + [vmem] * (1 + len(sources[side_x]) + len(more)),
             out_specs=(vmem,) * (6 + len(more_shapes)),
-            input_output_aliases={3 + len(sources[side_x]): 0} if side_x > 0 else {},
+            input_output_aliases={last: 0, last + 1: 1} if side_x > 0 else {},
             compiler_params=limit(12),
             cost_estimate=pl.CostEstimate(flops=800_000_000, bytes_accessed=1_000_000, transcendentals=0),
         )(crop_length, weights, *sources[side_x], *more)
-        tri = [tri]
-        parts += results[:5]
-        extra += results[5:]
+        tri = results[:2]
+        parts += results[2:6]
+        extra += results[6:]
 
     return pl.pallas_call(
         functools.partial(rest_kernel, n_row, n_col),
@@ -472,12 +494,13 @@
             jax.ShapeDtypeStruct(pair_act.shape, bf16),
             jax.ShapeDtypeStruct(weights.shape, f32),
         ),
-        in_specs=[vmem] * (4 + len(parts)),
+        in_specs=[vmem] * (5 + len(parts)),
         out_specs=(vmem, vmem, vmem),
         scratch_shapes=[
             pltpu.VMEM((pairs, channels), f32),
             pltpu.VMEM((pairs, channels), bf16),
             pltpu.VMEM((pairs, 5 * channels), bf16),
+            pltpu.VMEM((channels, 4 * channels), f32),
         ],
         compiler_params=limit(16),
     )(weights, *extra, *tri, *parts)

time: 24.2 us -> 24.1 us (level)
  no operation moved by 1% of the time
where the time goes in v20:
time: 24.1 us; the launch traced here: 23.8 us
  Pallas kernels  8.56 us (36%)
  starting transfers between devices  8.29 us (34%)
  waiting for transfers between devices  4.76 us (20%)
  between operations  1.38 us (6%)
  local copies, waits for them, and re-layouts  0.79 us (3%)
    ppermute x9, starting transfers between devices, flip(): return lax.ppermute(block, ('row', 'col'), pairs)  8.29 us
    ppermute x9, waiting for transfers between devices, flip(): return lax.ppermute(block, ('row', 'col'), pairs)  4.76 us
    pallas_call x1, Pallas kernels, gathered_body(): pl.pallas_call(functools.partial(rest_kernel, n_row, n_col), name='rest',...  4.35 us
    pallas_call x2, Pallas kernels, gathered_body(): pl.pallas_call(functools.partial(columns_kernel, n_row, n_col, side_x, ch...  2.6 us
    pallas_call x1, Pallas kernels, gathered_body(): pl.pallas_call(pack_kernel, name='pack', out_shape=jax.ShapeDtypeStruct((...  1.6 us
    unnamed x10, local copies, waits for them, and re-layouts  0.79 us
  transfers between devices with their start and end apart: 9, of which 4 were waited for; matrix products, arithmetic and copies ran while one was open for 0% of the time, Pallas kernels for 5%

profile of v20, /device:TPU:0, one launch (start us, length us, event | category | flops | bytes accessed | tf_op | source)
XLA Modules:
  0.0 23.8 jit_solution(2029376925267119228)
XLA Ops:
  0.6 1.6 %pack.1.in_ref = bf16[144,128]{1,0:T(8,128)(2,1)} custom-call(bf16[8,8,128]{2,1,0:T(8,128)(2,1)} %refs_7_.1, s32[8,8]{1,0:T(8,128)} %mask_hbm.1, bf16[64,128]{1,0:T(8,128)(2,1)} %bitcast.6, f32[1,128]{1,0:T(1,128)} %bitcast.3), custom_call_target="tpu_custom_call" | custom-call | tf_op jit(solution)/shard_map/pack/pallas_call | solution.py:412
  2.2 0.0 copy-start
  2.2 0.5 %collective-permute-start = (bf16[144,128]{1,0:T(8,128)(2,1)}, bf16[144,128]{1,0:T(8,128)(2,1)S(1)}, u32[]{:S(2)}, u32[]{:S(2)}) collective-permute-start(bf16[144,128]{1,0:T(8,128)(2,1)} %pack.1.in_ref), channel_id=1, source_target_pairs={{0,1},{1,0},{2,3},{3,2},{4,5},{5,4},{6,7},{7,6},{8,9},{9,8},{10,11... | collective-permute-start | bytes 110600 | tf_op jit(solution)/shard_map/ppermute | solution.py:394
  2.8 0.0 copy-start.1
  2.8 0.8 %copy-done.1 = bf16[144,128]{1,0:T(8,128)(2,1)S(1)} copy-done((bf16[144,128]{1,0:T(8,128)(2,1)S(1)}, bf16[144,128]{1,0:T(8,128)(2,1)}, u32[]{:S(2)}) %copy-start.1) | copy-done | bytes 36888
  3.5 0.0 copy-start.2
  3.5 0.3 %collective-permute-done.twin_ref = bf16[144,128]{1,0:T(8,128)(2,1)S(1)} collective-permute-done((bf16[144,128]{1,0:T(8,128)(2,1)}, bf16[144,128]{1,0:T(8,128)(2,1)S(1)}, u32[]{:S(2)}, u32[]{:S(2)}) %collective-permute-start) | collective-permute-done | bytes 36896 | tf_op jit(solution)/shard_map/ppermute | solution.py:394
  3.9 3.9 %collective-permute-start.1 = (bf16[272,128]{1,0:T(8,128)(2,1)S(1)}, bf16[272,128]{1,0:T(8,128)(2,1)S(1)}, u32[]{:S(2)}, u32[]{:S(2)}) collective-permute-start(bf16[272,128]{1,0:T(8,128)(2,1)S(1)} %join.1.refs_0_), channel_id=1, source_target_pairs={{0,8},{1,5},{2,10},{3,7},{4,12},{5,1},{6,14},{7,3},{8,0},{9,13},{1... | collective-permute-start | bytes 208904 | tf_op jit(solution)/shard_map/ppermute | solution.py:394
  7.8 1.3 %collective-permute-start.3 = (bf16[144,128]{1,0:T(8,128)(2,1)S(1)}, bf16[144,128]{1,0:T(8,128)(2,1)S(1)}, u32[]{:S(2)}, u32[]{:S(2)}) collective-permute-start(bf16[144,128]{1,0:T(8,128)(2,1)S(1)} %copy-done.1), channel_id=1, source_target_pairs={{0,12},{1,13},{2,14},{3,15},{4,8},{5,9},{6,10},{7,11},{8,4},{9,5},... | collective-permute-start | bytes 110600 | tf_op jit(solution)/shard_map/ppermute | solution.py:394
  9.1 1.2 %collective-permute-start.7 = (bf16[272,128]{1,0:T(8,128)(2,1)S(1)}, bf16[272,128]{1,0:T(8,128)(2,1)S(1)}, u32[]{:S(2)}, u32[]{:S(2)}) collective-permute-start(bf16[272,128]{1,0:T(8,128)(2,1)S(1)} %join.1.refs_0_), channel_id=1, source_target_pairs={{0,6},{1,15},{2,4},{3,13},{4,2},{5,11},{6,0},{7,9},{8,14},{9,7},{1... | collective-permute-start | bytes 208904 | tf_op jit(solution)/shard_map/ppermute | solution.py:394
  10.3 0.5 %collective-permute-start.5 = (bf16[272,128]{1,0:T(8,128)(2,1)S(1)}, bf16[272,128]{1,0:T(8,128)(2,1)S(1)}, u32[]{:S(2)}, u32[]{:S(2)}) collective-permute-start(bf16[272,128]{1,0:T(8,128)(2,1)S(1)} %join.1.refs_0_), channel_id=1, source_target_pairs={{0,2},{1,11},{2,0},{3,9},{4,6},{5,15},{6,4},{7,13},{8,10},{9,3},{1... | collective-permute-start | bytes 208904 | tf_op jit(solution)/shard_map/ppermute | solution.py:394
  10.8 0.0 collective-permute-done.1.refs_1_.refs_3_
  10.8 0.5 %collective-permute-start.2 = (bf16[272,128]{1,0:T(8,128)(2,1)S(1)}, bf16[272,128]{1,0:T(8,128)(2,1)S(1)}, u32[]{:S(2)}, u32[]{:S(2)}) collective-permute-start(bf16[272,128]{1,0:T(8,128)(2,1)S(1)} %collective-permute-done.1.refs_1_.refs_3_), channel_id=1, source_target_pairs={{0,1},{1,0},{2,3},{3,2},{4,5},{5,4},{6,7},{7,6},{8,9},{9,8},{10,11... | collective-permute-start | bytes 208904 | tf_op jit(solution)/shard_map/ppermute | solution.py:394
  11.3 2.3 %collective-permute-done.3.refs_5_ = bf16[144,128]{1,0:T(8,128)(2,1)S(1)} collective-permute-done((bf16[144,128]{1,0:T(8,128)(2,1)S(1)}, bf16[144,128]{1,0:T(8,128)(2,1)S(1)}, u32[]{:S(2)}, u32[]{:S(2)}) %collective-permute-start.3) | collective-permute-done | bytes 36896 | tf_op jit(solution)/shard_map/ppermute | solution.py:394
  13.6 0.0 collective-permute-start.4
  14.3 0.0 copy-start.3
  14.3 0.0 copy-start.4
  14.3 1.5 %collective-permute-done.7.refs_2_.refs_6_ = bf16[272,128]{1,0:T(8,128)(2,1)S(1)} collective-permute-done((bf16[272,128]{1,0:T(8,128)(2,1)S(1)}, bf16[272,128]{1,0:T(8,128)(2,1)S(1)}, u32[]{:S(2)}, u32[]{:S(2)}) %collective-permute-start.7) | collective-permute-done | bytes 69664 | tf_op jit(solution)/shard_map/ppermute | solution.py:394
  15.8 0.0 collective-permute-start.8
  15.8 0.7 %collective-permute-done.5.refs_0_.refs_4_ = bf16[272,128]{1,0:T(8,128)(2,1)S(1)} collective-permute-done((bf16[272,128]{1,0:T(8,128)(2,1)S(1)}, bf16[272,128]{1,0:T(8,128)(2,1)S(1)}, u32[]{:S(2)}, u32[]{:S(2)}) %collective-permute-start.5) | collective-permute-done | bytes 69664 | tf_op jit(solution)/shard_map/ppermute | solution.py:394
  16.5 0.3 %collective-permute-start.6 = (bf16[272,128]{1,0:T(8,128)(2,1)S(1)}, bf16[272,128]{1,0:T(8,128)(2,1)S(1)}, u32[]{:S(2)}, u32[]{:S(2)}) collective-permute-start(bf16[272,128]{1,0:T(8,128)(2,1)S(1)} %collective-permute-done.5.refs_0_.refs_4_), channel_id=1, source_target_pairs={{0,1},{1,0},{2,3},{3,2},{4,5},{5,4},{6,7},{7,6},{8,9},{9,8},{10,11... | collective-permute-start | bytes 208904 | tf_op jit(solution)/shard_map/ppermute | solution.py:394
  16.7 0.0 collective-permute-done.4.refs_6_
  16.8 0.0 collective-permute-done.2.refs_2_.refs_4_
  16.8 0.0 copy-done
  16.8 0.0 copy-done.2
  16.8 0.0 copy-done.3
  16.8 0.0 copy-done.4
  16.8 1.3 %columns_0.1 = (f32[1024,128]{1,0:T(8,128)S(1)}, bf16[2,4,128,256]{3,2,1,0:T(8,128)(2,1)S(1)}, f32[512,128]{1,0:T(8,128)S(1)}, f32[512,128]{1,0:T(8,128)S(1)}, f...) custom-call(s32[1]{0:T(128)S(6)} %copy.14.crop_ref, ...), custom_call_target="tpu_custom_call" | custom-call | flops 800000000 | bytes 1000000 | tf_op jit(solution)/shard_map/columns_0/pallas_call | solution.py:467
  18.1 0.0 collective-permute-done.8.refs_3_.refs_7_
  18.1 0.0 collective-permute-done.6.refs_1_.refs_5_
  18.1 1.3 %columns_1.1 = (f32[1024,128]{1,0:T(8,128)S(1)}, bf16[2,4,128,256]{3,2,1,0:T(8,128)(2,1)S(1)}, f32[512,128]{1,0:T(8,128)S(1)}, f32[512,128]{1,0:T(8,128)S(1)}, f...) custom-call(s32[1]{0:T(128)S(6)} %copy.14.crop_ref, ...), custom_call_target="tpu_custom_call", output_to_operand_aliasing={{0}: (11, {}), {1}: (12, {})} | custom-call | flops 800000000 | bytes 1000000 | tf_op jit(solution)/shard_map/columns_1/pallas_call | solution.py:467
  19.4 4.3 %rest.1 = (bf16[8,8,128]{2,1,0:T(8,128)(2,1)}, bf16[8,8,128]{2,1,0:T(8,128)(2,1)}, f32[6,128,128]{2,1,0:T(8,128)}) custom-call(bf16[6,128,128]{2,1,0:T(8,128)(2,1)S(1)} %copy-done, f32[3,64,128]{2,1,0:T(8,128)S(1)} %get-tuple-element.21.own_ref, f32[8,128]{1,0:T(8,128)S(1)} %get-tuple-element.22.refs_8_.gains_ref, ...), custom_call_target="tpu_custom_call" | custom-call | tf_op jit(solution)/shard_map/rest/pallas_call | solution.py:489
  (2 shorter events, 0.0 us)
Async XLA Ops:
  2.2 14.5 %copy-start = (bf16[6,128,128]{2,1,0:T(8,128)(2,1)S(1)}, bf16[6,128,128]{2,1,0:T(8,128)(2,1)}, u32[]{:S(2)}) copy-start(bf16[6,128,128]{2,1,0:T(8,128)(2,1)} %weights_ref.5) | copy-start | bytes 589828
  2.2 1.6 %collective-permute-start = (bf16[144,128]{1,0:T(8,128)(2,1)}, bf16[144,128]{1,0:T(8,128)(2,1)S(1)}, u32[]{:S(2)}, u32[]{:S(2)}) collective-permute-start(bf16[144,128]{1,0:T(8,128)(2,1)} %pack.1.in_ref), channel_id=1, source_target_pairs={{0,1},{1,0},{2,3},{3,2},{4,5},{5,4},{6,7},{7,6},{8,9},{9,8},{10,11... | collective-permute-start | bytes 110600 | tf_op jit(solution)/shard_map/ppermute | solution.py:394
  2.8 0.8 %copy-start.1 = (bf16[144,128]{1,0:T(8,128)(2,1)S(1)}, bf16[144,128]{1,0:T(8,128)(2,1)}, u32[]{:S(2)}) copy-start(bf16[144,128]{1,0:T(8,128)(2,1)} %pack.1.in_ref) | copy-start | bytes 110596
  3.5 13.2 %copy-start.2 = (bf16[8,8,128]{2,1,0:T(8,128)(2,1)S(1)}, bf16[8,8,128]{2,1,0:T(8,128)(2,1)}, u32[]{:S(2)}) copy-start(bf16[8,8,128]{2,1,0:T(8,128)(2,1)} %refs_7_.1) | copy-start | bytes 49156
  3.9 7.0 %collective-permute-start.1 = (bf16[272,128]{1,0:T(8,128)(2,1)S(1)}, bf16[272,128]{1,0:T(8,128)(2,1)S(1)}, u32[]{:S(2)}, u32[]{:S(2)}) collective-permute-start(bf16[272,128]{1,0:T(8,128)(2,1)S(1)} %join.1.refs_0_), channel_id=1, source_target_pairs={{0,8},{1,5},{2,10},{3,7},{4,12},{5,1},{6,14},{7,3},{8,0},{9,13},{1... | collective-permute-start | bytes 208904 | tf_op jit(solution)/shard_map/ppermute | solution.py:394
  7.8 5.9 %collective-permute-start.3 = (bf16[144,128]{1,0:T(8,128)(2,1)S(1)}, bf16[144,128]{1,0:T(8,128)(2,1)S(1)}, u32[]{:S(2)}, u32[]{:S(2)}) collective-permute-start(bf16[144,128]{1,0:T(8,128)(2,1)S(1)} %copy-done.1), channel_id=1, source_target_pairs={{0,12},{1,13},{2,14},{3,15},{4,8},{5,9},{6,10},{7,11},{8,4},{9,5},... | collective-permute-start | bytes 110600 | tf_op jit(solution)/shard_map/ppermute | solution.py:394
  9.1 6.6 %collective-permute-start.7 = (bf16[272,128]{1,0:T(8,128)(2,1)S(1)}, bf16[272,128]{1,0:T(8,128)(2,1)S(1)}, u32[]{:S(2)}, u32[]{:S(2)}) collective-permute-start(bf16[272,128]{1,0:T(8,128)(2,1)S(1)} %join.1.refs_0_), channel_id=1, source_target_pairs={{0,6},{1,15},{2,4},{3,13},{4,2},{5,11},{6,0},{7,9},{8,14},{9,7},{1... | collective-permute-start | bytes 208904 | tf_op jit(solution)/shard_map/ppermute | solution.py:394
  10.3 6.2 %collective-permute-start.5 = (bf16[272,128]{1,0:T(8,128)(2,1)S(1)}, bf16[272,128]{1,0:T(8,128)(2,1)S(1)}, u32[]{:S(2)}, u32[]{:S(2)}) collective-permute-start(bf16[272,128]{1,0:T(8,128)(2,1)S(1)} %join.1.refs_0_), channel_id=1, source_target_pairs={{0,2},{1,11},{2,0},{3,9},{4,6},{5,15},{6,4},{7,13},{8,10},{9,3},{1... | collective-permute-start | bytes 208904 | tf_op jit(solution)/shard_map/ppermute | solution.py:394
  10.8 5.9 %collective-permute-start.2 = (bf16[272,128]{1,0:T(8,128)(2,1)S(1)}, bf16[272,128]{1,0:T(8,128)(2,1)S(1)}, u32[]{:S(2)}, u32[]{:S(2)}) collective-permute-start(bf16[272,128]{1,0:T(8,128)(2,1)S(1)} %collective-permute-done.1.refs_1_.refs_3_), channel_id=1, source_target_pairs={{0,1},{1,0},{2,3},{3,2},{4,5},{5,4},{6,7},{7,6},{8,9},{9,8},{10,11... | collective-permute-start | bytes 208904 | tf_op jit(solution)/shard_map/ppermute | solution.py:394
  13.6 3.1 %collective-permute-start.4 = (bf16[144,128]{1,0:T(8,128)(2,1)S(1)}, bf16[144,128]{1,0:T(8,128)(2,1)S(1)}, u32[]{:S(2)}, u32[]{:S(2)}) collective-permute-start(bf16[144,128]{1,0:T(8,128)(2,1)S(1)} %collective-permute-done.3.refs_5_), channel_id=1, source_target_pairs={{0,1},{1,0},{2,3},{3,2},{4,5},{5,4},{6,7},{7,6},{8,9},{9,8},{10,11... | collective-permute-start | bytes 110600 | tf_op jit(solution)/shard_map/ppermute | solution.py:394
  14.3 2.5 %copy-start.3 = (f32[128]{0:T(128)S(1)}, f32[128]{0:T(128)}, u32[]{:S(2)}) copy-start(f32[128]{0:T(128)} %param.11) | copy-start | bytes 1540
  14.3 2.5 %copy-start.4 = (f32[128]{0:T(128)S(1)}, f32[128]{0:T(128)}, u32[]{:S(2)}) copy-start(f32[128]{0:T(128)} %param.12) | copy-start | bytes 1540
  15.8 2.3 %collective-permute-start.8 = (bf16[272,128]{1,0:T(8,128)(2,1)S(1)}, bf16[272,128]{1,0:T(8,128)(2,1)S(1)}, u32[]{:S(2)}, u32[]{:S(2)}) collective-permute-start(bf16[272,128]{1,0:T(8,128)(2,1)S(1)} %collective-permute-done.7.refs_2_.refs_6_), channel_id=1, source_target_pairs={{0,1},{1,0},{2,3},{3,2},{4,5},{5,4},{6,7},{7,6},{8,9},{9,8},{10,11... | collective-permute-start | bytes 208904 | tf_op jit(solution)/shard_map/ppermute | solution.py:394
  16.5 1.6 %collective-permute-start.6 = (bf16[272,128]{1,0:T(8,128)(2,1)S(1)}, bf16[272,128]{1,0:T(8,128)(2,1)S(1)}, u32[]{:S(2)}, u32[]{:S(2)}) collective-permute-start(bf16[272,128]{1,0:T(8,128)(2,1)S(1)} %collective-permute-done.5.refs_0_.refs_4_), channel_id=1, source_target_pairs={{0,1},{1,0},{2,3},{3,2},{4,5},{5,4},{6,7},{7,6},{8,9},{9,8},{10,11... | collective-permute-start | bytes 208904 | tf_op jit(solution)/shard_map/ppermute | solution.py:394

commit v21 on v20

--- a/solution.py
+++ b/solution.py
@@ -172,6 +172,10 @@
     return split
 
 
+def doubled(top, bottom):
+    return jnp.concatenate([top, bottom], axis=0).astype(jnp.bfloat16)
+
+
 def triangle(blocks, groups, steps, vectors_at, factors_at, start_at, store_at, beside=None):
     def block(a, _):
         if beside is not None:
@@ -180,13 +184,24 @@
             totals = list(totals)
             vectors = vectors_at(q)
             factors = factors_at(a, q)
-            for inner in range(SUB):
-                rows = [vectors(g, inner) for g in range(groups)]
-                for lane in range(SUB):
+            rows = [
+                [doubled(vectors(g, inner), vectors(g + 1, inner)) for g in range(0, groups, 2)]
+                for inner in range(SUB)
+            ]
+            for lane in range(SUB):
+                chains = [[None, None] for _ in range(groups // 2)]
+                for inner in range(SUB):
                     factor = factors(lane, inner)
-                    for g in range(groups):
-                        at = lane * groups + g
-                        totals[at] = totals[at] + factor * rows[g]
+                    factor = doubled(factor, factor)
+                    for g in range(groups // 2):
+                        term = factor * rows[inner][g]
+                        chain = chains[g][inner % 2]
+                        chains[g][inner % 2] = term if chain is None else chain + term
+                for g in range(groups // 2):
+                    wide = (chains[g][0] + chains[g][1]).astype(jnp.float32)
+                    at = lane * groups + 2 * g
+                    totals[at] = totals[at] + wide[0:SUB]
+                    totals[at + 1] = totals[at + 1] + wide[SUB:]
             return tuple(totals)
 
         totals = tuple(start_at(a, g, lane) for lane in range(SUB) for g in range(groups))

time: 24.1 us -> 23.4 us (0.971)
  Pallas kernels: 8.56 us -> 7.89 us
    pallas_call x2, Pallas kernels: 2.6 us -> 2.22 us  [gathered_body(): pl.pallas_call(functools.partial(columns_kernel, n_row, n_col, side_x, ch...]
    pallas_call x1, Pallas kernels: 4.35 us -> 4.05 us  [gathered_body(): pl.pallas_call(functools.partial(rest_kernel, n_row, n_col), name='rest',...]
where the time goes in v21:
time: 23.4 us; the launch traced here: 23.1 us
  starting transfers between devices  8.29 us (35%)
  Pallas kernels  7.89 us (34%)
  waiting for transfers between devices  4.76 us (20%)
  between operations  1.38 us (6%)
  local copies, waits for them, and re-layouts  0.79 us (3%)
    ppermute x9, starting transfers between devices, flip(): return lax.ppermute(block, ('row', 'col'), pairs)  8.29 us
    ppermute x9, waiting for transfers between devices, flip(): return lax.ppermute(block, ('row', 'col'), pairs)  4.76 us
    pallas_call x1, Pallas kernels, gathered_body(): pl.pallas_call(functools.partial(rest_kernel, n_row, n_col), name='rest',...  4.05 us
    pallas_call x2, Pallas kernels, gathered_body(): pl.pallas_call(functools.partial(columns_kernel, n_row, n_col, side_x, ch...  2.22 us
    pallas_call x1, Pallas kernels, gathered_body(): pl.pallas_call(pack_kernel, name='pack', out_shape=jax.ShapeDtypeStruct((...  1.6 us
    unnamed x10, local copies, waits for them, and re-layouts  0.79 us
  transfers between devices with their start and end apart: 9, of which 4 were waited for; matrix products, arithmetic and copies ran while one was open for 0% of the time, Pallas kernels for 5%

profile of v21, /device:TPU:0, one launch (start us, length us, event | category | flops | bytes accessed | tf_op | source)
XLA Modules:
  0.0 23.1 jit_solution(6106405664789130973)
XLA Ops:
  0.6 1.6 %pack.1.in_ref = bf16[144,128]{1,0:T(8,128)(2,1)} custom-call(bf16[8,8,128]{2,1,0:T(8,128)(2,1)} %refs_7_.1, s32[8,8]{1,0:T(8,128)} %mask_hbm.1, bf16[64,128]{1,0:T(8,128)(2,1)} %bitcast.6, f32[1,128]{1,0:T(1,128)} %bitcast.3), custom_call_target="tpu_custom_call" | custom-call | tf_op jit(solution)/shard_map/pack/pallas_call | solution.py:427
  2.2 0.0 copy-start
  2.2 0.5 %collective-permute-start = (bf16[144,128]{1,0:T(8,128)(2,1)}, bf16[144,128]{1,0:T(8,128)(2,1)S(1)}, u32[]{:S(2)}, u32[]{:S(2)}) collective-permute-start(bf16[144,128]{1,0:T(8,128)(2,1)} %pack.1.in_ref), channel_id=1, source_target_pairs={{0,1},{1,0},{2,3},{3,2},{4,5},{5,4},{6,7},{7,6},{8,9},{9,8},{10,11... | collective-permute-start | bytes 110600 | tf_op jit(solution)/shard_map/ppermute | solution.py:409
  2.8 0.0 copy-start.1
  2.8 0.8 %copy-done.1 = bf16[144,128]{1,0:T(8,128)(2,1)S(1)} copy-done((bf16[144,128]{1,0:T(8,128)(2,1)S(1)}, bf16[144,128]{1,0:T(8,128)(2,1)}, u32[]{:S(2)}) %copy-start.1) | copy-done | bytes 36888
  3.5 0.0 copy-start.2
  3.5 0.3 %collective-permute-done.twin_ref = bf16[144,128]{1,0:T(8,128)(2,1)S(1)} collective-permute-done((bf16[144,128]{1,0:T(8,128)(2,1)}, bf16[144,128]{1,0:T(8,128)(2,1)S(1)}, u32[]{:S(2)}, u32[]{:S(2)}) %collective-permute-start) | collective-permute-done | bytes 36896 | tf_op jit(solution)/shard_map/ppermute | solution.py:409
  3.9 3.9 %collective-permute-start.1 = (bf16[272,128]{1,0:T(8,128)(2,1)S(1)}, bf16[272,128]{1,0:T(8,128)(2,1)S(1)}, u32[]{:S(2)}, u32[]{:S(2)}) collective-permute-start(bf16[272,128]{1,0:T(8,128)(2,1)S(1)} %join.1.refs_0_), channel_id=1, source_target_pairs={{0,8},{1,5},{2,10},{3,7},{4,12},{5,1},{6,14},{7,3},{8,0},{9,13},{1... | collective-permute-start | bytes 208904 | tf_op jit(solution)/shard_map/ppermute | solution.py:409
  7.8 1.3 %collective-permute-start.3 = (bf16[144,128]{1,0:T(8,128)(2,1)S(1)}, bf16[144,128]{1,0:T(8,128)(2,1)S(1)}, u32[]{:S(2)}, u32[]{:S(2)}) collective-permute-start(bf16[144,128]{1,0:T(8,128)(2,1)S(1)} %copy-done.1), channel_id=1, source_target_pairs={{0,12},{1,13},{2,14},{3,15},{4,8},{5,9},{6,10},{7,11},{8,4},{9,5},... | collective-permute-start | bytes 110600 | tf_op jit(solution)/shard_map/ppermute | solution.py:409
  9.1 1.2 %collective-permute-start.7 = (bf16[272,128]{1,0:T(8,128)(2,1)S(1)}, bf16[272,128]{1,0:T(8,128)(2,1)S(1)}, u32[]{:S(2)}, u32[]{:S(2)}) collective-permute-start(bf16[272,128]{1,0:T(8,128)(2,1)S(1)} %join.1.refs_0_), channel_id=1, source_target_pairs={{0,6},{1,15},{2,4},{3,13},{4,2},{5,11},{6,0},{7,9},{8,14},{9,7},{1... | collective-permute-start | bytes 208904 | tf_op jit(solution)/shard_map/ppermute | solution.py:409
  10.3 0.5 %collective-permute-start.5 = (bf16[272,128]{1,0:T(8,128)(2,1)S(1)}, bf16[272,128]{1,0:T(8,128)(2,1)S(1)}, u32[]{:S(2)}, u32[]{:S(2)}) collective-permute-start(bf16[272,128]{1,0:T(8,128)(2,1)S(1)} %join.1.refs_0_), channel_id=1, source_target_pairs={{0,2},{1,11},{2,0},{3,9},{4,6},{5,15},{6,4},{7,13},{8,10},{9,3},{1... | collective-permute-start | bytes 208904 | tf_op jit(solution)/shard_map/ppermute | solution.py:409
  10.8 0.0 collective-permute-done.1.refs_1_.refs_3_
  10.8 0.5 %collective-permute-start.2 = (bf16[272,128]{1,0:T(8,128)(2,1)S(1)}, bf16[272,128]{1,0:T(8,128)(2,1)S(1)}, u32[]{:S(2)}, u32[]{:S(2)}) collective-permute-start(bf16[272,128]{1,0:T(8,128)(2,1)S(1)} %collective-permute-done.1.refs_1_.refs_3_), channel_id=1, source_target_pairs={{0,1},{1,0},{2,3},{3,2},{4,5},{5,4},{6,7},{7,6},{8,9},{9,8},{10,11... | collective-permute-start | bytes 208904 | tf_op jit(solution)/shard_map/ppermute | solution.py:409
  11.3 2.3 %collective-permute-done.3.refs_5_ = bf16[144,128]{1,0:T(8,128)(2,1)S(1)} collective-permute-done((bf16[144,128]{1,0:T(8,128)(2,1)S(1)}, bf16[144,128]{1,0:T(8,128)(2,1)S(1)}, u32[]{:S(2)}, u32[]{:S(2)}) %collective-permute-start.3) | collective-permute-done | bytes 36896 | tf_op jit(solution)/shard_map/ppermute | solution.py:409
  13.6 0.0 collective-permute-start.4
  14.3 0.0 copy-start.3
  14.3 0.0 copy-start.4
  14.3 1.5 %collective-permute-done.7.refs_2_.refs_6_ = bf16[272,128]{1,0:T(8,128)(2,1)S(1)} collective-permute-done((bf16[272,128]{1,0:T(8,128)(2,1)S(1)}, bf16[272,128]{1,0:T(8,128)(2,1)S(1)}, u32[]{:S(2)}, u32[]{:S(2)}) %collective-permute-start.7) | collective-permute-done | bytes 69664 | tf_op jit(solution)/shard_map/ppermute | solution.py:409
  15.8 0.0 collective-permute-start.8
  15.8 0.7 %collective-permute-done.5.refs_0_.refs_4_ = bf16[272,128]{1,0:T(8,128)(2,1)S(1)} collective-permute-done((bf16[272,128]{1,0:T(8,128)(2,1)S(1)}, bf16[272,128]{1,0:T(8,128)(2,1)S(1)}, u32[]{:S(2)}, u32[]{:S(2)}) %collective-permute-start.5) | collective-permute-done | bytes 69664 | tf_op jit(solution)/shard_map/ppermute | solution.py:409
  16.5 0.3 %collective-permute-start.6 = (bf16[272,128]{1,0:T(8,128)(2,1)S(1)}, bf16[272,128]{1,0:T(8,128)(2,1)S(1)}, u32[]{:S(2)}, u32[]{:S(2)}) collective-permute-start(bf16[272,128]{1,0:T(8,128)(2,1)S(1)} %collective-permute-done.5.refs_0_.refs_4_), channel_id=1, source_target_pairs={{0,1},{1,0},{2,3},{3,2},{4,5},{5,4},{6,7},{7,6},{8,9},{9,8},{10,11... | collective-permute-start | bytes 208904 | tf_op jit(solution)/shard_map/ppermute | solution.py:409
  16.7 0.0 collective-permute-done.4.refs_6_
  16.8 0.0 collective-permute-done.2.refs_2_.refs_4_
  16.8 0.0 copy-done
  16.8 0.0 copy-done.2
  16.8 0.0 copy-done.3
  16.8 0.0 copy-done.4
  16.8 1.1 %columns_0.1 = (f32[1024,128]{1,0:T(8,128)S(1)}, bf16[2,4,128,256]{3,2,1,0:T(8,128)(2,1)S(1)}, f32[512,128]{1,0:T(8,128)S(1)}, f32[512,128]{1,0:T(8,128)S(1)}, f...) custom-call(s32[1]{0:T(128)S(6)} %copy.14.crop_ref, ...), custom_call_target="tpu_custom_call" | custom-call | flops 800000000 | bytes 1000000 | tf_op jit(solution)/shard_map/columns_0/pallas_call | solution.py:482
  17.9 0.0 collective-permute-done.8.refs_3_.refs_7_
  17.9 0.0 collective-permute-done.6.refs_1_.refs_5_
  17.9 1.1 %columns_1.1 = (f32[1024,128]{1,0:T(8,128)S(1)}, bf16[2,4,128,256]{3,2,1,0:T(8,128)(2,1)S(1)}, f32[512,128]{1,0:T(8,128)S(1)}, f32[512,128]{1,0:T(8,128)S(1)}, f...) custom-call(s32[1]{0:T(128)S(6)} %copy.14.crop_ref, ...), custom_call_target="tpu_custom_call", output_to_operand_aliasing={{0}: (11, {}), {1}: (12, {})} | custom-call | flops 800000000 | bytes 1000000 | tf_op jit(solution)/shard_map/columns_1/pallas_call | solution.py:482
  19.1 4.1 %rest.1 = (bf16[8,8,128]{2,1,0:T(8,128)(2,1)}, bf16[8,8,128]{2,1,0:T(8,128)(2,1)}, f32[6,128,128]{2,1,0:T(8,128)}) custom-call(bf16[6,128,128]{2,1,0:T(8,128)(2,1)S(1)} %copy-done, f32[3,64,128]{2,1,0:T(8,128)S(1)} %get-tuple-element.21.own_ref, f32[8,128]{1,0:T(8,128)S(1)} %get-tuple-element.22.refs_8_.gains_ref, ...), custom_call_target="tpu_custom_call" | custom-call | tf_op jit(solution)/shard_map/rest/pallas_call | solution.py:504
  (2 shorter events, 0.0 us)
Async XLA Ops:
  2.2 14.5 %copy-start = (bf16[6,128,128]{2,1,0:T(8,128)(2,1)S(1)}, bf16[6,128,128]{2,1,0:T(8,128)(2,1)}, u32[]{:S(2)}) copy-start(bf16[6,128,128]{2,1,0:T(8,128)(2,1)} %weights_ref.5) | copy-start | bytes 589828
  2.2 1.6 %collective-permute-start = (bf16[144,128]{1,0:T(8,128)(2,1)}, bf16[144,128]{1,0:T(8,128)(2,1)S(1)}, u32[]{:S(2)}, u32[]{:S(2)}) collective-permute-start(bf16[144,128]{1,0:T(8,128)(2,1)} %pack.1.in_ref), channel_id=1, source_target_pairs={{0,1},{1,0},{2,3},{3,2},{4,5},{5,4},{6,7},{7,6},{8,9},{9,8},{10,11... | collective-permute-start | bytes 110600 | tf_op jit(solution)/shard_map/ppermute | solution.py:409
  2.8 0.8 %copy-start.1 = (bf16[144,128]{1,0:T(8,128)(2,1)S(1)}, bf16[144,128]{1,0:T(8,128)(2,1)}, u32[]{:S(2)}) copy-start(bf16[144,128]{1,0:T(8,128)(2,1)} %pack.1.in_ref) | copy-start | bytes 110596
  3.5 13.2 %copy-start.2 = (bf16[8,8,128]{2,1,0:T(8,128)(2,1)S(1)}, bf16[8,8,128]{2,1,0:T(8,128)(2,1)}, u32[]{:S(2)}) copy-start(bf16[8,8,128]{2,1,0:T(8,128)(2,1)} %refs_7_.1) | copy-start | bytes 49156
  3.9 7.0 %collective-permute-start.1 = (bf16[272,128]{1,0:T(8,128)(2,1)S(1)}, bf16[272,128]{1,0:T(8,128)(2,1)S(1)}, u32[]{:S(2)}, u32[]{:S(2)}) collective-permute-start(bf16[272,128]{1,0:T(8,128)(2,1)S(1)} %join.1.refs_0_), channel_id=1, source_target_pairs={{0,8},{1,5},{2,10},{3,7},{4,12},{5,1},{6,14},{7,3},{8,0},{9,13},{1... | collective-permute-start | bytes 208904 | tf_op jit(solution)/shard_map/ppermute | solution.py:409
  7.8 5.9 %collective-permute-start.3 = (bf16[144,128]{1,0:T(8,128)(2,1)S(1)}, bf16[144,128]{1,0:T(8,128)(2,1)S(1)}, u32[]{:S(2)}, u32[]{:S(2)}) collective-permute-start(bf16[144,128]{1,0:T(8,128)(2,1)S(1)} %copy-done.1), channel_id=1, source_target_pairs={{0,12},{1,13},{2,14},{3,15},{4,8},{5,9},{6,10},{7,11},{8,4},{9,5},... | collective-permute-start | bytes 110600 | tf_op jit(solution)/shard_map/ppermute | solution.py:409
  9.1 6.6 %collective-permute-start.7 = (bf16[272,128]{1,0:T(8,128)(2,1)S(1)}, bf16[272,128]{1,0:T(8,128)(2,1)S(1)}, u32[]{:S(2)}, u32[]{:S(2)}) collective-permute-start(bf16[272,128]{1,0:T(8,128)(2,1)S(1)} %join.1.refs_0_), channel_id=1, source_target_pairs={{0,6},{1,15},{2,4},{3,13},{4,2},{5,11},{6,0},{7,9},{8,14},{9,7},{1... | collective-permute-start | bytes 208904 | tf_op jit(solution)/shard_map/ppermute | solution.py:409
  10.3 6.2 %collective-permute-start.5 = (bf16[272,128]{1,0:T(8,128)(2,1)S(1)}, bf16[272,128]{1,0:T(8,128)(2,1)S(1)}, u32[]{:S(2)}, u32[]{:S(2)}) collective-permute-start(bf16[272,128]{1,0:T(8,128)(2,1)S(1)} %join.1.refs_0_), channel_id=1, source_target_pairs={{0,2},{1,11},{2,0},{3,9},{4,6},{5,15},{6,4},{7,13},{8,10},{9,3},{1... | collective-permute-start | bytes 208904 | tf_op jit(solution)/shard_map/ppermute | solution.py:409
  10.8 5.9 %collective-permute-start.2 = (bf16[272,128]{1,0:T(8,128)(2,1)S(1)}, bf16[272,128]{1,0:T(8,128)(2,1)S(1)}, u32[]{:S(2)}, u32[]{:S(2)}) collective-permute-start(bf16[272,128]{1,0:T(8,128)(2,1)S(1)} %collective-permute-done.1.refs_1_.refs_3_), channel_id=1, source_target_pairs={{0,1},{1,0},{2,3},{3,2},{4,5},{5,4},{6,7},{7,6},{8,9},{9,8},{10,11... | collective-permute-start | bytes 208904 | tf_op jit(solution)/shard_map/ppermute | solution.py:409
  13.6 3.1 %collective-permute-start.4 = (bf16[144,128]{1,0:T(8,128)(2,1)S(1)}, bf16[144,128]{1,0:T(8,128)(2,1)S(1)}, u32[]{:S(2)}, u32[]{:S(2)}) collective-permute-start(bf16[144,128]{1,0:T(8,128)(2,1)S(1)} %collective-permute-done.3.refs_5_), channel_id=1, source_target_pairs={{0,1},{1,0},{2,3},{3,2},{4,5},{5,4},{6,7},{7,6},{8,9},{9,8},{10,11... | collective-permute-start | bytes 110600 | tf_op jit(solution)/shard_map/ppermute | solution.py:409
  14.3 2.5 %copy-start.3 = (f32[128]{0:T(128)S(1)}, f32[128]{0:T(128)}, u32[]{:S(2)}) copy-start(f32[128]{0:T(128)} %param.11) | copy-start | bytes 1540
  14.3 2.5 %copy-start.4 = (f32[128]{0:T(128)S(1)}, f32[128]{0:T(128)}, u32[]{:S(2)}) copy-start(f32[128]{0:T(128)} %param.12) | copy-start | bytes 1540
  15.8 2.1 %collective-permute-start.8 = (bf16[272,128]{1,0:T(8,128)(2,1)S(1)}, bf16[272,128]{1,0:T(8,128)(2,1)S(1)}, u32[]{:S(2)}, u32[]{:S(2)}) collective-permute-start(bf16[272,128]{1,0:T(8,128)(2,1)S(1)} %collective-permute-done.7.refs_2_.refs_6_), channel_id=1, source_target_pairs={{0,1},{1,0},{2,3},{3,2},{4,5},{5,4},{6,7},{7,6},{8,9},{9,8},{10,11... | collective-permute-start | bytes 208904 | tf_op jit(solution)/shard_map/ppermute | solution.py:409
  16.5 1.5 %collective-permute-start.6 = (bf16[272,128]{1,0:T(8,128)(2,1)S(1)}, bf16[272,128]{1,0:T(8,128)(2,1)S(1)}, u32[]{:S(2)}, u32[]{:S(2)}) collective-permute-start(bf16[272,128]{1,0:T(8,128)(2,1)S(1)} %collective-permute-done.5.refs_0_.refs_4_), channel_id=1, source_target_pairs={{0,1},{1,0},{2,3},{3,2},{4,5},{5,4},{6,7},{7,6},{8,9},{9,8},{10,11... | collective-permute-start | bytes 208904 | tf_op jit(solution)/shard_map/ppermute | solution.py:409

commit v22 on v21

--- a/solution.py
+++ b/solution.py
@@ -312,7 +312,18 @@
 
 def rest_kernel(n_row, n_col, weights_ref, own_ref, gains_ref, tri_ref, flip_ref, *refs):
     groups = [refs[at * 4 : at * 4 + 4] for at in range(n_col // 2)]
-    update_ref, pair_grad_ref, weight_grad_ref, back_ref, hat_ref, d_ref, sum_ref = refs[4 * (n_col // 2) :]
+    outs, (back_ref, hat_ref, d_ref, sum_ref, update_ref, pair_grad_ref, weight_grad_ref, sems) = (
+        refs[4 * (n_col // 2) : 4 * (n_col // 2) + 3],
+        refs[4 * (n_col // 2) + 3 :],
+    )
+    copies = [
+        pltpu.make_async_copy(update_ref, outs[0], sems.at[0]),
+        pltpu.make_async_copy(pair_grad_ref, outs[1], sems.at[1]),
+    ]
+    copies += [
+        pltpu.make_async_copy(weight_grad_ref.at[at : at + 2], outs[2].at[at : at + 2], sems.at[2 + at // 2])
+        for at in range(0, 6, 2)
+    ]
     channels = tri_ref.shape[-1]
     tile = SUB * SUB
     size = n_row * tile
@@ -333,6 +344,7 @@
         lin = jnp.dot(normed_out, weights_ref[5], preferred_element_type=f32)
         if col == 0:
             update_ref[...] = (own_ref[2] * lin[0:tile]).astype(bf16).reshape(update_ref.shape)
+            copies[0].start()
         d_ref[rows, 4 * channels : 5 * channels] = (backs_ref[0] * lin).astype(bf16)
         back = backs_ref[1]
         second = jnp.mean(back * x_hat, axis=-1, keepdims=True)
@@ -378,26 +390,27 @@
         sum_ref[:, 2 * channels :] += jnp.dot(flip_ref[0, a], chunk(d_ref, a, 0, 2), preferred_element_type=f32)
 
     sum_ref[...] = jnp.zeros(sum_ref.shape, f32)
+    scale = 1.0 / residues
     triangle(n_row, n_col, n_col, by_right, along, zero, store(0), early_sums)
-    triangle(n_row, n_col, n_row, by_left, down, zero, store(1), left_sums)
-
-    scale = 1.0 / residues
-    flipped = jnp.concatenate([flip_ref[0, col] for col in range(n_col)], axis=1)
-    right_sums = jnp.dot(flipped, d_ref[:, 2 * channels : 4 * channels], preferred_element_type=f32)
-    for s in range(2):
-        part = slice(s * channels, (s + 1) * channels)
-        weight_grad_ref[s] = sum_ref[:, (2 + s) * channels : (3 + s) * channels] * scale
-        weight_grad_ref[2 + s] = right_sums[:, part] * scale
     weight_grad_ref[4] = sum_ref[:, 0:channels] * scale
     weight_grad_ref[5] = sum_ref[:, channels : 2 * channels].T * scale
-    total = jnp.zeros((tile, channels), f32)
-    for s in range(5):
-        total = total + lax.dot_general(
-            d_ref[0:tile, s * channels : (s + 1) * channels], weights_ref[s],
-            (((1,), (1,)), ((), ())), preferred_element_type=f32,
-        )
+    copies[4].start()
+    triangle(n_row, n_col, n_row, by_left, down, zero, store(1), left_sums)
+    weight_grad_ref[0] = sum_ref[:, 2 * channels : 3 * channels] * scale
+    weight_grad_ref[1] = sum_ref[:, 3 * channels :] * scale
+    copies[2].start()
+    wide = jnp.concatenate([weights_ref[s] for s in range(5)], axis=1)
+    total = lax.dot_general(d_ref[0:tile], wide, (((1,), (1,)), ((), ())), preferred_element_type=f32)
     grad = norm_back(total * gains_ref[0:1], own_ref[0], own_ref[1])
+    flipped = jnp.concatenate([flip_ref[0, col] for col in range(n_col)], axis=1)
+    right_sums = jnp.dot(flipped, d_ref[:, 2 * channels : 4 * channels], preferred_element_type=f32) * scale
     pair_grad_ref[...] = grad.astype(bf16).reshape(pair_grad_ref.shape)
+    weight_grad_ref[2] = right_sums[:, 0:channels]
+    weight_grad_ref[3] = right_sums[:, channels:]
+    copies[1].start()
+    copies[3].start()
+    for copy in copies:
+        copy.wait()
 
 
 def flip(block, n_row, n_col, even, odd):
@@ -418,6 +431,7 @@
     f32, bf16 = jnp.float32, jnp.bfloat16
     vmem = pl.BlockSpec(memory_space=pltpu.VMEM)
     smem = pl.BlockSpec(memory_space=pltpu.SMEM)
+    anywhere = pl.BlockSpec(memory_space=pl.ANY)
     hbm = pl.BlockSpec(memory_space=pltpu.HBM)
     in_gain, out_gain = in_gain.reshape(1, channels), out_gain.reshape(1, channels)
 
@@ -510,12 +524,16 @@
             jax.ShapeDtypeStruct(weights.shape, f32),
         ),
         in_specs=[vmem] * (5 + len(parts)),
-        out_specs=(vmem, vmem, vmem),
+        out_specs=(anywhere,) * 3,
         scratch_shapes=[
             pltpu.VMEM((pairs, channels), f32),
             pltpu.VMEM((pairs, channels), bf16),
             pltpu.VMEM((pairs, 5 * channels), bf16),
             pltpu.VMEM((channels, 4 * channels), f32),
+            pltpu.VMEM(pair_act.shape, bf16),
+            pltpu.VMEM(pair_act.shape, bf16),
+            pltpu.VMEM(weights.shape, f32),
+            pltpu.SemaphoreType.DMA((5,)),
         ],
         compiler_params=limit(16),
     )(weights, *extra, *tri, *parts)

time: 23.4 us -> 23.4 us (level)
  no operation moved by 1% of the time
where the time goes in v22:
time: 23.4 us; the launch traced here: 23 us
  starting transfers between devices  8.29 us (35%)
  Pallas kernels  7.83 us (33%)
  waiting for transfers between devices  4.76 us (20%)
  between operations  1.38 us (6%)
  local copies, waits for them, and re-layouts  0.79 us (3%)
    ppermute x9, starting transfers between devices, flip(): return lax.ppermute(block, ('row', 'col'), pairs)  8.29 us
    ppermute x9, waiting for transfers between devices, flip(): return lax.ppermute(block, ('row', 'col'), pairs)  4.76 us
    pallas_call x1, Pallas kernels, gathered_body(): pl.pallas_call(functools.partial(rest_kernel, n_row, n_col), name='rest',...  4 us
    pallas_call x2, Pallas kernels, gathered_body(): pl.pallas_call(functools.partial(columns_kernel, n_row, n_col, side_x, ch...  2.22 us
    pallas_call x1, Pallas kernels, gathered_body(): pl.pallas_call(pack_kernel, name='pack', out_shape=jax.ShapeDtypeStruct((...  1.6 us
    unnamed x10, local copies, waits for them, and re-layouts  0.79 us
  transfers between devices with their start and end apart: 9, of which 4 were waited for; matrix products, arithmetic and copies ran while one was open for 0% of the time, Pallas kernels for 5%

profile of v22, /device:TPU:0, one launch (start us, length us, event | category | flops | bytes accessed | tf_op | source)
XLA Modules:
  0.0 23.0 jit_solution(9088887843472085466)
XLA Ops:
  0.6 1.6 %pack.1.in_ref = bf16[144,128]{1,0:T(8,128)(2,1)} custom-call(bf16[8,8,128]{2,1,0:T(8,128)(2,1)} %refs_7_.1, s32[8,8]{1,0:T(8,128)} %mask_hbm.1, bf16[64,128]{1,0:T(8,128)(2,1)} %bitcast.6, f32[1,128]{1,0:T(1,128)} %bitcast.3), custom_call_target="tpu_custom_call" | custom-call | tf_op jit(solution)/shard_map/pack/pallas_call | solution.py:441
  2.2 0.0 copy-start
  2.2 0.5 %collective-permute-start = (bf16[144,128]{1,0:T(8,128)(2,1)}, bf16[144,128]{1,0:T(8,128)(2,1)S(1)}, u32[]{:S(2)}, u32[]{:S(2)}) collective-permute-start(bf16[144,128]{1,0:T(8,128)(2,1)} %pack.1.in_ref), channel_id=1, source_target_pairs={{0,1},{1,0},{2,3},{3,2},{4,5},{5,4},{6,7},{7,6},{8,9},{9,8},{10,11... | collective-permute-start | bytes 110600 | tf_op jit(solution)/shard_map/ppermute | solution.py:422
  2.8 0.0 copy-start.1
  2.8 0.8 %copy-done.1 = bf16[144,128]{1,0:T(8,128)(2,1)S(1)} copy-done((bf16[144,128]{1,0:T(8,128)(2,1)S(1)}, bf16[144,128]{1,0:T(8,128)(2,1)}, u32[]{:S(2)}) %copy-start.1) | copy-done | bytes 36888
  3.5 0.0 copy-start.2
  3.5 0.3 %collective-permute-done.twin_ref = bf16[144,128]{1,0:T(8,128)(2,1)S(1)} collective-permute-done((bf16[144,128]{1,0:T(8,128)(2,1)}, bf16[144,128]{1,0:T(8,128)(2,1)S(1)}, u32[]{:S(2)}, u32[]{:S(2)}) %collective-permute-start) | collective-permute-done | bytes 36896 | tf_op jit(solution)/shard_map/ppermute | solution.py:422
  3.9 3.9 %collective-permute-start.1 = (bf16[272,128]{1,0:T(8,128)(2,1)S(1)}, bf16[272,128]{1,0:T(8,128)(2,1)S(1)}, u32[]{:S(2)}, u32[]{:S(2)}) collective-permute-start(bf16[272,128]{1,0:T(8,128)(2,1)S(1)} %join.1.refs_0_), channel_id=1, source_target_pairs={{0,8},{1,5},{2,10},{3,7},{4,12},{5,1},{6,14},{7,3},{8,0},{9,13},{1... | collective-permute-start | bytes 208904 | tf_op jit(solution)/shard_map/ppermute | solution.py:422
  7.8 1.3 %collective-permute-start.3 = (bf16[144,128]{1,0:T(8,128)(2,1)S(1)}, bf16[144,128]{1,0:T(8,128)(2,1)S(1)}, u32[]{:S(2)}, u32[]{:S(2)}) collective-permute-start(bf16[144,128]{1,0:T(8,128)(2,1)S(1)} %copy-done.1), channel_id=1, source_target_pairs={{0,12},{1,13},{2,14},{3,15},{4,8},{5,9},{6,10},{7,11},{8,4},{9,5},... | collective-permute-start | bytes 110600 | tf_op jit(solution)/shard_map/ppermute | solution.py:422
  9.1 1.2 %collective-permute-start.7 = (bf16[272,128]{1,0:T(8,128)(2,1)S(1)}, bf16[272,128]{1,0:T(8,128)(2,1)S(1)}, u32[]{:S(2)}, u32[]{:S(2)}) collective-permute-start(bf16[272,128]{1,0:T(8,128)(2,1)S(1)} %join.1.refs_0_), channel_id=1, source_target_pairs={{0,6},{1,15},{2,4},{3,13},{4,2},{5,11},{6,0},{7,9},{8,14},{9,7},{1... | collective-permute-start | bytes 208904 | tf_op jit(solution)/shard_map/ppermute | solution.py:422
  10.3 0.5 %collective-permute-start.5 = (bf16[272,128]{1,0:T(8,128)(2,1)S(1)}, bf16[272,128]{1,0:T(8,128)(2,1)S(1)}, u32[]{:S(2)}, u32[]{:S(2)}) collective-permute-start(bf16[272,128]{1,0:T(8,128)(2,1)S(1)} %join.1.refs_0_), channel_id=1, source_target_pairs={{0,2},{1,11},{2,0},{3,9},{4,6},{5,15},{6,4},{7,13},{8,10},{9,3},{1... | collective-permute-start | bytes 208904 | tf_op jit(solution)/shard_map/ppermute | solution.py:422
  10.8 0.0 collective-permute-done.1.refs_1_.refs_3_
  10.8 0.5 %collective-permute-start.2 = (bf16[272,128]{1,0:T(8,128)(2,1)S(1)}, bf16[272,128]{1,0:T(8,128)(2,1)S(1)}, u32[]{:S(2)}, u32[]{:S(2)}) collective-permute-start(bf16[272,128]{1,0:T(8,128)(2,1)S(1)} %collective-permute-done.1.refs_1_.refs_3_), channel_id=1, source_target_pairs={{0,1},{1,0},{2,3},{3,2},{4,5},{5,4},{6,7},{7,6},{8,9},{9,8},{10,11... | collective-permute-start | bytes 208904 | tf_op jit(solution)/shard_map/ppermute | solution.py:422
  11.3 2.3 %collective-permute-done.3.refs_5_ = bf16[144,128]{1,0:T(8,128)(2,1)S(1)} collective-permute-done((bf16[144,128]{1,0:T(8,128)(2,1)S(1)}, bf16[144,128]{1,0:T(8,128)(2,1)S(1)}, u32[]{:S(2)}, u32[]{:S(2)}) %collective-permute-start.3) | collective-permute-done | bytes 36896 | tf_op jit(solution)/shard_map/ppermute | solution.py:422
  13.6 0.0 collective-permute-start.4
  14.3 0.0 copy-start.3
  14.3 0.0 copy-start.4
  14.3 1.5 %collective-permute-done.7.refs_2_.refs_6_ = bf16[272,128]{1,0:T(8,128)(2,1)S(1)} collective-permute-done((bf16[272,128]{1,0:T(8,128)(2,1)S(1)}, bf16[272,128]{1,0:T(8,128)(2,1)S(1)}, u32[]{:S(2)}, u32[]{:S(2)}) %collective-permute-start.7) | collective-permute-done | bytes 69664 | tf_op jit(solution)/shard_map/ppermute | solution.py:422
  15.8 0.0 collective-permute-start.8
  15.8 0.7 %collective-permute-done.5.refs_0_.refs_4_ = bf16[272,128]{1,0:T(8,128)(2,1)S(1)} collective-permute-done((bf16[272,128]{1,0:T(8,128)(2,1)S(1)}, bf16[272,128]{1,0:T(8,128)(2,1)S(1)}, u32[]{:S(2)}, u32[]{:S(2)}) %collective-permute-start.5) | collective-permute-done | bytes 69664 | tf_op jit(solution)/shard_map/ppermute | solution.py:422
  16.5 0.3 %collective-permute-start.6 = (bf16[272,128]{1,0:T(8,128)(2,1)S(1)}, bf16[272,128]{1,0:T(8,128)(2,1)S(1)}, u32[]{:S(2)}, u32[]{:S(2)}) collective-permute-start(bf16[272,128]{1,0:T(8,128)(2,1)S(1)} %collective-permute-done.5.refs_0_.refs_4_), channel_id=1, source_target_pairs={{0,1},{1,0},{2,3},{3,2},{4,5},{5,4},{6,7},{7,6},{8,9},{9,8},{10,11... | collective-permute-start | bytes 208904 | tf_op jit(solution)/shard_map/ppermute | solution.py:422
  16.7 0.0 collective-permute-done.4.refs_6_
  16.8 0.0 collective-permute-done.2.refs_2_.refs_4_
  16.8 0.0 copy-done
  16.8 0.0 copy-done.2
  16.8 0.0 copy-done.3
  16.8 0.0 copy-done.4
  16.8 1.1 %columns_0.1 = (f32[1024,128]{1,0:T(8,128)S(1)}, bf16[2,4,128,256]{3,2,1,0:T(8,128)(2,1)S(1)}, f32[512,128]{1,0:T(8,128)S(1)}, f32[512,128]{1,0:T(8,128)S(1)}, f...) custom-call(s32[1]{0:T(128)S(6)} %copy.14.crop_ref, ...), custom_call_target="tpu_custom_call" | custom-call | flops 800000000 | bytes 1000000 | tf_op jit(solution)/shard_map/columns_0/pallas_call | solution.py:496
  17.9 0.0 collective-permute-done.8.refs_3_.refs_7_
  17.9 0.0 collective-permute-done.6.refs_1_.refs_5_
  17.9 1.1 %columns_1.1 = (f32[1024,128]{1,0:T(8,128)S(1)}, bf16[2,4,128,256]{3,2,1,0:T(8,128)(2,1)S(1)}, f32[512,128]{1,0:T(8,128)S(1)}, f32[512,128]{1,0:T(8,128)S(1)}, f...) custom-call(s32[1]{0:T(128)S(6)} %copy.14.crop_ref, ...), custom_call_target="tpu_custom_call", output_to_operand_aliasing={{0}: (11, {}), {1}: (12, {})} | custom-call | flops 800000000 | bytes 1000000 | tf_op jit(solution)/shard_map/columns_1/pallas_call | solution.py:496
  19.1 4.0 %rest.1 = (bf16[8,8,128]{2,1,0:T(8,128)(2,1)}, bf16[8,8,128]{2,1,0:T(8,128)(2,1)}, f32[6,128,128]{2,1,0:T(8,128)}) custom-call(bf16[6,128,128]{2,1,0:T(8,128)(2,1)S(1)} %copy-done, f32[3,64,128]{2,1,0:T(8,128)S(1)} %get-tuple-element.21.own_ref, f32[8,128]{1,0:T(8,128)S(1)} %get-tuple-element.22.refs_8_.gains_ref, ...), custom_call_target="tpu_custom_call" | custom-call | tf_op jit(solution)/shard_map/rest/pallas_call | solution.py:518
  (2 shorter events, 0.0 us)
Async XLA Ops:
  2.2 14.5 %copy-start = (bf16[6,128,128]{2,1,0:T(8,128)(2,1)S(1)}, bf16[6,128,128]{2,1,0:T(8,128)(2,1)}, u32[]{:S(2)}) copy-start(bf16[6,128,128]{2,1,0:T(8,128)(2,1)} %weights_ref.5) | copy-start | bytes 589828
  2.2 1.6 %collective-permute-start = (bf16[144,128]{1,0:T(8,128)(2,1)}, bf16[144,128]{1,0:T(8,128)(2,1)S(1)}, u32[]{:S(2)}, u32[]{:S(2)}) collective-permute-start(bf16[144,128]{1,0:T(8,128)(2,1)} %pack.1.in_ref), channel_id=1, source_target_pairs={{0,1},{1,0},{2,3},{3,2},{4,5},{5,4},{6,7},{7,6},{8,9},{9,8},{10,11... | collective-permute-start | bytes 110600 | tf_op jit(solution)/shard_map/ppermute | solution.py:422
  2.8 0.8 %copy-start.1 = (bf16[144,128]{1,0:T(8,128)(2,1)S(1)}, bf16[144,128]{1,0:T(8,128)(2,1)}, u32[]{:S(2)}) copy-start(bf16[144,128]{1,0:T(8,128)(2,1)} %pack.1.in_ref) | copy-start | bytes 110596
  3.5 13.2 %copy-start.2 = (bf16[8,8,128]{2,1,0:T(8,128)(2,1)S(1)}, bf16[8,8,128]{2,1,0:T(8,128)(2,1)}, u32[]{:S(2)}) copy-start(bf16[8,8,128]{2,1,0:T(8,128)(2,1)} %refs_7_.1) | copy-start | bytes 49156
  3.9 7.0 %collective-permute-start.1 = (bf16[272,128]{1,0:T(8,128)(2,1)S(1)}, bf16[272,128]{1,0:T(8,128)(2,1)S(1)}, u32[]{:S(2)}, u32[]{:S(2)}) collective-permute-start(bf16[272,128]{1,0:T(8,128)(2,1)S(1)} %join.1.refs_0_), channel_id=1, source_target_pairs={{0,8},{1,5},{2,10},{3,7},{4,12},{5,1},{6,14},{7,3},{8,0},{9,13},{1... | collective-permute-start | bytes 208904 | tf_op jit(solution)/shard_map/ppermute | solution.py:422
  7.8 5.9 %collective-permute-start.3 = (bf16[144,128]{1,0:T(8,128)(2,1)S(1)}, bf16[144,128]{1,0:T(8,128)(2,1)S(1)}, u32[]{:S(2)}, u32[]{:S(2)}) collective-permute-start(bf16[144,128]{1,0:T(8,128)(2,1)S(1)} %copy-done.1), channel_id=1, source_target_pairs={{0,12},{1,13},{2,14},{3,15},{4,8},{5,9},{6,10},{7,11},{8,4},{9,5},... | collective-permute-start | bytes 110600 | tf_op jit(solution)/shard_map/ppermute | solution.py:422
  9.1 6.6 %collective-permute-start.7 = (bf16[272,128]{1,0:T(8,128)(2,1)S(1)}, bf16[272,128]{1,0:T(8,128)(2,1)S(1)}, u32[]{:S(2)}, u32[]{:S(2)}) collective-permute-start(bf16[272,128]{1,0:T(8,128)(2,1)S(1)} %join.1.refs_0_), channel_id=1, source_target_pairs={{0,6},{1,15},{2,4},{3,13},{4,2},{5,11},{6,0},{7,9},{8,14},{9,7},{1... | collective-permute-start | bytes 208904 | tf_op jit(solution)/shard_map/ppermute | solution.py:422
  10.3 6.2 %collective-permute-start.5 = (bf16[272,128]{1,0:T(8,128)(2,1)S(1)}, bf16[272,128]{1,0:T(8,128)(2,1)S(1)}, u32[]{:S(2)}, u32[]{:S(2)}) collective-permute-start(bf16[272,128]{1,0:T(8,128)(2,1)S(1)} %join.1.refs_0_), channel_id=1, source_target_pairs={{0,2},{1,11},{2,0},{3,9},{4,6},{5,15},{6,4},{7,13},{8,10},{9,3},{1... | collective-permute-start | bytes 208904 | tf_op jit(solution)/shard_map/ppermute | solution.py:422
  10.8 5.9 %collective-permute-start.2 = (bf16[272,128]{1,0:T(8,128)(2,1)S(1)}, bf16[272,128]{1,0:T(8,128)(2,1)S(1)}, u32[]{:S(2)}, u32[]{:S(2)}) collective-permute-start(bf16[272,128]{1,0:T(8,128)(2,1)S(1)} %collective-permute-done.1.refs_1_.refs_3_), channel_id=1, source_target_pairs={{0,1},{1,0},{2,3},{3,2},{4,5},{5,4},{6,7},{7,6},{8,9},{9,8},{10,11... | collective-permute-start | bytes 208904 | tf_op jit(solution)/shard_map/ppermute | solution.py:422
  13.6 3.1 %collective-permute-start.4 = (bf16[144,128]{1,0:T(8,128)(2,1)S(1)}, bf16[144,128]{1,0:T(8,128)(2,1)S(1)}, u32[]{:S(2)}, u32[]{:S(2)}) collective-permute-start(bf16[144,128]{1,0:T(8,128)(2,1)S(1)} %collective-permute-done.3.refs_5_), channel_id=1, source_target_pairs={{0,1},{1,0},{2,3},{3,2},{4,5},{5,4},{6,7},{7,6},{8,9},{9,8},{10,11... | collective-permute-start | bytes 110600 | tf_op jit(solution)/shard_map/ppermute | solution.py:422
  14.3 2.5 %copy-start.3 = (f32[128]{0:T(128)S(1)}, f32[128]{0:T(128)}, u32[]{:S(2)}) copy-start(f32[128]{0:T(128)} %param.11) | copy-start | bytes 1540
  14.3 2.5 %copy-start.4 = (f32[128]{0:T(128)S(1)}, f32[128]{0:T(128)}, u32[]{:S(2)}) copy-start(f32[128]{0:T(128)} %param.12) | copy-start | bytes 1540
  15.8 2.1 %collective-permute-start.8 = (bf16[272,128]{1,0:T(8,128)(2,1)S(1)}, bf16[272,128]{1,0:T(8,128)(2,1)S(1)}, u32[]{:S(2)}, u32[]{:S(2)}) collective-permute-start(bf16[272,128]{1,0:T(8,128)(2,1)S(1)} %collective-permute-done.7.refs_2_.refs_6_), channel_id=1, source_target_pairs={{0,1},{1,0},{2,3},{3,2},{4,5},{5,4},{6,7},{7,6},{8,9},{9,8},{10,11... | collective-permute-start | bytes 208904 | tf_op jit(solution)/shard_map/ppermute | solution.py:422
  16.5 1.5 %collective-permute-start.6 = (bf16[272,128]{1,0:T(8,128)(2,1)S(1)}, bf16[272,128]{1,0:T(8,128)(2,1)S(1)}, u32[]{:S(2)}, u32[]{:S(2)}) collective-permute-start(bf16[272,128]{1,0:T(8,128)(2,1)S(1)} %collective-permute-done.5.refs_0_.refs_4_), channel_id=1, source_target_pairs={{0,1},{1,0},{2,3},{3,2},{4,5},{5,4},{6,7},{7,6},{8,9},{9,8},{10,11... | collective-permute-start | bytes 208904 | tf_op jit(solution)/shard_map/ppermute | solution.py:422

commit v23 on v21

--- a/solution.py
+++ b/solution.py
@@ -177,7 +177,7 @@
 
 
 def triangle(blocks, groups, steps, vectors_at, factors_at, start_at, store_at, beside=None):
-    def block(a, _):
+    def block(a):
         if beside is not None:
             beside(a)
         def step(q, totals):
@@ -212,9 +212,9 @@
                 totals = step(q, totals)
         for g in range(groups):
             store_at(a, g, [totals[lane * groups + g] for lane in range(SUB)])
-        return 0
-
-    lax.fori_loop(0, blocks, block, 0)
+
+    for a in range(blocks):
+        block(a)
 
 
 def spread(ref, row):
@@ -390,12 +390,8 @@
         weight_grad_ref[2 + s] = right_sums[:, part] * scale
     weight_grad_ref[4] = sum_ref[:, 0:channels] * scale
     weight_grad_ref[5] = sum_ref[:, channels : 2 * channels].T * scale
-    total = jnp.zeros((tile, channels), f32)
-    for s in range(5):
-        total = total + lax.dot_general(
-            d_ref[0:tile, s * channels : (s + 1) * channels], weights_ref[s],
-            (((1,), (1,)), ((), ())), preferred_element_type=f32,
-        )
+    wide = jnp.concatenate([weights_ref[s] for s in range(5)], axis=1)
+    total = lax.dot_general(d_ref[0:tile], wide, (((1,), (1,)), ((), ())), preferred_element_type=f32)
     grad = norm_back(total * gains_ref[0:1], own_ref[0], own_ref[1])
     pair_grad_ref[...] = grad.astype(bf16).reshape(pair_grad_ref.shape)
 

time: 23.4 us -> 23.2 us (level)
  Pallas kernels: 7.89 us -> 7.64 us
    pallas_call x1, Pallas kernels: 4.05 us -> 3.64 us  [gathered_body(): pl.pallas_call(functools.partial(rest_kernel, n_row, n_col), name='rest',...]
where the time goes in v23:
time: 23.2 us; the launch traced here: 22.9 us
  starting transfers between devices  8.29 us (36%)
  Pallas kernels  7.64 us (33%)
  waiting for transfers between devices  4.76 us (21%)
  between operations  1.38 us (6%)
  local copies, waits for them, and re-layouts  0.79 us (3%)
    ppermute x9, starting transfers between devices, flip(): return lax.ppermute(block, ('row', 'col'), pairs)  8.29 us
    ppermute x9, waiting for transfers between devices, flip(): return lax.ppermute(block, ('row', 'col'), pairs)  4.76 us
    pallas_call x1, Pallas kernels, gathered_body(): pl.pallas_call(functools.partial(rest_kernel, n_row, n_col), name='rest',...  3.64 us
    pallas_call x2, Pallas kernels, gathered_body(): pl.pallas_call(functools.partial(columns_kernel, n_row, n_col, side_x, ch...  2.38 us
    pallas_call x1, Pallas kernels, gathered_body(): pl.pallas_call(pack_kernel, name='pack', out_shape=jax.ShapeDtypeStruct((...  1.6 us
    unnamed x10, local copies, waits for them, and re-layouts  0.79 us
  transfers between devices with their start and end apart: 9, of which 4 were waited for; matrix products, arithmetic and copies ran while one was open for 0% of the time, Pallas kernels for 5%

profile of v23, /device:TPU:0, one launch (start us, length us, event | category | flops | bytes accessed | tf_op | source)
XLA Modules:
  0.0 22.9 jit_solution(4149385437732974722)
XLA Ops:
  0.6 1.6 %pack.1.in_ref = bf16[144,128]{1,0:T(8,128)(2,1)} custom-call(bf16[8,8,128]{2,1,0:T(8,128)(2,1)} %refs_7_.1, s32[8,8]{1,0:T(8,128)} %mask_hbm.1, bf16[64,128]{1,0:T(8,128)(2,1)} %bitcast.6, f32[1,128]{1,0:T(1,128)} %bitcast.3), custom_call_target="tpu_custom_call" | custom-call | tf_op jit(solution)/shard_map/pack/pallas_call | solution.py:423
  2.2 0.0 copy-start
  2.2 0.5 %collective-permute-start = (bf16[144,128]{1,0:T(8,128)(2,1)}, bf16[144,128]{1,0:T(8,128)(2,1)S(1)}, u32[]{:S(2)}, u32[]{:S(2)}) collective-permute-start(bf16[144,128]{1,0:T(8,128)(2,1)} %pack.1.in_ref), channel_id=1, source_target_pairs={{0,1},{1,0},{2,3},{3,2},{4,5},{5,4},{6,7},{7,6},{8,9},{9,8},{10,11... | collective-permute-start | bytes 110600 | tf_op jit(solution)/shard_map/ppermute | solution.py:405
  2.8 0.0 copy-start.1
  2.8 0.8 %copy-done.1 = bf16[144,128]{1,0:T(8,128)(2,1)S(1)} copy-done((bf16[144,128]{1,0:T(8,128)(2,1)S(1)}, bf16[144,128]{1,0:T(8,128)(2,1)}, u32[]{:S(2)}) %copy-start.1) | copy-done | bytes 36888
  3.5 0.0 copy-start.2
  3.5 0.3 %collective-permute-done.twin_ref = bf16[144,128]{1,0:T(8,128)(2,1)S(1)} collective-permute-done((bf16[144,128]{1,0:T(8,128)(2,1)}, bf16[144,128]{1,0:T(8,128)(2,1)S(1)}, u32[]{:S(2)}, u32[]{:S(2)}) %collective-permute-start) | collective-permute-done | bytes 36896 | tf_op jit(solution)/shard_map/ppermute | solution.py:405
  3.9 3.9 %collective-permute-start.1 = (bf16[272,128]{1,0:T(8,128)(2,1)S(1)}, bf16[272,128]{1,0:T(8,128)(2,1)S(1)}, u32[]{:S(2)}, u32[]{:S(2)}) collective-permute-start(bf16[272,128]{1,0:T(8,128)(2,1)S(1)} %join.1.refs_0_), channel_id=1, source_target_pairs={{0,8},{1,5},{2,10},{3,7},{4,12},{5,1},{6,14},{7,3},{8,0},{9,13},{1... | collective-permute-start | bytes 208904 | tf_op jit(solution)/shard_map/ppermute | solution.py:405
  7.8 1.3 %collective-permute-start.3 = (bf16[144,128]{1,0:T(8,128)(2,1)S(1)}, bf16[144,128]{1,0:T(8,128)(2,1)S(1)}, u32[]{:S(2)}, u32[]{:S(2)}) collective-permute-start(bf16[144,128]{1,0:T(8,128)(2,1)S(1)} %copy-done.1), channel_id=1, source_target_pairs={{0,12},{1,13},{2,14},{3,15},{4,8},{5,9},{6,10},{7,11},{8,4},{9,5},... | collective-permute-start | bytes 110600 | tf_op jit(solution)/shard_map/ppermute | solution.py:405
  9.1 1.2 %collective-permute-start.7 = (bf16[272,128]{1,0:T(8,128)(2,1)S(1)}, bf16[272,128]{1,0:T(8,128)(2,1)S(1)}, u32[]{:S(2)}, u32[]{:S(2)}) collective-permute-start(bf16[272,128]{1,0:T(8,128)(2,1)S(1)} %join.1.refs_0_), channel_id=1, source_target_pairs={{0,6},{1,15},{2,4},{3,13},{4,2},{5,11},{6,0},{7,9},{8,14},{9,7},{1... | collective-permute-start | bytes 208904 | tf_op jit(solution)/shard_map/ppermute | solution.py:405
  10.3 0.5 %collective-permute-start.5 = (bf16[272,128]{1,0:T(8,128)(2,1)S(1)}, bf16[272,128]{1,0:T(8,128)(2,1)S(1)}, u32[]{:S(2)}, u32[]{:S(2)}) collective-permute-start(bf16[272,128]{1,0:T(8,128)(2,1)S(1)} %join.1.refs_0_), channel_id=1, source_target_pairs={{0,2},{1,11},{2,0},{3,9},{4,6},{5,15},{6,4},{7,13},{8,10},{9,3},{1... | collective-permute-start | bytes 208904 | tf_op jit(solution)/shard_map/ppermute | solution.py:405
  10.8 0.0 collective-permute-done.1.refs_1_.refs_3_
  10.8 0.5 %collective-permute-start.2 = (bf16[272,128]{1,0:T(8,128)(2,1)S(1)}, bf16[272,128]{1,0:T(8,128)(2,1)S(1)}, u32[]{:S(2)}, u32[]{:S(2)}) collective-permute-start(bf16[272,128]{1,0:T(8,128)(2,1)S(1)} %collective-permute-done.1.refs_1_.refs_3_), channel_id=1, source_target_pairs={{0,1},{1,0},{2,3},{3,2},{4,5},{5,4},{6,7},{7,6},{8,9},{9,8},{10,11... | collective-permute-start | bytes 208904 | tf_op jit(solution)/shard_map/ppermute | solution.py:405
  11.3 2.3 %collective-permute-done.3.refs_5_ = bf16[144,128]{1,0:T(8,128)(2,1)S(1)} collective-permute-done((bf16[144,128]{1,0:T(8,128)(2,1)S(1)}, bf16[144,128]{1,0:T(8,128)(2,1)S(1)}, u32[]{:S(2)}, u32[]{:S(2)}) %collective-permute-start.3) | collective-permute-done | bytes 36896 | tf_op jit(solution)/shard_map/ppermute | solution.py:405
  13.6 0.0 collective-permute-start.4
  14.3 0.0 copy-start.3
  14.3 0.0 copy-start.4
  14.3 1.5 %collective-permute-done.7.refs_2_.refs_6_ = bf16[272,128]{1,0:T(8,128)(2,1)S(1)} collective-permute-done((bf16[272,128]{1,0:T(8,128)(2,1)S(1)}, bf16[272,128]{1,0:T(8,128)(2,1)S(1)}, u32[]{:S(2)}, u32[]{:S(2)}) %collective-permute-start.7) | collective-permute-done | bytes 69664 | tf_op jit(solution)/shard_map/ppermute | solution.py:405
  15.8 0.0 collective-permute-start.8
  15.8 0.7 %collective-permute-done.5.refs_0_.refs_4_ = bf16[272,128]{1,0:T(8,128)(2,1)S(1)} collective-permute-done((bf16[272,128]{1,0:T(8,128)(2,1)S(1)}, bf16[272,128]{1,0:T(8,128)(2,1)S(1)}, u32[]{:S(2)}, u32[]{:S(2)}) %collective-permute-start.5) | collective-permute-done | bytes 69664 | tf_op jit(solution)/shard_map/ppermute | solution.py:405
  16.5 0.3 %collective-permute-start.6 = (bf16[272,128]{1,0:T(8,128)(2,1)S(1)}, bf16[272,128]{1,0:T(8,128)(2,1)S(1)}, u32[]{:S(2)}, u32[]{:S(2)}) collective-permute-start(bf16[272,128]{1,0:T(8,128)(2,1)S(1)} %collective-permute-done.5.refs_0_.refs_4_), channel_id=1, source_target_pairs={{0,1},{1,0},{2,3},{3,2},{4,5},{5,4},{6,7},{7,6},{8,9},{9,8},{10,11... | collective-permute-start | bytes 208904 | tf_op jit(solution)/shard_map/ppermute | solution.py:405
  16.7 0.0 collective-permute-done.4.refs_6_
  16.8 0.0 collective-permute-done.2.refs_2_.refs_4_
  16.8 0.0 copy-done
  16.8 0.0 copy-done.2
  16.8 0.0 copy-done.3
  16.8 0.0 copy-done.4
  16.8 1.2 %columns_0.1 = (f32[1024,128]{1,0:T(8,128)S(1)}, bf16[2,4,128,256]{3,2,1,0:T(8,128)(2,1)S(1)}, f32[512,128]{1,0:T(8,128)S(1)}, f32[512,128]{1,0:T(8,128)S(1)}, f...) custom-call(s32[1]{0:T(128)S(6)} %copy.14.crop_ref, ...), custom_call_target="tpu_custom_call" | custom-call | flops 800000000 | bytes 1000000 | tf_op jit(solution)/shard_map/columns_0/pallas_call | solution.py:478
  18.0 0.0 collective-permute-done.8.refs_3_.refs_7_
  18.0 0.0 collective-permute-done.6.refs_1_.refs_5_
  18.0 1.2 %columns_1.1 = (f32[1024,128]{1,0:T(8,128)S(1)}, bf16[2,4,128,256]{3,2,1,0:T(8,128)(2,1)S(1)}, f32[512,128]{1,0:T(8,128)S(1)}, f32[512,128]{1,0:T(8,128)S(1)}, f...) custom-call(s32[1]{0:T(128)S(6)} %copy.14.crop_ref, ...), custom_call_target="tpu_custom_call", output_to_operand_aliasing={{0}: (11, {}), {1}: (12, {})} | custom-call | flops 800000000 | bytes 1000000 | tf_op jit(solution)/shard_map/columns_1/pallas_call | solution.py:478
  19.2 3.6 %rest.1 = (bf16[8,8,128]{2,1,0:T(8,128)(2,1)}, bf16[8,8,128]{2,1,0:T(8,128)(2,1)}, f32[6,128,128]{2,1,0:T(8,128)}) custom-call(bf16[6,128,128]{2,1,0:T(8,128)(2,1)S(1)} %copy-done, f32[3,64,128]{2,1,0:T(8,128)S(1)} %get-tuple-element.21.own_ref, f32[8,128]{1,0:T(8,128)S(1)} %get-tuple-element.22.refs_8_.gains_ref, ...), custom_call_target="tpu_custom_call" | custom-call | tf_op jit(solution)/shard_map/rest/pallas_call | solution.py:500
  (2 shorter events, 0.0 us)
Async XLA Ops:
  2.2 14.5 %copy-start = (bf16[6,128,128]{2,1,0:T(8,128)(2,1)S(1)}, bf16[6,128,128]{2,1,0:T(8,128)(2,1)}, u32[]{:S(2)}) copy-start(bf16[6,128,128]{2,1,0:T(8,128)(2,1)} %weights_ref.5) | copy-start | bytes 589828
  2.2 1.6 %collective-permute-start = (bf16[144,128]{1,0:T(8,128)(2,1)}, bf16[144,128]{1,0:T(8,128)(2,1)S(1)}, u32[]{:S(2)}, u32[]{:S(2)}) collective-permute-start(bf16[144,128]{1,0:T(8,128)(2,1)} %pack.1.in_ref), channel_id=1, source_target_pairs={{0,1},{1,0},{2,3},{3,2},{4,5},{5,4},{6,7},{7,6},{8,9},{9,8},{10,11... | collective-permute-start | bytes 110600 | tf_op jit(solution)/shard_map/ppermute | solution.py:405
  2.8 0.8 %copy-start.1 = (bf16[144,128]{1,0:T(8,128)(2,1)S(1)}, bf16[144,128]{1,0:T(8,128)(2,1)}, u32[]{:S(2)}) copy-start(bf16[144,128]{1,0:T(8,128)(2,1)} %pack.1.in_ref) | copy-start | bytes 110596
  3.5 13.2 %copy-start.2 = (bf16[8,8,128]{2,1,0:T(8,128)(2,1)S(1)}, bf16[8,8,128]{2,1,0:T(8,128)(2,1)}, u32[]{:S(2)}) copy-start(bf16[8,8,128]{2,1,0:T(8,128)(2,1)} %refs_7_.1) | copy-start | bytes 49156
  3.9 7.0 %collective-permute-start.1 = (bf16[272,128]{1,0:T(8,128)(2,1)S(1)}, bf16[272,128]{1,0:T(8,128)(2,1)S(1)}, u32[]{:S(2)}, u32[]{:S(2)}) collective-permute-start(bf16[272,128]{1,0:T(8,128)(2,1)S(1)} %join.1.refs_0_), channel_id=1, source_target_pairs={{0,8},{1,5},{2,10},{3,7},{4,12},{5,1},{6,14},{7,3},{8,0},{9,13},{1... | collective-permute-start | bytes 208904 | tf_op jit(solution)/shard_map/ppermute | solution.py:405
  7.8 5.9 %collective-permute-start.3 = (bf16[144,128]{1,0:T(8,128)(2,1)S(1)}, bf16[144,128]{1,0:T(8,128)(2,1)S(1)}, u32[]{:S(2)}, u32[]{:S(2)}) collective-permute-start(bf16[144,128]{1,0:T(8,128)(2,1)S(1)} %copy-done.1), channel_id=1, source_target_pairs={{0,12},{1,13},{2,14},{3,15},{4,8},{5,9},{6,10},{7,11},{8,4},{9,5},... | collective-permute-start | bytes 110600 | tf_op jit(solution)/shard_map/ppermute | solution.py:405
  9.1 6.6 %collective-permute-start.7 = (bf16[272,128]{1,0:T(8,128)(2,1)S(1)}, bf16[272,128]{1,0:T(8,128)(2,1)S(1)}, u32[]{:S(2)}, u32[]{:S(2)}) collective-permute-start(bf16[272,128]{1,0:T(8,128)(2,1)S(1)} %join.1.refs_0_), channel_id=1, source_target_pairs={{0,6},{1,15},{2,4},{3,13},{4,2},{5,11},{6,0},{7,9},{8,14},{9,7},{1... | collective-permute-start | bytes 208904 | tf_op jit(solution)/shard_map/ppermute | solution.py:405
  10.3 6.2 %collective-permute-start.5 = (bf16[272,128]{1,0:T(8,128)(2,1)S(1)}, bf16[272,128]{1,0:T(8,128)(2,1)S(1)}, u32[]{:S(2)}, u32[]{:S(2)}) collective-permute-start(bf16[272,128]{1,0:T(8,128)(2,1)S(1)} %join.1.refs_0_), channel_id=1, source_target_pairs={{0,2},{1,11},{2,0},{3,9},{4,6},{5,15},{6,4},{7,13},{8,10},{9,3},{1... | collective-permute-start | bytes 208904 | tf_op jit(solution)/shard_map/ppermute | solution.py:405
  10.8 5.9 %collective-permute-start.2 = (bf16[272,128]{1,0:T(8,128)(2,1)S(1)}, bf16[272,128]{1,0:T(8,128)(2,1)S(1)}, u32[]{:S(2)}, u32[]{:S(2)}) collective-permute-start(bf16[272,128]{1,0:T(8,128)(2,1)S(1)} %collective-permute-done.1.refs_1_.refs_3_), channel_id=1, source_target_pairs={{0,1},{1,0},{2,3},{3,2},{4,5},{5,4},{6,7},{7,6},{8,9},{9,8},{10,11... | collective-permute-start | bytes 208904 | tf_op jit(solution)/shard_map/ppermute | solution.py:405
  13.6 3.1 %collective-permute-start.4 = (bf16[144,128]{1,0:T(8,128)(2,1)S(1)}, bf16[144,128]{1,0:T(8,128)(2,1)S(1)}, u32[]{:S(2)}, u32[]{:S(2)}) collective-permute-start(bf16[144,128]{1,0:T(8,128)(2,1)S(1)} %collective-permute-done.3.refs_5_), channel_id=1, source_target_pairs={{0,1},{1,0},{2,3},{3,2},{4,5},{5,4},{6,7},{7,6},{8,9},{9,8},{10,11... | collective-permute-start | bytes 110600 | tf_op jit(solution)/shard_map/ppermute | solution.py:405
  14.3 2.5 %copy-start.3 = (f32[128]{0:T(128)S(1)}, f32[128]{0:T(128)}, u32[]{:S(2)}) copy-start(f32[128]{0:T(128)} %param.11) | copy-start | bytes 1540
  14.3 2.5 %copy-start.4 = (f32[128]{0:T(128)S(1)}, f32[128]{0:T(128)}, u32[]{:S(2)}) copy-start(f32[128]{0:T(128)} %param.12) | copy-start | bytes 1540
  15.8 2.2 %collective-permute-start.8 = (bf16[272,128]{1,0:T(8,128)(2,1)S(1)}, bf16[272,128]{1,0:T(8,128)(2,1)S(1)}, u32[]{:S(2)}, u32[]{:S(2)}) collective-permute-start(bf16[272,128]{1,0:T(8,128)(2,1)S(1)} %collective-permute-done.7.refs_2_.refs_6_), channel_id=1, source_target_pairs={{0,1},{1,0},{2,3},{3,2},{4,5},{5,4},{6,7},{7,6},{8,9},{9,8},{10,11... | collective-permute-start | bytes 208904 | tf_op jit(solution)/shard_map/ppermute | solution.py:405
  16.5 1.5 %collective-permute-start.6 = (bf16[272,128]{1,0:T(8,128)(2,1)S(1)}, bf16[272,128]{1,0:T(8,128)(2,1)S(1)}, u32[]{:S(2)}, u32[]{:S(2)}) collective-permute-start(bf16[272,128]{1,0:T(8,128)(2,1)S(1)} %collective-permute-done.5.refs_0_.refs_4_), channel_id=1, source_target_pairs={{0,1},{1,0},{2,3},{3,2},{4,5},{5,4},{6,7},{7,6},{8,9},{9,8},{10,11... | collective-permute-start | bytes 208904 | tf_op jit(solution)/shard_map/ppermute | solution.py:405

commit v24 on v23

--- a/solution.py
+++ b/solution.py
@@ -176,7 +176,7 @@
     return jnp.concatenate([top, bottom], axis=0).astype(jnp.bfloat16)
 
 
-def triangle(blocks, groups, steps, vectors_at, factors_at, start_at, store_at, beside=None):
+def triangle(blocks, groups, steps, vectors_at, factors_at, start_at, store_at, beside=None, unrolled=False):
     def block(a):
         if beside is not None:
             beside(a)
@@ -213,8 +213,11 @@
         for g in range(groups):
             store_at(a, g, [totals[lane * groups + g] for lane in range(SUB)])
 
-    for a in range(blocks):
-        block(a)
+    if unrolled:
+        for a in range(blocks):
+            block(a)
+    else:
+        pl.loop(0, blocks)(block)
 
 
 def spread(ref, row):
@@ -378,8 +381,8 @@
         sum_ref[:, 2 * channels :] += jnp.dot(flip_ref[0, a], chunk(d_ref, a, 0, 2), preferred_element_type=f32)
 
     sum_ref[...] = jnp.zeros(sum_ref.shape, f32)
-    triangle(n_row, n_col, n_col, by_right, along, zero, store(0), early_sums)
-    triangle(n_row, n_col, n_row, by_left, down, zero, store(1), left_sums)
+    triangle(n_row, n_col, n_col, by_right, along, zero, store(0), early_sums, True)
+    triangle(n_row, n_col, n_row, by_left, down, zero, store(1), left_sums, True)
 
     scale = 1.0 / residues
     flipped = jnp.concatenate([flip_ref[0, col] for col in range(n_col)], axis=1)

time: 23.2 us -> 23 us (level)
  no operation moved by 1% of the time
where the time goes in v24:
time: 23 us; the launch traced here: 22.7 us
  starting transfers between devices  8.29 us (36%)
  Pallas kernels  7.48 us (33%)
  waiting for transfers between devices  4.76 us (21%)
  between operations  1.38 us (6%)
  local copies, waits for them, and re-layouts  0.79 us (3%)
    ppermute x9, starting transfers between devices, flip(): return lax.ppermute(block, ('row', 'col'), pairs)  8.29 us
    ppermute x9, waiting for transfers between devices, flip(): return lax.ppermute(block, ('row', 'col'), pairs)  4.76 us
    pallas_call x1, Pallas kernels, gathered_body(): pl.pallas_call(functools.partial(rest_kernel, n_row, n_col), name='rest',...  3.64 us
    pallas_call x2, Pallas kernels, gathered_body(): pl.pallas_call(functools.partial(columns_kernel, n_row, n_col, side_x, ch...  2.22 us
    pallas_call x1, Pallas kernels, gathered_body(): pl.pallas_call(pack_kernel, name='pack', out_shape=jax.ShapeDtypeStruct((...  1.6 us
    unnamed x10, local copies, waits for them, and re-layouts  0.79 us
  transfers between devices with their start and end apart: 9, of which 4 were waited for; matrix products, arithmetic and copies ran while one was open for 0% of the time, Pallas kernels for 5%

profile of v24, /device:TPU:0, one launch (start us, length us, event | category | flops | bytes accessed | tf_op | source)
XLA Modules:
  0.0 22.7 jit_solution(16019962751781193032)
XLA Ops:
  0.6 1.6 %pack.1.in_ref = bf16[144,128]{1,0:T(8,128)(2,1)} custom-call(bf16[8,8,128]{2,1,0:T(8,128)(2,1)} %refs_7_.1, s32[8,8]{1,0:T(8,128)} %mask_hbm.1, bf16[64,128]{1,0:T(8,128)(2,1)} %bitcast.6, f32[1,128]{1,0:T(1,128)} %bitcast.3), custom_call_target="tpu_custom_call" | custom-call | tf_op jit(solution)/shard_map/pack/pallas_call | solution.py:426
  2.2 0.0 copy-start
  2.2 0.5 %collective-permute-start = (bf16[144,128]{1,0:T(8,128)(2,1)}, bf16[144,128]{1,0:T(8,128)(2,1)S(1)}, u32[]{:S(2)}, u32[]{:S(2)}) collective-permute-start(bf16[144,128]{1,0:T(8,128)(2,1)} %pack.1.in_ref), channel_id=1, source_target_pairs={{0,1},{1,0},{2,3},{3,2},{4,5},{5,4},{6,7},{7,6},{8,9},{9,8},{10,11... | collective-permute-start | bytes 110600 | tf_op jit(solution)/shard_map/ppermute | solution.py:408
  2.8 0.0 copy-start.1
  2.8 0.8 %copy-done.1 = bf16[144,128]{1,0:T(8,128)(2,1)S(1)} copy-done((bf16[144,128]{1,0:T(8,128)(2,1)S(1)}, bf16[144,128]{1,0:T(8,128)(2,1)}, u32[]{:S(2)}) %copy-start.1) | copy-done | bytes 36888
  3.5 0.0 copy-start.2
  3.5 0.3 %collective-permute-done.twin_ref = bf16[144,128]{1,0:T(8,128)(2,1)S(1)} collective-permute-done((bf16[144,128]{1,0:T(8,128)(2,1)}, bf16[144,128]{1,0:T(8,128)(2,1)S(1)}, u32[]{:S(2)}, u32[]{:S(2)}) %collective-permute-start) | collective-permute-done | bytes 36896 | tf_op jit(solution)/shard_map/ppermute | solution.py:408
  3.9 3.9 %collective-permute-start.1 = (bf16[272,128]{1,0:T(8,128)(2,1)S(1)}, bf16[272,128]{1,0:T(8,128)(2,1)S(1)}, u32[]{:S(2)}, u32[]{:S(2)}) collective-permute-start(bf16[272,128]{1,0:T(8,128)(2,1)S(1)} %join.1.refs_0_), channel_id=1, source_target_pairs={{0,8},{1,5},{2,10},{3,7},{4,12},{5,1},{6,14},{7,3},{8,0},{9,13},{1... | collective-permute-start | bytes 208904 | tf_op jit(solution)/shard_map/ppermute | solution.py:408
  7.8 1.3 %collective-permute-start.3 = (bf16[144,128]{1,0:T(8,128)(2,1)S(1)}, bf16[144,128]{1,0:T(8,128)(2,1)S(1)}, u32[]{:S(2)}, u32[]{:S(2)}) collective-permute-start(bf16[144,128]{1,0:T(8,128)(2,1)S(1)} %copy-done.1), channel_id=1, source_target_pairs={{0,12},{1,13},{2,14},{3,15},{4,8},{5,9},{6,10},{7,11},{8,4},{9,5},... | collective-permute-start | bytes 110600 | tf_op jit(solution)/shard_map/ppermute | solution.py:408
  9.1 1.2 %collective-permute-start.7 = (bf16[272,128]{1,0:T(8,128)(2,1)S(1)}, bf16[272,128]{1,0:T(8,128)(2,1)S(1)}, u32[]{:S(2)}, u32[]{:S(2)}) collective-permute-start(bf16[272,128]{1,0:T(8,128)(2,1)S(1)} %join.1.refs_0_), channel_id=1, source_target_pairs={{0,6},{1,15},{2,4},{3,13},{4,2},{5,11},{6,0},{7,9},{8,14},{9,7},{1... | collective-permute-start | bytes 208904 | tf_op jit(solution)/shard_map/ppermute | solution.py:408
  10.3 0.5 %collective-permute-start.5 = (bf16[272,128]{1,0:T(8,128)(2,1)S(1)}, bf16[272,128]{1,0:T(8,128)(2,1)S(1)}, u32[]{:S(2)}, u32[]{:S(2)}) collective-permute-start(bf16[272,128]{1,0:T(8,128)(2,1)S(1)} %join.1.refs_0_), channel_id=1, source_target_pairs={{0,2},{1,11},{2,0},{3,9},{4,6},{5,15},{6,4},{7,13},{8,10},{9,3},{1... | collective-permute-start | bytes 208904 | tf_op jit(solution)/shard_map/ppermute | solution.py:408
  10.8 0.0 collective-permute-done.1.refs_1_.refs_3_
  10.8 0.5 %collective-permute-start.2 = (bf16[272,128]{1,0:T(8,128)(2,1)S(1)}, bf16[272,128]{1,0:T(8,128)(2,1)S(1)}, u32[]{:S(2)}, u32[]{:S(2)}) collective-permute-start(bf16[272,128]{1,0:T(8,128)(2,1)S(1)} %collective-permute-done.1.refs_1_.refs_3_), channel_id=1, source_target_pairs={{0,1},{1,0},{2,3},{3,2},{4,5},{5,4},{6,7},{7,6},{8,9},{9,8},{10,11... | collective-permute-start | bytes 208904 | tf_op jit(solution)/shard_map/ppermute | solution.py:408
  11.3 2.3 %collective-permute-done.3.refs_5_ = bf16[144,128]{1,0:T(8,128)(2,1)S(1)} collective-permute-done((bf16[144,128]{1,0:T(8,128)(2,1)S(1)}, bf16[144,128]{1,0:T(8,128)(2,1)S(1)}, u32[]{:S(2)}, u32[]{:S(2)}) %collective-permute-start.3) | collective-permute-done | bytes 36896 | tf_op jit(solution)/shard_map/ppermute | solution.py:408
  13.6 0.0 collective-permute-start.4
  14.3 0.0 copy-start.3
  14.3 0.0 copy-start.4
  14.3 1.5 %collective-permute-done.7.refs_2_.refs_6_ = bf16[272,128]{1,0:T(8,128)(2,1)S(1)} collective-permute-done((bf16[272,128]{1,0:T(8,128)(2,1)S(1)}, bf16[272,128]{1,0:T(8,128)(2,1)S(1)}, u32[]{:S(2)}, u32[]{:S(2)}) %collective-permute-start.7) | collective-permute-done | bytes 69664 | tf_op jit(solution)/shard_map/ppermute | solution.py:408
  15.8 0.0 collective-permute-start.8
  15.8 0.7 %collective-permute-done.5.refs_0_.refs_4_ = bf16[272,128]{1,0:T(8,128)(2,1)S(1)} collective-permute-done((bf16[272,128]{1,0:T(8,128)(2,1)S(1)}, bf16[272,128]{1,0:T(8,128)(2,1)S(1)}, u32[]{:S(2)}, u32[]{:S(2)}) %collective-permute-start.5) | collective-permute-done | bytes 69664 | tf_op jit(solution)/shard_map/ppermute | solution.py:408
  16.5 0.3 %collective-permute-start.6 = (bf16[272,128]{1,0:T(8,128)(2,1)S(1)}, bf16[272,128]{1,0:T(8,128)(2,1)S(1)}, u32[]{:S(2)}, u32[]{:S(2)}) collective-permute-start(bf16[272,128]{1,0:T(8,128)(2,1)S(1)} %collective-permute-done.5.refs_0_.refs_4_), channel_id=1, source_target_pairs={{0,1},{1,0},{2,3},{3,2},{4,5},{5,4},{6,7},{7,6},{8,9},{9,8},{10,11... | collective-permute-start | bytes 208904 | tf_op jit(solution)/shard_map/ppermute | solution.py:408
  16.7 0.0 collective-permute-done.4.refs_6_
  16.8 0.0 collective-permute-done.2.refs_2_.refs_4_
  16.8 0.0 copy-done
  16.8 0.0 copy-done.2
  16.8 0.0 copy-done.3
  16.8 0.0 copy-done.4
  16.8 1.1 %columns_0.1 = (f32[1024,128]{1,0:T(8,128)S(1)}, bf16[2,4,128,256]{3,2,1,0:T(8,128)(2,1)S(1)}, f32[512,128]{1,0:T(8,128)S(1)}, f32[512,128]{1,0:T(8,128)S(1)}, f...) custom-call(s32[1]{0:T(128)S(6)} %copy.14.crop_ref, ...), custom_call_target="tpu_custom_call" | custom-call | flops 800000000 | bytes 1000000 | tf_op jit(solution)/shard_map/columns_0/pallas_call | solution.py:481
  17.9 0.0 collective-permute-done.8.refs_3_.refs_7_
  17.9 0.0 collective-permute-done.6.refs_1_.refs_5_
  17.9 1.1 %columns_1.1 = (f32[1024,128]{1,0:T(8,128)S(1)}, bf16[2,4,128,256]{3,2,1,0:T(8,128)(2,1)S(1)}, f32[512,128]{1,0:T(8,128)S(1)}, f32[512,128]{1,0:T(8,128)S(1)}, f...) custom-call(s32[1]{0:T(128)S(6)} %copy.14.crop_ref, ...), custom_call_target="tpu_custom_call", output_to_operand_aliasing={{0}: (11, {}), {1}: (12, {})} | custom-call | flops 800000000 | bytes 1000000 | tf_op jit(solution)/shard_map/columns_1/pallas_call | solution.py:481
  19.1 3.6 %rest.1 = (bf16[8,8,128]{2,1,0:T(8,128)(2,1)}, bf16[8,8,128]{2,1,0:T(8,128)(2,1)}, f32[6,128,128]{2,1,0:T(8,128)}) custom-call(bf16[6,128,128]{2,1,0:T(8,128)(2,1)S(1)} %copy-done, f32[3,64,128]{2,1,0:T(8,128)S(1)} %get-tuple-element.21.own_ref, f32[8,128]{1,0:T(8,128)S(1)} %get-tuple-element.22.refs_8_.gains_ref, ...), custom_call_target="tpu_custom_call" | custom-call | tf_op jit(solution)/shard_map/rest/pallas_call | solution.py:503
  (2 shorter events, 0.0 us)
Async XLA Ops:
  2.2 14.5 %copy-start = (bf16[6,128,128]{2,1,0:T(8,128)(2,1)S(1)}, bf16[6,128,128]{2,1,0:T(8,128)(2,1)}, u32[]{:S(2)}) copy-start(bf16[6,128,128]{2,1,0:T(8,128)(2,1)} %weights_ref.5) | copy-start | bytes 589828
  2.2 1.6 %collective-permute-start = (bf16[144,128]{1,0:T(8,128)(2,1)}, bf16[144,128]{1,0:T(8,128)(2,1)S(1)}, u32[]{:S(2)}, u32[]{:S(2)}) collective-permute-start(bf16[144,128]{1,0:T(8,128)(2,1)} %pack.1.in_ref), channel_id=1, source_target_pairs={{0,1},{1,0},{2,3},{3,2},{4,5},{5,4},{6,7},{7,6},{8,9},{9,8},{10,11... | collective-permute-start | bytes 110600 | tf_op jit(solution)/shard_map/ppermute | solution.py:408
  2.8 0.8 %copy-start.1 = (bf16[144,128]{1,0:T(8,128)(2,1)S(1)}, bf16[144,128]{1,0:T(8,128)(2,1)}, u32[]{:S(2)}) copy-start(bf16[144,128]{1,0:T(8,128)(2,1)} %pack.1.in_ref) | copy-start | bytes 110596
  3.5 13.2 %copy-start.2 = (bf16[8,8,128]{2,1,0:T(8,128)(2,1)S(1)}, bf16[8,8,128]{2,1,0:T(8,128)(2,1)}, u32[]{:S(2)}) copy-start(bf16[8,8,128]{2,1,0:T(8,128)(2,1)} %refs_7_.1) | copy-start | bytes 49156
  3.9 7.0 %collective-permute-start.1 = (bf16[272,128]{1,0:T(8,128)(2,1)S(1)}, bf16[272,128]{1,0:T(8,128)(2,1)S(1)}, u32[]{:S(2)}, u32[]{:S(2)}) collective-permute-start(bf16[272,128]{1,0:T(8,128)(2,1)S(1)} %join.1.refs_0_), channel_id=1, source_target_pairs={{0,8},{1,5},{2,10},{3,7},{4,12},{5,1},{6,14},{7,3},{8,0},{9,13},{1... | collective-permute-start | bytes 208904 | tf_op jit(solution)/shard_map/ppermute | solution.py:408
  7.8 5.9 %collective-permute-start.3 = (bf16[144,128]{1,0:T(8,128)(2,1)S(1)}, bf16[144,128]{1,0:T(8,128)(2,1)S(1)}, u32[]{:S(2)}, u32[]{:S(2)}) collective-permute-start(bf16[144,128]{1,0:T(8,128)(2,1)S(1)} %copy-done.1), channel_id=1, source_target_pairs={{0,12},{1,13},{2,14},{3,15},{4,8},{5,9},{6,10},{7,11},{8,4},{9,5},... | collective-permute-start | bytes 110600 | tf_op jit(solution)/shard_map/ppermute | solution.py:408
  9.1 6.6 %collective-permute-start.7 = (bf16[272,128]{1,0:T(8,128)(2,1)S(1)}, bf16[272,128]{1,0:T(8,128)(2,1)S(1)}, u32[]{:S(2)}, u32[]{:S(2)}) collective-permute-start(bf16[272,128]{1,0:T(8,128)(2,1)S(1)} %join.1.refs_0_), channel_id=1, source_target_pairs={{0,6},{1,15},{2,4},{3,13},{4,2},{5,11},{6,0},{7,9},{8,14},{9,7},{1... | collective-permute-start | bytes 208904 | tf_op jit(solution)/shard_map/ppermute | solution.py:408
  10.3 6.2 %collective-permute-start.5 = (bf16[272,128]{1,0:T(8,128)(2,1)S(1)}, bf16[272,128]{1,0:T(8,128)(2,1)S(1)}, u32[]{:S(2)}, u32[]{:S(2)}) collective-permute-start(bf16[272,128]{1,0:T(8,128)(2,1)S(1)} %join.1.refs_0_), channel_id=1, source_target_pairs={{0,2},{1,11},{2,0},{3,9},{4,6},{5,15},{6,4},{7,13},{8,10},{9,3},{1... | collective-permute-start | bytes 208904 | tf_op jit(solution)/shard_map/ppermute | solution.py:408
  10.8 5.9 %collective-permute-start.2 = (bf16[272,128]{1,0:T(8,128)(2,1)S(1)}, bf16[272,128]{1,0:T(8,128)(2,1)S(1)}, u32[]{:S(2)}, u32[]{:S(2)}) collective-permute-start(bf16[272,128]{1,0:T(8,128)(2,1)S(1)} %collective-permute-done.1.refs_1_.refs_3_), channel_id=1, source_target_pairs={{0,1},{1,0},{2,3},{3,2},{4,5},{5,4},{6,7},{7,6},{8,9},{9,8},{10,11... | collective-permute-start | bytes 208904 | tf_op jit(solution)/shard_map/ppermute | solution.py:408
  13.6 3.1 %collective-permute-start.4 = (bf16[144,128]{1,0:T(8,128)(2,1)S(1)}, bf16[144,128]{1,0:T(8,128)(2,1)S(1)}, u32[]{:S(2)}, u32[]{:S(2)}) collective-permute-start(bf16[144,128]{1,0:T(8,128)(2,1)S(1)} %collective-permute-done.3.refs_5_), channel_id=1, source_target_pairs={{0,1},{1,0},{2,3},{3,2},{4,5},{5,4},{6,7},{7,6},{8,9},{9,8},{10,11... | collective-permute-start | bytes 110600 | tf_op jit(solution)/shard_map/ppermute | solution.py:408
  14.3 2.5 %copy-start.3 = (f32[128]{0:T(128)S(1)}, f32[128]{0:T(128)}, u32[]{:S(2)}) copy-start(f32[128]{0:T(128)} %param.11) | copy-start | bytes 1540
  14.3 2.5 %copy-start.4 = (f32[128]{0:T(128)S(1)}, f32[128]{0:T(128)}, u32[]{:S(2)}) copy-start(f32[128]{0:T(128)} %param.12) | copy-start | bytes 1540
  15.8 2.1 %collective-permute-start.8 = (bf16[272,128]{1,0:T(8,128)(2,1)S(1)}, bf16[272,128]{1,0:T(8,128)(2,1)S(1)}, u32[]{:S(2)}, u32[]{:S(2)}) collective-permute-start(bf16[272,128]{1,0:T(8,128)(2,1)S(1)} %collective-permute-done.7.refs_2_.refs_6_), channel_id=1, source_target_pairs={{0,1},{1,0},{2,3},{3,2},{4,5},{5,4},{6,7},{7,6},{8,9},{9,8},{10,11... | collective-permute-start | bytes 208904 | tf_op jit(solution)/shard_map/ppermute | solution.py:408
  16.5 1.5 %collective-permute-start.6 = (bf16[272,128]{1,0:T(8,128)(2,1)S(1)}, bf16[272,128]{1,0:T(8,128)(2,1)S(1)}, u32[]{:S(2)}, u32[]{:S(2)}) collective-permute-start(bf16[272,128]{1,0:T(8,128)(2,1)S(1)} %collective-permute-done.5.refs_0_.refs_4_), channel_id=1, source_target_pairs={{0,1},{1,0},{2,3},{3,2},{4,5},{5,4},{6,7},{7,6},{8,9},{9,8},{10,11... | collective-permute-start | bytes 208904 | tf_op jit(solution)/shard_map/ppermute | solution.py:408

commit v25 on v24

--- a/solution.py
+++ b/solution.py
@@ -107,8 +107,8 @@
 
 
 def pack_kernel(act_hbm, mask_hbm, cot_hbm, gain_hbm, out_ref, act_ref, mask_ref, gain_ref, sems):
-    tile_rows, tile_cols, channels = act_ref.shape
-    pairs = tile_rows * tile_cols
+    tile_rows, tile_cols = mask_ref.shape
+    pairs, channels = act_ref.shape
     head = out_ref.shape[0] - pairs
     pack_copies = [
         pltpu.make_async_copy(act_hbm, act_ref, sems.at[0]),
@@ -120,7 +120,7 @@
         copy.start()
     for copy in pack_copies:
         copy.wait()
-    z_hat, _ = normalize(act_ref[...].astype(jnp.float32).reshape(pairs, channels))
+    z_hat, _ = normalize(act_ref[...].astype(jnp.float32))
     out_ref[0:pairs] = (z_hat * gain_ref[...]).astype(jnp.bfloat16)
     keep = mask_ref[...].astype(jnp.float32)
     wide = jnp.concatenate([keep, jnp.zeros((tile_rows, channels - tile_cols), jnp.float32)], axis=1)
@@ -430,13 +430,13 @@
         in_specs=[hbm] * 4,
         out_specs=vmem,
         scratch_shapes=[
-            pltpu.VMEM(pair_act.shape, pair_act.dtype),
+            pltpu.VMEM((tile, channels), bf16),
             pltpu.VMEM(pair_mask.shape, jnp.int32),
             pltpu.VMEM((1, channels), f32),
             pltpu.SemaphoreType.DMA((4,)),
         ],
         compiler_params=limit(60),
-    )(pair_act, pair_mask, cotangent.reshape(tile, channels), in_gain)
+    )(pair_act.reshape(tile, channels), pair_mask, cotangent.reshape(tile, channels), in_gain)
     crop_length, own = lax.optimization_barrier((crop_length, own))
 
     def move(block, even, odd):

time: 23 us -> 23 us (level)
  no operation moved by 1% of the time
where the time goes in v25:
time: 23 us; the launch traced here: 22.7 us
  starting transfers between devices  8.29 us (36%)
  Pallas kernels  7.48 us (33%)
  waiting for transfers between devices  4.76 us (21%)
  between operations  1.38 us (6%)
  local copies, waits for them, and re-layouts  0.79 us (3%)
    ppermute x9, starting transfers between devices, flip(): return lax.ppermute(block, ('row', 'col'), pairs)  8.29 us
    ppermute x9, waiting for transfers between devices, flip(): return lax.ppermute(block, ('row', 'col'), pairs)  4.76 us
    pallas_call x1, Pallas kernels, gathered_body(): pl.pallas_call(functools.partial(rest_kernel, n_row, n_col), name='rest',...  3.64 us
    pallas_call x2, Pallas kernels, gathered_body(): pl.pallas_call(functools.partial(columns_kernel, n_row, n_col, side_x, ch...  2.22 us
    pallas_call x1, Pallas kernels, gathered_body(): pl.pallas_call(pack_kernel, name='pack', out_shape=jax.ShapeDtypeStruct((...  1.6 us
    unnamed x10, local copies, waits for them, and re-layouts  0.79 us
  transfers between devices with their start and end apart: 9, of which 4 were waited for; matrix products, arithmetic and copies ran while one was open for 0% of the time, Pallas kernels for 5%

profile of v25, /device:TPU:0, one launch (start us, length us, event | category | flops | bytes accessed | tf_op | source)
XLA Modules:
  0.0 22.7 jit_solution(16019962751781193032)
XLA Ops:
  0.6 1.6 %pack.1.in_ref = bf16[144,128]{1,0:T(8,128)(2,1)} custom-call(bf16[64,128]{1,0:T(8,128)(2,1)} %bitcast.4, s32[8,8]{1,0:T(8,128)} %mask_hbm.1, bf16[64,128]{1,0:T(8,128)(2,1)} %bitcast.8, f32[1,128]{1,0:T(1,128)} %bitcast.5), custom_call_target="tpu_custom_call" | custom-call | tf_op jit(solution)/shard_map/pack/pallas_call | solution.py:426
  2.2 0.0 copy-start
  2.2 0.5 %collective-permute-start = (bf16[144,128]{1,0:T(8,128)(2,1)}, bf16[144,128]{1,0:T(8,128)(2,1)S(1)}, u32[]{:S(2)}, u32[]{:S(2)}) collective-permute-start(bf16[144,128]{1,0:T(8,128)(2,1)} %pack.1.in_ref), channel_id=1, source_target_pairs={{0,1},{1,0},{2,3},{3,2},{4,5},{5,4},{6,7},{7,6},{8,9},{9,8},{10,11... | collective-permute-start | bytes 110600 | tf_op jit(solution)/shard_map/ppermute | solution.py:408
  2.8 0.0 copy-start.1
  2.8 0.8 %copy-done.1 = bf16[144,128]{1,0:T(8,128)(2,1)S(1)} copy-done((bf16[144,128]{1,0:T(8,128)(2,1)S(1)}, bf16[144,128]{1,0:T(8,128)(2,1)}, u32[]{:S(2)}) %copy-start.1) | copy-done | bytes 36888
  3.5 0.0 copy-start.2
  3.5 0.3 %collective-permute-done.twin_ref = bf16[144,128]{1,0:T(8,128)(2,1)S(1)} collective-permute-done((bf16[144,128]{1,0:T(8,128)(2,1)}, bf16[144,128]{1,0:T(8,128)(2,1)S(1)}, u32[]{:S(2)}, u32[]{:S(2)}) %collective-permute-start) | collective-permute-done | bytes 36896 | tf_op jit(solution)/shard_map/ppermute | solution.py:408
  3.9 3.9 %collective-permute-start.1 = (bf16[272,128]{1,0:T(8,128)(2,1)S(1)}, bf16[272,128]{1,0:T(8,128)(2,1)S(1)}, u32[]{:S(2)}, u32[]{:S(2)}) collective-permute-start(bf16[272,128]{1,0:T(8,128)(2,1)S(1)} %join.1.refs_0_), channel_id=1, source_target_pairs={{0,8},{1,5},{2,10},{3,7},{4,12},{5,1},{6,14},{7,3},{8,0},{9,13},{1... | collective-permute-start | bytes 208904 | tf_op jit(solution)/shard_map/ppermute | solution.py:408
  7.8 1.3 %collective-permute-start.3 = (bf16[144,128]{1,0:T(8,128)(2,1)S(1)}, bf16[144,128]{1,0:T(8,128)(2,1)S(1)}, u32[]{:S(2)}, u32[]{:S(2)}) collective-permute-start(bf16[144,128]{1,0:T(8,128)(2,1)S(1)} %copy-done.1), channel_id=1, source_target_pairs={{0,12},{1,13},{2,14},{3,15},{4,8},{5,9},{6,10},{7,11},{8,4},{9,5},... | collective-permute-start | bytes 110600 | tf_op jit(solution)/shard_map/ppermute | solution.py:408
  9.1 1.2 %collective-permute-start.7 = (bf16[272,128]{1,0:T(8,128)(2,1)S(1)}, bf16[272,128]{1,0:T(8,128)(2,1)S(1)}, u32[]{:S(2)}, u32[]{:S(2)}) collective-permute-start(bf16[272,128]{1,0:T(8,128)(2,1)S(1)} %join.1.refs_0_), channel_id=1, source_target_pairs={{0,6},{1,15},{2,4},{3,13},{4,2},{5,11},{6,0},{7,9},{8,14},{9,7},{1... | collective-permute-start | bytes 208904 | tf_op jit(solution)/shard_map/ppermute | solution.py:408
  10.3 0.5 %collective-permute-start.5 = (bf16[272,128]{1,0:T(8,128)(2,1)S(1)}, bf16[272,128]{1,0:T(8,128)(2,1)S(1)}, u32[]{:S(2)}, u32[]{:S(2)}) collective-permute-start(bf16[272,128]{1,0:T(8,128)(2,1)S(1)} %join.1.refs_0_), channel_id=1, source_target_pairs={{0,2},{1,11},{2,0},{3,9},{4,6},{5,15},{6,4},{7,13},{8,10},{9,3},{1... | collective-permute-start | bytes 208904 | tf_op jit(solution)/shard_map/ppermute | solution.py:408
  10.8 0.0 collective-permute-done.1.refs_1_.refs_3_
  10.8 0.5 %collective-permute-start.2 = (bf16[272,128]{1,0:T(8,128)(2,1)S(1)}, bf16[272,128]{1,0:T(8,128)(2,1)S(1)}, u32[]{:S(2)}, u32[]{:S(2)}) collective-permute-start(bf16[272,128]{1,0:T(8,128)(2,1)S(1)} %collective-permute-done.1.refs_1_.refs_3_), channel_id=1, source_target_pairs={{0,1},{1,0},{2,3},{3,2},{4,5},{5,4},{6,7},{7,6},{8,9},{9,8},{10,11... | collective-permute-start | bytes 208904 | tf_op jit(solution)/shard_map/ppermute | solution.py:408
  11.3 2.3 %collective-permute-done.3.refs_5_ = bf16[144,128]{1,0:T(8,128)(2,1)S(1)} collective-permute-done((bf16[144,128]{1,0:T(8,128)(2,1)S(1)}, bf16[144,128]{1,0:T(8,128)(2,1)S(1)}, u32[]{:S(2)}, u32[]{:S(2)}) %collective-permute-start.3) | collective-permute-done | bytes 36896 | tf_op jit(solution)/shard_map/ppermute | solution.py:408
  13.6 0.0 collective-permute-start.4
  14.3 0.0 copy-start.3
  14.3 0.0 copy-start.4
  14.3 1.5 %collective-permute-done.7.refs_2_.refs_6_ = bf16[272,128]{1,0:T(8,128)(2,1)S(1)} collective-permute-done((bf16[272,128]{1,0:T(8,128)(2,1)S(1)}, bf16[272,128]{1,0:T(8,128)(2,1)S(1)}, u32[]{:S(2)}, u32[]{:S(2)}) %collective-permute-start.7) | collective-permute-done | bytes 69664 | tf_op jit(solution)/shard_map/ppermute | solution.py:408
  15.8 0.0 collective-permute-start.8
  15.8 0.7 %collective-permute-done.5.refs_0_.refs_4_ = bf16[272,128]{1,0:T(8,128)(2,1)S(1)} collective-permute-done((bf16[272,128]{1,0:T(8,128)(2,1)S(1)}, bf16[272,128]{1,0:T(8,128)(2,1)S(1)}, u32[]{:S(2)}, u32[]{:S(2)}) %collective-permute-start.5) | collective-permute-done | bytes 69664 | tf_op jit(solution)/shard_map/ppermute | solution.py:408
  16.5 0.3 %collective-permute-start.6 = (bf16[272,128]{1,0:T(8,128)(2,1)S(1)}, bf16[272,128]{1,0:T(8,128)(2,1)S(1)}, u32[]{:S(2)}, u32[]{:S(2)}) collective-permute-start(bf16[272,128]{1,0:T(8,128)(2,1)S(1)} %collective-permute-done.5.refs_0_.refs_4_), channel_id=1, source_target_pairs={{0,1},{1,0},{2,3},{3,2},{4,5},{5,4},{6,7},{7,6},{8,9},{9,8},{10,11... | collective-permute-start | bytes 208904 | tf_op jit(solution)/shard_map/ppermute | solution.py:408
  16.7 0.0 collective-permute-done.4.refs_6_
  16.8 0.0 collective-permute-done.2.refs_2_.refs_4_
  16.8 0.0 copy-done
  16.8 0.0 copy-done.2
  16.8 0.0 copy-done.3
  16.8 0.0 copy-done.4
  16.8 1.1 %columns_0.1 = (f32[1024,128]{1,0:T(8,128)S(1)}, bf16[2,4,128,256]{3,2,1,0:T(8,128)(2,1)S(1)}, f32[512,128]{1,0:T(8,128)S(1)}, f32[512,128]{1,0:T(8,128)S(1)}, f...) custom-call(s32[1]{0:T(128)S(6)} %copy.14.crop_ref, ...), custom_call_target="tpu_custom_call" | custom-call | flops 800000000 | bytes 1000000 | tf_op jit(solution)/shard_map/columns_0/pallas_call | solution.py:481
  17.9 0.0 collective-permute-done.8.refs_3_.refs_7_
  17.9 0.0 collective-permute-done.6.refs_1_.refs_5_
  17.9 1.1 %columns_1.1 = (f32[1024,128]{1,0:T(8,128)S(1)}, bf16[2,4,128,256]{3,2,1,0:T(8,128)(2,1)S(1)}, f32[512,128]{1,0:T(8,128)S(1)}, f32[512,128]{1,0:T(8,128)S(1)}, f...) custom-call(s32[1]{0:T(128)S(6)} %copy.14.crop_ref, ...), custom_call_target="tpu_custom_call", output_to_operand_aliasing={{0}: (11, {}), {1}: (12, {})} | custom-call | flops 800000000 | bytes 1000000 | tf_op jit(solution)/shard_map/columns_1/pallas_call | solution.py:481
  19.1 3.6 %rest.1 = (bf16[8,8,128]{2,1,0:T(8,128)(2,1)}, bf16[8,8,128]{2,1,0:T(8,128)(2,1)}, f32[6,128,128]{2,1,0:T(8,128)}) custom-call(bf16[6,128,128]{2,1,0:T(8,128)(2,1)S(1)} %copy-done, f32[3,64,128]{2,1,0:T(8,128)S(1)} %get-tuple-element.21.own_ref, f32[8,128]{1,0:T(8,128)S(1)} %get-tuple-element.22.refs_8_.gains_ref, ...), custom_call_target="tpu_custom_call" | custom-call | tf_op jit(solution)/shard_map/rest/pallas_call | solution.py:503
  (2 shorter events, 0.0 us)
Async XLA Ops:
  2.2 14.5 %copy-start = (bf16[6,128,128]{2,1,0:T(8,128)(2,1)S(1)}, bf16[6,128,128]{2,1,0:T(8,128)(2,1)}, u32[]{:S(2)}) copy-start(bf16[6,128,128]{2,1,0:T(8,128)(2,1)} %weights_ref.5) | copy-start | bytes 589828
  2.2 1.6 %collective-permute-start = (bf16[144,128]{1,0:T(8,128)(2,1)}, bf16[144,128]{1,0:T(8,128)(2,1)S(1)}, u32[]{:S(2)}, u32[]{:S(2)}) collective-permute-start(bf16[144,128]{1,0:T(8,128)(2,1)} %pack.1.in_ref), channel_id=1, source_target_pairs={{0,1},{1,0},{2,3},{3,2},{4,5},{5,4},{6,7},{7,6},{8,9},{9,8},{10,11... | collective-permute-start | bytes 110600 | tf_op jit(solution)/shard_map/ppermute | solution.py:408
  2.8 0.8 %copy-start.1 = (bf16[144,128]{1,0:T(8,128)(2,1)S(1)}, bf16[144,128]{1,0:T(8,128)(2,1)}, u32[]{:S(2)}) copy-start(bf16[144,128]{1,0:T(8,128)(2,1)} %pack.1.in_ref) | copy-start | bytes 110596
  3.5 13.2 %copy-start.2 = (bf16[8,8,128]{2,1,0:T(8,128)(2,1)S(1)}, bf16[8,8,128]{2,1,0:T(8,128)(2,1)}, u32[]{:S(2)}) copy-start(bf16[8,8,128]{2,1,0:T(8,128)(2,1)} %refs_7_.1) | copy-start | bytes 49156
  3.9 7.0 %collective-permute-start.1 = (bf16[272,128]{1,0:T(8,128)(2,1)S(1)}, bf16[272,128]{1,0:T(8,128)(2,1)S(1)}, u32[]{:S(2)}, u32[]{:S(2)}) collective-permute-start(bf16[272,128]{1,0:T(8,128)(2,1)S(1)} %join.1.refs_0_), channel_id=1, source_target_pairs={{0,8},{1,5},{2,10},{3,7},{4,12},{5,1},{6,14},{7,3},{8,0},{9,13},{1... | collective-permute-start | bytes 208904 | tf_op jit(solution)/shard_map/ppermute | solution.py:408
  7.8 5.9 %collective-permute-start.3 = (bf16[144,128]{1,0:T(8,128)(2,1)S(1)}, bf16[144,128]{1,0:T(8,128)(2,1)S(1)}, u32[]{:S(2)}, u32[]{:S(2)}) collective-permute-start(bf16[144,128]{1,0:T(8,128)(2,1)S(1)} %copy-done.1), channel_id=1, source_target_pairs={{0,12},{1,13},{2,14},{3,15},{4,8},{5,9},{6,10},{7,11},{8,4},{9,5},... | collective-permute-start | bytes 110600 | tf_op jit(solution)/shard_map/ppermute | solution.py:408
  9.1 6.6 %collective-permute-start.7 = (bf16[272,128]{1,0:T(8,128)(2,1)S(1)}, bf16[272,128]{1,0:T(8,128)(2,1)S(1)}, u32[]{:S(2)}, u32[]{:S(2)}) collective-permute-start(bf16[272,128]{1,0:T(8,128)(2,1)S(1)} %join.1.refs_0_), channel_id=1, source_target_pairs={{0,6},{1,15},{2,4},{3,13},{4,2},{5,11},{6,0},{7,9},{8,14},{9,7},{1... | collective-permute-start | bytes 208904 | tf_op jit(solution)/shard_map/ppermute | solution.py:408
  10.3 6.2 %collective-permute-start.5 = (bf16[272,128]{1,0:T(8,128)(2,1)S(1)}, bf16[272,128]{1,0:T(8,128)(2,1)S(1)}, u32[]{:S(2)}, u32[]{:S(2)}) collective-permute-start(bf16[272,128]{1,0:T(8,128)(2,1)S(1)} %join.1.refs_0_), channel_id=1, source_target_pairs={{0,2},{1,11},{2,0},{3,9},{4,6},{5,15},{6,4},{7,13},{8,10},{9,3},{1... | collective-permute-start | bytes 208904 | tf_op jit(solution)/shard_map/ppermute | solution.py:408
  10.8 5.9 %collective-permute-start.2 = (bf16[272,128]{1,0:T(8,128)(2,1)S(1)}, bf16[272,128]{1,0:T(8,128)(2,1)S(1)}, u32[]{:S(2)}, u32[]{:S(2)}) collective-permute-start(bf16[272,128]{1,0:T(8,128)(2,1)S(1)} %collective-permute-done.1.refs_1_.refs_3_), channel_id=1, source_target_pairs={{0,1},{1,0},{2,3},{3,2},{4,5},{5,4},{6,7},{7,6},{8,9},{9,8},{10,11... | collective-permute-start | bytes 208904 | tf_op jit(solution)/shard_map/ppermute | solution.py:408
  13.6 3.1 %collective-permute-start.4 = (bf16[144,128]{1,0:T(8,128)(2,1)S(1)}, bf16[144,128]{1,0:T(8,128)(2,1)S(1)}, u32[]{:S(2)}, u32[]{:S(2)}) collective-permute-start(bf16[144,128]{1,0:T(8,128)(2,1)S(1)} %collective-permute-done.3.refs_5_), channel_id=1, source_target_pairs={{0,1},{1,0},{2,3},{3,2},{4,5},{5,4},{6,7},{7,6},{8,9},{9,8},{10,11... | collective-permute-start | bytes 110600 | tf_op jit(solution)/shard_map/ppermute | solution.py:408
  14.3 2.5 %copy-start.3 = (f32[128]{0:T(128)S(1)}, f32[128]{0:T(128)}, u32[]{:S(2)}) copy-start(f32[128]{0:T(128)} %param.11) | copy-start | bytes 1540
  14.3 2.5 %copy-start.4 = (f32[128]{0:T(128)S(1)}, f32[128]{0:T(128)}, u32[]{:S(2)}) copy-start(f32[128]{0:T(128)} %param.12) | copy-start | bytes 1540
  15.8 2.1 %collective-permute-start.8 = (bf16[272,128]{1,0:T(8,128)(2,1)S(1)}, bf16[272,128]{1,0:T(8,128)(2,1)S(1)}, u32[]{:S(2)}, u32[]{:S(2)}) collective-permute-start(bf16[272,128]{1,0:T(8,128)(2,1)S(1)} %collective-permute-done.7.refs_2_.refs_6_), channel_id=1, source_target_pairs={{0,1},{1,0},{2,3},{3,2},{4,5},{5,4},{6,7},{7,6},{8,9},{9,8},{10,11... | collective-permute-start | bytes 208904 | tf_op jit(solution)/shard_map/ppermute | solution.py:408
  16.5 1.5 %collective-permute-start.6 = (bf16[272,128]{1,0:T(8,128)(2,1)S(1)}, bf16[272,128]{1,0:T(8,128)(2,1)S(1)}, u32[]{:S(2)}, u32[]{:S(2)}) collective-permute-start(bf16[272,128]{1,0:T(8,128)(2,1)S(1)} %collective-permute-done.5.refs_0_.refs_4_), channel_id=1, source_target_pairs={{0,1},{1,0},{2,3},{3,2},{4,5},{5,4},{6,7},{7,6},{8,9},{9,8},{10,11... | collective-permute-start | bytes 208904 | tf_op jit(solution)/shard_map/ppermute | solution.py:408
